TPU v7x, 32 devices: a whole 2x2x4 slice. The times are simulated.
32 devices in a mesh: groups: 2 (over x), ctx: 8 (over z, y), head: 2 (over core).
Axes of the slice: x: 2, y: 2, z: 4, core: 2. Of those that a mesh axis runs over, the one named last changes fastest.
Arguments:
- q_nope: bfloat16 [2048, 8192], P(('groups', 'ctx'), 'head'), parts along dimension 0, may hold values from -6 to 6
- q_rope: bfloat16 [2048, 4096], P(('groups', 'ctx'), 'head'), parts along dimension 0, may hold values from -18 to 18
- latent_cache: bfloat16 [2304, 512], P(('groups', 'ctx')), parts along dimension 0, may hold values from -6 to 6
- rope_keys: bfloat16 [2304, 64], P(('groups', 'ctx')), parts along dimension 0, may hold values from -6 to 6
- w_absorb: bfloat16 [64, 128, 512], P('head'), may hold values from -0.5 to 0.5
- w_value: bfloat16 [64, 512, 128], P('head'), may hold values from -0.25 to 0.25
- w_output: bfloat16 [8192, 7168], P('head', 'ctx'), may hold values from -0.0625 to 0.0625
- span_offset: int32 [2], P('groups'), parts along dimension 0, may hold values from 0 to 128
- valid_lengths: int32 [16], P('groups'), parts along dimension 0, may hold values from 72 to 144, as said below
Outputs:
- mixed: bfloat16 [2048, 7168], P(('groups', 'head'), 'ctx'), parts along dimension 0
There are 2 independent parts, one for each index of `groups`. A program takes and returns all parts, laid end to end along the dimension named above; an argument that names none is the same for every part. Nothing has to cross between parts.
Inputs may be any that keep to these rules, and one draw needn't show every extreme that they name: `valid_lengths`: one shard of each part has exactly 144 valid rows.
All inputs are finite; a program needn't handle non-finite values.
Results may differ from a plain program's by a relative error of at most 0.009.
Values may be sent and summed in bfloat16 or wider, within the bound.
No kernel may reach another device: no remote copies, remote signals or barrier semaphores. Data moves between devices by JAX's collectives and lax.ppermute only.
A program may use at most 128 MiB of HBM per device.

v0:
```python
import math

import jax
import jax.numpy as jnp
from jax import lax
from jax.sharding import PartitionSpec as P


def local(
    q_nope, q_rope, latent_cache, rope_keys, w_absorb, w_value, w_output, span_offset, valid_lengths
):
    head_count = w_absorb.shape[0]
    tok_rows = q_nope.shape[0]
    nope_dim = w_absorb.shape[1]
    latent = w_absorb.shape[2]
    rope_dim = rope_keys.shape[1]
    per_shard = latent_cache.shape[0]
    shards = valid_lengths.shape[0]
    group_size = math.gcd(head_count, 8)
    blocks = head_count // group_size
    query_lat = jnp.einsum(
        "qhd,hdc->hqc",
        q_nope.reshape(tok_rows, head_count, nope_dim),
        w_absorb,
        preferred_element_type=jnp.float32,
    ).astype(jnp.bfloat16)
    query_lat = query_lat.reshape(blocks, group_size, tok_rows, latent)
    query_rot = q_rope.reshape(tok_rows, head_count, rope_dim).transpose(1, 0, 2)
    query_rot = query_rot.reshape(blocks, group_size, tok_rows, rope_dim)
    positions = (
        span_offset[0] + lax.axis_index("ctx") * tok_rows + jnp.arange(tok_rows, dtype=jnp.int32)
    )
    score_scale = 1.0 / math.sqrt(nope_dim + rope_dim)

    def block_scores(query_block, rot_block, cache_rows, rope_rows, visible):
        scores = (
            jnp.einsum("hqc,kc->hqk", query_block, cache_rows, preferred_element_type=jnp.float32)
            + jnp.einsum("hqr,kr->hqk", rot_block, rope_rows, preferred_element_type=jnp.float32)
        ) * score_scale
        return jnp.where(visible[None], scores, jnp.float32(-1e30))

    cache_all, rope_all = (
        lax.all_gather(latent_cache, "ctx", axis=0, tiled=True),
        lax.all_gather(rope_keys, "ctx", axis=0, tiled=True),
    )
    key_index = jnp.arange(cache_all.shape[0], dtype=jnp.int32)
    owner_shard = key_index // per_shard
    match = owner_shard[:, None] == jnp.arange(shards, dtype=jnp.int32)[None, :]
    shard_limit = jnp.sum(jnp.where(match, valid_lengths[None, :], 0), axis=1)
    inside = key_index - owner_shard * per_shard < shard_limit
    visible = inside[None, :] & (key_index[None, :] <= positions[:, None])

    def attend(operands):
        query_block, rot_block = operands
        scores = block_scores(query_block, rot_block, cache_all, rope_all, visible)
        row_max = jnp.max(scores, axis=-1, keepdims=True)
        expo = jnp.where(visible[None], jnp.exp(scores - row_max), jnp.float32(0.0))
        row_total = jnp.sum(expo, axis=-1, keepdims=True)
        weighted = jnp.einsum(
            "hqk,kc->hqc", expo.astype(jnp.bfloat16), cache_all, preferred_element_type=jnp.float32
        )
        return (weighted / row_total).astype(jnp.bfloat16)

    latent_out = lax.map(attend, (query_lat, query_rot))
    value_maps = w_value.reshape(blocks, group_size, latent, w_value.shape[2])
    head_out = jnp.einsum(
        "ghqc,ghcv->qghv", latent_out, value_maps, preferred_element_type=jnp.float32
    )
    head_out = head_out.astype(jnp.bfloat16).reshape(tok_rows, head_count * w_value.shape[2])
    partial_value = jnp.dot(
        lax.all_gather(head_out, "ctx", axis=0, tiled=True),
        w_output,
        preferred_element_type=jnp.float32,
    )
    return lax.psum_scatter(
        partial_value.astype(jnp.bfloat16), "head", scatter_dimension=0, tiled=True
    )


def solution(mesh):
    return jax.shard_map(
        local,
        mesh=mesh,
        in_specs=(
            P(("groups", "ctx"), "head"),
            P(("groups", "ctx"), "head"),
            P(("groups", "ctx"), None),
            P(("groups", "ctx"), None),
            P("head", None, None),
            P("head", None, None),
            P("head", "ctx"),
            P("groups"),
            P("groups"),
        ),
        out_specs=P(("groups", "head"), "ctx"),
        check_vma=False,
    )
```

profile of v0, /device:TPU:0, one launch (start us, length us, event | category | flops | bytes accessed | tf_op | source)
XLA Modules:
  0.0 269.9 jit_solution(9985000256230401427)
XLA Ops:
  6.5 0.7 all-gather.4.cloned.1.call-update
  7.3 0.0 all-gather.6.cloned.1.call-start
  7.3 33.1 %all-gather = bf16[8,144,64]{1,2,0:T(8,128)(2,1)S(1)} all-gather(bf16[1,144,64]{1,2,0:T(8,128)(2,1)} %bitcast.68), channel_id=1, replica_groups=mesh['groups'=2,'ctx'=8,'head'=2] {'ctx'}, dimensions={0}, use_global_device_ids=true | all-gather | bytes 165888 | tf_op jit(solution)/shard_map/all_gather | solution.py:44
  40.4 0.1 copy.27
  40.5 0.3 reshape.65
  40.8 1.3 copy.26
  42.8 0.7 select_reduce_fusion
  43.6 5.5 %convolution_convert_fusion = bf16[32,128,512]{2,1,0:T(8,128)(2,1)} fusion(bf16[32,128,512]{2,1,0:T(8,128)(2,1)} %param.15, bf16[128,4096]{1,0:T(8,128)(2,1)S(1)} %copy-done), kind=kOutput, calls=%fused_computation.24 | convolution fusion | flops 538968064 | bytes 9437184 | tf_op jit(solution)/shard_map/qhd,hdc->hqc/dot_general | solution.py:21
  49.0 4.7 %all-gather.4.cloned.1.call-done = bf16[1152,512]{1,0:T(8,128)(2,1)} async-done(((bf16[144,512]{1,0:T(8,128)(2,1)}), bf16[1152,512]{1,0:T(8,128)(2,1)}) %all-gather.4.cloned.1.call-update) | async-done | bytes 1179664 | tf_op jit(solution)/shard_map/all_gather | solution.py:43
  53.7 57.4 %while.11 = (s32[]{:T(128)}, bf16[4,8,128,512]{3,2,1,0:T(8,128)(2,1)}, bf16[4,8,128,512]{3,2,1,0:T(8,128)(2,1)}, bf16[1152,512]{1,0:T(8,128)(2,1)}, bf16[4,8,128...) while((s32[]{:T(128)}, ...), condition=%wide.region_4.5_spmd.clone, body=%wide.region_1.4_spmd.clone.sunk | while | flops 2576516096 | bytes 24062716 | solution.py:64
  53.7 2.9 %fusion.62 = f32[8,128,1152]{2,1,0:T(8,128)} fusion(bf16[1152,64]{0,1:T(8,128)(2,1)S(1)} %get-tuple-element.159, bf16[4,8,128,64]{2,3,1,0:T(8,128)(2,1)S(1)} %get-tuple-element.158, s32[]{:T(128)} %get-tuple-element.145), kind=kOutput, calls=%fused_computation.18.clone.1 | convolution fusion | flops 150994944 | bytes 4997124 | tf_op jit(solution)/shard_map/while/body/eval_jaxpr/hqr,kr->hqk/dot_general | solution.py:38
  56.6 0.2 fusion.61
  56.8 7.1 %fusion.63 = (f32[8,128]{1,0:T(8,128)S(1)}, bf16[8,128,1152]{2,1,0:T(8,128)(2,1)}) fusion(pred[128,1152]{1,0:T(8,128)(4,1)S(1)} %fusion.61, f32[8,128,1152]{2,1,0:T(8,128)} %fusion.62, bf16[1152,512]{1,0:T(8,128)(2,1)S(1)} %copy-done.1, bf16[4,8,128,512]{3,2,1,0:T(8,128)(2,1)} %get-tuple-element.156, s32[]{:T(128)} %get-tuple-element.145), kind=kOutput, calls=%fused_computation.41.clone.1 | convolution fusion | flops 1216218240 | bytes 9605632 | tf_op jit(solution)/shard_map/while/body/eval_jaxpr/sub | solution.py:57
  63.9 4.2 %fusion.64 = bf16[4,8,128,512]{3,2,1,0:T(8,128)(2,1)} fusion(bf16[4,8,128,512]{3,2,1,0:T(8,128)(2,1)} %get-tuple-element.146, s32[]{:T(128)} %get-tuple-element.145, bf16[8,128,1152]{2,1,0:T(8,128)(2,1)} %get-tuple-element.134, bf16[1152,512]{1,0:T(8,128)(2,1)S(1)} %copy-done.1, f32[8,128]{1,0:T(8,128)S(1)} %get-tuple-element.135), kind=kOutput, calls=%fused_computation.11.clone.1 | convolution fusion | flops 1209008128 | bytes 4592128 | tf_op jit(solution)/shard_map/while/body/eval_jaxpr/hqk,kc->hqc/dot_general | solution.py:59
  68.1 2.9 %fusion.62 = f32[8,128,1152]{2,1,0:T(8,128)} fusion(bf16[1152,64]{0,1:T(8,128)(2,1)S(1)} %get-tuple-element.159, bf16[4,8,128,64]{2,3,1,0:T(8,128)(2,1)S(1)} %get-tuple-element.158, s32[]{:T(128)} %get-tuple-element.145), kind=kOutput, calls=%fused_computation.18.clone.1 | convolution fusion | flops 150994944 | bytes 4997124 | tf_op jit(solution)/shard_map/while/body/eval_jaxpr/hqr,kr->hqk/dot_general | solution.py:38
  71.0 0.2 fusion.61
  71.2 7.1 %fusion.63 = (f32[8,128]{1,0:T(8,128)S(1)}, bf16[8,128,1152]{2,1,0:T(8,128)(2,1)}) fusion(pred[128,1152]{1,0:T(8,128)(4,1)S(1)} %fusion.61, f32[8,128,1152]{2,1,0:T(8,128)} %fusion.62, bf16[1152,512]{1,0:T(8,128)(2,1)S(1)} %copy-done.1, bf16[4,8,128,512]{3,2,1,0:T(8,128)(2,1)} %get-tuple-element.156, s32[]{:T(128)} %get-tuple-element.145), kind=kOutput, calls=%fused_computation.41.clone.1 | convolution fusion | flops 1216218240 | bytes 9605632 | tf_op jit(solution)/shard_map/while/body/eval_jaxpr/sub | solution.py:57
  78.2 4.2 %fusion.64 = bf16[4,8,128,512]{3,2,1,0:T(8,128)(2,1)} fusion(bf16[4,8,128,512]{3,2,1,0:T(8,128)(2,1)} %get-tuple-element.146, s32[]{:T(128)} %get-tuple-element.145, bf16[8,128,1152]{2,1,0:T(8,128)(2,1)} %get-tuple-element.134, bf16[1152,512]{1,0:T(8,128)(2,1)S(1)} %copy-done.1, f32[8,128]{1,0:T(8,128)S(1)} %get-tuple-element.135), kind=kOutput, calls=%fused_computation.11.clone.1 | convolution fusion | flops 1209008128 | bytes 4592128 | tf_op jit(solution)/shard_map/while/body/eval_jaxpr/hqk,kc->hqc/dot_general | solution.py:59
  82.4 2.9 %fusion.62 = f32[8,128,1152]{2,1,0:T(8,128)} fusion(bf16[1152,64]{0,1:T(8,128)(2,1)S(1)} %get-tuple-element.159, bf16[4,8,128,64]{2,3,1,0:T(8,128)(2,1)S(1)} %get-tuple-element.158, s32[]{:T(128)} %get-tuple-element.145), kind=kOutput, calls=%fused_computation.18.clone.1 | convolution fusion | flops 150994944 | bytes 4997124 | tf_op jit(solution)/shard_map/while/body/eval_jaxpr/hqr,kr->hqk/dot_general | solution.py:38
  85.4 0.2 fusion.61
  85.5 7.1 %fusion.63 = (f32[8,128]{1,0:T(8,128)S(1)}, bf16[8,128,1152]{2,1,0:T(8,128)(2,1)}) fusion(pred[128,1152]{1,0:T(8,128)(4,1)S(1)} %fusion.61, f32[8,128,1152]{2,1,0:T(8,128)} %fusion.62, bf16[1152,512]{1,0:T(8,128)(2,1)S(1)} %copy-done.1, bf16[4,8,128,512]{3,2,1,0:T(8,128)(2,1)} %get-tuple-element.156, s32[]{:T(128)} %get-tuple-element.145), kind=kOutput, calls=%fused_computation.41.clone.1 | convolution fusion | flops 1216218240 | bytes 9605632 | tf_op jit(solution)/shard_map/while/body/eval_jaxpr/sub | solution.py:57
  92.6 4.2 %fusion.64 = bf16[4,8,128,512]{3,2,1,0:T(8,128)(2,1)} fusion(bf16[4,8,128,512]{3,2,1,0:T(8,128)(2,1)} %get-tuple-element.146, s32[]{:T(128)} %get-tuple-element.145, bf16[8,128,1152]{2,1,0:T(8,128)(2,1)} %get-tuple-element.134, bf16[1152,512]{1,0:T(8,128)(2,1)S(1)} %copy-done.1, f32[8,128]{1,0:T(8,128)S(1)} %get-tuple-element.135), kind=kOutput, calls=%fused_computation.11.clone.1 | convolution fusion | flops 1209008128 | bytes 4592128 | tf_op jit(solution)/shard_map/while/body/eval_jaxpr/hqk,kc->hqc/dot_general | solution.py:59
  96.7 2.9 %fusion.62 = f32[8,128,1152]{2,1,0:T(8,128)} fusion(bf16[1152,64]{0,1:T(8,128)(2,1)S(1)} %get-tuple-element.159, bf16[4,8,128,64]{2,3,1,0:T(8,128)(2,1)S(1)} %get-tuple-element.158, s32[]{:T(128)} %get-tuple-element.145), kind=kOutput, calls=%fused_computation.18.clone.1 | convolution fusion | flops 150994944 | bytes 4997124 | tf_op jit(solution)/shard_map/while/body/eval_jaxpr/hqr,kr->hqk/dot_general | solution.py:38
  99.7 0.2 fusion.61
  99.8 7.0 %fusion.63 = (f32[8,128]{1,0:T(8,128)S(1)}, bf16[8,128,1152]{2,1,0:T(8,128)(2,1)}) fusion(pred[128,1152]{1,0:T(8,128)(4,1)S(1)} %fusion.61, f32[8,128,1152]{2,1,0:T(8,128)} %fusion.62, bf16[1152,512]{1,0:T(8,128)(2,1)S(1)} %copy-done.1, bf16[4,8,128,512]{3,2,1,0:T(8,128)(2,1)} %get-tuple-element.156, s32[]{:T(128)} %get-tuple-element.145), kind=kOutput, calls=%fused_computation.41.clone.1 | convolution fusion | flops 1216218240 | bytes 9605632 | tf_op jit(solution)/shard_map/while/body/eval_jaxpr/sub | solution.py:57
  106.9 4.2 %fusion.64 = bf16[4,8,128,512]{3,2,1,0:T(8,128)(2,1)} fusion(bf16[4,8,128,512]{3,2,1,0:T(8,128)(2,1)} %get-tuple-element.146, s32[]{:T(128)} %get-tuple-element.145, bf16[8,128,1152]{2,1,0:T(8,128)(2,1)} %get-tuple-element.134, bf16[1152,512]{1,0:T(8,128)(2,1)S(1)} %copy-done.1, f32[8,128]{1,0:T(8,128)S(1)} %get-tuple-element.135), kind=kOutput, calls=%fused_computation.11.clone.1 | convolution fusion | flops 1209008128 | bytes 4592128 | tf_op jit(solution)/shard_map/while/body/eval_jaxpr/hqk,kc->hqc/dot_general | solution.py:59
  111.1 5.8 %convolution_convert_fusion.2 = bf16[4,8,128,128]{2,3,1,0:T(8,128)(2,1)} fusion(bf16[4,8,128,512]{3,2,1,0:T(8,128)(2,1)} %get-tuple-element.42, bf16[4,8,512,128]{3,2,1,0:T(8,128)(2,1)} %bitcast.65), kind=kOutput, calls=%fused_computation.26 | convolution fusion | flops 537395200 | bytes 9437184 | tf_op jit(solution)/shard_map/ghqc,ghcv->qghv/dot_general | solution.py:66
  116.8 0.0 all-gather.6.cloned.1.call-update
  116.9 0.0 reduce-scatter.2.cloned.1.call-start
  116.9 124.4 %all-gather.6.cloned.1.call-done = bf16[1024,4096]{0,1:T(8,128)(2,1)} async-done(((bf16[128,4096]{0,1:T(8,128)(2,1)}), bf16[1024,4096]{0,1:T(8,128)(2,1)}) %all-gather.6.cloned.1.call-update) | async-done | bytes 8388624 | tf_op jit(solution)/shard_map/all_gather | solution.py:71
  241.3 14.3 %convolution_convert_fusion.1 = bf16[1024,896]{1,0:T(8,128)(2,1)} fusion(bf16[1024,4096]{0,1:T(8,128)(2,1)} %all-gather.6.cloned.1.call-done, bf16[4096,896]{1,0:T(8,128)(2,1)} %param.17), kind=kOutput, calls=%fused_computation.25 | convolution fusion | flops 7517110272 | bytes 17563648 | tf_op jit(solution)/shard_map/dot_general | solution.py:70
  255.7 7.7 %reduce-scatter.2.cloned.1.call-done = bf16[512,896]{1,0:T(8,128)(2,1)} async-done(((bf16[1024,896]{1,0:T(8,128)(2,1)}), bf16[512,896]{1,0:T(8,128)(2,1)}) %reduce-scatter.2.cloned.1.call-update) | async-done | bytes 917520 | tf_op jit(solution)/shard_map/reduce_scatter | solution.py:75
  (16 shorter events, 0.1 us)
Async XLA Ops:
  6.5 37.0 %copy-start = (bf16[128,4096]{1,0:T(8,128)(2,1)S(1)}, bf16[128,4096]{1,0:T(8,128)(2,1)}, u32[]{:S(2)}) copy-start(bf16[128,4096]{1,0:T(8,128)(2,1)} %param.11) | copy-start | bytes 3145732
  6.5 47.2 %all-gather.4.cloned.1.call-start = ((), (), s32[]{:S(2)}) async-start(), calls=%async_computation.1 | async-start | bytes 1327104 | tf_op jit(solution)/shard_map/all_gather | solution.py:43
  7.3 234.1 %all-gather.6.cloned.1.call-start = ((), (), s32[]{:S(2)}) async-start(), calls=%async_computation.2 | async-start | bytes 9437184 | tf_op jit(solution)/shard_map/all_gather | solution.py:71
  53.7 3.1 %copy-start.1 = (bf16[1152,512]{1,0:T(8,128)(2,1)S(1)}, bf16[1152,512]{1,0:T(8,128)(2,1)}, u32[]{:S(2)}) copy-start(bf16[1152,512]{1,0:T(8,128)(2,1)} %get-tuple-element.157) | copy-start | bytes 3538948 | tf_op jit(solution)/shard_map/while
  68.1 3.1 %copy-start.1 = (bf16[1152,512]{1,0:T(8,128)(2,1)S(1)}, bf16[1152,512]{1,0:T(8,128)(2,1)}, u32[]{:S(2)}) copy-start(bf16[1152,512]{1,0:T(8,128)(2,1)} %get-tuple-element.157) | copy-start | bytes 3538948 | tf_op jit(solution)/shard_map/while
  82.4 3.1 %copy-start.1 = (bf16[1152,512]{1,0:T(8,128)(2,1)S(1)}, bf16[1152,512]{1,0:T(8,128)(2,1)}, u32[]{:S(2)}) copy-start(bf16[1152,512]{1,0:T(8,128)(2,1)} %get-tuple-element.157) | copy-start | bytes 3538948 | tf_op jit(solution)/shard_map/while
  96.7 3.1 %copy-start.1 = (bf16[1152,512]{1,0:T(8,128)(2,1)S(1)}, bf16[1152,512]{1,0:T(8,128)(2,1)}, u32[]{:S(2)}) copy-start(bf16[1152,512]{1,0:T(8,128)(2,1)} %get-tuple-element.157) | copy-start | bytes 3538948 | tf_op jit(solution)/shard_map/while
  116.9 146.5 %reduce-scatter.2.cloned.1.call-start = ((), (), s32[]{:S(2)}) async-start(), calls=%async_computation.3 | async-start | bytes 2752512 | tf_op jit(solution)/shard_map/reduce_scatter | solution.py:75
Sparse Core Ops, SparseCore 0:
  9.5 44.1 all-gather.3
  117.0 124.2 all-gather.5
  255.8 7.5 reduce-scatter.1
where the time goes:
time: 270 us
  waiting for transfers between devices  138 us (51%)
  matrix products  82.2 us (30%)
  blocking collectives  33.1 us (12%)
  between operations  13.8 us (5%)
    all_gather x1, waiting for transfers between devices, local(): lax.all_gather(head_out, 'ctx', axis=0, tiled=True)  124 us
    all_gather x1, blocking collectives, local(): lax.all_gather(rope_keys, 'ctx', axis=0, tiled=True)  33.1 us
    sub x4, matrix products, attend(): expo = jnp.where(visible[None], jnp.exp(scores - row_max), jnp.float32(0.0))  28.2 us
    dot_general x4, matrix products, attend(): jnp.einsum('hqk,kc->hqc', expo.astype(jnp.bfloat16), cache_all, preferred...  16.7 us
    dot_general x1, matrix products, local(): jnp.dot(lax.all_gather(head_out, 'ctx', axis=0, tiled=True), w_output, pr...  14.3 us
    dot_general x4, matrix products, block_scores(): jnp.einsum('hqr,kr->hqk', rot_block, rope_rows, preferred_element_type=jn...  11.7 us
    reduce_scatter x1, waiting for transfers between devices, local(): lax.psum_scatter(partial_value.astype(jnp.bfloat16), 'head', scatter_dime...  7.69 us
    dot_general x1, matrix products, local(): jnp.einsum('ghqc,ghcv->qghv', latent_out, value_maps, preferred_element_t...  5.77 us
  transfers between devices with their start and end apart: 3, of which 3 were waited for; matrix products, arithmetic and copies ran while one was open for 3% of the time, Pallas kernels for 0%

commit v1 on v0

v1 whole, which is shorter than its diff:
```python
import functools
import math

import jax
import jax.numpy as jnp
from jax import lax
from jax.experimental import pallas as pl
from jax.experimental.pallas import tpu as pltpu
from jax.sharding import PartitionSpec as P

F32 = jnp.float32
BF16 = jnp.bfloat16
MASKED = -1e30
CHUNKS = 8


def params(mib):
    return pltpu.CompilerParams(vmem_limit_bytes=mib * 1024 * 1024)


def basis_of(shards):
    if shards == 8:
        return (6, 2, 1)
    return tuple(1 << bit for bit in reversed(range(shards.bit_length() - 1)))


def exchange(x, mask, shards):
    return lax.ppermute(x, "ctx", [(i, i ^ mask) for i in range(shards)])


def spread(x, shards):
    blocks = {0: x}
    for mask in basis_of(shards):
        blocks.update({key ^ mask: exchange(block, mask, shards) for key, block in blocks.items()})
    return blocks


def prep_kernel(heads, nope, rope, per_shard, order, limits, base, q_ref, r_ref, w_ref, lat_ref, bias_ref):
    tokens = q_ref.shape[0]
    latent = w_ref.shape[2]
    for head in range(heads):
        rows = slice(head * tokens, (head + 1) * tokens)
        lat = jnp.dot(
            q_ref[:, head * nope : (head + 1) * nope], w_ref[head], preferred_element_type=F32
        )
        lat_ref[rows, :latent] = lat.astype(BF16)
        lat_ref[rows, latent:] = r_ref[:, head * rope : (head + 1) * rope]

    @pl.when(pl.program_id(0) == 0)
    def _():
        keys = bias_ref.shape[1]
        column = lax.broadcasted_iota(jnp.int32, (1, keys), 1)
        place = jnp.full((1, keys), 2**30, jnp.int32)
        for at in range(keys // per_shard):
            inner = column - at * per_shard
            mine = (inner >= 0) & (inner < limits[at])
            place = jnp.where(mine, inner + order[at] * per_shard, place)
        position = base[0] + lax.broadcasted_iota(jnp.int32, bias_ref.shape, 0)
        bias_ref[...] = jnp.where(place <= position, F32(0.0), F32(MASKED))


def prep(q_nope, q_rope, w_absorb, order, limits, base, per_shard):
    heads, nope, latent = w_absorb.shape
    tokens = q_nope.shape[0]
    rope = q_rope.shape[1] // heads
    step = 4
    keys = per_shard * order.shape[0]
    smem = pl.BlockSpec(memory_space=pltpu.SMEM)
    return pl.pallas_call(
        functools.partial(prep_kernel, step, nope, rope, per_shard),
        grid=(heads // step,),
        in_specs=[
            smem,
            smem,
            smem,
            pl.BlockSpec((tokens, step * nope), lambda i: (0, i)),
            pl.BlockSpec((tokens, step * rope), lambda i: (0, i)),
            pl.BlockSpec((step, nope, latent), lambda i: (i, 0, 0)),
        ],
        out_specs=[
            pl.BlockSpec((step * tokens, latent + rope), lambda i: (i, 0)),
            pl.BlockSpec((tokens, keys), lambda i: (0, 0)),
        ],
        out_shape=[
            jax.ShapeDtypeStruct((heads * tokens, latent + rope), BF16),
            jax.ShapeDtypeStruct((tokens, keys), F32),
        ],
        compiler_params=params(32),
        cost_estimate=pl.CostEstimate(
            flops=2 * heads * tokens * nope * latent, bytes_accessed=12 << 20, transcendentals=0
        ),
        name="prep",
    )(order, limits, base, q_nope, q_rope, w_absorb)


def attend_kernel(heads, shards, scale, *refs):
    q_ref, bias_ref, w_ref = refs[:3]
    parts = refs[3 : 3 + shards]
    out_ref, kv, scores, probs, total, sem = refs[3 + shards :]
    tokens = bias_ref.shape[0]
    per_shard = parts[0].shape[0]
    latent, value = w_ref.shape[1:]
    copies = [
        pltpu.make_async_copy(part, kv.at[pl.ds(at * per_shard, per_shard)], sem.at[at])
        for at, part in enumerate(parts)
    ]
    for copy in copies:
        copy.start()
    for copy in copies:
        copy.wait()
    scores[...] = lax.dot_general(
        q_ref[...], kv[...], (((1,), (1,)), ((), ())), preferred_element_type=F32
    )
    for head in range(heads):
        rows = slice(head * tokens, (head + 1) * tokens)
        masked = scores[rows, :] + bias_ref[...]
        top = jnp.max(masked, axis=-1, keepdims=True)
        expo = jnp.exp2((masked - top) * F32(scale))
        total[rows, :] = jnp.sum(expo, axis=-1, keepdims=True)
        probs[rows, :] = expo.astype(BF16)
    weighted = jnp.dot(probs[...], kv[:, :latent], preferred_element_type=F32)
    mixed = (weighted / total[...]).astype(BF16)
    for head in range(heads):
        rows = slice(head * tokens, (head + 1) * tokens)
        out = jnp.dot(mixed[rows, :], w_ref[head], preferred_element_type=F32)
        out_ref[:, head * value : (head + 1) * value] = out.astype(BF16)


def attend(chunk, heads, queries, bias, w_value, parts, scale):
    tokens, keys = bias.shape
    depth = queries.shape[1]
    _, latent, value = w_value.shape
    shards = len(parts)
    rows = heads * tokens
    return pl.pallas_call(
        functools.partial(attend_kernel, heads, shards, scale * math.log2(math.e)),
        grid=(1,),
        in_specs=[
            pl.BlockSpec((rows, depth), lambda i: (chunk, 0)),
            pl.BlockSpec((tokens, keys), lambda i: (0, 0)),
            pl.BlockSpec((heads, latent, value), lambda i: (chunk, 0, 0)),
        ]
        + [pl.BlockSpec(memory_space=pl.ANY)] * shards,
        out_specs=pl.BlockSpec((tokens, heads * value), lambda i: (0, 0)),
        out_shape=jax.ShapeDtypeStruct((tokens, heads * value), BF16),
        scratch_shapes=[
            pltpu.VMEM((keys, depth), BF16),
            pltpu.VMEM((rows, keys), F32),
            pltpu.VMEM((rows, keys), BF16),
            pltpu.VMEM((rows, 1), F32),
            pltpu.SemaphoreType.DMA((shards,)),
        ],
        compiler_params=params(40),
        cost_estimate=pl.CostEstimate(
            flops=2 * rows * (keys * (depth + latent) + latent * value),
            bytes_accessed=4 << 20,
            transcendentals=rows * keys,
        ),
        name=f"attend{chunk}",
    )(queries, bias, w_value, *parts)


def project_kernel(shards, first, *refs):
    w_ref = refs[0]
    parts = refs[1 : 1 + shards]
    refs = refs[1 + shards :]
    if first:
        out_ref, gathered, sem = refs
        acc_ref = None
    else:
        acc_ref, out_ref, gathered, sem = refs
    tokens = parts[0].shape[0]
    step = pl.program_id(0)
    each = shards // pl.num_programs(0)
    copies = [
        pltpu.make_async_copy(part, gathered.at[pl.ds(at * tokens, tokens)], sem.at[at])
        for at, part in enumerate(parts)
    ]

    @pl.when(step == 0)
    def _():
        for copy in copies:
            copy.start()

    for at in range(shards):
        @pl.when(step == at // each)
        def _(at=at):
            copies[at].wait()

    rows = each * tokens
    start = pl.multiple_of(step * rows, rows)
    product = jnp.dot(gathered[pl.ds(start, rows), :], w_ref[...], preferred_element_type=F32)
    if first:
        out_ref[...] = product
    else:
        out_ref[...] = acc_ref[...] + product


def project(chunk, parts, w_output, acc, each=2):
    shards = len(parts)
    tokens, depth = parts[0].shape
    columns = w_output.shape[1]
    block = pl.BlockSpec((each * tokens, columns), lambda i: (i, 0))
    return pl.pallas_call(
        functools.partial(project_kernel, shards, acc is None),
        grid=(shards // each,),
        in_specs=[pl.BlockSpec((depth, columns), lambda i: (chunk, 0))]
        + [pl.BlockSpec(memory_space=pl.ANY)] * shards
        + ([] if acc is None else [block]),
        out_specs=block,
        out_shape=jax.ShapeDtypeStruct((shards * tokens, columns), F32),
        scratch_shapes=[
            pltpu.VMEM((shards * tokens, depth), BF16),
            pltpu.SemaphoreType.DMA((shards,)),
        ],
        input_output_aliases={} if acc is None else {1 + shards: 0},
        compiler_params=params(32),
        cost_estimate=pl.CostEstimate(
            flops=2 * shards * tokens * depth * columns,
            bytes_accessed=8 << 20,
            transcendentals=0,
        ),
        name=f"project{chunk}",
    )(w_output, *parts, *([] if acc is None else [acc]))


def finish_kernel(shards, half, *refs):
    choice, w_ref = refs[:2]
    parts = refs[2 : 2 + shards]
    acc_ref, out_ref, gathered, sem = refs[2 + shards :]
    tokens = parts[0].shape[0]
    width = shards // 2
    for side in range(2):
        copies = [
            pltpu.make_async_copy(part, gathered.at[pl.ds(at * tokens, tokens)], sem.at[at])
            for at, part in enumerate(parts[side * width : (side + 1) * width])
        ]

        @pl.when(choice[half] == side)
        def _(copies=copies):
            for copy in copies:
                copy.start()
            for copy in copies:
                copy.wait()

    product = jnp.dot(gathered[...], w_ref[...], preferred_element_type=F32)
    out_ref[...] = (acc_ref[...] + product).astype(out_ref.dtype)


def finish(chunk, half, choice, parts, w_output, acc, dtype):
    shards = len(parts)
    tokens, depth = parts[0].shape
    columns = w_output.shape[1]
    rows = shards * tokens // 2
    return pl.pallas_call(
        functools.partial(finish_kernel, shards, half),
        grid_spec=pltpu.PrefetchScalarGridSpec(
            num_scalar_prefetch=1,
            grid=(1,),
            in_specs=[pl.BlockSpec((depth, columns), lambda i, choice: (chunk, 0))]
            + [pl.BlockSpec(memory_space=pl.ANY)] * shards
            + [pl.BlockSpec((rows, columns), lambda i, choice: (choice[half], 0))],
            out_specs=pl.BlockSpec((rows, columns), lambda i, choice: (0, 0)),
            scratch_shapes=[
                pltpu.VMEM((rows, depth), BF16),
                pltpu.SemaphoreType.DMA((shards // 2,)),
            ],
        ),
        out_shape=jax.ShapeDtypeStruct((rows, columns), dtype),
        compiler_params=params(32),
        cost_estimate=pl.CostEstimate(
            flops=2 * rows * depth * columns, bytes_accessed=4 << 20, transcendentals=0
        ),
        name=f"finish{half}",
    )(choice, w_output, *parts, acc)


def join_kernel(order, mine_ref, other_ref, out_ref):
    out_ref[...] = (mine_ref[...] + other_ref[...].astype(F32)).astype(BF16)


def join(order, mine, other, tokens):
    rows, columns = mine.shape
    block = pl.BlockSpec((tokens, columns), lambda i, order: (i, 0))
    return pl.pallas_call(
        join_kernel,
        grid_spec=pltpu.PrefetchScalarGridSpec(
            num_scalar_prefetch=1,
            grid=(rows // tokens,),
            in_specs=[block, block],
            out_specs=pl.BlockSpec((tokens, columns), lambda i, order: (order[i], 0)),
        ),
        out_shape=jax.ShapeDtypeStruct((rows, columns), BF16),
        cost_estimate=pl.CostEstimate(
            flops=rows * columns, bytes_accessed=4 << 20, transcendentals=0
        ),
        name="join",
    )(order, mine, other)


def local(
    q_nope, q_rope, latent_cache, rope_keys, w_absorb, w_value, w_output, span_offset, valid_lengths
):
    head_count, nope_dim, _ = w_absorb.shape
    tokens = q_nope.shape[0]
    rope_dim = rope_keys.shape[1]
    per_shard = latent_cache.shape[0]
    shards = valid_lengths.shape[0]
    me = lax.axis_index("ctx")
    side = lax.axis_index("head")

    cache = spread(jnp.concatenate([latent_cache, rope_keys], axis=1), shards)
    keys = sorted(cache)
    order = jnp.asarray(keys, jnp.int32) ^ me
    limits = valid_lengths[order]
    base = span_offset + me * tokens
    queries, bias = prep(q_nope, q_rope, w_absorb, order, limits, base, per_shard)
    cache = [cache[key] for key in keys]

    mine = me // (shards // 2)
    choice = jnp.stack([jnp.where(mine == side, 1, 0), jnp.where(mine == side, 0, 1)])
    scale = 1.0 / math.sqrt(nope_dim + rope_dim)
    heads = head_count // CHUNKS
    acc = None
    for chunk in range(CHUNKS):
        out = attend(chunk, heads, queries, bias, w_value, cache, scale)
        gathered = spread(out, shards)
        parts = [gathered[key] for key in keys]
        if chunk < CHUNKS - 1:
            acc = project(chunk, parts, w_output, acc)
    last = CHUNKS - 1
    give = finish(last, 0, choice, parts, w_output, acc, BF16)
    other = lax.ppermute(give, "head", [(0, 1), (1, 0)])
    kept = finish(last, 1, choice, parts, w_output, acc, F32)
    places = jnp.arange(shards // 2, dtype=jnp.int32) ^ (me % (shards // 2))
    return join(places, kept, other, tokens)


def solution(mesh):
    return jax.shard_map(
        local,
        mesh=mesh,
        in_specs=(
            P(("groups", "ctx"), "head"),
            P(("groups", "ctx"), "head"),
            P(("groups", "ctx"), None),
            P(("groups", "ctx"), None),
            P("head", None, None),
            P("head", None, None),
            P("head", "ctx"),
            P("groups"),
            P("groups"),
        ),
        out_specs=P(("groups", "head"), "ctx"),
        check_vma=False,
    )
```

time: 270 us -> 190 us (0.70)
  waiting for transfers between devices: 138 us -> 23.3 us
  matrix products: 82.2 us -> 0 us
  starting transfers between devices: 0.08 us -> 72.4 us
  Pallas kernels: 0 us -> 71.8 us
  blocking collectives: 33.1 us -> 0 us
  local copies, waits for them, and re-layouts: 1.74 us -> 19.6 us
  between operations: 13.8 us -> 1.2 us
    all_gather x2 -> x0, waiting for transfers between devices: 129 us -> none  [the longest x1 124 us: local(): lax.all_gather(head_out, 'ctx', axis=0, tiled=True)]
    ppermute x0 -> x64, starting transfers between devices: none -> 72.4 us  [the longest x63 72.3 us: exchange(): return lax.ppermute(x, 'ctx', [(i, i ^ mask) for i in range(shards)])]
    pallas_call x0 -> x19, Pallas kernels: none -> 71.8 us  [the longest x8 37.1 us: attend(): pl.pallas_call(functools.partial(attend_kernel, heads, shards, scale * ma...]
    dot_general x11 -> x0, matrix products: 54 us -> none  [the longest x4 16.7 us: attend(): jnp.einsum('hqk,kc->hqc', expo.astype(jnp.bfloat16), cache_all, preferred...]
    all_gather x1 -> x0, blocking collectives: 33.1 us -> none  [local(): lax.all_gather(rope_keys, 'ctx', axis=0, tiled=True)]
    sub x4 -> x0, matrix products: 28.2 us -> none  [attend(): expo = jnp.where(visible[None], jnp.exp(scores - row_max), jnp.float32(0.0))]
    ppermute x0 -> x64, waiting for transfers between devices: none -> 23.3 us  [the longest x63 23.3 us: exchange(): return lax.ppermute(x, 'ctx', [(i, i ^ mask) for i in range(shards)])]
    unnamed x4 -> x59, local copies, waits for them, and re-layouts: 1.58 us -> 19 us
  transfers between devices with their start and end apart: 3 -> 64, of which waited for: 3 -> 16; matrix products, arithmetic and copies ran while one was open for 3% -> 1% of each run, Pallas kernels for 0% -> 32%
where the time goes in v1:
time: 190 us
  starting transfers between devices  72.4 us (38%)
  Pallas kernels  71.8 us (38%)
  waiting for transfers between devices  23.3 us (12%)
  local copies, waits for them, and re-layouts  19.6 us (10%)
    ppermute x63, starting transfers between devices, exchange(): return lax.ppermute(x, 'ctx', [(i, i ^ mask) for i in range(shards)])  72.3 us
    pallas_call x8, Pallas kernels, attend(): pl.pallas_call(functools.partial(attend_kernel, heads, shards, scale * ma...  37.1 us
    ppermute x63, waiting for transfers between devices, exchange(): return lax.ppermute(x, 'ctx', [(i, i ^ mask) for i in range(shards)])  23.3 us
    pallas_call x7, Pallas kernels, project(): pl.pallas_call(functools.partial(project_kernel, shards, acc is None), gr...  23.1 us
    unnamed x59, local copies, waits for them, and re-layouts  19 us
    pallas_call x1, Pallas kernels, join(): pl.pallas_call(join_kernel, grid_spec=pltpu.PrefetchScalarGridSpec(num_sc...  4.34 us
    pallas_call x2, Pallas kernels, finish(): pl.pallas_call(functools.partial(finish_kernel, shards, half), grid_spec=...  4 us
  transfers between devices with their start and end apart: 64, of which 16 were waited for; matrix products, arithmetic and copies ran while one was open for 1% of the time, Pallas kernels for 32%

profile of v1, /device:TPU:0, one launch (start us, length us, event | category | flops | bytes accessed | tf_op | source)
XLA Modules:
  0.0 189.9 jit_solution(10883216681262639167)
XLA Ops:
  1.8 5.1 %collective-permute-start.3 = (bf16[144,576]{1,0:T(8,128)(2,1)S(1)}, bf16[144,576]{1,0:T(8,128)(2,1)S(1)}, u32[]{:S(2)}, u32[]{:S(2)}) collective-permute-start(bf16[144,576]{1,0:T(8,128)(2,1)S(1)} %pad_maximum_fusion.refs_3_), channel_id=1, source_target_pairs={{0,12},{2,14},{4,8},{6,10},{8,4},{10,6},{12,0},{14,2},{1,13},{3,15... | collective-permute-start | bytes 497672 | tf_op jit(solution)/shard_map/ppermute | solution.py:28
  6.9 5.5 %collective-permute-done.3.refs_9_ = bf16[144,576]{1,0:T(8,128)(2,1)S(1)} collective-permute-done((bf16[144,576]{1,0:T(8,128)(2,1)S(1)}, bf16[144,576]{1,0:T(8,128)(2,1)S(1)}, u32[]{:S(2)}, u32[]{:S(2)}) %collective-permute-start.3) | collective-permute-done | bytes 165920 | tf_op jit(solution)/shard_map/ppermute | solution.py:28
  12.5 2.8 %collective-permute-start.4 = (bf16[144,576]{1,0:T(8,128)(2,1)S(1)}, bf16[144,576]{1,0:T(8,128)(2,1)S(1)}, u32[]{:S(2)}, u32[]{:S(2)}) collective-permute-start(bf16[144,576]{1,0:T(8,128)(2,1)S(1)} %collective-permute-done.3.refs_9_), channel_id=1, source_target_pairs={{0,4},{2,6},{4,0},{6,2},{8,12},{10,14},{12,8},{14,10},{1,5},{3,7},... | collective-permute-start | bytes 497672 | tf_op jit(solution)/shard_map/ppermute | solution.py:28
  22.4 2.3 %copy-done.7 = bf16[32,128,512]{2,1,0:T(8,128)(2,1)S(1)} copy-done((bf16[32,128,512]{2,1,0:T(8,128)(2,1)S(1)}, bf16[32,128,512]{2,1,0:T(8,128)(2,1)}, u32[]{:S(2)}) %copy-start.7) | copy-done | bytes 4194328
  27.2 3.3 %prep.1 = (bf16[4096,576]{1,0:T(8,128)(2,1)S(1)}, f32[128,1152]{1,0:T(8,128)S(1)}) custom-call(s32[8]{0:T(128)S(1)} %get-tuple-element.10.order, s32[8]{0:T(128)S(1)} %gather_fusion, s32[1]{0:T(128)S(6)} %add.17.base, bf16[128,4096]{1,0:T(8,128)(2,1)S(1)} %copy-done.8, bf16[128,2048]{1,0:T(8,128)(2,1)S(1)} %copy-done.9, bf16[32,128,512]{2,1,0:T(8,128)(2,1)S(1)} %copy-done.7), custom_call_target="tpu_custom_call" | custom-call | flops 536870912 | bytes 12582912 | tf_op jit(solution)/shard_map/prep/pallas_call | solution.py:69
  30.5 2.0 %collective-permute-done.5.refs_8_ = bf16[144,576]{1,0:T(8,128)(2,1)S(1)} collective-permute-done((bf16[144,576]{1,0:T(8,128)(2,1)S(1)}, bf16[144,576]{1,0:T(8,128)(2,1)S(1)}, u32[]{:S(2)}, u32[]{:S(2)}) %collective-permute-start.5) | collective-permute-done | bytes 165920 | tf_op jit(solution)/shard_map/ppermute | solution.py:28
  32.5 4.6 %attend6.1.refs_1_ = bf16[128,512]{1,0:T(8,128)(2,1)S(1)} custom-call(bf16[4096,576]{1,0:T(8,128)(2,1)S(1)} %get-tuple-element.7.refs_0_, f32[128,1152]{1,0:T(8,128)S(1)} %get-tuple-element.8.refs_1_, bf16[32,512,128]{2,1,0:T(8,128)(2,1)S(1)} %copy-done.5, bf16[144,576]{1,0:T(8,128)(2,1)S(1)} %pad_maximum_fusion.refs_3_, ...), custom_call_target="tpu_custom_call" | custom-call | flops 1350565888 | bytes 4194304 | tf_op jit(solution)/shard_map/attend6/pallas_call | solution.py:135
  37.1 2.1 %collective-permute-start.17 = (bf16[128,512]{1,0:T(8,128)(2,1)S(1)}, bf16[128,512]{1,0:T(8,128)(2,1)S(1)}, u32[]{:S(2)}, u32[]{:S(2)}) collective-permute-start(bf16[128,512]{1,0:T(8,128)(2,1)S(1)} %attend6.1.refs_1_), channel_id=1, source_target_pairs={{0,12},{2,14},{4,8},{6,10},{8,4},{10,6},{12,0},{14,2},{1,13},{3,15... | collective-permute-start | bytes 393224 | tf_op jit(solution)/shard_map/ppermute | solution.py:28
  40.8 4.6 %attend5.1.refs_1_ = bf16[128,512]{1,0:T(8,128)(2,1)S(1)} custom-call(bf16[4096,576]{1,0:T(8,128)(2,1)S(1)} %get-tuple-element.7.refs_0_, f32[128,1152]{1,0:T(8,128)S(1)} %get-tuple-element.8.refs_1_, bf16[32,512,128]{2,1,0:T(8,128)(2,1)S(1)} %copy-done.5, bf16[144,576]{1,0:T(8,128)(2,1)S(1)} %pad_maximum_fusion.refs_3_, ...), custom_call_target="tpu_custom_call" | custom-call | flops 1350565888 | bytes 4194304 | tf_op jit(solution)/shard_map/attend5/pallas_call | solution.py:135
  48.9 4.6 %attend4.1.refs_1_ = bf16[128,512]{1,0:T(8,128)(2,1)S(1)} custom-call(bf16[4096,576]{1,0:T(8,128)(2,1)S(1)} %get-tuple-element.7.refs_0_, f32[128,1152]{1,0:T(8,128)S(1)} %get-tuple-element.8.refs_1_, bf16[32,512,128]{2,1,0:T(8,128)(2,1)S(1)} %copy-done.5, bf16[144,576]{1,0:T(8,128)(2,1)S(1)} %pad_maximum_fusion.refs_3_, ...), custom_call_target="tpu_custom_call" | custom-call | flops 1350565888 | bytes 4194304 | tf_op jit(solution)/shard_map/attend4/pallas_call | solution.py:135
  53.5 2.1 %collective-permute-start.31 = (bf16[128,512]{1,0:T(8,128)(2,1)S(1)}, bf16[128,512]{1,0:T(8,128)(2,1)S(1)}, u32[]{:S(2)}, u32[]{:S(2)}) collective-permute-start(bf16[128,512]{1,0:T(8,128)(2,1)S(1)} %attend4.1.refs_1_), channel_id=1, source_target_pairs={{0,12},{2,14},{4,8},{6,10},{8,4},{10,6},{12,0},{14,2},{1,13},{3,15... | collective-permute-start | bytes 393224 | tf_op jit(solution)/shard_map/ppermute | solution.py:28
  55.6 4.6 %attend3.1.refs_1_ = bf16[128,512]{1,0:T(8,128)(2,1)S(1)} custom-call(bf16[4096,576]{1,0:T(8,128)(2,1)S(1)} %get-tuple-element.7.refs_0_, f32[128,1152]{1,0:T(8,128)S(1)} %get-tuple-element.8.refs_1_, bf16[32,512,128]{2,1,0:T(8,128)(2,1)S(1)} %copy-done.5, bf16[144,576]{1,0:T(8,128)(2,1)S(1)} %pad_maximum_fusion.refs_3_, ...), custom_call_target="tpu_custom_call" | custom-call | flops 1350565888 | bytes 4194304 | tf_op jit(solution)/shard_map/attend3/pallas_call | solution.py:135
  64.8 4.6 %attend1.1.refs_1_ = bf16[128,512]{1,0:T(8,128)(2,1)S(1)} custom-call(bf16[4096,576]{1,0:T(8,128)(2,1)S(1)} %get-tuple-element.7.refs_0_, f32[128,1152]{1,0:T(8,128)S(1)} %get-tuple-element.8.refs_1_, bf16[32,512,128]{2,1,0:T(8,128)(2,1)S(1)} %copy-done.5, bf16[144,576]{1,0:T(8,128)(2,1)S(1)} %pad_maximum_fusion.refs_3_, ...), custom_call_target="tpu_custom_call" | custom-call | flops 1350565888 | bytes 4194304 | tf_op jit(solution)/shard_map/attend1/pallas_call | solution.py:135
  70.0 4.8 %attend2.1.refs_1_ = bf16[128,512]{1,0:T(8,128)(2,1)S(1)} custom-call(bf16[4096,576]{1,0:T(8,128)(2,1)S(1)} %get-tuple-element.7.refs_0_, f32[128,1152]{1,0:T(8,128)S(1)} %get-tuple-element.8.refs_1_, bf16[32,512,128]{2,1,0:T(8,128)(2,1)S(1)} %copy-done.5, bf16[144,576]{1,0:T(8,128)(2,1)S(1)} %pad_maximum_fusion.refs_3_, ...), custom_call_target="tpu_custom_call" | custom-call | flops 1350565888 | bytes 4194304 | tf_op jit(solution)/shard_map/attend2/pallas_call | solution.py:135
  74.8 2.1 %collective-permute-start.45 = (bf16[128,512]{1,0:T(8,128)(2,1)S(1)}, bf16[128,512]{1,0:T(8,128)(2,1)}, u32[]{:S(2)}, u32[]{:S(2)}) collective-permute-start(bf16[128,512]{1,0:T(8,128)(2,1)S(1)} %attend2.1.refs_1_), channel_id=1, source_target_pairs={{0,12},{2,14},{4,8},{6,10},{8,4},{10,6},{12,0},{14,2},{1,13},{3,15... | collective-permute-start | bytes 393224 | tf_op jit(solution)/shard_map/ppermute | solution.py:28
  82.0 4.6 %attend0.1.refs_1_ = bf16[128,512]{1,0:T(8,128)(2,1)S(1)} custom-call(bf16[4096,576]{1,0:T(8,128)(2,1)S(1)} %get-tuple-element.7.refs_0_, f32[128,1152]{1,0:T(8,128)S(1)} %get-tuple-element.8.refs_1_, bf16[32,512,128]{2,1,0:T(8,128)(2,1)S(1)} %copy-done.5, bf16[144,576]{1,0:T(8,128)(2,1)S(1)} %pad_maximum_fusion.refs_3_, ...), custom_call_target="tpu_custom_call" | custom-call | flops 1350565888 | bytes 4194304 | tf_op jit(solution)/shard_map/attend0/pallas_call | solution.py:135
  87.2 2.0 %collective-permute-start.59 = (bf16[128,512]{1,0:T(8,128)(2,1)S(1)}, bf16[128,512]{1,0:T(8,128)(2,1)}, u32[]{:S(2)}, u32[]{:S(2)}) collective-permute-start(bf16[128,512]{1,0:T(8,128)(2,1)S(1)} %attend0.1.refs_1_), channel_id=1, source_target_pairs={{0,12},{2,14},{4,8},{6,10},{8,4},{10,6},{12,0},{14,2},{1,13},{3,15... | collective-permute-start | bytes 393224 | tf_op jit(solution)/shard_map/ppermute | solution.py:28
  90.9 4.6 %attend7.1.refs_2_ = bf16[128,512]{1,0:T(8,128)(2,1)S(1)} custom-call(bf16[4096,576]{1,0:T(8,128)(2,1)S(1)} %get-tuple-element.7.refs_0_, f32[128,1152]{1,0:T(8,128)S(1)} %get-tuple-element.8.refs_1_, bf16[32,512,128]{2,1,0:T(8,128)(2,1)S(1)} %copy-done.5, bf16[144,576]{1,0:T(8,128)(2,1)S(1)} %pad_maximum_fusion.refs_3_, ...), custom_call_target="tpu_custom_call" | custom-call | flops 1350565888 | bytes 4194304 | tf_op jit(solution)/shard_map/attend7/pallas_call | solution.py:135
  95.5 1.9 collective-permute-start.10
  129.3 3.1 %copy-done.1 = bf16[4096,896]{1,0:T(8,128)(2,1)S(1)} copy-done((bf16[4096,896]{1,0:T(8,128)(2,1)S(1)}, bf16[4096,896]{1,0:T(8,128)(2,1)}, u32[]{:S(2)}) %copy-start.1) | copy-done | bytes 7340056
  133.3 2.7 %project0.1.refs_9_ = f32[1024,896]{1,0:T(8,128)S(1)} custom-call(bf16[4096,896]{1,0:T(8,128)(2,1)S(1)} %copy-done.1, bf16[128,512]{1,0:T(8,128)(2,1)S(1)} %attend0.1.refs_1_, bf16[128,512]{1,0:T(8,128)(2,1)S(1)} %copy-done.27, bf16[128,512]{1,0:T(8,128)(2,1)} %collective-permute-done.57.refs_3_, bf16[128,512]{1,0:T(8,128)(2,1)} %collective-permute-done.58.refs_4_, ...), custom_call_target="tpu_custom_call" | custom-call | flops 939524096 | bytes 8388608 | tf_op jit(solution)/shard_map/project0/pallas_call | solution.py:204
  140.4 3.1 %project1.1.refs_9_ = f32[1024,896]{1,0:T(8,128)S(1)} custom-call(bf16[4096,896]{1,0:T(8,128)(2,1)S(1)} %copy-done.1, bf16[128,512]{1,0:T(8,128)(2,1)S(1)} %attend1.1.refs_1_, bf16[128,512]{1,0:T(8,128)(2,1)S(1)} %copy-done.25, bf16[128,512]{1,0:T(8,128)(2,1)} %collective-permute-done.50.refs_3_, ...), custom_call_target="tpu_custom_call", output_to_operand_aliasing={{}: (9, {})} | custom-call | flops 939524096 | bytes 8388608 | tf_op jit(solution)/shard_map/project1/pallas_call | solution.py:204
  144.5 3.3 %project2.1.refs_9_ = f32[1024,896]{1,0:T(8,128)S(1)} custom-call(bf16[4096,896]{1,0:T(8,128)(2,1)S(1)} %copy-done.1, bf16[128,512]{1,0:T(8,128)(2,1)S(1)} %attend2.1.refs_1_, bf16[128,512]{1,0:T(8,128)(2,1)S(1)} %copy-done.23, bf16[128,512]{1,0:T(8,128)(2,1)S(1)} %copy-done.21, ...), custom_call_target="tpu_custom_call", output_to_operand_aliasing={{}: (9, {})} | custom-call | flops 939524096 | bytes 8388608 | tf_op jit(solution)/shard_map/project2/pallas_call | solution.py:204
  154.5 3.5 %project3.1.refs_9_ = f32[1024,896]{1,0:T(8,128)S(1)} custom-call(bf16[4096,896]{1,0:T(8,128)(2,1)S(1)} %copy-done.1, bf16[128,512]{1,0:T(8,128)(2,1)S(1)} %attend3.1.refs_1_, bf16[128,512]{1,0:T(8,128)(2,1)S(1)} %copy-done.19, bf16[128,512]{1,0:T(8,128)(2,1)S(1)} %copy-done.17, ...), custom_call_target="tpu_custom_call", output_to_operand_aliasing={{}: (9, {})} | custom-call | flops 939524096 | bytes 8388608 | tf_op jit(solution)/shard_map/project3/pallas_call | solution.py:204
  158.9 3.5 %project4.1.refs_9_ = f32[1024,896]{1,0:T(8,128)S(1)} custom-call(bf16[4096,896]{1,0:T(8,128)(2,1)S(1)} %copy-done.1, bf16[128,512]{1,0:T(8,128)(2,1)S(1)} %attend4.1.refs_1_, bf16[128,512]{1,0:T(8,128)(2,1)S(1)} %copy-done.13, bf16[128,512]{1,0:T(8,128)(2,1)S(1)} %copy-done.11, ...), custom_call_target="tpu_custom_call", output_to_operand_aliasing={{}: (9, {})} | custom-call | flops 939524096 | bytes 8388608 | tf_op jit(solution)/shard_map/project4/pallas_call | solution.py:204
  166.5 3.5 %project5.1.refs_9_ = f32[1024,896]{1,0:T(8,128)S(1)} custom-call(bf16[4096,896]{1,0:T(8,128)(2,1)S(1)} %copy-done.1, bf16[128,512]{1,0:T(8,128)(2,1)S(1)} %attend5.1.refs_1_, bf16[128,512]{1,0:T(8,128)(2,1)S(1)} %collective-permute-done.21.refs_2_, bf16[128,512]{1,0:T(8,128)(2,1)S(1)} %collective-permute-done.22.refs_3_, ...), custom_call_target="tpu_custom_call", output_to_operand_aliasing={{}: (9, {})} | custom-call | flops 939524096 | bytes 8388608 | tf_op jit(solution)/shard_map/project5/pallas_call | solution.py:204
  170.0 3.5 %project6.1.refs_10_ = f32[1024,896]{1,0:T(8,128)S(1)} custom-call(bf16[4096,896]{1,0:T(8,128)(2,1)S(1)} %copy-done.1, bf16[128,512]{1,0:T(8,128)(2,1)S(1)} %attend6.1.refs_1_, bf16[128,512]{1,0:T(8,128)(2,1)S(1)} %collective-permute-done.14.refs_2_, bf16[128,512]{1,0:T(8,128)(2,1)S(1)} %collective-permute-done.15.refs_3_, ...), custom_call_target="tpu_custom_call", output_to_operand_aliasing={{}: (9, {})} | custom-call | flops 939524096 | bytes 8388608 | tf_op jit(solution)/shard_map/project6/pallas_call | solution.py:204
  173.6 2.0 %finish0.1 = bf16[512,896]{1,0:T(8,128)(2,1)S(1)} custom-call(s32[2]{0:T(128)S(1)} %pad_add_fusion.refs_0_, bf16[4096,896]{1,0:T(8,128)(2,1)S(1)} %copy-done.1, bf16[128,512]{1,0:T(8,128)(2,1)S(1)} %attend7.1.refs_2_, bf16[128,512]{1,0:T(8,128)(2,1)S(1)} %collective-permute-done.7.refs_3_, bf16[128,512]{1,0:T(8,128)(2,1)S(1)} %collective-permute-done.8.refs_4_, ...), custom_call_target="tpu_custom_call" | custom-call | flops 469762048 | bytes 4194304 | tf_op jit(solution)/shard_map/finish0/pallas_call | solution.py:255
  176.2 3.1 %copy-done.2 = bf16[4096,896]{1,0:T(8,128)(2,1)S(1)} copy-done((bf16[4096,896]{1,0:T(8,128)(2,1)S(1)}, bf16[4096,896]{1,0:T(8,128)(2,1)}, u32[]{:S(2)}) %copy-start.2) | copy-done | bytes 7340056
  179.3 2.0 %copy-done.4 = f32[1024,896]{1,0:T(8,128)S(1)} copy-done((f32[1024,896]{1,0:T(8,128)S(1)}, f32[1024,896]{1,0:T(8,128)}, u32[]{:S(2)}) %copy-start.4) | copy-done | bytes 3670040
  181.4 2.0 %finish1.1.mine_ref = f32[512,896]{1,0:T(8,128)S(1)} custom-call(s32[2]{0:T(128)S(1)} %pad_add_fusion.refs_0_, bf16[4096,896]{1,0:T(8,128)(2,1)S(1)} %copy-done.2, bf16[128,512]{1,0:T(8,128)(2,1)S(1)} %attend7.1.refs_2_, bf16[128,512]{1,0:T(8,128)(2,1)S(1)} %collective-permute-done.7.refs_3_, bf16[128,512]{1,0:T(8,128)(2,1)S(1)} %collective-permute-done.8.refs_4_, ...), custom_call_target="tpu_custom_call" | custom-call | flops 469762048 | bytes 4194304 | tf_op jit(solution)/shard_map/finish1/pallas_call | solution.py:255
  185.5 4.3 %join.1 = bf16[512,896]{1,0:T(8,128)(2,1)} custom-call(s32[4]{0:T(128)} %iota_xor_fusion.order, f32[512,896]{1,0:T(8,128)} %copy-done.6, bf16[512,896]{1,0:T(8,128)(2,1)} %copy-done.28), custom_call_target="tpu_custom_call" | custom-call | flops 458752 | bytes 4194304 | tf_op jit(solution)/shard_map/join/pallas_call | solution.py:285
  (180 shorter events, 80.8 us)
Async XLA Ops:
  15.2 15.2 %collective-permute-start = (bf16[144,576]{1,0:T(8,128)(2,1)S(1)}, bf16[144,576]{1,0:T(8,128)(2,1)S(1)}, u32[]{:S(2)}, u32[]{:S(2)}) collective-permute-start(bf16[144,576]{1,0:T(8,128)(2,1)S(1)} %pad_maximum_fusion.refs_3_), channel_id=1, source_target_pairs={{0,2},{2,0},{4,6},{6,4},{8,10},{10,8},{12,14},{14,12},{1,3},{3,1},... | collective-permute-start | bytes 497672 | tf_op jit(solution)/shard_map/ppermute | solution.py:28
  16.8 13.7 %collective-permute-start.6 = (bf16[144,576]{1,0:T(8,128)(2,1)S(1)}, bf16[144,576]{1,0:T(8,128)(2,1)S(1)}, u32[]{:S(2)}, u32[]{:S(2)}) collective-permute-start(bf16[144,576]{1,0:T(8,128)(2,1)S(1)} %collective-permute-done.3.refs_9_), channel_id=1, source_target_pairs={{0,2},{2,0},{4,6},{6,4},{8,10},{10,8},{12,14},{14,12},{1,3},{3,1},... | collective-permute-start | bytes 497672 | tf_op jit(solution)/shard_map/ppermute | solution.py:28
  17.3 13.3 %collective-permute-start.2 = (bf16[144,576]{1,0:T(8,128)(2,1)S(1)}, bf16[144,576]{1,0:T(8,128)(2,1)S(1)}, u32[]{:S(2)}, u32[]{:S(2)}) collective-permute-start(bf16[144,576]{1,0:T(8,128)(2,1)S(1)} %collective-permute-done.1.refs_5_), channel_id=1, source_target_pairs={{0,2},{2,0},{4,6},{6,4},{8,10},{10,8},{12,14},{14,12},{1,3},{3,1},... | collective-permute-start | bytes 497672 | tf_op jit(solution)/shard_map/ppermute | solution.py:28
  19.6 12.9 %collective-permute-start.5 = (bf16[144,576]{1,0:T(8,128)(2,1)S(1)}, bf16[144,576]{1,0:T(8,128)(2,1)S(1)}, u32[]{:S(2)}, u32[]{:S(2)}) collective-permute-start(bf16[144,576]{1,0:T(8,128)(2,1)S(1)} %collective-permute-done.4.refs_7_), channel_id=1, source_target_pairs={{0,2},{2,0},{4,6},{6,4},{8,10},{10,8},{12,14},{14,12},{1,3},{3,1},... | collective-permute-start | bytes 497672 | tf_op jit(solution)/shard_map/ppermute | solution.py:28
  39.2 14.3 %collective-permute-start.15 = (bf16[128,512]{1,0:T(8,128)(2,1)S(1)}, bf16[128,512]{1,0:T(8,128)(2,1)S(1)}, u32[]{:S(2)}, u32[]{:S(2)}) collective-permute-start(bf16[128,512]{1,0:T(8,128)(2,1)S(1)} %attend6.1.refs_1_), channel_id=1, source_target_pairs={{0,4},{2,6},{4,0},{6,2},{8,12},{10,14},{12,8},{14,10},{1,5},{3,7},... | collective-permute-start | bytes 393224 | tf_op jit(solution)/shard_map/ppermute | solution.py:28
  39.2 21.0 %collective-permute-start.14 = (bf16[128,512]{1,0:T(8,128)(2,1)S(1)}, bf16[128,512]{1,0:T(8,128)(2,1)S(1)}, u32[]{:S(2)}, u32[]{:S(2)}) collective-permute-start(bf16[128,512]{1,0:T(8,128)(2,1)S(1)} %attend6.1.refs_1_), channel_id=1, source_target_pairs={{0,2},{2,0},{4,6},{6,4},{8,10},{10,8},{12,14},{14,12},{1,3},{3,1},... | collective-permute-start | bytes 393224 | tf_op jit(solution)/shard_map/ppermute | solution.py:28
  45.4 14.9 %collective-permute-start.24 = (bf16[128,512]{1,0:T(8,128)(2,1)S(1)}, bf16[128,512]{1,0:T(8,128)(2,1)S(1)}, u32[]{:S(2)}, u32[]{:S(2)}) collective-permute-start(bf16[128,512]{1,0:T(8,128)(2,1)S(1)} %attend5.1.refs_1_), channel_id=1, source_target_pairs={{0,12},{2,14},{4,8},{6,10},{8,4},{10,6},{12,0},{14,2},{1,13},{3,15... | collective-permute-start | bytes 393224 | tf_op jit(solution)/shard_map/ppermute | solution.py:28
  47.2 14.7 %collective-permute-start.22 = (bf16[128,512]{1,0:T(8,128)(2,1)S(1)}, bf16[128,512]{1,0:T(8,128)(2,1)S(1)}, u32[]{:S(2)}, u32[]{:S(2)}) collective-permute-start(bf16[128,512]{1,0:T(8,128)(2,1)S(1)} %attend5.1.refs_1_), channel_id=1, source_target_pairs={{0,4},{2,6},{4,0},{6,2},{8,12},{10,14},{12,8},{14,10},{1,5},{3,7},... | collective-permute-start | bytes 393224 | tf_op jit(solution)/shard_map/ppermute | solution.py:28
  48.4 15.3 %collective-permute-start.21 = (bf16[128,512]{1,0:T(8,128)(2,1)S(1)}, bf16[128,512]{1,0:T(8,128)(2,1)S(1)}, u32[]{:S(2)}, u32[]{:S(2)}) collective-permute-start(bf16[128,512]{1,0:T(8,128)(2,1)S(1)} %attend5.1.refs_1_), channel_id=1, source_target_pairs={{0,2},{2,0},{4,6},{6,4},{8,10},{10,8},{12,14},{14,12},{1,3},{3,1},... | collective-permute-start | bytes 393224 | tf_op jit(solution)/shard_map/ppermute | solution.py:28
  53.5 15.9 %collective-permute-start.31 = (bf16[128,512]{1,0:T(8,128)(2,1)S(1)}, bf16[128,512]{1,0:T(8,128)(2,1)S(1)}, u32[]{:S(2)}, u32[]{:S(2)}) collective-permute-start(bf16[128,512]{1,0:T(8,128)(2,1)S(1)} %attend4.1.refs_1_), channel_id=1, source_target_pairs={{0,12},{2,14},{4,8},{6,10},{8,4},{10,6},{12,0},{14,2},{1,13},{3,15... | collective-permute-start | bytes 393224 | tf_op jit(solution)/shard_map/ppermute | solution.py:28
  60.2 14.5 %collective-permute-start.29 = (bf16[128,512]{1,0:T(8,128)(2,1)S(1)}, bf16[128,512]{1,0:T(8,128)(2,1)S(1)}, u32[]{:S(2)}, u32[]{:S(2)}) collective-permute-start(bf16[128,512]{1,0:T(8,128)(2,1)S(1)} %attend4.1.refs_1_), channel_id=1, source_target_pairs={{0,4},{2,6},{4,0},{6,2},{8,12},{10,14},{12,8},{14,10},{1,5},{3,7},... | collective-permute-start | bytes 393224 | tf_op jit(solution)/shard_map/ppermute | solution.py:28
  60.3 16.6 %collective-permute-start.28 = (bf16[128,512]{1,0:T(8,128)(2,1)S(1)}, bf16[128,512]{1,0:T(8,128)(2,1)S(1)}, u32[]{:S(2)}, u32[]{:S(2)}) collective-permute-start(bf16[128,512]{1,0:T(8,128)(2,1)S(1)} %attend4.1.refs_1_), channel_id=1, source_target_pairs={{0,2},{2,0},{4,6},{6,4},{8,10},{10,8},{12,14},{14,12},{1,3},{3,1},... | collective-permute-start | bytes 393224 | tf_op jit(solution)/shard_map/ppermute | solution.py:28
  61.9 15.7 %collective-permute-start.38 = (bf16[128,512]{1,0:T(8,128)(2,1)S(1)}, bf16[128,512]{1,0:T(8,128)(2,1)S(1)}, u32[]{:S(2)}, u32[]{:S(2)}) collective-permute-start(bf16[128,512]{1,0:T(8,128)(2,1)S(1)} %attend3.1.refs_1_), channel_id=1, source_target_pairs={{0,12},{2,14},{4,8},{6,10},{8,4},{10,6},{12,0},{14,2},{1,13},{3,15... | collective-permute-start | bytes 393224 | tf_op jit(solution)/shard_map/ppermute | solution.py:28
  63.7 15.4 %collective-permute-start.36 = (bf16[128,512]{1,0:T(8,128)(2,1)S(1)}, bf16[128,512]{1,0:T(8,128)(2,1)S(1)}, u32[]{:S(2)}, u32[]{:S(2)}) collective-permute-start(bf16[128,512]{1,0:T(8,128)(2,1)S(1)} %attend3.1.refs_1_), channel_id=1, source_target_pairs={{0,4},{2,6},{4,0},{6,2},{8,12},{10,14},{12,8},{14,10},{1,5},{3,7},... | collective-permute-start | bytes 393224 | tf_op jit(solution)/shard_map/ppermute | solution.py:28
  74.8 11.9 %collective-permute-start.45 = (bf16[128,512]{1,0:T(8,128)(2,1)S(1)}, bf16[128,512]{1,0:T(8,128)(2,1)}, u32[]{:S(2)}, u32[]{:S(2)}) collective-permute-start(bf16[128,512]{1,0:T(8,128)(2,1)S(1)} %attend2.1.refs_1_), channel_id=1, source_target_pairs={{0,12},{2,14},{4,8},{6,10},{8,4},{10,6},{12,0},{14,2},{1,13},{3,15... | collective-permute-start | bytes 393224 | tf_op jit(solution)/shard_map/ppermute | solution.py:28
  77.6 11.6 %collective-permute-start.42 = (bf16[128,512]{1,0:T(8,128)(2,1)S(1)}, bf16[128,512]{1,0:T(8,128)(2,1)S(1)}, u32[]{:S(2)}, u32[]{:S(2)}) collective-permute-start(bf16[128,512]{1,0:T(8,128)(2,1)S(1)} %attend2.1.refs_1_), channel_id=1, source_target_pairs={{0,2},{2,0},{4,6},{6,4},{8,10},{10,8},{12,14},{14,12},{1,3},{3,1},... | collective-permute-start | bytes 393224 | tf_op jit(solution)/shard_map/ppermute | solution.py:28
  80.9 14.6 %collective-permute-start.50 = (bf16[128,512]{1,0:T(8,128)(2,1)S(1)}, bf16[128,512]{1,0:T(8,128)(2,1)}, u32[]{:S(2)}, u32[]{:S(2)}) collective-permute-start(bf16[128,512]{1,0:T(8,128)(2,1)S(1)} %attend1.1.refs_1_), channel_id=1, source_target_pairs={{0,4},{2,6},{4,0},{6,2},{8,12},{10,14},{12,8},{14,10},{1,5},{3,7},... | collective-permute-start | bytes 393224 | tf_op jit(solution)/shard_map/ppermute | solution.py:28
  87.2 11.9 %collective-permute-start.59 = (bf16[128,512]{1,0:T(8,128)(2,1)S(1)}, bf16[128,512]{1,0:T(8,128)(2,1)}, u32[]{:S(2)}, u32[]{:S(2)}) collective-permute-start(bf16[128,512]{1,0:T(8,128)(2,1)S(1)} %attend0.1.refs_1_), channel_id=1, source_target_pairs={{0,12},{2,14},{4,8},{6,10},{8,4},{10,6},{12,0},{14,2},{1,13},{3,15... | collective-permute-start | bytes 393224 | tf_op jit(solution)/shard_map/ppermute | solution.py:28
  119.0 18.0 %collective-permute-start.55 = (bf16[128,512]{1,0:T(8,128)(2,1)}, bf16[128,512]{1,0:T(8,128)(2,1)S(1)}, u32[]{:S(2)}, u32[]{:S(2)}) collective-permute-start(bf16[128,512]{1,0:T(8,128)(2,1)} %collective-permute-done.52.refs_7_), channel_id=1, source_target_pairs={{0,2},{2,0},{4,6},{6,4},{8,10},{10,8},{12,14},{14,12},{1,3},{3,1},... | collective-permute-start | bytes 393224 | tf_op jit(solution)/shard_map/ppermute | solution.py:28
  120.1 16.0 %collective-permute-start.44 = (bf16[128,512]{1,0:T(8,128)(2,1)}, bf16[128,512]{1,0:T(8,128)(2,1)S(1)}, u32[]{:S(2)}, u32[]{:S(2)}) collective-permute-start(bf16[128,512]{1,0:T(8,128)(2,1)} %copy-done.20), channel_id=1, source_target_pairs={{0,2},{2,0},{4,6},{6,4},{8,10},{10,8},{12,14},{14,12},{1,3},{3,1},... | collective-permute-start | bytes 393224 | tf_op jit(solution)/shard_map/ppermute | solution.py:28
  122.5 15.7 %collective-permute-start.51 = (bf16[128,512]{1,0:T(8,128)(2,1)}, bf16[128,512]{1,0:T(8,128)(2,1)S(1)}, u32[]{:S(2)}, u32[]{:S(2)}) collective-permute-start(bf16[128,512]{1,0:T(8,128)(2,1)} %collective-permute-done.50.refs_3_), channel_id=1, source_target_pairs={{0,2},{2,0},{4,6},{6,4},{8,10},{10,8},{12,14},{14,12},{1,3},{3,1},... | collective-permute-start | bytes 393224 | tf_op jit(solution)/shard_map/ppermute | solution.py:28
  125.3 13.9 %collective-permute-start.54 = (bf16[128,512]{1,0:T(8,128)(2,1)S(1)}, bf16[128,512]{1,0:T(8,128)(2,1)S(1)}, u32[]{:S(2)}, u32[]{:S(2)}) collective-permute-start(bf16[128,512]{1,0:T(8,128)(2,1)S(1)} %collective-permute-done.53.refs_5_), channel_id=1, source_target_pairs={{0,2},{2,0},{4,6},{6,4},{8,10},{10,8},{12,14},{14,12},{1,3},{3,1},... | collective-permute-start | bytes 393224 | tf_op jit(solution)/shard_map/ppermute | solution.py:28
  128.1 15.4 %collective-permute-start.47 = (bf16[128,512]{1,0:T(8,128)(2,1)S(1)}, bf16[128,512]{1,0:T(8,128)(2,1)S(1)}, u32[]{:S(2)}, u32[]{:S(2)}) collective-permute-start(bf16[128,512]{1,0:T(8,128)(2,1)S(1)} %collective-permute-done.46.refs_5_), channel_id=1, source_target_pairs={{0,2},{2,0},{4,6},{6,4},{8,10},{10,8},{12,14},{14,12},{1,3},{3,1},... | collective-permute-start | bytes 393224 | tf_op jit(solution)/shard_map/ppermute | solution.py:28
  136.1 13.0 %collective-permute-start.41 = (bf16[128,512]{1,0:T(8,128)(2,1)S(1)}, bf16[128,512]{1,0:T(8,128)(2,1)S(1)}, u32[]{:S(2)}, u32[]{:S(2)}) collective-permute-start(bf16[128,512]{1,0:T(8,128)(2,1)S(1)} %copy-done.15), channel_id=1, source_target_pairs={{0,2},{2,0},{4,6},{6,4},{8,10},{10,8},{12,14},{14,12},{1,3},{3,1},... | collective-permute-start | bytes 393224 | tf_op jit(solution)/shard_map/ppermute | solution.py:28
  138.2 12.3 %collective-permute-start.37 = (bf16[128,512]{1,0:T(8,128)(2,1)S(1)}, bf16[128,512]{1,0:T(8,128)(2,1)S(1)}, u32[]{:S(2)}, u32[]{:S(2)}) collective-permute-start(bf16[128,512]{1,0:T(8,128)(2,1)S(1)} %copy-done.17), channel_id=1, source_target_pairs={{0,2},{2,0},{4,6},{6,4},{8,10},{10,8},{12,14},{14,12},{1,3},{3,1},... | collective-permute-start | bytes 393224 | tf_op jit(solution)/shard_map/ppermute | solution.py:28
  139.3 14.0 %collective-permute-start.40 = (bf16[128,512]{1,0:T(8,128)(2,1)S(1)}, bf16[128,512]{1,0:T(8,128)(2,1)S(1)}, u32[]{:S(2)}, u32[]{:S(2)}) collective-permute-start(bf16[128,512]{1,0:T(8,128)(2,1)S(1)} %collective-permute-done.39.refs_5_), channel_id=1, source_target_pairs={{0,2},{2,0},{4,6},{6,4},{8,10},{10,8},{12,14},{14,12},{1,3},{3,1},... | collective-permute-start | bytes 393224 | tf_op jit(solution)/shard_map/ppermute | solution.py:28
  143.6 14.3 %collective-permute-start.33 = (bf16[128,512]{1,0:T(8,128)(2,1)S(1)}, bf16[128,512]{1,0:T(8,128)(2,1)S(1)}, u32[]{:S(2)}, u32[]{:S(2)}) collective-permute-start(bf16[128,512]{1,0:T(8,128)(2,1)S(1)} %collective-permute-done.32.refs_5_), channel_id=1, source_target_pairs={{0,2},{2,0},{4,6},{6,4},{8,10},{10,8},{12,14},{14,12},{1,3},{3,1},... | collective-permute-start | bytes 393224 | tf_op jit(solution)/shard_map/ppermute | solution.py:28
  147.9 14.5 %collective-permute-start.27 = (bf16[128,512]{1,0:T(8,128)(2,1)S(1)}, bf16[128,512]{1,0:T(8,128)(2,1)S(1)}, u32[]{:S(2)}, u32[]{:S(2)}) collective-permute-start(bf16[128,512]{1,0:T(8,128)(2,1)S(1)} %collective-permute-done.24.refs_7_), channel_id=1, source_target_pairs={{0,2},{2,0},{4,6},{6,4},{8,10},{10,8},{12,14},{14,12},{1,3},{3,1},... | collective-permute-start | bytes 393224 | tf_op jit(solution)/shard_map/ppermute | solution.py:28
  149.1 14.5 %collective-permute-start.23 = (bf16[128,512]{1,0:T(8,128)(2,1)S(1)}, bf16[128,512]{1,0:T(8,128)(2,1)S(1)}, u32[]{:S(2)}, u32[]{:S(2)}) collective-permute-start(bf16[128,512]{1,0:T(8,128)(2,1)S(1)} %collective-permute-done.22.refs_3_), channel_id=1, source_target_pairs={{0,2},{2,0},{4,6},{6,4},{8,10},{10,8},{12,14},{14,12},{1,3},{3,1},... | collective-permute-start | bytes 393224 | tf_op jit(solution)/shard_map/ppermute | solution.py:28
  150.5 14.0 %collective-permute-start.11 = (bf16[128,512]{1,0:T(8,128)(2,1)S(1)}, bf16[128,512]{1,0:T(8,128)(2,1)S(1)}, u32[]{:S(2)}, u32[]{:S(2)}) collective-permute-start(bf16[128,512]{1,0:T(8,128)(2,1)S(1)} %collective-permute-done.10.refs_8_), channel_id=1, source_target_pairs={{0,4},{2,6},{4,0},{6,2},{8,12},{10,14},{12,8},{14,10},{1,5},{3,7},... | collective-permute-start | bytes 393224 | tf_op jit(solution)/shard_map/ppermute | solution.py:28
  153.3 12.3 %collective-permute-start.26 = (bf16[128,512]{1,0:T(8,128)(2,1)S(1)}, bf16[128,512]{1,0:T(8,128)(2,1)S(1)}, u32[]{:S(2)}, u32[]{:S(2)}) collective-permute-start(bf16[128,512]{1,0:T(8,128)(2,1)S(1)} %collective-permute-done.25.refs_5_), channel_id=1, source_target_pairs={{0,2},{2,0},{4,6},{6,4},{8,10},{10,8},{12,14},{14,12},{1,3},{3,1},... | collective-permute-start | bytes 393224 | tf_op jit(solution)/shard_map/ppermute | solution.py:28
  157.9 12.1 %collective-permute-start.19 = (bf16[128,512]{1,0:T(8,128)(2,1)S(1)}, bf16[128,512]{1,0:T(8,128)(2,1)S(1)}, u32[]{:S(2)}, u32[]{:S(2)}) collective-permute-start(bf16[128,512]{1,0:T(8,128)(2,1)S(1)} %collective-permute-done.18.refs_5_), channel_id=1, source_target_pairs={{0,2},{2,0},{4,6},{6,4},{8,10},{10,8},{12,14},{14,12},{1,3},{3,1},... | collective-permute-start | bytes 393224 | tf_op jit(solution)/shard_map/ppermute | solution.py:28
  (61 other events, 462.4 us)

commit v2 on v0

v2 whole, which is shorter than its diff:
```python
import functools
import math

import jax
import jax.numpy as jnp
from jax import lax
from jax.experimental import pallas as pl
from jax.experimental.pallas import tpu as pltpu
from jax.sharding import PartitionSpec as P

F32 = jnp.float32
BF16 = jnp.bfloat16
MASKED = -1e30
LANES = 128
STEP = 4
PIECES = (1, 2, 2, 2, 1)
ANYWHERE = pl.BlockSpec(memory_space=pl.ANY)
SCALARS = pl.BlockSpec(memory_space=pltpu.SMEM)


def params():
    return pltpu.CompilerParams(vmem_limit_bytes=58 * 1024 * 1024)


def cost(flops, size, exps=0):
    return pl.CostEstimate(flops=flops, bytes_accessed=size, transcendentals=exps)


def basis_of(shards):
    if shards == 8:
        return (6, 2, 1)
    return tuple(1 << bit for bit in reversed(range(shards.bit_length() - 1)))


def exchange(x, mask, shards):
    return lax.ppermute(x, "ctx", [(i, i ^ mask) for i in range(shards)])


def sibling(x):
    return lax.ppermute(x, "head", [(0, 1), (1, 0)])


def stack_kernel(first_ref, second_ref, out_ref):
    out_ref[0] = first_ref[...]
    out_ref[1] = second_ref[...]


def stack(first, second):
    return pl.pallas_call(
        stack_kernel,
        out_shape=jax.ShapeDtypeStruct((2, *first.shape), first.dtype),
        compiler_params=params(),
        cost_estimate=cost(0, 4 * first.size * first.dtype.itemsize),
        name="stack",
    )(first, second)


def spread(x, shards):
    first, *rest = basis_of(shards)
    pairs = {0: stack(x, exchange(x, first, shards))}
    for mask in rest:
        pairs.update({key ^ mask: exchange(pair, mask, shards) for key, pair in pairs.items()})
    return pairs


def pack_kernel(own, side, latent_ref, rope_ref, out_ref):
    rows, latent = latent_ref.shape
    rope = rope_ref.shape[0]
    turned = rope_ref[...].astype(F32).T.astype(BF16)
    out_ref[:, latent:] = jnp.zeros((own, out_ref.shape[1] - latent), BF16)
    for at in range(2):
        span = slice(0, own) if at == 0 else slice(rows - own, rows)

        @pl.when(side[0] == at)
        def _(span=span):
            out_ref[:, :latent] = latent_ref[span, :]
            out_ref[:, latent : latent + rope] = turned[span, :]


def pack(side, latent_cache, rope_keys, own, depth):
    return pl.pallas_call(
        functools.partial(pack_kernel, own),
        in_specs=[SCALARS, pl.BlockSpec(), pl.BlockSpec()],
        out_shape=jax.ShapeDtypeStruct((own, depth), BF16),
        compiler_params=params(),
        cost_estimate=cost(0, 1 << 20),
        name="pack",
    )(side, latent_cache, rope_keys.T)


def prep_kernel(nope, rope, per_shard, own, order, limits, base, q_ref, r_ref, w_ref, lat_ref, bias_ref):
    tokens = q_ref.shape[0]
    heads, _, latent = w_ref.shape
    lat_ref[:, latent + rope :] = jnp.zeros(
        (heads * tokens, lat_ref.shape[1] - latent - rope), BF16
    )
    for head in range(heads):
        rows = slice(head * tokens, (head + 1) * tokens)
        lat = jnp.dot(
            q_ref[:, head * nope : (head + 1) * nope], w_ref[head], preferred_element_type=F32
        )
        lat_ref[rows, :latent] = lat.astype(BF16)
        lat_ref[rows, latent : latent + rope] = r_ref[:, head * rope : (head + 1) * rope]

    @pl.when(pl.program_id(0) == 0)
    def _():
        keys = bias_ref.shape[1]
        column = lax.broadcasted_iota(jnp.int32, (1, keys), 1)
        place = jnp.full((1, keys), 2**30, jnp.int32)
        side = base[1]
        for at in range(keys // per_shard):
            inner = column - at * per_shard
            mine = jnp.where(side == 0, inner, inner + (per_shard - own))
            others = jnp.where(side == 0, inner, inner - own)
            row = jnp.where(inner < own, mine, others)
            here = (inner >= 0) & (inner < per_shard) & (row < limits[at])
            place = jnp.where(here, row + order[at] * per_shard, place)
        position = base[0] + lax.broadcasted_iota(jnp.int32, bias_ref.shape, 0)
        bias_ref[...] = jnp.where(place <= position, F32(0.0), F32(MASKED))


def prep(q_nope, q_rope, w_absorb, order, limits, base, per_shard, own, depth):
    heads, nope, latent = w_absorb.shape
    tokens = q_nope.shape[0]
    rope = q_rope.shape[1] // heads
    keys = per_shard * order.shape[0]
    return pl.pallas_call(
        functools.partial(prep_kernel, nope, rope, per_shard, own),
        grid=(heads // STEP,),
        in_specs=[
            SCALARS,
            SCALARS,
            SCALARS,
            pl.BlockSpec((tokens, STEP * nope), lambda i: (0, i)),
            pl.BlockSpec((tokens, STEP * rope), lambda i: (0, i)),
            pl.BlockSpec((STEP, nope, latent), lambda i: (i, 0, 0)),
        ],
        out_specs=[
            pl.BlockSpec((STEP * tokens, depth), lambda i: (i, 0)),
            pl.BlockSpec((tokens, keys), lambda i: (0, 0)),
        ],
        out_shape=[
            jax.ShapeDtypeStruct((heads * tokens, depth), BF16),
            jax.ShapeDtypeStruct((tokens, keys), F32),
        ],
        compiler_params=params(),
        cost_estimate=cost(2 * heads * tokens * nope * latent, 12 << 20),
        name="prep",
    )(order, limits, base, q_nope, q_rope, w_absorb)


def join_kernel(groups, own, side, *refs):
    mine = refs[:groups]
    theirs = refs[groups : 2 * groups]
    out_ref, sem = refs[2 * groups :]
    per_shard = out_ref.shape[0] // (2 * groups)
    rest = per_shard - own
    skip = pl.multiple_of((1 - side[0]) * (own - rest), own - rest)
    copies = []
    for at in range(2 * groups):
        group, inner = at // 2, at % 2
        start = at * per_shard
        copies.append(
            pltpu.make_async_copy(
                mine[group].at[inner], out_ref.at[pl.ds(start, own)], sem.at[2 * at]
            )
        )
        copies.append(
            pltpu.make_async_copy(
                theirs[group].at[inner, pl.ds(skip, rest)],
                out_ref.at[pl.ds(start + own, rest)],
                sem.at[2 * at + 1],
            )
        )
    for copy in copies:
        copy.start()
    for copy in copies:
        copy.wait()


def join(side, mine, theirs, per_shard):
    groups = len(mine)
    _, own, depth = mine[0].shape
    return pl.pallas_call(
        functools.partial(join_kernel, groups, own),
        in_specs=[SCALARS] + [ANYWHERE] * (2 * groups),
        out_shape=jax.ShapeDtypeStruct((2 * groups * per_shard, depth), BF16),
        scratch_shapes=[pltpu.SemaphoreType.DMA((4 * groups,))],
        compiler_params=params(),
        cost_estimate=cost(0, 4 << 20),
        name="join",
    )(side, *mine, *theirs)


def attend_kernel(scale, q_ref, bias_ref, w_ref, kv_ref, *refs):
    out_ref, scores, probs = refs[-3:]
    tokens = bias_ref.shape[0]
    heads, latent, value = w_ref.shape
    pair = scores.shape[1] // tokens

    def score(at):
        rows = slice(at * pair * tokens, (at + 1) * pair * tokens)
        scores[at % 2] = lax.dot_general(
            q_ref[rows, :], kv_ref[...], (((1,), (1,)), ((), ())), preferred_element_type=F32
        )

    def weigh(at):
        totals = []
        for head in range(pair):
            rows = slice(head * tokens, (head + 1) * tokens)
            masked = scores[at % 2, rows, :] + bias_ref[...]
            top = jnp.max(masked, axis=-1, keepdims=True)
            expo = jnp.exp2((masked - top) * F32(scale))
            totals.append(jnp.sum(expo, axis=-1, keepdims=True))
            probs[at % 2, rows, :] = expo.astype(BF16)
        weighted = jnp.dot(probs[at % 2], kv_ref[:, :latent], preferred_element_type=F32)
        for head in range(pair):
            rows = slice(head * tokens, (head + 1) * tokens)
            mixed = (weighted[rows, :] / totals[head]).astype(BF16)
            which = at * pair + head
            out = jnp.dot(mixed, w_ref[which], preferred_element_type=F32)
            out_ref[:, which * value : (which + 1) * value] = out.astype(BF16)

    score(0)
    for at in range(heads // pair):
        if at + 1 < heads // pair:
            score(at + 1)
        weigh(at)


def attend(start, steps, queries, bias, w_value, kv, scale, after=()):
    tokens, keys = bias.shape
    depth = queries.shape[1]
    _, latent, value = w_value.shape
    rows = STEP * tokens
    return pl.pallas_call(
        functools.partial(attend_kernel, scale * math.log2(math.e)),
        grid=(steps,),
        in_specs=[
            pl.BlockSpec((rows, depth), lambda i: (start + i, 0)),
            pl.BlockSpec((tokens, keys), lambda i: (0, 0)),
            pl.BlockSpec((STEP, latent, value), lambda i: (start + i, 0, 0)),
            pl.BlockSpec((keys, depth), lambda i: (0, 0)),
        ]
        + [ANYWHERE] * len(after),
        out_specs=pl.BlockSpec((tokens, STEP * value), lambda i: (0, i)),
        out_shape=jax.ShapeDtypeStruct((tokens, steps * STEP * value), BF16),
        scratch_shapes=[
            pltpu.VMEM((2, rows // 2, keys), F32),
            pltpu.VMEM((2, rows // 2, keys), BF16),
        ],
        compiler_params=params(),
        cost_estimate=cost(
            steps * 2 * rows * (keys * (depth + latent) + latent * value),
            (2 + steps) << 20,
            steps * rows * keys,
        ),
        name=f"attend{start}",
    )(queries, bias, w_value, kv, *after)


def project_kernel(start, groups, first, *refs):
    w_ref = refs[0]
    pairs = refs[1 : 1 + groups]
    out_ref, gathered, weights, sem = refs[-4:]
    tokens, depth = pairs[0].shape[1:]
    step = pl.program_id(0)
    each = 2 * groups // pl.num_programs(0)
    copies = [
        pltpu.make_async_copy(
            pairs[at % groups].at[at // groups],
            gathered.at[pl.ds(at * tokens, tokens)],
            sem.at[at],
        )
        for at in range(2 * groups)
    ]
    fetch = pltpu.make_async_copy(w_ref.at[pl.ds(start, depth)], weights, sem.at[2 * groups])

    @pl.when(step == 0)
    def _():
        fetch.start()
        for copy in copies:
            copy.start()
        fetch.wait()

    for at in range(2 * groups):
        @pl.when(step == at // each)
        def _(at=at):
            copies[at].wait()

    rows = each * tokens
    span = pl.ds(pl.multiple_of(step * rows, rows), rows)
    product = jnp.dot(gathered[span, :], weights[...], preferred_element_type=F32)
    out_ref[...] = product if first else refs[1 + groups][...] + product


def project(start, pairs, w_output, acc, each=2):
    groups = len(pairs)
    _, tokens, depth = pairs[0].shape
    columns = w_output.shape[1]
    rows = 2 * groups * tokens
    block = pl.BlockSpec((each * tokens, columns), lambda i: (i, 0))
    return pl.pallas_call(
        functools.partial(project_kernel, start, groups, acc is None),
        grid=(2 * groups // each,),
        in_specs=[ANYWHERE] * (1 + groups) + ([] if acc is None else [block]),
        out_specs=block,
        out_shape=jax.ShapeDtypeStruct((rows, columns), F32),
        scratch_shapes=[
            pltpu.VMEM((rows, depth), BF16),
            pltpu.VMEM((depth, columns), BF16),
            pltpu.SemaphoreType.DMA((2 * groups + 1,)),
        ],
        input_output_aliases={} if acc is None else {1 + groups: 0},
        compiler_params=params(),
        cost_estimate=cost(2 * rows * depth * columns, 10 << 20),
        name=f"project{start}",
    )(w_output, *pairs, *([] if acc is None else [acc]))


def finish_kernel(start, groups, choice, places, w_ref, *refs):
    pairs = refs[:groups]
    acc_ref, out_ref, gathered, weights, sem = refs[groups:]
    tokens, depth = pairs[0].shape[1:]
    copies = [
        pltpu.make_async_copy(
            pairs[at].at[choice[0]], gathered.at[pl.ds(at * tokens, tokens)], sem.at[at]
        )
        for at in range(groups)
    ]
    copies.append(pltpu.make_async_copy(w_ref.at[pl.ds(start, depth)], weights, sem.at[groups]))
    for copy in copies:
        copy.start()
    for copy in copies:
        copy.wait()
    product = jnp.dot(gathered[...], weights[...], preferred_element_type=F32)
    for at in range(groups):
        rows = slice(at * tokens, (at + 1) * tokens)
        to = pl.ds(pl.multiple_of(places[at] * tokens, tokens), tokens)
        out_ref[to, :] = (acc_ref[rows, :] + product[rows, :]).astype(out_ref.dtype)


def finish(start, choice, places, pairs, w_output, acc, dtype):
    groups = len(pairs)
    _, tokens, depth = pairs[0].shape
    columns = w_output.shape[1]
    rows = groups * tokens
    return pl.pallas_call(
        functools.partial(finish_kernel, start, groups),
        grid_spec=pltpu.PrefetchScalarGridSpec(
            num_scalar_prefetch=2,
            grid=(1,),
            in_specs=[ANYWHERE] * (1 + groups)
            + [pl.BlockSpec((rows, columns), lambda i, choice, places: (choice[0], 0))],
            out_specs=pl.BlockSpec((rows, columns), lambda i, choice, places: (0, 0)),
            scratch_shapes=[
                pltpu.VMEM((rows, depth), BF16),
                pltpu.VMEM((depth, columns), BF16),
                pltpu.SemaphoreType.DMA((groups + 1,)),
            ],
        ),
        out_shape=jax.ShapeDtypeStruct((rows, columns), dtype),
        compiler_params=params(),
        cost_estimate=cost(2 * rows * depth * columns, 6 << 20),
        name="finish",
    )(choice, places, w_output, *pairs, acc)


def local(
    q_nope, q_rope, latent_cache, rope_keys, w_absorb, w_value, w_output, span_offset, valid_lengths
):
    head_count, nope_dim, latent = w_absorb.shape
    tokens = q_nope.shape[0]
    rope_dim = rope_keys.shape[1]
    per_shard = latent_cache.shape[0]
    shards = valid_lengths.shape[0]
    value = w_value.shape[2]
    depth = -(-(latent + rope_dim) // LANES) * LANES
    own = -(-per_shard // 32) * 16
    me = lax.axis_index("ctx").astype(jnp.int32)
    side = lax.axis_index("head").astype(jnp.int32)
    sides = side[None]

    far = basis_of(shards)[0]
    mine = spread(pack(sides, latent_cache, rope_keys, own, depth), shards)
    keys = sorted(mine)
    theirs = {key: sibling(pair) for key, pair in mine.items()}
    owners = [key ^ (far * inner) for key in keys for inner in range(2)]
    order = jnp.asarray(owners, jnp.int32) ^ me
    limits = valid_lengths[order]
    base = jnp.concatenate([span_offset + me * tokens, sides])
    queries, bias = prep(
        q_nope, q_rope, w_absorb, order, limits, base, per_shard, own, depth
    )
    kv = join(sides, [mine[key] for key in keys], [theirs[key] for key in keys], per_shard)

    scale = 1.0 / math.sqrt(nope_dim + rope_dim)
    acc = None
    start = 0
    stacks = []
    for chunk, piece in enumerate(PIECES):
        steps = piece * head_count // (STEP * sum(PIECES))
        after = stacks[:-1][-1:]
        out = attend(start, steps, queries, bias, w_value, kv, scale, after)
        gathered = spread(out, shards)
        pairs = [gathered[key] for key in keys]
        stacks.append(gathered[0])
        row = start * STEP * value
        if chunk < len(PIECES) - 1:
            acc = project(row, pairs, w_output, acc)
        start += steps

    half = shards // 2
    keep = jnp.where(me // half == side, 0, 1).astype(jnp.int32)
    near = jnp.asarray(keys, jnp.int32) ^ me
    give = 1 - keep
    kept_places = (near ^ (far * keep)) % half
    give_places = (near ^ (far * give)) % half
    sent = finish(row, give[None], give_places, pairs, w_output, acc, BF16)
    other = sibling(sent)
    kept = finish(row, keep[None], kept_places, pairs, w_output, acc, F32)
    return (kept + other.astype(F32)).astype(BF16)


def solution(mesh):
    return jax.shard_map(
        local,
        mesh=mesh,
        in_specs=(
            P(("groups", "ctx"), "head"),
            P(("groups", "ctx"), "head"),
            P(("groups", "ctx"), None),
            P(("groups", "ctx"), None),
            P("head", None, None),
            P("head", None, None),
            P("head", "ctx"),
            P("groups"),
            P("groups"),
        ),
        out_specs=P(("groups", "head"), "ctx"),
        check_vma=False,
    )
```

time: 270 us -> 201 us (0.74)
  Pallas kernels: 0 us -> 94.5 us
  waiting for transfers between devices: 138 us -> 53.8 us
  matrix products: 82.2 us -> 0 us
  starting transfers between devices: 0.08 us -> 37.9 us
  blocking collectives: 33.1 us -> 0 us
  between operations: 13.8 us -> 1.01 us
  local copies, waits for them, and re-layouts: 1.74 us -> 6.99 us
  other arithmetic: 1.42 us -> 5.73 us
    all_gather x2 -> x0, waiting for transfers between devices: 129 us -> none  [the longest x1 124 us: local(): lax.all_gather(head_out, 'ctx', axis=0, tiled=True)]
    pallas_call x0 -> x20, Pallas kernels: none -> 94.5 us  [the longest x5 32.1 us: attend(): pl.pallas_call(functools.partial(attend_kernel, scale * math.log2(math.e)...]
    dot_general x11 -> x0, matrix products: 54 us -> none  [the longest x4 16.7 us: attend(): jnp.einsum('hqk,kc->hqc', expo.astype(jnp.bfloat16), cache_all, preferred...]
    ppermute x0 -> x29, waiting for transfers between devices: none -> 53.8 us  [the longest x24 53.8 us: exchange(): return lax.ppermute(x, 'ctx', [(i, i ^ mask) for i in range(shards)])]
    ppermute x0 -> x29, starting transfers between devices: none -> 37.9 us  [the longest x24 37.2 us: exchange(): return lax.ppermute(x, 'ctx', [(i, i ^ mask) for i in range(shards)])]
    all_gather x1 -> x0, blocking collectives: 33.1 us -> none  [local(): lax.all_gather(rope_keys, 'ctx', axis=0, tiled=True)]
    sub x4 -> x0, matrix products: 28.2 us -> none  [attend(): expo = jnp.where(visible[None], jnp.exp(scores - row_max), jnp.float32(0.0))]
    reduce_scatter x1 -> x0, waiting for transfers between devices: 7.69 us -> none  [local(): lax.psum_scatter(partial_value.astype(jnp.bfloat16), 'head', scatter_dime...]
  transfers between devices with their start and end apart: 3 -> 29, of which waited for: 3 -> 9; matrix products, arithmetic and copies ran while one was open for 3% -> 2% of each run, Pallas kernels for 0% -> 39%
where the time goes in v2:
time: 201 us; the launch traced here: 200 us
  Pallas kernels  94.5 us (47%)
  waiting for transfers between devices  53.8 us (27%)
  starting transfers between devices  37.9 us (19%)
  local copies, waits for them, and re-layouts  6.99 us (3%)
  other arithmetic  5.73 us (3%)
    ppermute x24, waiting for transfers between devices, exchange(): return lax.ppermute(x, 'ctx', [(i, i ^ mask) for i in range(shards)])  53.8 us
    ppermute x24, starting transfers between devices, exchange(): return lax.ppermute(x, 'ctx', [(i, i ^ mask) for i in range(shards)])  37.2 us
    pallas_call x5, Pallas kernels, attend(): pl.pallas_call(functools.partial(attend_kernel, scale * math.log2(math.e)...  32.1 us
    pallas_call x4, Pallas kernels, project(): pl.pallas_call(functools.partial(project_kernel, start, groups, acc is No...  27.8 us
    pallas_call x2, Pallas kernels, finish(): pl.pallas_call(functools.partial(finish_kernel, start, groups), grid_spec...  10.9 us
    pallas_call x6, Pallas kernels, stack(): pl.pallas_call(stack_kernel, out_shape=jax.ShapeDtypeStruct((2, *first.sh...  10.6 us
    pallas_call x1, Pallas kernels, prep(): pl.pallas_call(functools.partial(prep_kernel, nope, rope, per_shard, own)...  8.67 us
    unnamed x60, local copies, waits for them, and re-layouts  5.78 us
  transfers between devices with their start and end apart: 29, of which 9 were waited for; matrix products, arithmetic and copies ran while one was open for 2% of the time, Pallas kernels for 39%

profile of v2, /device:TPU:0, one launch (start us, length us, event | category | flops | bytes accessed | tf_op | source)
XLA Modules:
  0.0 200.0 jit_solution(1456565662327547081)
XLA Ops:
  1.7 5.0 %collective-permute-start = (bf16[80,640]{1,0:T(8,128)(2,1)}, bf16[80,640]{1,0:T(8,128)(2,1)S(1)}, u32[]{:S(2)}, u32[]{:S(2)}) collective-permute-start(bf16[80,640]{1,0:T(8,128)(2,1)} %pack.1.first_ref), channel_id=1, source_target_pairs={{0,12},{2,14},{4,8},{6,10},{8,4},{10,6},{12,0},{14,2},{1,13},{3,15... | collective-permute-start | bytes 307208 | tf_op jit(solution)/shard_map/ppermute | solution.py:36
  6.7 3.2 %collective-permute-done.second_ref = bf16[80,640]{1,0:T(8,128)(2,1)S(1)} collective-permute-done((bf16[80,640]{1,0:T(8,128)(2,1)}, bf16[80,640]{1,0:T(8,128)(2,1)S(1)}, u32[]{:S(2)}, u32[]{:S(2)}) %collective-permute-start) | collective-permute-done | bytes 102432 | tf_op jit(solution)/shard_map/ppermute | solution.py:36
  12.2 1.8 collective-permute-start.2
  15.5 3.1 %collective-permute-done.2.refs_2_ = bf16[2,80,640]{2,1,0:T(8,128)(2,1)S(1)} collective-permute-done((bf16[2,80,640]{2,1,0:T(8,128)(2,1)}, bf16[2,80,640]{2,1,0:T(8,128)(2,1)S(1)}, u32[]{:S(2)}, u32[]{:S(2)}) %collective-permute-start.2) | collective-permute-done | bytes 204832 | tf_op jit(solution)/shard_map/ppermute | solution.py:36
  22.0 2.5 %collective-permute-done.3.refs_3_ = bf16[2,80,640]{2,1,0:T(8,128)(2,1)S(1)} collective-permute-done((bf16[2,80,640]{2,1,0:T(8,128)(2,1)S(1)}, bf16[2,80,640]{2,1,0:T(8,128)(2,1)S(1)}, u32[]{:S(2)}, u32[]{:S(2)}) %collective-permute-start.3) | collective-permute-done | bytes 204832 | tf_op jit(solution)/shard_map/ppermute | solution.py:36
  27.0 8.7 %prep.1 = (bf16[4096,640]{1,0:T(8,128)(2,1)}, f32[128,1152]{1,0:T(8,128)}) custom-call(s32[8]{0:T(128)} %get-tuple-element.10.order, s32[8]{0:T(128)} %gather_fusion, s32[2]{0:T(128)} %pad_add_fusion.base, bf16[128,4096]{1,0:T(8,128)(2,1)} %q_ref.1, bf16[128,2048]{1,0:T(8,128)(2,1)} %r_ref.1, bf16[32,128,512]{2,1,0:T(8,128)(2,1)} %w_ref.8), custom_call_target="tpu_custom_call" | custom-call | flops 536870912 | bytes 12582912 | tf_op jit(solution)/shard_map/prep/pallas_call | solution.py:127
  37.2 2.8 %join.1.kv_ref = bf16[1152,640]{1,0:T(8,128)(2,1)} custom-call(s32[1]{0:T(128)} %bitcast.2.side, bf16[2,80,640]{2,1,0:T(8,128)(2,1)} %stack.6.refs_0_, bf16[2,80,640]{2,1,0:T(8,128)(2,1)} %copy-done.21, bf16[2,80,640]{2,1,0:T(8,128)(2,1)} %copy-done.20, bf16[2,80,640]{2,1,0:T(8,128)(2,1)} %copy-done.22, bf16[2,80,640]{2,1,0:T(8,128)(2,1)} %copy-done.23, ...), custom_call_target="tpu_custom_call" | custom-call | bytes 4194304 | tf_op jit(solution)/shard_map/join/pallas_call | solution.py:184
  40.0 5.0 %attend0.1.first_ref = bf16[128,512]{1,0:T(8,128)(2,1)} custom-call(bf16[4096,640]{1,0:T(8,128)(2,1)} %get-tuple-element.7.q_ref, f32[128,1152]{1,0:T(8,128)} %get-tuple-element.8.bias_ref, bf16[32,512,128]{2,1,0:T(8,128)(2,1)} %w_ref.13, bf16[1152,640]{1,0:T(8,128)(2,1)} %join.1.kv_ref), custom_call_target="tpu_custom_call" | custom-call | flops 1426063360 | bytes 3145728 | tf_op jit(solution)/shard_map/attend0/pallas_call | solution.py:236
  45.0 3.0 %collective-permute-start.8 = (bf16[128,512]{1,0:T(8,128)(2,1)}, bf16[128,512]{1,0:T(8,128)(2,1)S(1)}, u32[]{:S(2)}, u32[]{:S(2)}) collective-permute-start(bf16[128,512]{1,0:T(8,128)(2,1)} %attend0.1.first_ref), channel_id=1, source_target_pairs={{0,12},{2,14},{4,8},{6,10},{8,4},{10,6},{12,0},{14,2},{1,13},{3,15... | collective-permute-start | bytes 393224 | tf_op jit(solution)/shard_map/ppermute | solution.py:36
  48.0 7.4 %attend1.1.first_ref = bf16[128,1024]{1,0:T(8,128)(2,1)} custom-call(bf16[4096,640]{1,0:T(8,128)(2,1)} %get-tuple-element.7.q_ref, f32[128,1152]{1,0:T(8,128)} %get-tuple-element.8.bias_ref, bf16[32,512,128]{2,1,0:T(8,128)(2,1)} %w_ref.13, bf16[1152,640]{1,0:T(8,128)(2,1)} %join.1.kv_ref), custom_call_target="tpu_custom_call" | custom-call | flops 2852126720 | bytes 4194304 | tf_op jit(solution)/shard_map/attend1/pallas_call | solution.py:236
  56.9 1.7 stack.7.refs_0_.refs_1_
  58.6 7.4 %attend3.1.first_ref = bf16[128,1024]{1,0:T(8,128)(2,1)} custom-call(bf16[4096,640]{1,0:T(8,128)(2,1)} %get-tuple-element.7.q_ref, f32[128,1152]{1,0:T(8,128)} %get-tuple-element.8.bias_ref, bf16[32,512,128]{2,1,0:T(8,128)(2,1)} %w_ref.13, bf16[1152,640]{1,0:T(8,128)(2,1)} %join.1.kv_ref, bf16[2,128,512]{2,1,0:T(8,128)(2,1)} %stack.7.refs_0_.refs_1_), custom_call_target="tpu_custom_call" | custom-call | flops 2852126720 | bytes 4194304 | tf_op jit(solution)/shard_map/attend3/pallas_call | solution.py:236
  66.0 3.0 %collective-permute-start.9 = (bf16[128,1024]{1,0:T(8,128)(2,1)}, bf16[128,1024]{1,0:T(8,128)(2,1)S(1)}, u32[]{:S(2)}, u32[]{:S(2)}) collective-permute-start(bf16[128,1024]{1,0:T(8,128)(2,1)} %attend3.1.first_ref), channel_id=1, source_target_pairs={{0,12},{2,14},{4,8},{6,10},{8,4},{10,6},{12,0},{14,2},{1,13},{3,15... | collective-permute-start | bytes 786440 | tf_op jit(solution)/shard_map/ppermute | solution.py:36
  69.7 1.9 stack.10.refs_0_.refs_1_
  72.8 7.4 %attend5.1.first_ref = bf16[128,1024]{1,0:T(8,128)(2,1)} custom-call(bf16[4096,640]{1,0:T(8,128)(2,1)} %get-tuple-element.7.q_ref, f32[128,1152]{1,0:T(8,128)} %get-tuple-element.8.bias_ref, bf16[32,512,128]{2,1,0:T(8,128)(2,1)} %w_ref.13, bf16[1152,640]{1,0:T(8,128)(2,1)} %join.1.kv_ref, bf16[2,128,1024]{2,1,0:T(8,128)(2,1)} %stack.10.refs_0_.refs_1_), custom_call_target="tpu_custom_call" | custom-call | flops 2852126720 | bytes 4194304 | tf_op jit(solution)/shard_map/attend5/pallas_call | solution.py:236
  83.9 1.9 stack.8.refs_0_.refs_1_
  85.8 2.0 %collective-permute-start.20 = (bf16[2,128,1024]{2,1,0:T(8,128)(2,1)}, bf16[2,128,1024]{2,1,0:T(8,128)(2,1)S(1)}, u32[]{:S(2)}, u32[]{:S(2)}) collective-permute-start(bf16[2,128,1024]{2,1,0:T(8,128)(2,1)} %stack.8.refs_0_.refs_1_), channel_id=1, source_target_pairs={{0,4},{2,6},{4,0},{6,2},{8,12},{10,14},{12,8},{14,10},{1,5},{3,7},... | collective-permute-start | bytes 1572872 | tf_op jit(solution)/shard_map/ppermute | solution.py:36
  87.8 5.0 %attend7.1.first_ref = bf16[128,512]{1,0:T(8,128)(2,1)} custom-call(bf16[4096,640]{1,0:T(8,128)(2,1)} %get-tuple-element.7.q_ref, f32[128,1152]{1,0:T(8,128)} %get-tuple-element.8.bias_ref, bf16[32,512,128]{2,1,0:T(8,128)(2,1)} %w_ref.13, bf16[1152,640]{1,0:T(8,128)(2,1)} %join.1.kv_ref, bf16[2,128,1024]{2,1,0:T(8,128)(2,1)} %stack.8.refs_0_.refs_1_), custom_call_target="tpu_custom_call" | custom-call | flops 1426063360 | bytes 3145728 | tf_op jit(solution)/shard_map/attend7/pallas_call | solution.py:236
  94.0 3.0 %collective-permute-start.10 = (bf16[128,512]{1,0:T(8,128)(2,1)}, bf16[128,512]{1,0:T(8,128)(2,1)S(1)}, u32[]{:S(2)}, u32[]{:S(2)}) collective-permute-start(bf16[128,512]{1,0:T(8,128)(2,1)} %attend7.1.first_ref), channel_id=1, source_target_pairs={{0,12},{2,14},{4,8},{6,10},{8,4},{10,6},{12,0},{14,2},{1,13},{3,15... | collective-permute-start | bytes 393224 | tf_op jit(solution)/shard_map/ppermute | solution.py:36
  97.1 1.9 stack.11.refs_1_
  102.4 11.3 %collective-permute-done.10.second_ref = bf16[128,512]{1,0:T(8,128)(2,1)S(1)} collective-permute-done((bf16[128,512]{1,0:T(8,128)(2,1)}, bf16[128,512]{1,0:T(8,128)(2,1)S(1)}, u32[]{:S(2)}, u32[]{:S(2)}) %collective-permute-start.10) | collective-permute-done | bytes 131104 | tf_op jit(solution)/shard_map/ppermute | solution.py:36
  115.2 12.6 %collective-permute-done.27.refs_4_ = bf16[2,128,512]{2,1,0:T(8,128)(2,1)S(1)} collective-permute-done((bf16[2,128,512]{2,1,0:T(8,128)(2,1)S(1)}, bf16[2,128,512]{2,1,0:T(8,128)(2,1)S(1)}, u32[]{:S(2)}, u32[]{:S(2)}) %collective-permute-start.27) | collective-permute-done | bytes 262176 | tf_op jit(solution)/shard_map/ppermute | solution.py:36
  134.4 4.8 %project0.1.refs_5_ = f32[1024,896]{1,0:T(8,128)} custom-call(bf16[4096,896]{1,0:T(8,128)(2,1)} %w_ref.15, bf16[2,128,512]{2,1,0:T(8,128)(2,1)} %stack.7.refs_0_.refs_1_, bf16[2,128,512]{2,1,0:T(8,128)(2,1)} %copy-done.14, bf16[2,128,512]{2,1,0:T(8,128)(2,1)} %copy-done.15, bf16[2,128,512]{2,1,0:T(8,128)(2,1)} %copy-done.16), custom_call_target="tpu_custom_call" | custom-call | flops 939524096 | bytes 10485760 | tf_op jit(solution)/shard_map/project0/pallas_call | solution.py:303
  139.2 7.7 %project512.1.refs_5_ = f32[1024,896]{1,0:T(8,128)} custom-call(bf16[4096,896]{1,0:T(8,128)(2,1)} %w_ref.15, bf16[2,128,1024]{2,1,0:T(8,128)(2,1)} %stack.10.refs_0_.refs_1_, bf16[2,128,1024]{2,1,0:T(8,128)(2,1)} %copy-done.11, bf16[2,128,1024]{2,1,0:T(8,128)(2,1)} %copy-done.8, ...), custom_call_target="tpu_custom_call", output_to_operand_aliasing={{}: (5, {})} | custom-call | flops 1879048192 | bytes 10485760 | tf_op jit(solution)/shard_map/project512/pallas_call | solution.py:303
  149.0 5.0 %collective-permute-done.21.refs_4_ = bf16[2,128,1024]{2,1,0:T(8,128)(2,1)} collective-permute-done((bf16[2,128,1024]{2,1,0:T(8,128)(2,1)S(1)}, bf16[2,128,1024]{2,1,0:T(8,128)(2,1)}, u32[]{:S(2)}, u32[]{:S(2)}) %collective-permute-start.21) | collective-permute-done | bytes 524320 | tf_op jit(solution)/shard_map/ppermute | solution.py:36
  154.0 7.7 %project1536.1.refs_5_ = f32[1024,896]{1,0:T(8,128)} custom-call(bf16[4096,896]{1,0:T(8,128)(2,1)} %w_ref.15, bf16[2,128,1024]{2,1,0:T(8,128)(2,1)} %stack.8.refs_0_.refs_1_, bf16[2,128,1024]{2,1,0:T(8,128)(2,1)} %collective-permute-done.19.refs_2_, bf16[2,128,1024]{2,1,0:T(8,128)(2,1)} %copy-done.9, ...), custom_call_target="tpu_custom_call", output_to_operand_aliasing={{}: (5, {})} | custom-call | flops 1879048192 | bytes 10485760 | tf_op jit(solution)/shard_map/project1536/pallas_call | solution.py:303
  161.7 3.5 %collective-permute-done.16.refs_2_ = bf16[2,128,1024]{2,1,0:T(8,128)(2,1)S(1)} collective-permute-done((bf16[2,128,1024]{2,1,0:T(8,128)(2,1)}, bf16[2,128,1024]{2,1,0:T(8,128)(2,1)S(1)}, u32[]{:S(2)}, u32[]{:S(2)}) %collective-permute-start.16) | collective-permute-done | bytes 524320 | tf_op jit(solution)/shard_map/ppermute | solution.py:36
  165.2 11.2 %collective-permute-done.18.refs_4_ = bf16[2,128,1024]{2,1,0:T(8,128)(2,1)S(1)} collective-permute-done((bf16[2,128,1024]{2,1,0:T(8,128)(2,1)S(1)}, bf16[2,128,1024]{2,1,0:T(8,128)(2,1)S(1)}, u32[]{:S(2)}, u32[]{:S(2)}) %collective-permute-start.18) | collective-permute-done | bytes 524320 | tf_op jit(solution)/shard_map/ppermute | solution.py:36
  177.2 7.7 %project2560.1.refs_4_ = f32[1024,896]{1,0:T(8,128)} custom-call(bf16[4096,896]{1,0:T(8,128)(2,1)} %w_ref.15, bf16[2,128,1024]{2,1,0:T(8,128)(2,1)} %stack.11.refs_1_, bf16[2,128,1024]{2,1,0:T(8,128)(2,1)} %copy-done.12, bf16[2,128,1024]{2,1,0:T(8,128)(2,1)} %copy-done.10, bf16[2,128,1024]{2,1,0:T(8,128)(2,1)} %copy-done.13, ...), custom_call_target="tpu_custom_call", output_to_operand_aliasing={{}: (5, {})} | custom-call | flops 1879048192 | bytes 10485760 | tf_op jit(solution)/shard_map/project2560/pallas_call | solution.py:303
  185.7 5.3 %finish.3 = bf16[512,896]{1,0:T(8,128)(2,1)} custom-call(s32[1]{0:T(128)} %bitcast.4.choice, s32[4]{0:T(128)} %and_select_fusion.places, bf16[4096,896]{1,0:T(8,128)(2,1)} %w_ref.15, bf16[2,128,512]{2,1,0:T(8,128)(2,1)} %stack.9.refs_0_, bf16[2,128,512]{2,1,0:T(8,128)(2,1)} %copy-done.6, bf16[2,128,512]{2,1,0:T(8,128)(2,1)} %copy-done.5, ...), custom_call_target="tpu_custom_call" | custom-call | flops 469762048 | bytes 6291456 | tf_op jit(solution)/shard_map/finish/pallas_call | solution.py:348
  191.7 5.6 %finish.2 = f32[512,896]{1,0:T(8,128)} custom-call(s32[1]{0:T(128)} %bitcast.choice, s32[4]{0:T(128)} %and_select_fusion.1.places, bf16[4096,896]{1,0:T(8,128)(2,1)} %w_ref.15, bf16[2,128,512]{2,1,0:T(8,128)(2,1)} %stack.9.refs_0_, bf16[2,128,512]{2,1,0:T(8,128)(2,1)} %copy-done.6, bf16[2,128,512]{2,1,0:T(8,128)(2,1)} %copy-done.5, ...), custom_call_target="tpu_custom_call" | custom-call | flops 469762048 | bytes 6291456 | tf_op jit(solution)/shard_map/finish/pallas_call | solution.py:348
  197.3 2.6 %add_convert_fusion = bf16[512,896]{1,0:T(8,128)(2,1)} fusion(f32[512,896]{1,0:T(8,128)} %finish.2, bf16[512,896]{1,0:T(8,128)(2,1)S(1)} %collective-permute-done.28), kind=kLoop, calls=%fused_computation.1 | loop fusion | flops 1376256 | bytes 3670016 | tf_op jit(solution)/shard_map/convert_element_type | solution.py:422
  (113 shorter events, 36.4 us)
Async XLA Ops:
  1.7 8.3 %collective-permute-start = (bf16[80,640]{1,0:T(8,128)(2,1)}, bf16[80,640]{1,0:T(8,128)(2,1)S(1)}, u32[]{:S(2)}, u32[]{:S(2)}) collective-permute-start(bf16[80,640]{1,0:T(8,128)(2,1)} %pack.1.first_ref), channel_id=1, source_target_pairs={{0,12},{2,14},{4,8},{6,10},{8,4},{10,6},{12,0},{14,2},{1,13},{3,15... | collective-permute-start | bytes 307208 | tf_op jit(solution)/shard_map/ppermute | solution.py:36
  12.2 6.4 %collective-permute-start.2 = (bf16[2,80,640]{2,1,0:T(8,128)(2,1)}, bf16[2,80,640]{2,1,0:T(8,128)(2,1)S(1)}, u32[]{:S(2)}, u32[]{:S(2)}) collective-permute-start(bf16[2,80,640]{2,1,0:T(8,128)(2,1)} %stack.6.refs_0_), channel_id=1, source_target_pairs={{0,4},{2,6},{4,0},{6,2},{8,12},{10,14},{12,8},{14,10},{1,5},{3,7},... | collective-permute-start | bytes 614408 | tf_op jit(solution)/shard_map/ppermute | solution.py:36
  14.0 7.9 %collective-permute-start.1 = (bf16[2,80,640]{2,1,0:T(8,128)(2,1)}, bf16[2,80,640]{2,1,0:T(8,128)(2,1)S(1)}, u32[]{:S(2)}, u32[]{:S(2)}) collective-permute-start(bf16[2,80,640]{2,1,0:T(8,128)(2,1)} %stack.6.refs_0_), channel_id=1, source_target_pairs={{0,2},{2,0},{4,6},{6,4},{8,10},{10,8},{12,14},{14,12},{1,3},{3,1},... | collective-permute-start | bytes 614408 | tf_op jit(solution)/shard_map/ppermute | solution.py:36
  18.6 5.8 %collective-permute-start.3 = (bf16[2,80,640]{2,1,0:T(8,128)(2,1)S(1)}, bf16[2,80,640]{2,1,0:T(8,128)(2,1)S(1)}, u32[]{:S(2)}, u32[]{:S(2)}) collective-permute-start(bf16[2,80,640]{2,1,0:T(8,128)(2,1)S(1)} %collective-permute-done.2.refs_2_), channel_id=1, source_target_pairs={{0,2},{2,0},{4,6},{6,4},{8,10},{10,8},{12,14},{14,12},{1,3},{3,1},... | collective-permute-start | bytes 614408 | tf_op jit(solution)/shard_map/ppermute | solution.py:36
  21.4 14.3 %collective-permute-start.4 = (bf16[2,80,640]{2,1,0:T(8,128)(2,1)}, bf16[2,80,640]{2,1,0:T(8,128)(2,1)S(1)}, u32[]{:S(2)}, u32[]{:S(2)}) collective-permute-start(bf16[2,80,640]{2,1,0:T(8,128)(2,1)} %stack.6.refs_0_), channel_id=1, source_target_pairs={{0,1},{1,0},{2,3},{3,2},{4,5},{5,4},{6,7},{7,6},{8,9},{9,8},{10,11... | collective-permute-start | bytes 614408 | tf_op jit(solution)/shard_map/ppermute | solution.py:40
  21.4 14.3 %collective-permute-start.6 = (bf16[2,80,640]{2,1,0:T(8,128)(2,1)S(1)}, bf16[2,80,640]{2,1,0:T(8,128)(2,1)S(1)}, u32[]{:S(2)}, u32[]{:S(2)}) collective-permute-start(bf16[2,80,640]{2,1,0:T(8,128)(2,1)S(1)} %collective-permute-done.2.refs_2_), channel_id=1, source_target_pairs={{0,1},{1,0},{2,3},{3,2},{4,5},{5,4},{6,7},{7,6},{8,9},{9,8},{10,11... | collective-permute-start | bytes 614408 | tf_op jit(solution)/shard_map/ppermute | solution.py:40
  21.9 13.8 %collective-permute-start.5 = (bf16[2,80,640]{2,1,0:T(8,128)(2,1)S(1)}, bf16[2,80,640]{2,1,0:T(8,128)(2,1)S(1)}, u32[]{:S(2)}, u32[]{:S(2)}) collective-permute-start(bf16[2,80,640]{2,1,0:T(8,128)(2,1)S(1)} %collective-permute-done.1.refs_1_), channel_id=1, source_target_pairs={{0,1},{1,0},{2,3},{3,2},{4,5},{5,4},{6,7},{7,6},{8,9},{9,8},{10,11... | collective-permute-start | bytes 614408 | tf_op jit(solution)/shard_map/ppermute | solution.py:40
  24.5 11.3 %collective-permute-start.7 = (bf16[2,80,640]{2,1,0:T(8,128)(2,1)S(1)}, bf16[2,80,640]{2,1,0:T(8,128)(2,1)S(1)}, u32[]{:S(2)}, u32[]{:S(2)}) collective-permute-start(bf16[2,80,640]{2,1,0:T(8,128)(2,1)S(1)} %collective-permute-done.3.refs_3_), channel_id=1, source_target_pairs={{0,1},{1,0},{2,3},{3,2},{4,5},{5,4},{6,7},{7,6},{8,9},{9,8},{10,11... | collective-permute-start | bytes 614408 | tf_op jit(solution)/shard_map/ppermute | solution.py:40
  45.0 11.3 %collective-permute-start.8 = (bf16[128,512]{1,0:T(8,128)(2,1)}, bf16[128,512]{1,0:T(8,128)(2,1)S(1)}, u32[]{:S(2)}, u32[]{:S(2)}) collective-permute-start(bf16[128,512]{1,0:T(8,128)(2,1)} %attend0.1.first_ref), channel_id=1, source_target_pairs={{0,12},{2,14},{4,8},{6,10},{8,4},{10,6},{12,0},{14,2},{1,13},{3,15... | collective-permute-start | bytes 393224 | tf_op jit(solution)/shard_map/ppermute | solution.py:36
  55.4 13.6 %collective-permute-start.14 = (bf16[128,1024]{1,0:T(8,128)(2,1)}, bf16[128,1024]{1,0:T(8,128)(2,1)S(1)}, u32[]{:S(2)}, u32[]{:S(2)}) collective-permute-start(bf16[128,1024]{1,0:T(8,128)(2,1)} %attend1.1.first_ref), channel_id=1, source_target_pairs={{0,12},{2,14},{4,8},{6,10},{8,4},{10,6},{12,0},{14,2},{1,13},{3,15... | collective-permute-start | bytes 786440 | tf_op jit(solution)/shard_map/ppermute | solution.py:36
  66.0 17.2 %collective-permute-start.9 = (bf16[128,1024]{1,0:T(8,128)(2,1)}, bf16[128,1024]{1,0:T(8,128)(2,1)S(1)}, u32[]{:S(2)}, u32[]{:S(2)}) collective-permute-start(bf16[128,1024]{1,0:T(8,128)(2,1)} %attend3.1.first_ref), channel_id=1, source_target_pairs={{0,12},{2,14},{4,8},{6,10},{8,4},{10,6},{12,0},{14,2},{1,13},{3,15... | collective-permute-start | bytes 786440 | tf_op jit(solution)/shard_map/ppermute | solution.py:36
  71.6 29.3 %collective-permute-start.23 = (bf16[2,128,1024]{2,1,0:T(8,128)(2,1)}, bf16[2,128,1024]{2,1,0:T(8,128)(2,1)S(1)}, u32[]{:S(2)}, u32[]{:S(2)}) collective-permute-start(bf16[2,128,1024]{2,1,0:T(8,128)(2,1)} %stack.10.refs_0_.refs_1_), channel_id=1, source_target_pairs={{0,4},{2,6},{4,0},{6,2},{8,12},{10,14},{12,8},{14,10},{1,5},{3,7},... | collective-permute-start | bytes 1572872 | tf_op jit(solution)/shard_map/ppermute | solution.py:36
  80.2 13.8 %collective-permute-start.15 = (bf16[128,1024]{1,0:T(8,128)(2,1)}, bf16[128,1024]{1,0:T(8,128)(2,1)S(1)}, u32[]{:S(2)}, u32[]{:S(2)}) collective-permute-start(bf16[128,1024]{1,0:T(8,128)(2,1)} %attend5.1.first_ref), channel_id=1, source_target_pairs={{0,12},{2,14},{4,8},{6,10},{8,4},{10,6},{12,0},{14,2},{1,13},{3,15... | collective-permute-start | bytes 786440 | tf_op jit(solution)/shard_map/ppermute | solution.py:36
  81.7 17.3 %collective-permute-start.25 = (bf16[2,128,512]{2,1,0:T(8,128)(2,1)S(1)}, bf16[2,128,512]{2,1,0:T(8,128)(2,1)S(1)}, u32[]{:S(2)}, u32[]{:S(2)}) collective-permute-start(bf16[2,128,512]{2,1,0:T(8,128)(2,1)S(1)} %copy-done.3), channel_id=1, source_target_pairs={{0,2},{2,0},{4,6},{6,4},{8,10},{10,8},{12,14},{14,12},{1,3},{3,1},... | collective-permute-start | bytes 786440 | tf_op jit(solution)/shard_map/ppermute | solution.py:36
  83.2 17.3 %collective-permute-start.26 = (bf16[2,128,512]{2,1,0:T(8,128)(2,1)S(1)}, bf16[2,128,512]{2,1,0:T(8,128)(2,1)S(1)}, u32[]{:S(2)}, u32[]{:S(2)}) collective-permute-start(bf16[2,128,512]{2,1,0:T(8,128)(2,1)S(1)} %copy-done.3), channel_id=1, source_target_pairs={{0,4},{2,6},{4,0},{6,2},{8,12},{10,14},{12,8},{14,10},{1,5},{3,7},... | collective-permute-start | bytes 786440 | tf_op jit(solution)/shard_map/ppermute | solution.py:36
  85.8 42.1 %copy-start.2 = (bf16[2,128,1024]{2,1,0:T(8,128)(2,1)S(1)}, bf16[2,128,1024]{2,1,0:T(8,128)(2,1)}, u32[]{:S(2)}) copy-start(bf16[2,128,1024]{2,1,0:T(8,128)(2,1)} %stack.8.refs_0_.refs_1_) | copy-start | bytes 1572868
  85.8 43.6 %collective-permute-start.20 = (bf16[2,128,1024]{2,1,0:T(8,128)(2,1)}, bf16[2,128,1024]{2,1,0:T(8,128)(2,1)S(1)}, u32[]{:S(2)}, u32[]{:S(2)}) collective-permute-start(bf16[2,128,1024]{2,1,0:T(8,128)(2,1)} %stack.8.refs_0_.refs_1_), channel_id=1, source_target_pairs={{0,4},{2,6},{4,0},{6,2},{8,12},{10,14},{12,8},{14,10},{1,5},{3,7},... | collective-permute-start | bytes 1572872 | tf_op jit(solution)/shard_map/ppermute | solution.py:36
  94.0 19.7 %collective-permute-start.10 = (bf16[128,512]{1,0:T(8,128)(2,1)}, bf16[128,512]{1,0:T(8,128)(2,1)S(1)}, u32[]{:S(2)}, u32[]{:S(2)}) collective-permute-start(bf16[128,512]{1,0:T(8,128)(2,1)} %attend7.1.first_ref), channel_id=1, source_target_pairs={{0,12},{2,14},{4,8},{6,10},{8,4},{10,6},{12,0},{14,2},{1,13},{3,15... | collective-permute-start | bytes 393224 | tf_op jit(solution)/shard_map/ppermute | solution.py:36
  98.9 35.4 %copy-start.14 = (bf16[2,128,512]{2,1,0:T(8,128)(2,1)}, bf16[2,128,512]{2,1,0:T(8,128)(2,1)S(1)}, u32[]{:S(2)}) copy-start(bf16[2,128,512]{2,1,0:T(8,128)(2,1)S(1)} %collective-permute-done.25.refs_2_) | copy-start | bytes 786436
  98.9 31.1 %collective-permute-start.22 = (bf16[2,128,1024]{2,1,0:T(8,128)(2,1)S(1)}, bf16[2,128,1024]{2,1,0:T(8,128)(2,1)S(1)}, u32[]{:S(2)}, u32[]{:S(2)}) collective-permute-start(bf16[2,128,1024]{2,1,0:T(8,128)(2,1)S(1)} %copy-done.1), channel_id=1, source_target_pairs={{0,2},{2,0},{4,6},{6,4},{8,10},{10,8},{12,14},{14,12},{1,3},{3,1},... | collective-permute-start | bytes 1572872 | tf_op jit(solution)/shard_map/ppermute | solution.py:36
  100.5 31.0 %collective-permute-start.17 = (bf16[2,128,1024]{2,1,0:T(8,128)(2,1)}, bf16[2,128,1024]{2,1,0:T(8,128)(2,1)S(1)}, u32[]{:S(2)}, u32[]{:S(2)}) collective-permute-start(bf16[2,128,1024]{2,1,0:T(8,128)(2,1)} %stack.11.refs_1_), channel_id=1, source_target_pairs={{0,4},{2,6},{4,0},{6,2},{8,12},{10,14},{12,8},{14,10},{1,5},{3,7},... | collective-permute-start | bytes 1572872 | tf_op jit(solution)/shard_map/ppermute | solution.py:36
  100.9 38.2 %copy-start.8 = (bf16[2,128,1024]{2,1,0:T(8,128)(2,1)}, bf16[2,128,1024]{2,1,0:T(8,128)(2,1)S(1)}, u32[]{:S(2)}) copy-start(bf16[2,128,1024]{2,1,0:T(8,128)(2,1)S(1)} %collective-permute-done.23.refs_3_) | copy-start | bytes 1572868
  100.9 33.4 %collective-permute-start.24 = (bf16[2,128,1024]{2,1,0:T(8,128)(2,1)S(1)}, bf16[2,128,1024]{2,1,0:T(8,128)(2,1)}, u32[]{:S(2)}, u32[]{:S(2)}) collective-permute-start(bf16[2,128,1024]{2,1,0:T(8,128)(2,1)S(1)} %collective-permute-done.23.refs_3_), channel_id=1, source_target_pairs={{0,2},{2,0},{4,6},{6,4},{8,10},{10,8},{12,14},{14,12},{1,3},{3,1},... | collective-permute-start | bytes 1572872 | tf_op jit(solution)/shard_map/ppermute | solution.py:36
  113.7 14.1 %collective-permute-start.27 = (bf16[2,128,512]{2,1,0:T(8,128)(2,1)S(1)}, bf16[2,128,512]{2,1,0:T(8,128)(2,1)S(1)}, u32[]{:S(2)}, u32[]{:S(2)}) collective-permute-start(bf16[2,128,512]{2,1,0:T(8,128)(2,1)S(1)} %collective-permute-done.26.refs_3_), channel_id=1, source_target_pairs={{0,2},{2,0},{4,6},{6,4},{8,10},{10,8},{12,14},{14,12},{1,3},{3,1},... | collective-permute-start | bytes 786440 | tf_op jit(solution)/shard_map/ppermute | solution.py:36
  127.8 20.6 %collective-permute-start.19 = (bf16[2,128,1024]{2,1,0:T(8,128)(2,1)S(1)}, bf16[2,128,1024]{2,1,0:T(8,128)(2,1)}, u32[]{:S(2)}, u32[]{:S(2)}) collective-permute-start(bf16[2,128,1024]{2,1,0:T(8,128)(2,1)S(1)} %copy-done.2), channel_id=1, source_target_pairs={{0,2},{2,0},{4,6},{6,4},{8,10},{10,8},{12,14},{14,12},{1,3},{3,1},... | collective-permute-start | bytes 1572872 | tf_op jit(solution)/shard_map/ppermute | solution.py:36
  129.4 24.7 %collective-permute-start.21 = (bf16[2,128,1024]{2,1,0:T(8,128)(2,1)S(1)}, bf16[2,128,1024]{2,1,0:T(8,128)(2,1)}, u32[]{:S(2)}, u32[]{:S(2)}) collective-permute-start(bf16[2,128,1024]{2,1,0:T(8,128)(2,1)S(1)} %collective-permute-done.20.refs_3_), channel_id=1, source_target_pairs={{0,2},{2,0},{4,6},{6,4},{8,10},{10,8},{12,14},{14,12},{1,3},{3,1},... | collective-permute-start | bytes 1572872 | tf_op jit(solution)/shard_map/ppermute | solution.py:36
  130.0 35.1 %collective-permute-start.16 = (bf16[2,128,1024]{2,1,0:T(8,128)(2,1)}, bf16[2,128,1024]{2,1,0:T(8,128)(2,1)S(1)}, u32[]{:S(2)}, u32[]{:S(2)}) collective-permute-start(bf16[2,128,1024]{2,1,0:T(8,128)(2,1)} %stack.11.refs_1_), channel_id=1, source_target_pairs={{0,2},{2,0},{4,6},{6,4},{8,10},{10,8},{12,14},{14,12},{1,3},{3,1},... | collective-permute-start | bytes 1572872 | tf_op jit(solution)/shard_map/ppermute | solution.py:36
  131.5 44.9 %collective-permute-start.18 = (bf16[2,128,1024]{2,1,0:T(8,128)(2,1)S(1)}, bf16[2,128,1024]{2,1,0:T(8,128)(2,1)S(1)}, u32[]{:S(2)}, u32[]{:S(2)}) collective-permute-start(bf16[2,128,1024]{2,1,0:T(8,128)(2,1)S(1)} %collective-permute-done.17.refs_3_), channel_id=1, source_target_pairs={{0,2},{2,0},{4,6},{6,4},{8,10},{10,8},{12,14},{14,12},{1,3},{3,1},... | collective-permute-start | bytes 1572872 | tf_op jit(solution)/shard_map/ppermute | solution.py:36
  134.3 12.5 %collective-permute-start.12 = (bf16[2,128,512]{2,1,0:T(8,128)(2,1)}, bf16[2,128,512]{2,1,0:T(8,128)(2,1)S(1)}, u32[]{:S(2)}, u32[]{:S(2)}) collective-permute-start(bf16[2,128,512]{2,1,0:T(8,128)(2,1)} %stack.9.refs_0_), channel_id=1, source_target_pairs={{0,4},{2,6},{4,0},{6,2},{8,12},{10,14},{12,8},{14,10},{1,5},{3,7},... | collective-permute-start | bytes 786440 | tf_op jit(solution)/shard_map/ppermute | solution.py:36
  146.9 38.0 %collective-permute-start.11 = (bf16[2,128,512]{2,1,0:T(8,128)(2,1)S(1)}, bf16[2,128,512]{2,1,0:T(8,128)(2,1)S(1)}, u32[]{:S(2)}, u32[]{:S(2)}) collective-permute-start(bf16[2,128,512]{2,1,0:T(8,128)(2,1)S(1)} %copy-done.4), channel_id=1, source_target_pairs={{0,2},{2,0},{4,6},{6,4},{8,10},{10,8},{12,14},{14,12},{1,3},{3,1},... | collective-permute-start | bytes 786440 | tf_op jit(solution)/shard_map/ppermute | solution.py:36
  148.4 36.5 %collective-permute-start.13 = (bf16[2,128,512]{2,1,0:T(8,128)(2,1)S(1)}, bf16[2,128,512]{2,1,0:T(8,128)(2,1)S(1)}, u32[]{:S(2)}, u32[]{:S(2)}) collective-permute-start(bf16[2,128,512]{2,1,0:T(8,128)(2,1)S(1)} %collective-permute-done.12.refs_2_), channel_id=1, source_target_pairs={{0,2},{2,0},{4,6},{6,4},{8,10},{10,8},{12,14},{14,12},{1,3},{3,1},... | collective-permute-start | bytes 786440 | tf_op jit(solution)/shard_map/ppermute | solution.py:36
  191.0 6.3 %collective-permute-start.28 = (bf16[512,896]{1,0:T(8,128)(2,1)}, bf16[512,896]{1,0:T(8,128)(2,1)S(1)}, u32[]{:S(2)}, u32[]{:S(2)}) collective-permute-start(bf16[512,896]{1,0:T(8,128)(2,1)} %finish.3), channel_id=1, source_target_pairs={{0,1},{1,0},{2,3},{3,2},{4,5},{5,4},{6,7},{7,6},{8,9},{9,8},{10,11... | collective-permute-start | bytes 2752520 | tf_op jit(solution)/shard_map/ppermute | solution.py:40
  (27 other events, 211.4 us)

commit v3 on v0

v3 whole, which is shorter than its diff:
```python
import functools
import math

import jax
import jax.numpy as jnp
from jax import lax
from jax.experimental import pallas as pl
from jax.experimental.pallas import tpu as pltpu
from jax.sharding import PartitionSpec as P

F32 = jnp.float32
BF16 = jnp.bfloat16
MASKED = -1e30
LANES = 128
STEP = 4
PIECES = (1, 2, 2, 2, 1)
LOCAL = pl.BlockSpec(memory_space=pltpu.VMEM)
ANYWHERE = pl.BlockSpec(memory_space=pl.ANY)
SCALARS = pl.BlockSpec(memory_space=pltpu.SMEM)


def params(mib):
    return pltpu.CompilerParams(vmem_limit_bytes=mib * 1024 * 1024)


def cost(flops, size, exps=0):
    return pl.CostEstimate(flops=flops, bytes_accessed=size, transcendentals=exps)


def held(x):
    return pltpu.with_memory_space_constraint(x, pltpu.VMEM)


def basis_of(shards):
    if shards == 8:
        return (6, 2, 1)
    return tuple(1 << bit for bit in reversed(range(shards.bit_length() - 1)))


def exchange(x, mask, shards):
    return lax.ppermute(x, "ctx", [(i, i ^ mask) for i in range(shards)])


def sibling(x):
    return lax.ppermute(x, "head", [(0, 1), (1, 0)])


def stack_kernel(first_ref, second_ref, *refs):
    out_ref = refs[-1]
    out_ref[0] = first_ref[...]
    out_ref[1] = second_ref[...]


def stack(first, second, after=()):
    return pl.pallas_call(
        stack_kernel,
        in_specs=[LOCAL, LOCAL] + [ANYWHERE] * len(after),
        out_specs=LOCAL,
        out_shape=pltpu.VMEM((2, *first.shape), first.dtype),
        compiler_params=params(2),
        cost_estimate=cost(0, 1024),
        name="stack",
    )(held(first), held(second), *after)


def spread(x, shards, after=()):
    first, *rest = basis_of(shards)
    pairs = {0: stack(x, exchange(x, first, shards), after)}
    for mask in rest:
        pairs.update({key ^ mask: exchange(pair, mask, shards) for key, pair in pairs.items()})
    return pairs


def pack_kernel(own, latent_ref, rope_ref, out_ref):
    rows, latent = latent_ref.shape
    rope = rope_ref.shape[0]
    side = lax.axis_index("head")
    turned = rope_ref[...].astype(F32).T.astype(BF16)
    out_ref[:, latent:] = jnp.zeros((own, out_ref.shape[1] - latent), BF16)
    for at in range(2):
        span = slice(0, own) if at == 0 else slice(rows - own, rows)

        @pl.when(side == at)
        def _(span=span):
            out_ref[:, :latent] = latent_ref[span, :]
            out_ref[:, latent : latent + rope] = turned[span, :]


def pack(latent_cache, rope_keys, own, depth):
    return pl.pallas_call(
        functools.partial(pack_kernel, own),
        in_specs=[LOCAL, LOCAL],
        out_specs=LOCAL,
        out_shape=pltpu.VMEM((own, depth), BF16),
        compiler_params=params(2),
        cost_estimate=cost(0, 1024),
        name="pack",
    )(latent_cache, rope_keys.T)


def mask_kernel(own, owners, span_ref, valid_ref, bias_ref):
    tokens, keys = bias_ref.shape
    per_shard = keys // len(owners)
    me, side = lax.axis_index("ctx"), lax.axis_index("head")
    column = lax.broadcasted_iota(jnp.int32, (1, keys), 1)
    place = jnp.full((1, keys), 2**30, jnp.int32)
    for at, owner in enumerate(owners):
        shard = me ^ owner
        inner = column - at * per_shard
        mine = jnp.where(side == 0, inner, inner + (per_shard - own))
        others = jnp.where(side == 0, inner, inner - own)
        row = jnp.where(inner < own, mine, others)
        here = (inner >= 0) & (inner < per_shard) & (row < valid_ref[shard])
        place = jnp.where(here, row + shard * per_shard, place)
    position = span_ref[0] + me * tokens + lax.broadcasted_iota(jnp.int32, (tokens, keys), 0)
    bias_ref[...] = jnp.where(place <= position, F32(0.0), F32(MASKED))


def mask(span_offset, valid_lengths, owners, tokens, per_shard, own):
    return pl.pallas_call(
        functools.partial(mask_kernel, own, owners),
        in_specs=[SCALARS, SCALARS],
        out_specs=LOCAL,
        out_shape=pltpu.VMEM((tokens, per_shard * len(owners)), F32),
        compiler_params=params(4),
        cost_estimate=cost(0, 1024),
        name="mask",
    )(span_offset, valid_lengths)


def prep_kernel(q_hbm, r_hbm, w_hbm, lat_ref, q_ref, r_ref, w_ref, sem):
    tokens = q_ref.shape[0]
    heads, nope, latent = w_ref.shape
    rope = r_ref.shape[1] // heads
    whole = (
        pltpu.make_async_copy(q_hbm, q_ref, sem.at[0]),
        pltpu.make_async_copy(r_hbm, r_ref, sem.at[1]),
    )
    pieces = [
        pltpu.make_async_copy(
            w_hbm.at[pl.ds(at, STEP)], w_ref.at[pl.ds(at, STEP)], sem.at[2 + at // STEP]
        )
        for at in range(0, heads, STEP)
    ]
    for copy in (*whole, *pieces):
        copy.start()
    lat_ref[:, latent + rope :] = jnp.zeros(
        (heads * tokens, lat_ref.shape[1] - latent - rope), BF16
    )
    for copy in whole:
        copy.wait()
    for head in range(heads):
        if head % STEP == 0:
            pieces[head // STEP].wait()
        rows = slice(head * tokens, (head + 1) * tokens)
        lat = jnp.dot(
            q_ref[:, head * nope : (head + 1) * nope], w_ref[head], preferred_element_type=F32
        )
        lat_ref[rows, :latent] = lat.astype(BF16)
        lat_ref[rows, latent : latent + rope] = r_ref[:, head * rope : (head + 1) * rope]


def prep(q_nope, q_rope, w_absorb, depth):
    heads = w_absorb.shape[0]
    tokens = q_nope.shape[0]
    arrays = (q_nope, q_rope, w_absorb)
    return pl.pallas_call(
        prep_kernel,
        in_specs=[ANYWHERE] * 3,
        out_specs=LOCAL,
        out_shape=pltpu.VMEM((heads * tokens, depth), BF16),
        scratch_shapes=[pltpu.VMEM(x.shape, x.dtype) for x in arrays]
        + [pltpu.SemaphoreType.DMA((2 + heads // STEP,))],
        compiler_params=params(10),
        cost_estimate=cost(0, 1024),
        name="prep",
    )(*(pltpu.with_memory_space_constraint(x, pltpu.HBM) for x in arrays))


def join_kernel(groups, own, *refs):
    mine = refs[:groups]
    theirs = refs[groups : 2 * groups]
    out_ref = refs[-1]
    per_shard = out_ref.shape[0] // (2 * groups)
    rest = per_shard - own
    side = lax.axis_index("head")
    for at in range(2 * groups):
        group, inner = at // 2, at % 2
        start = at * per_shard
        out_ref[start : start + own] = mine[group][inner]
    for half in range(2):

        @pl.when(side == half)
        def _(skip=(1 - half) * (own - rest)):
            for at in range(2 * groups):
                start = at * per_shard + own
                out_ref[start : start + rest] = theirs[at // 2][at % 2, skip : skip + rest]


def join(mine, theirs, per_shard):
    groups = len(mine)
    _, own, depth = mine[0].shape
    return pl.pallas_call(
        functools.partial(join_kernel, groups, own),
        in_specs=[LOCAL] * (2 * groups),
        out_specs=LOCAL,
        out_shape=pltpu.VMEM((2 * groups * per_shard, depth), BF16),
        compiler_params=params(2),
        cost_estimate=cost(0, 1024),
        name="join",
    )(*map(held, mine), *map(held, theirs))


def attend_kernel(scale, start, heads, q_ref, bias_ref, w_ref, kv_ref, *refs):
    out_ref, scores, probs = refs[-3:]
    tokens = bias_ref.shape[0]
    _, latent, value = w_ref.shape
    pair = scores.shape[1] // tokens

    def score(at):
        row = (start + at * pair) * tokens
        scores[at % 2] = lax.dot_general(
            q_ref[row : row + pair * tokens, :],
            kv_ref[...],
            (((1,), (1,)), ((), ())),
            preferred_element_type=F32,
        )

    def weigh(at):
        totals = []
        for head in range(pair):
            rows = slice(head * tokens, (head + 1) * tokens)
            masked = scores[at % 2, rows, :] + bias_ref[...]
            top = jnp.max(masked, axis=-1, keepdims=True)
            expo = jnp.exp2((masked - top) * F32(scale))
            totals.append(jnp.sum(expo, axis=-1, keepdims=True))
            probs[at % 2, rows, :] = expo.astype(BF16)
        weighted = jnp.dot(probs[at % 2], kv_ref[:, :latent], preferred_element_type=F32)
        for head in range(pair):
            rows = slice(head * tokens, (head + 1) * tokens)
            mixed = (weighted[rows, :] / totals[head]).astype(BF16)
            which = at * pair + head
            out = jnp.dot(mixed, w_ref[start + which], preferred_element_type=F32)
            out_ref[:, which * value : (which + 1) * value] = out.astype(BF16)

    score(0)
    for at in range(heads // pair):
        if at + 1 < heads // pair:
            score(at + 1)
        weigh(at)


def attend(start, heads, queries, bias, w_value, kv, scale, after=()):
    tokens, keys = bias.shape
    value = w_value.shape[2]
    return pl.pallas_call(
        functools.partial(attend_kernel, scale * math.log2(math.e), start, heads),
        in_specs=[LOCAL] * 4 + [ANYWHERE] * len(after),
        out_specs=LOCAL,
        out_shape=pltpu.VMEM((tokens, heads * value), BF16),
        scratch_shapes=[
            pltpu.VMEM((2, 2 * tokens, keys), F32),
            pltpu.VMEM((2, 2 * tokens, keys), BF16),
        ],
        compiler_params=params(12),
        cost_estimate=cost(heads << 30, 1024),
        name=f"attend{start}",
    )(held(queries), held(bias), held(w_value), held(kv), *after)


def project_kernel(start, groups, fresh, w_ref, *refs):
    pairs = refs[:groups]
    out_ref, gathered = refs[-2:]
    tokens, depth = pairs[0].shape[1:]
    for side in range(2):
        for at in range(groups):
            gathered[side, at * tokens : (at + 1) * tokens] = pairs[at][side]
    weights = w_ref[start : start + depth]
    each = 2 * tokens
    for side in range(2):
        for row in range(0, groups * tokens, each):
            rows = slice(row, row + each)
            product = jnp.dot(gathered[side, rows], weights, preferred_element_type=F32)
            out_ref[side, rows] = product if fresh else refs[groups][side, rows] + product


def project(start, pairs, w_output, acc):
    groups = len(pairs)
    _, tokens, depth = pairs[0].shape
    columns = w_output.shape[1]
    return pl.pallas_call(
        functools.partial(project_kernel, start, groups, acc is None),
        in_specs=[LOCAL] * (1 + groups + (acc is not None)),
        out_specs=LOCAL,
        out_shape=pltpu.VMEM((2, groups * tokens, columns), F32),
        scratch_shapes=[pltpu.VMEM((2, groups * tokens, depth), BF16)],
        input_output_aliases={} if acc is None else {1 + groups: 0},
        compiler_params=params(12),
        cost_estimate=cost(0, 1024),
        name=f"project{start}",
    )(held(w_output), *map(held, pairs), *([] if acc is None else [held(acc)]))


def finish_kernel(start, keys, far, keep, w_ref, *refs):
    groups = len(keys)
    pairs = refs[:groups]
    acc_ref, out_ref, gathered = refs[groups:]
    tokens, depth = pairs[0].shape[1:]
    me, side = lax.axis_index("ctx"), lax.axis_index("head")
    other = ((me // groups) ^ side ^ (1 - keep)).astype(jnp.int32)
    for at in range(groups):
        gathered[at * tokens : (at + 1) * tokens] = pairs[at][other]
    product = jnp.dot(
        gathered[...], w_ref[start : start + depth], preferred_element_type=F32
    )
    for at, key in enumerate(keys):
        rows = slice(at * tokens, (at + 1) * tokens)
        place = (me ^ key ^ (far * other)) % groups
        to = pl.ds(pl.multiple_of(place * tokens, tokens), tokens)
        out_ref[to, :] = (acc_ref[other, rows] + product[rows]).astype(out_ref.dtype)


def finish(start, keys, far, keep, pairs, w_output, acc, dtype):
    groups = len(pairs)
    _, tokens, depth = pairs[0].shape
    columns = w_output.shape[1]
    rows = groups * tokens
    return pl.pallas_call(
        functools.partial(finish_kernel, start, keys, far, keep),
        in_specs=[LOCAL] * (2 + groups),
        out_specs=LOCAL,
        out_shape=pltpu.VMEM((rows, columns), dtype),
        scratch_shapes=[pltpu.VMEM((rows, depth), BF16)],
        compiler_params=params(12),
        cost_estimate=cost(0, 1024),
        name=f"finish{keep}",
    )(held(w_output), *map(held, pairs), held(acc))


def local(
    q_nope, q_rope, latent_cache, rope_keys, w_absorb, w_value, w_output, span_offset, valid_lengths
):
    head_count, nope_dim, latent = w_absorb.shape
    tokens = q_nope.shape[0]
    rope_dim = rope_keys.shape[1]
    per_shard = latent_cache.shape[0]
    shards = valid_lengths.shape[0]
    value = w_value.shape[2]
    depth = -(-(latent + rope_dim) // LANES) * LANES
    own = -(-per_shard // 32) * 16
    scale = 1.0 / math.sqrt(nope_dim + rope_dim)

    far = basis_of(shards)[0]
    packed = pack(latent_cache, rope_keys, own, depth)
    queries = prep(q_nope, q_rope, w_absorb, depth)
    mine = spread(packed, shards, [queries])
    keys = sorted(mine)
    theirs = {key: sibling(pair) for key, pair in mine.items()}
    owners = [key ^ (far * inner) for key in keys for inner in range(2)]
    bias = mask(span_offset, valid_lengths, owners, tokens, per_shard, own)
    kv = join([mine[key] for key in keys], [theirs[key] for key in keys], per_shard)

    acc = None
    start = 0
    sent = []
    for chunk, piece in enumerate(PIECES):
        heads = piece * head_count // sum(PIECES)
        after = [sent[-2][0]] if chunk > 1 else []
        if chunk > 2:
            after += [sent[-3][key] for key in basis_of(shards)[1:]]
        if chunk > 3:
            after += [sent[-4][key] for key in keys]
        out = attend(start, heads, queries, bias, w_value, kv, scale, after)
        gathered = spread(out, shards)
        pairs = [gathered[key] for key in keys]
        sent.append(gathered)
        row = start * value
        if chunk < len(PIECES) - 1:
            acc = project(row, pairs, w_output, acc)
        start += heads

    given = finish(row, keys, far, 0, pairs, w_output, acc, BF16)
    other = sibling(given)
    kept = finish(row, keys, far, 1, pairs, w_output, acc, F32)
    return (kept + other.astype(F32)).astype(BF16)


def solution(mesh):
    return jax.shard_map(
        local,
        mesh=mesh,
        in_specs=(
            P(("groups", "ctx"), "head"),
            P(("groups", "ctx"), "head"),
            P(("groups", "ctx"), None),
            P(("groups", "ctx"), None),
            P("head", None, None),
            P("head", None, None),
            P("head", "ctx"),
            P("groups"),
            P("groups"),
        ),
        out_specs=P(("groups", "head"), "ctx"),
        check_vma=False,
    )
```

time: 270 us -> 146 us (0.54)
  matrix products: 82.2 us -> 0 us
  waiting for transfers between devices: 138 us -> 69.8 us
  starting transfers between devices: 0.08 us -> 37.1 us
  Pallas kernels: 0 us -> 35.3 us
  blocking collectives: 33.1 us -> 0 us
  between operations: 13.8 us -> 0.95 us
    all_gather x2 -> x0, waiting for transfers between devices: 129 us -> none  [the longest x1 124 us: local(): lax.all_gather(head_out, 'ctx', axis=0, tiled=True)]
    ppermute x0 -> x29, waiting for transfers between devices: none -> 69.8 us  [the longest x24 68 us: exchange(): return lax.ppermute(x, 'ctx', [(i, i ^ mask) for i in range(shards)])]
    dot_general x11 -> x0, matrix products: 54 us -> none  [the longest x4 16.7 us: attend(): jnp.einsum('hqk,kc->hqc', expo.astype(jnp.bfloat16), cache_all, preferred...]
    ppermute x0 -> x29, starting transfers between devices: none -> 37.1 us  [the longest x24 36.5 us: exchange(): return lax.ppermute(x, 'ctx', [(i, i ^ mask) for i in range(shards)])]
    pallas_call x0 -> x21, Pallas kernels: none -> 35.3 us  [the longest x5 19 us: attend(): pl.pallas_call(functools.partial(attend_kernel, scale * math.log2(math.e)...]
    all_gather x1 -> x0, blocking collectives: 33.1 us -> none  [local(): lax.all_gather(rope_keys, 'ctx', axis=0, tiled=True)]
    sub x4 -> x0, matrix products: 28.2 us -> none  [attend(): expo = jnp.where(visible[None], jnp.exp(scores - row_max), jnp.float32(0.0))]
    reduce_scatter x1 -> x0, waiting for transfers between devices: 7.69 us -> none  [local(): lax.psum_scatter(partial_value.astype(jnp.bfloat16), 'head', scatter_dime...]
  transfers between devices with their start and end apart: 3 -> 29, of which waited for: 3 -> 13; matrix products, arithmetic and copies ran while one was open for 3% -> 0% of each run, Pallas kernels for 0% -> 22%
where the time goes in v3:
time: 146 us
  waiting for transfers between devices  69.8 us (48%)
  starting transfers between devices  37.1 us (25%)
  Pallas kernels  35.3 us (24%)
  local copies, waits for them, and re-layouts  1.69 us (1%)
    ppermute x24, waiting for transfers between devices, exchange(): return lax.ppermute(x, 'ctx', [(i, i ^ mask) for i in range(shards)])  68 us
    ppermute x24, starting transfers between devices, exchange(): return lax.ppermute(x, 'ctx', [(i, i ^ mask) for i in range(shards)])  36.5 us
    pallas_call x5, Pallas kernels, attend(): pl.pallas_call(functools.partial(attend_kernel, scale * math.log2(math.e)...  19 us
    pallas_call x4, Pallas kernels, project(): pl.pallas_call(functools.partial(project_kernel, start, groups, acc is No...  9.64 us
    pallas_call x1, Pallas kernels, prep(): pl.pallas_call(prep_kernel, in_specs=[ANYWHERE] * 3, out_specs=LOCAL, out...  3.98 us
  transfers between devices with their start and end apart: 29, of which 13 were waited for; matrix products, arithmetic and copies ran while one was open for 0% of the time, Pallas kernels for 22%

profile of v3, /device:TPU:0, one launch (start us, length us, event | category | flops | bytes accessed | tf_op | source)
XLA Modules:
  0.0 146.0 jit_solution(13662247386122147941)
XLA Ops:
  1.8 5.1 %collective-permute-start = (bf16[80,640]{1,0:T(8,128)(2,1)S(1)}, bf16[80,640]{1,0:T(8,128)(2,1)S(1)}, u32[]{:S(2)}, u32[]{:S(2)}) collective-permute-start(bf16[80,640]{1,0:T(8,128)(2,1)S(1)} %pack.1.first_ref), channel_id=1, source_target_pairs={{0,12},{2,14},{4,8},{6,10},{8,4},{10,6},{12,0},{14,2},{1,13},{3,15... | collective-permute-start | bytes 307208 | tf_op jit(solution)/shard_map/ppermute | solution.py:41
  6.9 4.0 %prep.1.refs_0_.q_ref = bf16[4096,640]{1,0:T(8,128)(2,1)S(1)} custom-call(bf16[128,4096]{1,0:T(8,128)(2,1)} %q_hbm.1, bf16[128,2048]{1,0:T(8,128)(2,1)} %r_hbm.1, bf16[32,128,512]{2,1,0:T(8,128)(2,1)} %w_hbm.1), custom_call_target="tpu_custom_call" | custom-call | bytes 1024 | tf_op jit(solution)/shard_map/prep/pallas_call | solution.py:167
  11.8 1.5 %collective-permute-start.1 = (bf16[2,80,640]{2,1,0:T(8,128)(2,1)S(1)}, bf16[2,80,640]{2,1,0:T(8,128)(2,1)S(1)}, u32[]{:S(2)}, u32[]{:S(2)}) collective-permute-start(bf16[2,80,640]{2,1,0:T(8,128)(2,1)S(1)} %stack.6.refs_0_), channel_id=1, source_target_pairs={{0,2},{2,0},{4,6},{6,4},{8,10},{10,8},{12,14},{14,12},{1,3},{3,1},... | collective-permute-start | bytes 614408 | tf_op jit(solution)/shard_map/ppermute | solution.py:41
  13.3 4.3 %collective-permute-done.2.refs_2_ = bf16[2,80,640]{2,1,0:T(8,128)(2,1)S(1)} collective-permute-done((bf16[2,80,640]{2,1,0:T(8,128)(2,1)S(1)}, bf16[2,80,640]{2,1,0:T(8,128)(2,1)S(1)}, u32[]{:S(2)}, u32[]{:S(2)}) %collective-permute-start.2) | collective-permute-done | bytes 204832 | tf_op jit(solution)/shard_map/ppermute | solution.py:41
  17.6 1.5 %collective-permute-start.3 = (bf16[2,80,640]{2,1,0:T(8,128)(2,1)S(1)}, bf16[2,80,640]{2,1,0:T(8,128)(2,1)S(1)}, u32[]{:S(2)}, u32[]{:S(2)}) collective-permute-start(bf16[2,80,640]{2,1,0:T(8,128)(2,1)S(1)} %collective-permute-done.2.refs_2_), channel_id=1, source_target_pairs={{0,2},{2,0},{4,6},{6,4},{8,10},{10,8},{12,14},{14,12},{1,3},{3,1},... | collective-permute-start | bytes 614408 | tf_op jit(solution)/shard_map/ppermute | solution.py:41
  19.6 3.7 %collective-permute-done.3.refs_3_ = bf16[2,80,640]{2,1,0:T(8,128)(2,1)S(1)} collective-permute-done((bf16[2,80,640]{2,1,0:T(8,128)(2,1)S(1)}, bf16[2,80,640]{2,1,0:T(8,128)(2,1)S(1)}, u32[]{:S(2)}, u32[]{:S(2)}) %collective-permute-start.3) | collective-permute-done | bytes 204832 | tf_op jit(solution)/shard_map/ppermute | solution.py:41
  25.1 2.4 %attend0.1.first_ref = bf16[128,512]{1,0:T(8,128)(2,1)S(1)} custom-call(bf16[4096,640]{1,0:T(8,128)(2,1)S(1)} %prep.1.refs_0_.q_ref, f32[128,1152]{1,0:T(8,128)S(1)} %mask.1.bias_ref, bf16[32,512,128]{2,1,0:T(8,128)(2,1)S(1)} %copy-done.3, bf16[1152,640]{1,0:T(8,128)(2,1)S(1)} %join.1.kv_ref), custom_call_target="tpu_custom_call" | custom-call | flops 4294967296 | bytes 1024 | tf_op jit(solution)/shard_map/attend0/pallas_call | solution.py:256
  27.5 1.8 %collective-permute-start.8 = (bf16[128,512]{1,0:T(8,128)(2,1)S(1)}, bf16[128,512]{1,0:T(8,128)(2,1)S(1)}, u32[]{:S(2)}, u32[]{:S(2)}) collective-permute-start(bf16[128,512]{1,0:T(8,128)(2,1)S(1)} %attend0.1.first_ref), channel_id=1, source_target_pairs={{0,12},{2,14},{4,8},{6,10},{8,4},{10,6},{12,0},{14,2},{1,13},{3,15... | collective-permute-start | bytes 393224 | tf_op jit(solution)/shard_map/ppermute | solution.py:41
  29.3 4.7 %attend4.1.first_ref = bf16[128,1024]{1,0:T(8,128)(2,1)S(1)} custom-call(bf16[4096,640]{1,0:T(8,128)(2,1)S(1)} %prep.1.refs_0_.q_ref, f32[128,1152]{1,0:T(8,128)S(1)} %mask.1.bias_ref, bf16[32,512,128]{2,1,0:T(8,128)(2,1)S(1)} %copy-done.3, bf16[1152,640]{1,0:T(8,128)(2,1)S(1)} %join.1.kv_ref), custom_call_target="tpu_custom_call" | custom-call | flops 8589934592 | bytes 1024 | tf_op jit(solution)/shard_map/attend4/pallas_call | solution.py:256
  33.9 2.2 %collective-permute-start.10 = (bf16[128,1024]{1,0:T(8,128)(2,1)S(1)}, bf16[128,1024]{1,0:T(8,128)(2,1)S(1)}, u32[]{:S(2)}, u32[]{:S(2)}) collective-permute-start(bf16[128,1024]{1,0:T(8,128)(2,1)S(1)} %attend4.1.first_ref), channel_id=1, source_target_pairs={{0,12},{2,14},{4,8},{6,10},{8,4},{10,6},{12,0},{14,2},{1,13},{3,15... | collective-permute-start | bytes 786440 | tf_op jit(solution)/shard_map/ppermute | solution.py:41
  36.6 1.5 %collective-permute-start.13 = (bf16[2,128,512]{2,1,0:T(8,128)(2,1)S(1)}, bf16[2,128,512]{2,1,0:T(8,128)(2,1)S(1)}, u32[]{:S(2)}, u32[]{:S(2)}) collective-permute-start(bf16[2,128,512]{2,1,0:T(8,128)(2,1)S(1)} %stack.7.refs_0_.refs_3_), channel_id=1, source_target_pairs={{0,2},{2,0},{4,6},{6,4},{8,10},{10,8},{12,14},{14,12},{1,3},{3,1},... | collective-permute-start | bytes 786440 | tf_op jit(solution)/shard_map/ppermute | solution.py:41
  38.1 4.7 %attend12.1.first_ref = bf16[128,1024]{1,0:T(8,128)(2,1)S(1)} custom-call(bf16[4096,640]{1,0:T(8,128)(2,1)S(1)} %prep.1.refs_0_.q_ref, f32[128,1152]{1,0:T(8,128)S(1)} %mask.1.bias_ref, bf16[32,512,128]{2,1,0:T(8,128)(2,1)S(1)} %copy-done.3, bf16[1152,640]{1,0:T(8,128)(2,1)S(1)} %join.1.kv_ref, bf16[2,128,512]{2,1,0:T(8,128)(2,1)S(1)} %stack.7.refs_0_.refs_3_), custom_call_target="tpu_custom_call" | custom-call | flops 8589934592 | bytes 1024 | tf_op jit(solution)/shard_map/attend12/pallas_call | solution.py:256
  42.8 2.4 %collective-permute-start.9 = (bf16[128,1024]{1,0:T(8,128)(2,1)S(1)}, bf16[128,1024]{1,0:T(8,128)(2,1)S(1)}, u32[]{:S(2)}, u32[]{:S(2)}) collective-permute-start(bf16[128,1024]{1,0:T(8,128)(2,1)S(1)} %attend12.1.first_ref), channel_id=1, source_target_pairs={{0,12},{2,14},{4,8},{6,10},{8,4},{10,6},{12,0},{14,2},{1,13},{3,15... | collective-permute-start | bytes 786440 | tf_op jit(solution)/shard_map/ppermute | solution.py:41
  46.7 3.6 %collective-permute-start.11 = (bf16[2,128,1024]{2,1,0:T(8,128)(2,1)S(1)}, bf16[2,128,1024]{2,1,0:T(8,128)(2,1)S(1)}, u32[]{:S(2)}, u32[]{:S(2)}) collective-permute-start(bf16[2,128,1024]{2,1,0:T(8,128)(2,1)S(1)} %stack.9.refs_0_), channel_id=1, source_target_pairs={{0,4},{2,6},{4,0},{6,2},{8,12},{10,14},{12,8},{14,10},{1,5},{3,7},... | collective-permute-start | bytes 1572872 | tf_op jit(solution)/shard_map/ppermute | solution.py:41
  50.8 4.9 %attend20.1.first_ref = bf16[128,1024]{1,0:T(8,128)(2,1)S(1)} custom-call(bf16[4096,640]{1,0:T(8,128)(2,1)S(1)} %prep.1.refs_0_.q_ref, f32[128,1152]{1,0:T(8,128)S(1)} %mask.1.bias_ref, bf16[32,512,128]{2,1,0:T(8,128)(2,1)S(1)} %copy-done.3, bf16[1152,640]{1,0:T(8,128)(2,1)S(1)} %join.1.kv_ref, bf16[2,128,1024]{2,1,0:T(8,128)(2,1)S(1)} %stack.9.refs_0_, ...), custom_call_target="tpu_custom_call" | custom-call | flops 8589934592 | bytes 1024 | tf_op jit(solution)/shard_map/attend20/pallas_call | solution.py:256
  55.8 1.6 %collective-permute-start.20 = (bf16[128,1024]{1,0:T(8,128)(2,1)S(1)}, bf16[128,1024]{1,0:T(8,128)(2,1)S(1)}, u32[]{:S(2)}, u32[]{:S(2)}) collective-permute-start(bf16[128,1024]{1,0:T(8,128)(2,1)S(1)} %attend20.1.first_ref), channel_id=1, source_target_pairs={{0,12},{2,14},{4,8},{6,10},{8,4},{10,6},{12,0},{14,2},{1,13},{3,15... | collective-permute-start | bytes 786440 | tf_op jit(solution)/shard_map/ppermute | solution.py:41
  57.4 2.2 %collective-permute-start.15 = (bf16[2,128,512]{2,1,0:T(8,128)(2,1)S(1)}, bf16[2,128,512]{2,1,0:T(8,128)(2,1)S(1)}, u32[]{:S(2)}, u32[]{:S(2)}) collective-permute-start(bf16[2,128,512]{2,1,0:T(8,128)(2,1)S(1)} %collective-permute-done.14.refs_5_.refs_1_.refs_2_), channel_id=1, source_target_pairs={{0,2},{2,0},{4,6},{6,4},{8,10},{10,8},{12,14},{14,12},{1,3},{3,1},... | collective-permute-start | bytes 786440 | tf_op jit(solution)/shard_map/ppermute | solution.py:41
  60.0 13.2 %collective-permute-done.20.second_ref = bf16[128,1024]{1,0:T(8,128)(2,1)S(1)} collective-permute-done((bf16[128,1024]{1,0:T(8,128)(2,1)S(1)}, bf16[128,1024]{1,0:T(8,128)(2,1)S(1)}, u32[]{:S(2)}, u32[]{:S(2)}) %collective-permute-start.20) | collective-permute-done | bytes 262176 | tf_op jit(solution)/shard_map/ppermute | solution.py:41
  75.4 2.4 %attend28.1.first_ref = bf16[128,512]{1,0:T(8,128)(2,1)S(1)} custom-call(bf16[4096,640]{1,0:T(8,128)(2,1)S(1)} %prep.1.refs_0_.q_ref, f32[128,1152]{1,0:T(8,128)S(1)} %mask.1.bias_ref, bf16[32,512,128]{2,1,0:T(8,128)(2,1)S(1)} %copy-done.3, bf16[1152,640]{1,0:T(8,128)(2,1)S(1)} %join.1.kv_ref, bf16[2,128,1024]{2,1,0:T(8,128)(2,1)S(1)} %stack.8.refs_0_, ...), custom_call_target="tpu_custom_call" | custom-call | flops 4294967296 | bytes 1024 | tf_op jit(solution)/shard_map/attend28/pallas_call | solution.py:256
  77.8 2.1 %collective-permute-start.16 = (bf16[128,512]{1,0:T(8,128)(2,1)S(1)}, bf16[128,512]{1,0:T(8,128)(2,1)S(1)}, u32[]{:S(2)}, u32[]{:S(2)}) collective-permute-start(bf16[128,512]{1,0:T(8,128)(2,1)S(1)} %attend28.1.first_ref), channel_id=1, source_target_pairs={{0,12},{2,14},{4,8},{6,10},{8,4},{10,6},{12,0},{14,2},{1,13},{3,15... | collective-permute-start | bytes 393224 | tf_op jit(solution)/shard_map/ppermute | solution.py:41
  80.0 3.8 %collective-permute-done.25.refs_2_ = bf16[2,128,1024]{2,1,0:T(8,128)(2,1)S(1)} collective-permute-done((bf16[2,128,1024]{2,1,0:T(8,128)(2,1)S(1)}, bf16[2,128,1024]{2,1,0:T(8,128)(2,1)S(1)}, u32[]{:S(2)}, u32[]{:S(2)}) %collective-permute-start.25) | collective-permute-done | bytes 524320 | tf_op jit(solution)/shard_map/ppermute | solution.py:41
  85.1 12.5 %collective-permute-done.16.second_ref = bf16[128,512]{1,0:T(8,128)(2,1)S(1)} collective-permute-done((bf16[128,512]{1,0:T(8,128)(2,1)S(1)}, bf16[128,512]{1,0:T(8,128)(2,1)S(1)}, u32[]{:S(2)}, u32[]{:S(2)}) %collective-permute-start.16) | collective-permute-done | bytes 131104 | tf_op jit(solution)/shard_map/ppermute | solution.py:41
  99.8 6.6 %collective-permute-done.18.refs_2_ = bf16[2,128,512]{2,1,0:T(8,128)(2,1)S(1)} collective-permute-done((bf16[2,128,512]{2,1,0:T(8,128)(2,1)S(1)}, bf16[2,128,512]{2,1,0:T(8,128)(2,1)S(1)}, u32[]{:S(2)}, u32[]{:S(2)}) %collective-permute-start.18) | collective-permute-done | bytes 262176 | tf_op jit(solution)/shard_map/ppermute | solution.py:41
  106.9 1.5 %collective-permute-start.19 = (bf16[2,128,512]{2,1,0:T(8,128)(2,1)S(1)}, bf16[2,128,512]{2,1,0:T(8,128)(2,1)S(1)}, u32[]{:S(2)}, u32[]{:S(2)}) collective-permute-start(bf16[2,128,512]{2,1,0:T(8,128)(2,1)S(1)} %collective-permute-done.18.refs_2_), channel_id=1, source_target_pairs={{0,2},{2,0},{4,6},{6,4},{8,10},{10,8},{12,14},{14,12},{1,3},{3,1},... | collective-permute-start | bytes 786440 | tf_op jit(solution)/shard_map/ppermute | solution.py:41
  109.7 2.8 %project512.1.refs_4_ = f32[2,512,896]{2,1,0:T(8,128)S(1)} custom-call(bf16[4096,896]{1,0:T(8,128)(2,1)S(1)} %bitcast.2, bf16[2,128,1024]{2,1,0:T(8,128)(2,1)S(1)} %stack.9.refs_0_, bf16[2,128,1024]{2,1,0:T(8,128)(2,1)S(1)} %collective-permute-done.12.refs_2_.refs_1_, ...), custom_call_target="tpu_custom_call", output_to_operand_aliasing={{}: (5, {})} | custom-call | bytes 1024 | tf_op jit(solution)/shard_map/project512/pallas_call | solution.py:291
  112.5 9.3 %collective-permute-done.26.refs_3_ = bf16[2,128,1024]{2,1,0:T(8,128)(2,1)S(1)} collective-permute-done((bf16[2,128,1024]{2,1,0:T(8,128)(2,1)S(1)}, bf16[2,128,1024]{2,1,0:T(8,128)(2,1)S(1)}, u32[]{:S(2)}, u32[]{:S(2)}) %collective-permute-start.26) | collective-permute-done | bytes 524320 | tf_op jit(solution)/shard_map/ppermute | solution.py:41
  121.8 2.8 %project1536.1.refs_4_ = f32[2,512,896]{2,1,0:T(8,128)S(1)} custom-call(bf16[4096,896]{1,0:T(8,128)(2,1)S(1)} %bitcast.2, bf16[2,128,1024]{2,1,0:T(8,128)(2,1)S(1)} %stack.8.refs_0_, bf16[2,128,1024]{2,1,0:T(8,128)(2,1)S(1)} %collective-permute-done.24.refs_1_, ...), custom_call_target="tpu_custom_call", output_to_operand_aliasing={{}: (5, {})} | custom-call | bytes 1024 | tf_op jit(solution)/shard_map/project1536/pallas_call | solution.py:291
  124.6 8.4 %collective-permute-done.23.refs_3_ = bf16[2,128,1024]{2,1,0:T(8,128)(2,1)S(1)} collective-permute-done((bf16[2,128,1024]{2,1,0:T(8,128)(2,1)S(1)}, bf16[2,128,1024]{2,1,0:T(8,128)(2,1)S(1)}, u32[]{:S(2)}, u32[]{:S(2)}) %collective-permute-start.23) | collective-permute-done | bytes 524320 | tf_op jit(solution)/shard_map/ppermute | solution.py:41
  133.0 2.8 %project2560.1.refs_4_ = f32[2,512,896]{2,1,0:T(8,128)S(1)} custom-call(bf16[4096,896]{1,0:T(8,128)(2,1)S(1)} %bitcast.2, bf16[2,128,1024]{2,1,0:T(8,128)(2,1)S(1)} %stack.11.refs_0_, bf16[2,128,1024]{2,1,0:T(8,128)(2,1)S(1)} %collective-permute-done.21.refs_1_, ...), custom_call_target="tpu_custom_call", output_to_operand_aliasing={{}: (5, {})} | custom-call | bytes 1024 | tf_op jit(solution)/shard_map/project2560/pallas_call | solution.py:291
  135.8 2.8 %collective-permute-done.17.refs_1_ = bf16[2,128,512]{2,1,0:T(8,128)(2,1)S(1)} collective-permute-done((bf16[2,128,512]{2,1,0:T(8,128)(2,1)S(1)}, bf16[2,128,512]{2,1,0:T(8,128)(2,1)S(1)}, u32[]{:S(2)}, u32[]{:S(2)}) %collective-permute-start.17) | collective-permute-done | bytes 262176 | tf_op jit(solution)/shard_map/ppermute | solution.py:41
  138.6 3.0 %collective-permute-done.19.refs_3_ = bf16[2,128,512]{2,1,0:T(8,128)(2,1)S(1)} collective-permute-done((bf16[2,128,512]{2,1,0:T(8,128)(2,1)S(1)}, bf16[2,128,512]{2,1,0:T(8,128)(2,1)S(1)}, u32[]{:S(2)}, u32[]{:S(2)}) %collective-permute-start.19) | collective-permute-done | bytes 262176 | tf_op jit(solution)/shard_map/ppermute | solution.py:41
  143.1 1.7 %collective-permute-done.28 = bf16[512,896]{1,0:T(8,128)(2,1)S(1)} collective-permute-done((bf16[512,896]{1,0:T(8,128)(2,1)S(1)}, bf16[512,896]{1,0:T(8,128)(2,1)S(1)}, u32[]{:S(2)}, u32[]{:S(2)}) %collective-permute-start.28) | collective-permute-done | bytes 917536 | tf_op jit(solution)/shard_map/ppermute | solution.py:45
  (61 shorter events, 17.3 us)
Async XLA Ops:
  1.8 9.1 %collective-permute-start = (bf16[80,640]{1,0:T(8,128)(2,1)S(1)}, bf16[80,640]{1,0:T(8,128)(2,1)S(1)}, u32[]{:S(2)}, u32[]{:S(2)}) collective-permute-start(bf16[80,640]{1,0:T(8,128)(2,1)S(1)} %pack.1.first_ref), channel_id=1, source_target_pairs={{0,12},{2,14},{4,8},{6,10},{8,4},{10,6},{12,0},{14,2},{1,13},{3,15... | collective-permute-start | bytes 307208 | tf_op jit(solution)/shard_map/ppermute | solution.py:41
  10.9 14.2 %copy-start.3 = (bf16[32,512,128]{2,1,0:T(8,128)(2,1)S(1)}, bf16[32,512,128]{2,1,0:T(8,128)(2,1)}, u32[]{:S(2)}) copy-start(bf16[32,512,128]{2,1,0:T(8,128)(2,1)} %w_ref.15) | copy-start | bytes 12582916
  10.9 6.6 %collective-permute-start.2 = (bf16[2,80,640]{2,1,0:T(8,128)(2,1)S(1)}, bf16[2,80,640]{2,1,0:T(8,128)(2,1)S(1)}, u32[]{:S(2)}, u32[]{:S(2)}) collective-permute-start(bf16[2,80,640]{2,1,0:T(8,128)(2,1)S(1)} %stack.6.refs_0_), channel_id=1, source_target_pairs={{0,4},{2,6},{4,0},{6,2},{8,12},{10,14},{12,8},{14,10},{1,5},{3,7},... | collective-permute-start | bytes 614408 | tf_op jit(solution)/shard_map/ppermute | solution.py:41
  11.8 7.8 %collective-permute-start.1 = (bf16[2,80,640]{2,1,0:T(8,128)(2,1)S(1)}, bf16[2,80,640]{2,1,0:T(8,128)(2,1)S(1)}, u32[]{:S(2)}, u32[]{:S(2)}) collective-permute-start(bf16[2,80,640]{2,1,0:T(8,128)(2,1)S(1)} %stack.6.refs_0_), channel_id=1, source_target_pairs={{0,2},{2,0},{4,6},{6,4},{8,10},{10,8},{12,14},{14,12},{1,3},{3,1},... | collective-permute-start | bytes 614408 | tf_op jit(solution)/shard_map/ppermute | solution.py:41
  17.6 5.8 %collective-permute-start.3 = (bf16[2,80,640]{2,1,0:T(8,128)(2,1)S(1)}, bf16[2,80,640]{2,1,0:T(8,128)(2,1)S(1)}, u32[]{:S(2)}, u32[]{:S(2)}) collective-permute-start(bf16[2,80,640]{2,1,0:T(8,128)(2,1)S(1)} %collective-permute-done.2.refs_2_), channel_id=1, source_target_pairs={{0,2},{2,0},{4,6},{6,4},{8,10},{10,8},{12,14},{14,12},{1,3},{3,1},... | collective-permute-start | bytes 614408 | tf_op jit(solution)/shard_map/ppermute | solution.py:41
  19.1 5.5 %collective-permute-start.4 = (bf16[2,80,640]{2,1,0:T(8,128)(2,1)S(1)}, bf16[2,80,640]{2,1,0:T(8,128)(2,1)S(1)}, u32[]{:S(2)}, u32[]{:S(2)}) collective-permute-start(bf16[2,80,640]{2,1,0:T(8,128)(2,1)S(1)} %stack.6.refs_0_), channel_id=1, source_target_pairs={{0,1},{1,0},{2,3},{3,2},{4,5},{5,4},{6,7},{7,6},{8,9},{9,8},{10,11... | collective-permute-start | bytes 614408 | tf_op jit(solution)/shard_map/ppermute | solution.py:45
  19.1 5.5 %collective-permute-start.6 = (bf16[2,80,640]{2,1,0:T(8,128)(2,1)S(1)}, bf16[2,80,640]{2,1,0:T(8,128)(2,1)S(1)}, u32[]{:S(2)}, u32[]{:S(2)}) collective-permute-start(bf16[2,80,640]{2,1,0:T(8,128)(2,1)S(1)} %collective-permute-done.2.refs_2_), channel_id=1, source_target_pairs={{0,1},{1,0},{2,3},{3,2},{4,5},{5,4},{6,7},{7,6},{8,9},{9,8},{10,11... | collective-permute-start | bytes 614408 | tf_op jit(solution)/shard_map/ppermute | solution.py:45
  19.6 5.0 %collective-permute-start.5 = (bf16[2,80,640]{2,1,0:T(8,128)(2,1)S(1)}, bf16[2,80,640]{2,1,0:T(8,128)(2,1)S(1)}, u32[]{:S(2)}, u32[]{:S(2)}) collective-permute-start(bf16[2,80,640]{2,1,0:T(8,128)(2,1)S(1)} %collective-permute-done.1.refs_1_), channel_id=1, source_target_pairs={{0,1},{1,0},{2,3},{3,2},{4,5},{5,4},{6,7},{7,6},{8,9},{9,8},{10,11... | collective-permute-start | bytes 614408 | tf_op jit(solution)/shard_map/ppermute | solution.py:45
  23.3 1.5 collective-permute-start.7
  27.5 8.7 %collective-permute-start.8 = (bf16[128,512]{1,0:T(8,128)(2,1)S(1)}, bf16[128,512]{1,0:T(8,128)(2,1)S(1)}, u32[]{:S(2)}, u32[]{:S(2)}) collective-permute-start(bf16[128,512]{1,0:T(8,128)(2,1)S(1)} %attend0.1.first_ref), channel_id=1, source_target_pairs={{0,12},{2,14},{4,8},{6,10},{8,4},{10,6},{12,0},{14,2},{1,13},{3,15... | collective-permute-start | bytes 393224 | tf_op jit(solution)/shard_map/ppermute | solution.py:41
  33.9 11.3 %collective-permute-start.10 = (bf16[128,1024]{1,0:T(8,128)(2,1)S(1)}, bf16[128,1024]{1,0:T(8,128)(2,1)S(1)}, u32[]{:S(2)}, u32[]{:S(2)}) collective-permute-start(bf16[128,1024]{1,0:T(8,128)(2,1)S(1)} %attend4.1.first_ref), channel_id=1, source_target_pairs={{0,12},{2,14},{4,8},{6,10},{8,4},{10,6},{12,0},{14,2},{1,13},{3,15... | collective-permute-start | bytes 786440 | tf_op jit(solution)/shard_map/ppermute | solution.py:41
  36.2 14.7 %collective-permute-start.14 = (bf16[2,128,512]{2,1,0:T(8,128)(2,1)S(1)}, bf16[2,128,512]{2,1,0:T(8,128)(2,1)S(1)}, u32[]{:S(2)}, u32[]{:S(2)}) collective-permute-start(bf16[2,128,512]{2,1,0:T(8,128)(2,1)S(1)} %stack.7.refs_0_.refs_3_), channel_id=1, source_target_pairs={{0,4},{2,6},{4,0},{6,2},{8,12},{10,14},{12,8},{14,10},{1,5},{3,7},... | collective-permute-start | bytes 786440 | tf_op jit(solution)/shard_map/ppermute | solution.py:41
  36.6 14.3 %collective-permute-start.13 = (bf16[2,128,512]{2,1,0:T(8,128)(2,1)S(1)}, bf16[2,128,512]{2,1,0:T(8,128)(2,1)S(1)}, u32[]{:S(2)}, u32[]{:S(2)}) collective-permute-start(bf16[2,128,512]{2,1,0:T(8,128)(2,1)S(1)} %stack.7.refs_0_.refs_3_), channel_id=1, source_target_pairs={{0,2},{2,0},{4,6},{6,4},{8,10},{10,8},{12,14},{14,12},{1,3},{3,1},... | collective-permute-start | bytes 786440 | tf_op jit(solution)/shard_map/ppermute | solution.py:41
  42.8 16.8 %collective-permute-start.9 = (bf16[128,1024]{1,0:T(8,128)(2,1)S(1)}, bf16[128,1024]{1,0:T(8,128)(2,1)S(1)}, u32[]{:S(2)}, u32[]{:S(2)}) collective-permute-start(bf16[128,1024]{1,0:T(8,128)(2,1)S(1)} %attend12.1.first_ref), channel_id=1, source_target_pairs={{0,12},{2,14},{4,8},{6,10},{8,4},{10,6},{12,0},{14,2},{1,13},{3,15... | collective-permute-start | bytes 786440 | tf_op jit(solution)/shard_map/ppermute | solution.py:41
  45.3 30.2 %collective-permute-start.12 = (bf16[2,128,1024]{2,1,0:T(8,128)(2,1)S(1)}, bf16[2,128,1024]{2,1,0:T(8,128)(2,1)S(1)}, u32[]{:S(2)}, u32[]{:S(2)}) collective-permute-start(bf16[2,128,1024]{2,1,0:T(8,128)(2,1)S(1)} %stack.9.refs_0_), channel_id=1, source_target_pairs={{0,2},{2,0},{4,6},{6,4},{8,10},{10,8},{12,14},{14,12},{1,3},{3,1},... | collective-permute-start | bytes 1572872 | tf_op jit(solution)/shard_map/ppermute | solution.py:41
  46.7 28.2 %collective-permute-start.11 = (bf16[2,128,1024]{2,1,0:T(8,128)(2,1)S(1)}, bf16[2,128,1024]{2,1,0:T(8,128)(2,1)S(1)}, u32[]{:S(2)}, u32[]{:S(2)}) collective-permute-start(bf16[2,128,1024]{2,1,0:T(8,128)(2,1)S(1)} %stack.9.refs_0_), channel_id=1, source_target_pairs={{0,4},{2,6},{4,0},{6,2},{8,12},{10,14},{12,8},{14,10},{1,5},{3,7},... | collective-permute-start | bytes 1572872 | tf_op jit(solution)/shard_map/ppermute | solution.py:41
  55.8 17.4 %collective-permute-start.20 = (bf16[128,1024]{1,0:T(8,128)(2,1)S(1)}, bf16[128,1024]{1,0:T(8,128)(2,1)S(1)}, u32[]{:S(2)}, u32[]{:S(2)}) collective-permute-start(bf16[128,1024]{1,0:T(8,128)(2,1)S(1)} %attend20.1.first_ref), channel_id=1, source_target_pairs={{0,12},{2,14},{4,8},{6,10},{8,4},{10,6},{12,0},{14,2},{1,13},{3,15... | collective-permute-start | bytes 786440 | tf_op jit(solution)/shard_map/ppermute | solution.py:41
  57.4 17.4 %collective-permute-start.15 = (bf16[2,128,512]{2,1,0:T(8,128)(2,1)S(1)}, bf16[2,128,512]{2,1,0:T(8,128)(2,1)S(1)}, u32[]{:S(2)}, u32[]{:S(2)}) collective-permute-start(bf16[2,128,512]{2,1,0:T(8,128)(2,1)S(1)} %collective-permute-done.14.refs_5_.refs_1_.refs_2_), channel_id=1, source_target_pairs={{0,2},{2,0},{4,6},{6,4},{8,10},{10,8},{12,14},{14,12},{1,3},{3,1},... | collective-permute-start | bytes 786440 | tf_op jit(solution)/shard_map/ppermute | solution.py:41
  59.6 24.1 %collective-permute-start.25 = (bf16[2,128,1024]{2,1,0:T(8,128)(2,1)S(1)}, bf16[2,128,1024]{2,1,0:T(8,128)(2,1)S(1)}, u32[]{:S(2)}, u32[]{:S(2)}) collective-permute-start(bf16[2,128,1024]{2,1,0:T(8,128)(2,1)S(1)} %stack.8.refs_0_), channel_id=1, source_target_pairs={{0,4},{2,6},{4,0},{6,2},{8,12},{10,14},{12,8},{14,10},{1,5},{3,7},... | collective-permute-start | bytes 1572872 | tf_op jit(solution)/shard_map/ppermute | solution.py:41
  73.2 25.9 %collective-permute-start.24 = (bf16[2,128,1024]{2,1,0:T(8,128)(2,1)S(1)}, bf16[2,128,1024]{2,1,0:T(8,128)(2,1)S(1)}, u32[]{:S(2)}, u32[]{:S(2)}) collective-permute-start(bf16[2,128,1024]{2,1,0:T(8,128)(2,1)S(1)} %stack.8.refs_0_), channel_id=1, source_target_pairs={{0,2},{2,0},{4,6},{6,4},{8,10},{10,8},{12,14},{14,12},{1,3},{3,1},... | collective-permute-start | bytes 1572872 | tf_op jit(solution)/shard_map/ppermute | solution.py:41
  74.7 33.7 %slice-start = ((s8[7340032]{0:T(1024)(128)(4,1)}), s8[4194304]{0:T(1024)(128)(4,1)S(1)}, s32[]{:S(2)}) async-start(s8[7340032]{0:T(1024)(128)(4,1)} %bitcast.1), calls=%async_computation | async-start | bytes 8388608
  74.8 33.7 %slice-start.1 = ((s8[7340032]{0:T(1024)(128)(4,1)}), s8[3145728]{0:T(1024)(128)(4,1)S(1)}, s32[]{:S(2)}) async-start(s8[7340032]{0:T(1024)(128)(4,1)} %bitcast.1), calls=%async_computation.1 | async-start | bytes 6291456
  74.8 24.5 %collective-permute-start.22 = (bf16[2,128,1024]{2,1,0:T(8,128)(2,1)S(1)}, bf16[2,128,1024]{2,1,0:T(8,128)(2,1)S(1)}, u32[]{:S(2)}, u32[]{:S(2)}) collective-permute-start(bf16[2,128,1024]{2,1,0:T(8,128)(2,1)S(1)} %stack.11.refs_0_), channel_id=1, source_target_pairs={{0,4},{2,6},{4,0},{6,2},{8,12},{10,14},{12,8},{14,10},{1,5},{3,7},... | collective-permute-start | bytes 1572872 | tf_op jit(solution)/shard_map/ppermute | solution.py:41
  74.9 32.0 %collective-permute-start.27 = (bf16[2,128,1024]{2,1,0:T(8,128)(2,1)S(1)}, bf16[2,128,1024]{2,1,0:T(8,128)(2,1)S(1)}, u32[]{:S(2)}, u32[]{:S(2)}) collective-permute-start(bf16[2,128,1024]{2,1,0:T(8,128)(2,1)S(1)} %collective-permute-done.11.refs_1_.refs_2_), channel_id=1, source_target_pairs={{0,2},{2,0},{4,6},{6,4},{8,10},{10,8},{12,14},{14,12},{1,3},{3,1},... | collective-permute-start | bytes 1572872 | tf_op jit(solution)/shard_map/ppermute | solution.py:41
  77.8 19.8 %collective-permute-start.16 = (bf16[128,512]{1,0:T(8,128)(2,1)S(1)}, bf16[128,512]{1,0:T(8,128)(2,1)S(1)}, u32[]{:S(2)}, u32[]{:S(2)}) collective-permute-start(bf16[128,512]{1,0:T(8,128)(2,1)S(1)} %attend28.1.first_ref), channel_id=1, source_target_pairs={{0,12},{2,14},{4,8},{6,10},{8,4},{10,6},{12,0},{14,2},{1,13},{3,15... | collective-permute-start | bytes 393224 | tf_op jit(solution)/shard_map/ppermute | solution.py:41
  83.7 40.8 %collective-permute-start.21 = (bf16[2,128,1024]{2,1,0:T(8,128)(2,1)S(1)}, bf16[2,128,1024]{2,1,0:T(8,128)(2,1)S(1)}, u32[]{:S(2)}, u32[]{:S(2)}) collective-permute-start(bf16[2,128,1024]{2,1,0:T(8,128)(2,1)S(1)} %stack.11.refs_0_), channel_id=1, source_target_pairs={{0,2},{2,0},{4,6},{6,4},{8,10},{10,8},{12,14},{14,12},{1,3},{3,1},... | collective-permute-start | bytes 1572872 | tf_op jit(solution)/shard_map/ppermute | solution.py:41
  97.6 24.2 %collective-permute-start.26 = (bf16[2,128,1024]{2,1,0:T(8,128)(2,1)S(1)}, bf16[2,128,1024]{2,1,0:T(8,128)(2,1)S(1)}, u32[]{:S(2)}, u32[]{:S(2)}) collective-permute-start(bf16[2,128,1024]{2,1,0:T(8,128)(2,1)S(1)} %collective-permute-done.25.refs_2_), channel_id=1, source_target_pairs={{0,2},{2,0},{4,6},{6,4},{8,10},{10,8},{12,14},{14,12},{1,3},{3,1},... | collective-permute-start | bytes 1572872 | tf_op jit(solution)/shard_map/ppermute | solution.py:41
  99.2 7.2 %collective-permute-start.18 = (bf16[2,128,512]{2,1,0:T(8,128)(2,1)S(1)}, bf16[2,128,512]{2,1,0:T(8,128)(2,1)S(1)}, u32[]{:S(2)}, u32[]{:S(2)}) collective-permute-start(bf16[2,128,512]{2,1,0:T(8,128)(2,1)S(1)} %stack.10.refs_0_), channel_id=1, source_target_pairs={{0,4},{2,6},{4,0},{6,2},{8,12},{10,14},{12,8},{14,10},{1,5},{3,7},... | collective-permute-start | bytes 786440 | tf_op jit(solution)/shard_map/ppermute | solution.py:41
  99.2 33.8 %collective-permute-start.23 = (bf16[2,128,1024]{2,1,0:T(8,128)(2,1)S(1)}, bf16[2,128,1024]{2,1,0:T(8,128)(2,1)S(1)}, u32[]{:S(2)}, u32[]{:S(2)}) collective-permute-start(bf16[2,128,1024]{2,1,0:T(8,128)(2,1)S(1)} %collective-permute-done.22.refs_2_), channel_id=1, source_target_pairs={{0,2},{2,0},{4,6},{6,4},{8,10},{10,8},{12,14},{14,12},{1,3},{3,1},... | collective-permute-start | bytes 1572872 | tf_op jit(solution)/shard_map/ppermute | solution.py:41
  106.4 32.2 %collective-permute-start.17 = (bf16[2,128,512]{2,1,0:T(8,128)(2,1)S(1)}, bf16[2,128,512]{2,1,0:T(8,128)(2,1)S(1)}, u32[]{:S(2)}, u32[]{:S(2)}) collective-permute-start(bf16[2,128,512]{2,1,0:T(8,128)(2,1)S(1)} %stack.10.refs_0_), channel_id=1, source_target_pairs={{0,2},{2,0},{4,6},{6,4},{8,10},{10,8},{12,14},{14,12},{1,3},{3,1},... | collective-permute-start | bytes 786440 | tf_op jit(solution)/shard_map/ppermute | solution.py:41
  106.9 34.7 %collective-permute-start.19 = (bf16[2,128,512]{2,1,0:T(8,128)(2,1)S(1)}, bf16[2,128,512]{2,1,0:T(8,128)(2,1)S(1)}, u32[]{:S(2)}, u32[]{:S(2)}) collective-permute-start(bf16[2,128,512]{2,1,0:T(8,128)(2,1)S(1)} %collective-permute-done.18.refs_2_), channel_id=1, source_target_pairs={{0,2},{2,0},{4,6},{6,4},{8,10},{10,8},{12,14},{14,12},{1,3},{3,1},... | collective-permute-start | bytes 786440 | tf_op jit(solution)/shard_map/ppermute | solution.py:41
  142.3 2.5 %collective-permute-start.28 = (bf16[512,896]{1,0:T(8,128)(2,1)S(1)}, bf16[512,896]{1,0:T(8,128)(2,1)S(1)}, u32[]{:S(2)}, u32[]{:S(2)}) collective-permute-start(bf16[512,896]{1,0:T(8,128)(2,1)S(1)} %finish0.1), channel_id=1, source_target_pairs={{0,1},{1,0},{2,3},{3,2},{4,5},{5,4},{6,7},{7,6},{8,9},{9,8},{10,11... | collective-permute-start | bytes 2752520 | tf_op jit(solution)/shard_map/ppermute | solution.py:45
  (3 other events, 14.8 us)

commit v4 on v3

--- a/solution.py
+++ b/solution.py
@@ -13,7 +13,9 @@
 MASKED = -1e30
 LANES = 128
 STEP = 4
-PIECES = (1, 2, 2, 2, 1)
+PLAN = ((4, 0), (8, 0), (8, 1), (8, 0), (4, 0))
+AHEAD_Y = 2
+AHEAD_Z = 3
 LOCAL = pl.BlockSpec(memory_space=pltpu.VMEM)
 ANYWHERE = pl.BlockSpec(memory_space=pl.ANY)
 SCALARS = pl.BlockSpec(memory_space=pltpu.SMEM)
@@ -69,6 +71,34 @@
     for mask in rest:
         pairs.update({key ^ mask: exchange(pair, mask, shards) for key, pair in pairs.items()})
     return pairs
+
+
+def gate_kernel(x_ref, *refs):
+    refs[-1][...] = x_ref[...]
+
+
+def gate(x, after):
+    return pl.pallas_call(
+        gate_kernel,
+        in_specs=[LOCAL] + [ANYWHERE] * len(after),
+        out_specs=LOCAL,
+        out_shape=pltpu.VMEM(x.shape, x.dtype),
+        compiler_params=params(2),
+        cost_estimate=cost(0, 1024),
+        name="gate",
+    )(held(x), *after)
+
+
+class Queue:
+    def __init__(self, ahead, shards):
+        self.ahead, self.shards, self.sent = ahead, shards, []
+
+    def send(self, x, mask, also=()):
+        after = self.sent[-self.ahead :][:1] if len(self.sent) >= self.ahead else []
+        after = [*after, *also]
+        got = exchange(gate(x, after) if after else x, mask, self.shards)
+        self.sent.append(got)
+        return got
 
 
 def pack_kernel(own, latent_ref, rope_ref, out_ref):
@@ -263,7 +293,7 @@
             pltpu.VMEM((2, 2 * tokens, keys), BF16),
         ],
         compiler_params=params(12),
-        cost_estimate=cost(heads << 30, 1024),
+        cost_estimate=cost(heads << 26, 1024),
         name=f"attend{start}",
     )(held(queries), held(bias), held(w_value), held(kv), *after)
 
@@ -360,25 +390,38 @@
     bias = mask(span_offset, valid_lengths, owners, tokens, per_shard, own)
     kv = join([mine[key] for key in keys], [theirs[key] for key in keys], per_shard)
 
-    acc = None
-    start = 0
-    sent = []
-    for chunk, piece in enumerate(PIECES):
-        heads = piece * head_count // sum(PIECES)
-        after = [sent[-2][0]] if chunk > 1 else []
-        if chunk > 2:
-            after += [sent[-3][key] for key in basis_of(shards)[1:]]
-        if chunk > 3:
-            after += [sent[-4][key] for key in keys]
-        out = attend(start, heads, queries, bias, w_value, kv, scale, after)
-        gathered = spread(out, shards)
-        pairs = [gathered[key] for key in keys]
-        sent.append(gathered)
-        row = start * value
-        if chunk < len(PIECES) - 1:
-            acc = project(row, pairs, w_output, acc)
-        start += heads
-
+    heads = [count * head_count // 32 for count, _ in PLAN]
+    starts = [sum(heads[:chunk]) for chunk in range(len(heads))]
+    along_z = Queue(AHEAD_Z, shards)
+    along_y = Queue(AHEAD_Y, shards)
+    outs, crossed, pairs, accs = [], [], [], [None]
+    def last_step(chunk):
+        base, side, near = pairs[chunk]
+        got = along_z.send(side, 2) if PLAN[chunk][1] else along_y.send(near, 1)
+        pairs[chunk].append(got)
+
+    for stage in range(len(heads) + 1):
+        if stage < len(heads):
+            outs.append(attend(starts[stage], heads[stage], queries, bias, w_value, kv, scale))
+        if stage > 0 and shards == 8:
+            base = stack(outs[stage - 1], crossed[stage - 1])
+            near = along_z.send(base, 2)
+            side = along_y.send(base, 1, [accs[-2]] if stage > 4 else [])
+        if stage < len(heads):
+            crossed.append(along_z.send(outs[stage], far))
+        if stage > 0:
+            if shards != 8:
+                gathered = spread(outs[stage - 1], shards)
+                pairs.append([gathered[key] for key in keys])
+            elif PLAN[stage - 1][1]:
+                pairs.append([base, side, near, along_z.send(side, 2)])
+            else:
+                pairs.append([base, side, near, along_y.send(near, 1)])
+            if stage < len(heads):
+                row = starts[stage - 1] * value
+                accs.append(project(row, pairs[-1], w_output, accs[-1]))
+
+    row, pairs, acc = starts[-1] * value, pairs[-1], accs[-1]
     given = finish(row, keys, far, 0, pairs, w_output, acc, BF16)
     other = sibling(given)
     kept = finish(row, keys, far, 1, pairs, w_output, acc, F32)

time: 146 us -> 140 us (0.959)
  waiting for transfers between devices: 69.8 us -> 60 us
  starting transfers between devices: 37.1 us -> 40.5 us
    ppermute x24, waiting for transfers between devices: 68 us -> 58.1 us  [exchange(): return lax.ppermute(x, 'ctx', [(i, i ^ mask) for i in range(shards)])]
    ppermute x24, starting transfers between devices: 36.5 us -> 39.9 us  [exchange(): return lax.ppermute(x, 'ctx', [(i, i ^ mask) for i in range(shards)])]
  transfers between devices with their start and end apart: 29 -> 29, of which waited for: 13 -> 15; matrix products, arithmetic and copies ran while one was open for 0% -> 0% of each run, Pallas kernels for 22% -> 23%
where the time goes in v4:
time: 140 us
  waiting for transfers between devices  60 us (43%)
  starting transfers between devices  40.5 us (29%)
  Pallas kernels  35.7 us (26%)
  local copies, waits for them, and re-layouts  1.69 us (1%)
    ppermute x24, waiting for transfers between devices, exchange(): return lax.ppermute(x, 'ctx', [(i, i ^ mask) for i in range(shards)])  58.1 us
    ppermute x24, starting transfers between devices, exchange(): return lax.ppermute(x, 'ctx', [(i, i ^ mask) for i in range(shards)])  39.9 us
    pallas_call x5, Pallas kernels, attend(): pl.pallas_call(functools.partial(attend_kernel, scale * math.log2(math.e)...  19 us
    pallas_call x4, Pallas kernels, project(): pl.pallas_call(functools.partial(project_kernel, start, groups, acc is No...  9.62 us
    pallas_call x1, Pallas kernels, prep(): pl.pallas_call(prep_kernel, in_specs=[ANYWHERE] * 3, out_specs=LOCAL, out...  3.98 us
  transfers between devices with their start and end apart: 29, of which 15 were waited for; matrix products, arithmetic and copies ran while one was open for 0% of the time, Pallas kernels for 23%

profile of v4, /device:TPU:0, one launch (start us, length us, event | category | flops | bytes accessed | tf_op | source)
XLA Modules:
  0.0 140.0 jit_solution(5246202151696720844)
XLA Ops:
  1.8 5.1 %collective-permute-start = (bf16[80,640]{1,0:T(8,128)(2,1)S(1)}, bf16[80,640]{1,0:T(8,128)(2,1)S(1)}, u32[]{:S(2)}, u32[]{:S(2)}) collective-permute-start(bf16[80,640]{1,0:T(8,128)(2,1)S(1)} %pack.1.first_ref), channel_id=1, source_target_pairs={{0,12},{2,14},{4,8},{6,10},{8,4},{10,6},{12,0},{14,2},{1,13},{3,15... | collective-permute-start | bytes 307208 | tf_op jit(solution)/shard_map/ppermute | solution.py:43
  6.9 4.0 %prep.1.refs_0_.q_ref = bf16[4096,640]{1,0:T(8,128)(2,1)S(1)} custom-call(bf16[128,4096]{1,0:T(8,128)(2,1)} %q_hbm.1, bf16[128,2048]{1,0:T(8,128)(2,1)} %r_hbm.1, bf16[32,128,512]{2,1,0:T(8,128)(2,1)} %w_hbm.1), custom_call_target="tpu_custom_call" | custom-call | bytes 1024 | tf_op jit(solution)/shard_map/prep/pallas_call | solution.py:197
  13.3 4.3 %collective-permute-done.2.refs_2_ = bf16[2,80,640]{2,1,0:T(8,128)(2,1)S(1)} collective-permute-done((bf16[2,80,640]{2,1,0:T(8,128)(2,1)S(1)}, bf16[2,80,640]{2,1,0:T(8,128)(2,1)S(1)}, u32[]{:S(2)}, u32[]{:S(2)}) %collective-permute-start.2) | collective-permute-done | bytes 204832 | tf_op jit(solution)/shard_map/ppermute | solution.py:43
  19.6 3.7 %collective-permute-done.3.refs_3_ = bf16[2,80,640]{2,1,0:T(8,128)(2,1)S(1)} collective-permute-done((bf16[2,80,640]{2,1,0:T(8,128)(2,1)S(1)}, bf16[2,80,640]{2,1,0:T(8,128)(2,1)S(1)}, u32[]{:S(2)}, u32[]{:S(2)}) %collective-permute-start.3) | collective-permute-done | bytes 204832 | tf_op jit(solution)/shard_map/ppermute | solution.py:43
  25.1 2.4 %attend0.1.first_ref = bf16[128,512]{1,0:T(8,128)(2,1)S(1)} custom-call(bf16[4096,640]{1,0:T(8,128)(2,1)S(1)} %prep.1.refs_0_.q_ref, f32[128,1152]{1,0:T(8,128)S(1)} %mask.1.bias_ref, bf16[32,512,128]{2,1,0:T(8,128)(2,1)S(1)} %copy-done, bf16[1152,640]{1,0:T(8,128)(2,1)S(1)} %join.1.kv_ref), custom_call_target="tpu_custom_call" | custom-call | flops 268435456 | bytes 1024 | tf_op jit(solution)/shard_map/attend0/pallas_call | solution.py:286
  27.5 1.8 %collective-permute-start.9 = (bf16[128,512]{1,0:T(8,128)(2,1)S(1)}, bf16[128,512]{1,0:T(8,128)(2,1)S(1)}, u32[]{:S(2)}, u32[]{:S(2)}) collective-permute-start(bf16[128,512]{1,0:T(8,128)(2,1)S(1)} %attend0.1.first_ref), channel_id=1, source_target_pairs={{0,12},{2,14},{4,8},{6,10},{8,4},{10,6},{12,0},{14,2},{1,13},{3,15... | collective-permute-start | bytes 393224 | tf_op jit(solution)/shard_map/ppermute | solution.py:43
  29.3 4.7 %attend4.1.first_ref = bf16[128,1024]{1,0:T(8,128)(2,1)S(1)} custom-call(bf16[4096,640]{1,0:T(8,128)(2,1)S(1)} %prep.1.refs_0_.q_ref, f32[128,1152]{1,0:T(8,128)S(1)} %mask.1.bias_ref, bf16[32,512,128]{2,1,0:T(8,128)(2,1)S(1)} %copy-done, bf16[1152,640]{1,0:T(8,128)(2,1)S(1)} %join.1.kv_ref), custom_call_target="tpu_custom_call" | custom-call | flops 536870912 | bytes 1024 | tf_op jit(solution)/shard_map/attend4/pallas_call | solution.py:286
  33.9 2.2 %collective-permute-start.8 = (bf16[128,1024]{1,0:T(8,128)(2,1)S(1)}, bf16[128,1024]{1,0:T(8,128)(2,1)S(1)}, u32[]{:S(2)}, u32[]{:S(2)}) collective-permute-start(bf16[128,1024]{1,0:T(8,128)(2,1)S(1)} %attend4.1.first_ref), channel_id=1, source_target_pairs={{0,12},{2,14},{4,8},{6,10},{8,4},{10,6},{12,0},{14,2},{1,13},{3,15... | collective-permute-start | bytes 786440 | tf_op jit(solution)/shard_map/ppermute | solution.py:43
  38.1 4.7 %attend12.1.x_ref.first_ref = bf16[128,1024]{1,0:T(8,128)(2,1)S(1)} custom-call(bf16[4096,640]{1,0:T(8,128)(2,1)S(1)} %prep.1.refs_0_.q_ref, f32[128,1152]{1,0:T(8,128)S(1)} %mask.1.bias_ref, bf16[32,512,128]{2,1,0:T(8,128)(2,1)S(1)} %copy-done, bf16[1152,640]{1,0:T(8,128)(2,1)S(1)} %join.1.kv_ref), custom_call_target="tpu_custom_call" | custom-call | flops 536870912 | bytes 1024 | tf_op jit(solution)/shard_map/attend12/pallas_call | solution.py:286
  42.8 2.2 %collective-permute-done.8.second_ref.refs_0_ = bf16[128,1024]{1,0:T(8,128)(2,1)S(1)} collective-permute-done((bf16[128,1024]{1,0:T(8,128)(2,1)S(1)}, bf16[128,1024]{1,0:T(8,128)(2,1)S(1)}, u32[]{:S(2)}, u32[]{:S(2)}) %collective-permute-start.8) | collective-permute-done | bytes 262176 | tf_op jit(solution)/shard_map/ppermute | solution.py:43
  45.1 2.8 %collective-permute-start.10 = (bf16[2,128,1024]{2,1,0:T(8,128)(2,1)S(1)}, bf16[2,128,1024]{2,1,0:T(8,128)(2,1)S(1)}, u32[]{:S(2)}, u32[]{:S(2)}) collective-permute-start(bf16[2,128,1024]{2,1,0:T(8,128)(2,1)S(1)} %gate.15), channel_id=1, source_target_pairs={{0,4},{2,6},{4,0},{6,2},{8,12},{10,14},{12,8},{14,10},{1,5},{3,7},... | collective-permute-start | bytes 1572872 | tf_op jit(solution)/shard_map/ppermute | solution.py:43
  48.0 2.0 %collective-permute-done.13.refs_0_.refs_2_ = bf16[2,128,512]{2,1,0:T(8,128)(2,1)S(1)} collective-permute-done((bf16[2,128,512]{2,1,0:T(8,128)(2,1)S(1)}, bf16[2,128,512]{2,1,0:T(8,128)(2,1)S(1)}, u32[]{:S(2)}, u32[]{:S(2)}) %collective-permute-start.13) | collective-permute-done | bytes 262176 | tf_op jit(solution)/shard_map/ppermute | solution.py:43
  49.9 2.2 %collective-permute-start.17 = (bf16[128,1024]{1,0:T(8,128)(2,1)S(1)}, bf16[128,1024]{1,0:T(8,128)(2,1)S(1)}, u32[]{:S(2)}, u32[]{:S(2)}) collective-permute-start(bf16[128,1024]{1,0:T(8,128)(2,1)S(1)} %gate.20), channel_id=1, source_target_pairs={{0,12},{2,14},{4,8},{6,10},{8,4},{10,6},{12,0},{14,2},{1,13},{3,15... | collective-permute-start | bytes 786440 | tf_op jit(solution)/shard_map/ppermute | solution.py:43
  52.1 1.6 %collective-permute-start.19 = (bf16[2,128,1024]{2,1,0:T(8,128)(2,1)S(1)}, bf16[2,128,1024]{2,1,0:T(8,128)(2,1)S(1)}, u32[]{:S(2)}, u32[]{:S(2)}) collective-permute-start(bf16[2,128,1024]{2,1,0:T(8,128)(2,1)S(1)} %gate.21), channel_id=1, source_target_pairs={{0,2},{2,0},{4,6},{6,4},{8,10},{10,8},{12,14},{14,12},{1,3},{3,1},... | collective-permute-start | bytes 1572872 | tf_op jit(solution)/shard_map/ppermute | solution.py:43
  53.7 13.2 %collective-permute-done.17.second_ref.refs_0_ = bf16[128,1024]{1,0:T(8,128)(2,1)S(1)} collective-permute-done((bf16[128,1024]{1,0:T(8,128)(2,1)S(1)}, bf16[128,1024]{1,0:T(8,128)(2,1)S(1)}, u32[]{:S(2)}, u32[]{:S(2)}) %collective-permute-start.17) | collective-permute-done | bytes 262176 | tf_op jit(solution)/shard_map/ppermute | solution.py:43
  67.1 4.9 %attend20.1.x_ref.first_ref = bf16[128,1024]{1,0:T(8,128)(2,1)S(1)} custom-call(bf16[4096,640]{1,0:T(8,128)(2,1)S(1)} %prep.1.refs_0_.q_ref, f32[128,1152]{1,0:T(8,128)S(1)} %mask.1.bias_ref, bf16[32,512,128]{2,1,0:T(8,128)(2,1)S(1)} %copy-done, bf16[1152,640]{1,0:T(8,128)(2,1)S(1)} %join.1.kv_ref), custom_call_target="tpu_custom_call" | custom-call | flops 536870912 | bytes 1024 | tf_op jit(solution)/shard_map/attend20/pallas_call | solution.py:286
  73.7 1.8 %collective-permute-start.11 = (bf16[128,1024]{1,0:T(8,128)(2,1)S(1)}, bf16[128,1024]{1,0:T(8,128)(2,1)S(1)}, u32[]{:S(2)}, u32[]{:S(2)}) collective-permute-start(bf16[128,1024]{1,0:T(8,128)(2,1)S(1)} %gate.16), channel_id=1, source_target_pairs={{0,12},{2,14},{4,8},{6,10},{8,4},{10,6},{12,0},{14,2},{1,13},{3,15... | collective-permute-start | bytes 786440 | tf_op jit(solution)/shard_map/ppermute | solution.py:43
  76.1 5.3 %collective-permute-done.14.refs_0_.refs_3_ = bf16[2,128,512]{2,1,0:T(8,128)(2,1)S(1)} collective-permute-done((bf16[2,128,512]{2,1,0:T(8,128)(2,1)S(1)}, bf16[2,128,512]{2,1,0:T(8,128)(2,1)S(1)}, u32[]{:S(2)}, u32[]{:S(2)}) %collective-permute-start.14) | collective-permute-done | bytes 262176 | tf_op jit(solution)/shard_map/ppermute | solution.py:43
  83.0 2.3 %collective-permute-done.11.refs_0_.second_ref = bf16[128,1024]{1,0:T(8,128)(2,1)S(1)} collective-permute-done((bf16[128,1024]{1,0:T(8,128)(2,1)S(1)}, bf16[128,1024]{1,0:T(8,128)(2,1)S(1)}, u32[]{:S(2)}, u32[]{:S(2)}) %collective-permute-start.11) | collective-permute-done | bytes 262176 | tf_op jit(solution)/shard_map/ppermute | solution.py:43
  85.4 2.4 %collective-permute-start.25 = (bf16[2,128,1024]{2,1,0:T(8,128)(2,1)S(1)}, bf16[2,128,1024]{2,1,0:T(8,128)(2,1)S(1)}, u32[]{:S(2)}, u32[]{:S(2)}) collective-permute-start(bf16[2,128,1024]{2,1,0:T(8,128)(2,1)S(1)} %gate.27), channel_id=1, source_target_pairs={{0,4},{2,6},{4,0},{6,2},{8,12},{10,14},{12,8},{14,10},{1,5},{3,7},... | collective-permute-start | bytes 1572872 | tf_op jit(solution)/shard_map/ppermute | solution.py:43
  87.8 4.8 %collective-permute-done.20.x_ref.refs_1_.refs_0_ = bf16[2,128,1024]{2,1,0:T(8,128)(2,1)S(1)} collective-permute-done((bf16[2,128,1024]{2,1,0:T(8,128)(2,1)S(1)}, bf16[2,128,1024]{2,1,0:T(8,128)(2,1)S(1)}, u32[]{:S(2)}, u32[]{:S(2)}) %collective-permute-start.20) | collective-permute-done | bytes 524320 | tf_op jit(solution)/shard_map/ppermute | solution.py:43
  92.7 2.1 %collective-permute-start.22 = (bf16[2,128,1024]{2,1,0:T(8,128)(2,1)S(1)}, bf16[2,128,1024]{2,1,0:T(8,128)(2,1)S(1)}, u32[]{:S(2)}, u32[]{:S(2)}) collective-permute-start(bf16[2,128,1024]{2,1,0:T(8,128)(2,1)S(1)} %gate.24), channel_id=1, source_target_pairs={{0,4},{2,6},{4,0},{6,2},{8,12},{10,14},{12,8},{14,10},{1,5},{3,7},... | collective-permute-start | bytes 1572872 | tf_op jit(solution)/shard_map/ppermute | solution.py:43
  94.7 6.7 %collective-permute-done.15.refs_0_.refs_3_ = bf16[2,128,1024]{2,1,0:T(8,128)(2,1)S(1)} collective-permute-done((bf16[2,128,1024]{2,1,0:T(8,128)(2,1)S(1)}, bf16[2,128,1024]{2,1,0:T(8,128)(2,1)S(1)}, u32[]{:S(2)}, u32[]{:S(2)}) %collective-permute-start.15) | collective-permute-done | bytes 524320 | tf_op jit(solution)/shard_map/ppermute | solution.py:43
  103.7 2.4 %attend28.1.x_ref.first_ref = bf16[128,512]{1,0:T(8,128)(2,1)S(1)} custom-call(bf16[4096,640]{1,0:T(8,128)(2,1)S(1)} %prep.1.refs_0_.q_ref, f32[128,1152]{1,0:T(8,128)S(1)} %mask.1.bias_ref, bf16[32,512,128]{2,1,0:T(8,128)(2,1)S(1)} %copy-done, bf16[1152,640]{1,0:T(8,128)(2,1)S(1)} %join.1.kv_ref), custom_call_target="tpu_custom_call" | custom-call | flops 268435456 | bytes 1024 | tf_op jit(solution)/shard_map/attend28/pallas_call | solution.py:286
  106.1 1.8 %collective-permute-start.12 = (bf16[128,512]{1,0:T(8,128)(2,1)S(1)}, bf16[128,512]{1,0:T(8,128)(2,1)S(1)}, u32[]{:S(2)}, u32[]{:S(2)}) collective-permute-start(bf16[128,512]{1,0:T(8,128)(2,1)S(1)} %gate.17), channel_id=1, source_target_pairs={{0,12},{2,14},{4,8},{6,10},{8,4},{10,6},{12,0},{14,2},{1,13},{3,15... | collective-permute-start | bytes 393224 | tf_op jit(solution)/shard_map/ppermute | solution.py:43
  107.9 5.3 %collective-permute-done.12.second_ref = bf16[128,512]{1,0:T(8,128)(2,1)S(1)} collective-permute-done((bf16[128,512]{1,0:T(8,128)(2,1)S(1)}, bf16[128,512]{1,0:T(8,128)(2,1)S(1)}, u32[]{:S(2)}, u32[]{:S(2)}) %collective-permute-start.12) | collective-permute-done | bytes 131104 | tf_op jit(solution)/shard_map/ppermute | solution.py:43
  115.7 2.8 %project512.1.refs_4_ = f32[2,512,896]{2,1,0:T(8,128)S(1)} custom-call(bf16[4096,896]{1,0:T(8,128)(2,1)S(1)} %bitcast.2, bf16[2,128,1024]{2,1,0:T(8,128)(2,1)S(1)} %stack.7.x_ref.refs_0_, bf16[2,128,1024]{2,1,0:T(8,128)(2,1)S(1)} %collective-permute-done.19.refs_0_.refs_1_, ...), custom_call_target="tpu_custom_call", output_to_operand_aliasing={{}: (5, {})} | custom-call | bytes 1024 | tf_op jit(solution)/shard_map/project512/pallas_call | solution.py:321
  118.5 2.8 %project1536.1.refs_1_.refs_4_ = f32[2,512,896]{2,1,0:T(8,128)S(1)} custom-call(bf16[4096,896]{1,0:T(8,128)(2,1)S(1)} %bitcast.2, bf16[2,128,1024]{2,1,0:T(8,128)(2,1)S(1)} %stack.11.x_ref.refs_0_, bf16[2,128,1024]{2,1,0:T(8,128)(2,1)S(1)} %collective-permute-done.20.x_ref.refs_1_.refs_0_, ...), custom_call_target="tpu_custom_call", output_to_operand_aliasing={{}: (5, {})} | custom-call | bytes 1024 | tf_op jit(solution)/shard_map/project1536/pallas_call | solution.py:321
  122.9 4.8 %collective-permute-done.26.refs_0_.refs_3_ = bf16[2,128,1024]{2,1,0:T(8,128)(2,1)S(1)} collective-permute-done((bf16[2,128,1024]{2,1,0:T(8,128)(2,1)S(1)}, bf16[2,128,1024]{2,1,0:T(8,128)(2,1)S(1)}, u32[]{:S(2)}, u32[]{:S(2)}) %collective-permute-start.26) | collective-permute-done | bytes 524320 | tf_op jit(solution)/shard_map/ppermute | solution.py:43
  129.3 2.8 %project2560.1.refs_4_ = f32[2,512,896]{2,1,0:T(8,128)S(1)} custom-call(bf16[4096,896]{1,0:T(8,128)(2,1)S(1)} %bitcast.2, bf16[2,128,1024]{2,1,0:T(8,128)(2,1)S(1)} %stack.9.x_ref.refs_0_, bf16[2,128,1024]{2,1,0:T(8,128)(2,1)S(1)} %collective-permute-done.16.refs_0_.refs_1_, ...), custom_call_target="tpu_custom_call", output_to_operand_aliasing={{}: (5, {})} | custom-call | bytes 1024 | tf_op jit(solution)/shard_map/project2560/pallas_call | solution.py:321
  132.8 2.8 %collective-permute-done.27.refs_3_ = bf16[2,128,512]{2,1,0:T(8,128)(2,1)S(1)} collective-permute-done((bf16[2,128,512]{2,1,0:T(8,128)(2,1)S(1)}, bf16[2,128,512]{2,1,0:T(8,128)(2,1)S(1)}, u32[]{:S(2)}, u32[]{:S(2)}) %collective-permute-start.27) | collective-permute-done | bytes 262176 | tf_op jit(solution)/shard_map/ppermute | solution.py:43
  137.2 1.7 %collective-permute-done.28 = bf16[512,896]{1,0:T(8,128)(2,1)S(1)} collective-permute-done((bf16[512,896]{1,0:T(8,128)(2,1)S(1)}, bf16[512,896]{1,0:T(8,128)(2,1)S(1)}, u32[]{:S(2)}, u32[]{:S(2)}) %collective-permute-start.28) | collective-permute-done | bytes 917536 | tf_op jit(solution)/shard_map/ppermute | solution.py:47
  (76 shorter events, 24.7 us)
Async XLA Ops:
  1.8 9.1 %collective-permute-start = (bf16[80,640]{1,0:T(8,128)(2,1)S(1)}, bf16[80,640]{1,0:T(8,128)(2,1)S(1)}, u32[]{:S(2)}, u32[]{:S(2)}) collective-permute-start(bf16[80,640]{1,0:T(8,128)(2,1)S(1)} %pack.1.first_ref), channel_id=1, source_target_pairs={{0,12},{2,14},{4,8},{6,10},{8,4},{10,6},{12,0},{14,2},{1,13},{3,15... | collective-permute-start | bytes 307208 | tf_op jit(solution)/shard_map/ppermute | solution.py:43
  10.9 13.1 %copy-start.3 = (s32[8]{0:T(128)S(1)}, s32[8]{0:T(128)}, u32[]{:S(2)}) copy-start(s32[8]{0:T(128)} %valid_ref.1) | copy-start | bytes 100
  10.9 14.2 %copy-start = (bf16[32,512,128]{2,1,0:T(8,128)(2,1)S(1)}, bf16[32,512,128]{2,1,0:T(8,128)(2,1)}, u32[]{:S(2)}) copy-start(bf16[32,512,128]{2,1,0:T(8,128)(2,1)} %w_ref.15) | copy-start | bytes 12582916
  10.9 6.6 %collective-permute-start.2 = (bf16[2,80,640]{2,1,0:T(8,128)(2,1)S(1)}, bf16[2,80,640]{2,1,0:T(8,128)(2,1)S(1)}, u32[]{:S(2)}, u32[]{:S(2)}) collective-permute-start(bf16[2,80,640]{2,1,0:T(8,128)(2,1)S(1)} %stack.6.refs_0_), channel_id=1, source_target_pairs={{0,4},{2,6},{4,0},{6,2},{8,12},{10,14},{12,8},{14,10},{1,5},{3,7},... | collective-permute-start | bytes 614408 | tf_op jit(solution)/shard_map/ppermute | solution.py:43
  11.8 7.8 %collective-permute-start.1 = (bf16[2,80,640]{2,1,0:T(8,128)(2,1)S(1)}, bf16[2,80,640]{2,1,0:T(8,128)(2,1)S(1)}, u32[]{:S(2)}, u32[]{:S(2)}) collective-permute-start(bf16[2,80,640]{2,1,0:T(8,128)(2,1)S(1)} %stack.6.refs_0_), channel_id=1, source_target_pairs={{0,2},{2,0},{4,6},{6,4},{8,10},{10,8},{12,14},{14,12},{1,3},{3,1},... | collective-permute-start | bytes 614408 | tf_op jit(solution)/shard_map/ppermute | solution.py:43
  17.6 5.8 %collective-permute-start.3 = (bf16[2,80,640]{2,1,0:T(8,128)(2,1)S(1)}, bf16[2,80,640]{2,1,0:T(8,128)(2,1)S(1)}, u32[]{:S(2)}, u32[]{:S(2)}) collective-permute-start(bf16[2,80,640]{2,1,0:T(8,128)(2,1)S(1)} %collective-permute-done.2.refs_2_), channel_id=1, source_target_pairs={{0,2},{2,0},{4,6},{6,4},{8,10},{10,8},{12,14},{14,12},{1,3},{3,1},... | collective-permute-start | bytes 614408 | tf_op jit(solution)/shard_map/ppermute | solution.py:43
  19.1 5.5 %collective-permute-start.4 = (bf16[2,80,640]{2,1,0:T(8,128)(2,1)S(1)}, bf16[2,80,640]{2,1,0:T(8,128)(2,1)S(1)}, u32[]{:S(2)}, u32[]{:S(2)}) collective-permute-start(bf16[2,80,640]{2,1,0:T(8,128)(2,1)S(1)} %stack.6.refs_0_), channel_id=1, source_target_pairs={{0,1},{1,0},{2,3},{3,2},{4,5},{5,4},{6,7},{7,6},{8,9},{9,8},{10,11... | collective-permute-start | bytes 614408 | tf_op jit(solution)/shard_map/ppermute | solution.py:47
  19.1 5.5 %collective-permute-start.6 = (bf16[2,80,640]{2,1,0:T(8,128)(2,1)S(1)}, bf16[2,80,640]{2,1,0:T(8,128)(2,1)S(1)}, u32[]{:S(2)}, u32[]{:S(2)}) collective-permute-start(bf16[2,80,640]{2,1,0:T(8,128)(2,1)S(1)} %collective-permute-done.2.refs_2_), channel_id=1, source_target_pairs={{0,1},{1,0},{2,3},{3,2},{4,5},{5,4},{6,7},{7,6},{8,9},{9,8},{10,11... | collective-permute-start | bytes 614408 | tf_op jit(solution)/shard_map/ppermute | solution.py:47
  19.6 5.0 %collective-permute-start.5 = (bf16[2,80,640]{2,1,0:T(8,128)(2,1)S(1)}, bf16[2,80,640]{2,1,0:T(8,128)(2,1)S(1)}, u32[]{:S(2)}, u32[]{:S(2)}) collective-permute-start(bf16[2,80,640]{2,1,0:T(8,128)(2,1)S(1)} %collective-permute-done.1.refs_1_), channel_id=1, source_target_pairs={{0,1},{1,0},{2,3},{3,2},{4,5},{5,4},{6,7},{7,6},{8,9},{9,8},{10,11... | collective-permute-start | bytes 614408 | tf_op jit(solution)/shard_map/ppermute | solution.py:47
  23.3 1.5 %collective-permute-start.7 = (bf16[2,80,640]{2,1,0:T(8,128)(2,1)S(1)}, bf16[2,80,640]{2,1,0:T(8,128)(2,1)S(1)}, u32[]{:S(2)}, u32[]{:S(2)}) collective-permute-start(bf16[2,80,640]{2,1,0:T(8,128)(2,1)S(1)} %collective-permute-done.3.refs_3_), channel_id=1, source_target_pairs={{0,1},{1,0},{2,3},{3,2},{4,5},{5,4},{6,7},{7,6},{8,9},{9,8},{10,11... | collective-permute-start | bytes 614408 | tf_op jit(solution)/shard_map/ppermute | solution.py:47
  27.5 8.7 %collective-permute-start.9 = (bf16[128,512]{1,0:T(8,128)(2,1)S(1)}, bf16[128,512]{1,0:T(8,128)(2,1)S(1)}, u32[]{:S(2)}, u32[]{:S(2)}) collective-permute-start(bf16[128,512]{1,0:T(8,128)(2,1)S(1)} %attend0.1.first_ref), channel_id=1, source_target_pairs={{0,12},{2,14},{4,8},{6,10},{8,4},{10,6},{12,0},{14,2},{1,13},{3,15... | collective-permute-start | bytes 393224 | tf_op jit(solution)/shard_map/ppermute | solution.py:43
  33.9 11.1 %collective-permute-start.8 = (bf16[128,1024]{1,0:T(8,128)(2,1)S(1)}, bf16[128,1024]{1,0:T(8,128)(2,1)S(1)}, u32[]{:S(2)}, u32[]{:S(2)}) collective-permute-start(bf16[128,1024]{1,0:T(8,128)(2,1)S(1)} %attend4.1.first_ref), channel_id=1, source_target_pairs={{0,12},{2,14},{4,8},{6,10},{8,4},{10,6},{12,0},{14,2},{1,13},{3,15... | collective-permute-start | bytes 786440 | tf_op jit(solution)/shard_map/ppermute | solution.py:43
  36.2 13.8 %collective-permute-start.13 = (bf16[2,128,512]{2,1,0:T(8,128)(2,1)S(1)}, bf16[2,128,512]{2,1,0:T(8,128)(2,1)S(1)}, u32[]{:S(2)}, u32[]{:S(2)}) collective-permute-start(bf16[2,128,512]{2,1,0:T(8,128)(2,1)S(1)} %stack.10.refs_0_), channel_id=1, source_target_pairs={{0,4},{2,6},{4,0},{6,2},{8,12},{10,14},{12,8},{14,10},{1,5},{3,7},... | collective-permute-start | bytes 786440 | tf_op jit(solution)/shard_map/ppermute | solution.py:43
  36.6 15.5 %collective-permute-start.18 = (bf16[2,128,512]{2,1,0:T(8,128)(2,1)S(1)}, bf16[2,128,512]{2,1,0:T(8,128)(2,1)S(1)}, u32[]{:S(2)}, u32[]{:S(2)}) collective-permute-start(bf16[2,128,512]{2,1,0:T(8,128)(2,1)S(1)} %stack.10.refs_0_), channel_id=1, source_target_pairs={{0,2},{2,0},{4,6},{6,4},{8,10},{10,8},{12,14},{14,12},{1,3},{3,1},... | collective-permute-start | bytes 786440 | tf_op jit(solution)/shard_map/ppermute | solution.py:43
  45.1 28.5 %collective-permute-start.10 = (bf16[2,128,1024]{2,1,0:T(8,128)(2,1)S(1)}, bf16[2,128,1024]{2,1,0:T(8,128)(2,1)S(1)}, u32[]{:S(2)}, u32[]{:S(2)}) collective-permute-start(bf16[2,128,1024]{2,1,0:T(8,128)(2,1)S(1)} %gate.15), channel_id=1, source_target_pairs={{0,4},{2,6},{4,0},{6,2},{8,12},{10,14},{12,8},{14,10},{1,5},{3,7},... | collective-permute-start | bytes 1572872 | tf_op jit(solution)/shard_map/ppermute | solution.py:43
  49.9 17.0 %collective-permute-start.17 = (bf16[128,1024]{1,0:T(8,128)(2,1)S(1)}, bf16[128,1024]{1,0:T(8,128)(2,1)S(1)}, u32[]{:S(2)}, u32[]{:S(2)}) collective-permute-start(bf16[128,1024]{1,0:T(8,128)(2,1)S(1)} %gate.20), channel_id=1, source_target_pairs={{0,12},{2,14},{4,8},{6,10},{8,4},{10,6},{12,0},{14,2},{1,13},{3,15... | collective-permute-start | bytes 786440 | tf_op jit(solution)/shard_map/ppermute | solution.py:43
  52.1 23.4 %collective-permute-start.19 = (bf16[2,128,1024]{2,1,0:T(8,128)(2,1)S(1)}, bf16[2,128,1024]{2,1,0:T(8,128)(2,1)S(1)}, u32[]{:S(2)}, u32[]{:S(2)}) collective-permute-start(bf16[2,128,1024]{2,1,0:T(8,128)(2,1)S(1)} %gate.21), channel_id=1, source_target_pairs={{0,2},{2,0},{4,6},{6,4},{8,10},{10,8},{12,14},{14,12},{1,3},{3,1},... | collective-permute-start | bytes 1572872 | tf_op jit(solution)/shard_map/ppermute | solution.py:43
  67.1 18.3 %collective-permute-start.21 = (bf16[2,128,1024]{2,1,0:T(8,128)(2,1)S(1)}, bf16[2,128,1024]{2,1,0:T(8,128)(2,1)S(1)}, u32[]{:S(2)}, u32[]{:S(2)}) collective-permute-start(bf16[2,128,1024]{2,1,0:T(8,128)(2,1)S(1)} %gate.23), channel_id=1, source_target_pairs={{0,4},{2,6},{4,0},{6,2},{8,12},{10,14},{12,8},{14,10},{1,5},{3,7},... | collective-permute-start | bytes 1572872 | tf_op jit(solution)/shard_map/ppermute | solution.py:43
  72.1 9.3 %collective-permute-start.14 = (bf16[2,128,512]{2,1,0:T(8,128)(2,1)S(1)}, bf16[2,128,512]{2,1,0:T(8,128)(2,1)S(1)}, u32[]{:S(2)}, u32[]{:S(2)}) collective-permute-start(bf16[2,128,512]{2,1,0:T(8,128)(2,1)S(1)} %collective-permute-done.13.refs_0_.refs_2_), channel_id=1, source_target_pairs={{0,2},{2,0},{4,6},{6,4},{8,10},{10,8},{12,14},{14,12},{1,3},{3,1},... | collective-permute-start | bytes 786440 | tf_op jit(solution)/shard_map/ppermute | solution.py:43
  73.7 11.6 %collective-permute-start.11 = (bf16[128,1024]{1,0:T(8,128)(2,1)S(1)}, bf16[128,1024]{1,0:T(8,128)(2,1)S(1)}, u32[]{:S(2)}, u32[]{:S(2)}) collective-permute-start(bf16[128,1024]{1,0:T(8,128)(2,1)S(1)} %gate.16), channel_id=1, source_target_pairs={{0,12},{2,14},{4,8},{6,10},{8,4},{10,6},{12,0},{14,2},{1,13},{3,15... | collective-permute-start | bytes 786440 | tf_op jit(solution)/shard_map/ppermute | solution.py:43
  75.6 17.1 %collective-permute-start.20 = (bf16[2,128,1024]{2,1,0:T(8,128)(2,1)S(1)}, bf16[2,128,1024]{2,1,0:T(8,128)(2,1)S(1)}, u32[]{:S(2)}, u32[]{:S(2)}) collective-permute-start(bf16[2,128,1024]{2,1,0:T(8,128)(2,1)S(1)} %gate.22), channel_id=1, source_target_pairs={{0,2},{2,0},{4,6},{6,4},{8,10},{10,8},{12,14},{14,12},{1,3},{3,1},... | collective-permute-start | bytes 1572872 | tf_op jit(solution)/shard_map/ppermute | solution.py:43
  81.4 20.1 %collective-permute-start.15 = (bf16[2,128,1024]{2,1,0:T(8,128)(2,1)S(1)}, bf16[2,128,1024]{2,1,0:T(8,128)(2,1)S(1)}, u32[]{:S(2)}, u32[]{:S(2)}) collective-permute-start(bf16[2,128,1024]{2,1,0:T(8,128)(2,1)S(1)} %gate.18), channel_id=1, source_target_pairs={{0,2},{2,0},{4,6},{6,4},{8,10},{10,8},{12,14},{14,12},{1,3},{3,1},... | collective-permute-start | bytes 1572872 | tf_op jit(solution)/shard_map/ppermute | solution.py:43
  85.4 17.7 %collective-permute-start.25 = (bf16[2,128,1024]{2,1,0:T(8,128)(2,1)S(1)}, bf16[2,128,1024]{2,1,0:T(8,128)(2,1)S(1)}, u32[]{:S(2)}, u32[]{:S(2)}) collective-permute-start(bf16[2,128,1024]{2,1,0:T(8,128)(2,1)S(1)} %gate.27), channel_id=1, source_target_pairs={{0,4},{2,6},{4,0},{6,2},{8,12},{10,14},{12,8},{14,10},{1,5},{3,7},... | collective-permute-start | bytes 1572872 | tf_op jit(solution)/shard_map/ppermute | solution.py:43
  92.7 20.6 %collective-permute-start.22 = (bf16[2,128,1024]{2,1,0:T(8,128)(2,1)S(1)}, bf16[2,128,1024]{2,1,0:T(8,128)(2,1)S(1)}, u32[]{:S(2)}, u32[]{:S(2)}) collective-permute-start(bf16[2,128,1024]{2,1,0:T(8,128)(2,1)S(1)} %gate.24), channel_id=1, source_target_pairs={{0,4},{2,6},{4,0},{6,2},{8,12},{10,14},{12,8},{14,10},{1,5},{3,7},... | collective-permute-start | bytes 1572872 | tf_op jit(solution)/shard_map/ppermute | solution.py:43
  101.5 19.8 %collective-permute-start.16 = (bf16[2,128,1024]{2,1,0:T(8,128)(2,1)S(1)}, bf16[2,128,1024]{2,1,0:T(8,128)(2,1)S(1)}, u32[]{:S(2)}, u32[]{:S(2)}) collective-permute-start(bf16[2,128,1024]{2,1,0:T(8,128)(2,1)S(1)} %gate.19), channel_id=1, source_target_pairs={{0,2},{2,0},{4,6},{6,4},{8,10},{10,8},{12,14},{14,12},{1,3},{3,1},... | collective-permute-start | bytes 1572872 | tf_op jit(solution)/shard_map/ppermute | solution.py:43
  103.1 11.3 %slice-start = ((s8[7340032]{0:T(1024)(128)(4,1)}), s8[4194304]{0:T(1024)(128)(4,1)S(1)}, s32[]{:S(2)}) async-start(s8[7340032]{0:T(1024)(128)(4,1)} %bitcast.1), calls=%async_computation | async-start | bytes 8388608
  103.2 24.5 %collective-permute-start.26 = (bf16[2,128,1024]{2,1,0:T(8,128)(2,1)S(1)}, bf16[2,128,1024]{2,1,0:T(8,128)(2,1)S(1)}, u32[]{:S(2)}, u32[]{:S(2)}) collective-permute-start(bf16[2,128,1024]{2,1,0:T(8,128)(2,1)S(1)} %gate.28), channel_id=1, source_target_pairs={{0,2},{2,0},{4,6},{6,4},{8,10},{10,8},{12,14},{14,12},{1,3},{3,1},... | collective-permute-start | bytes 1572872 | tf_op jit(solution)/shard_map/ppermute | solution.py:43
  106.1 7.0 %collective-permute-start.12 = (bf16[128,512]{1,0:T(8,128)(2,1)S(1)}, bf16[128,512]{1,0:T(8,128)(2,1)S(1)}, u32[]{:S(2)}, u32[]{:S(2)}) collective-permute-start(bf16[128,512]{1,0:T(8,128)(2,1)S(1)} %gate.17), channel_id=1, source_target_pairs={{0,12},{2,14},{4,8},{6,10},{8,4},{10,6},{12,0},{14,2},{1,13},{3,15... | collective-permute-start | bytes 393224 | tf_op jit(solution)/shard_map/ppermute | solution.py:43
  113.3 9.7 %collective-permute-start.24 = (bf16[2,128,512]{2,1,0:T(8,128)(2,1)S(1)}, bf16[2,128,512]{2,1,0:T(8,128)(2,1)S(1)}, u32[]{:S(2)}, u32[]{:S(2)}) collective-permute-start(bf16[2,128,512]{2,1,0:T(8,128)(2,1)S(1)} %gate.26), channel_id=1, source_target_pairs={{0,4},{2,6},{4,0},{6,2},{8,12},{10,14},{12,8},{14,10},{1,5},{3,7},... | collective-permute-start | bytes 786440 | tf_op jit(solution)/shard_map/ppermute | solution.py:43
  121.3 11.5 %collective-permute-start.23 = (bf16[2,128,512]{2,1,0:T(8,128)(2,1)S(1)}, bf16[2,128,512]{2,1,0:T(8,128)(2,1)S(1)}, u32[]{:S(2)}, u32[]{:S(2)}) collective-permute-start(bf16[2,128,512]{2,1,0:T(8,128)(2,1)S(1)} %gate.25), channel_id=1, source_target_pairs={{0,2},{2,0},{4,6},{6,4},{8,10},{10,8},{12,14},{14,12},{1,3},{3,1},... | collective-permute-start | bytes 786440 | tf_op jit(solution)/shard_map/ppermute | solution.py:43
  127.7 7.9 %collective-permute-start.27 = (bf16[2,128,512]{2,1,0:T(8,128)(2,1)S(1)}, bf16[2,128,512]{2,1,0:T(8,128)(2,1)S(1)}, u32[]{:S(2)}, u32[]{:S(2)}) collective-permute-start(bf16[2,128,512]{2,1,0:T(8,128)(2,1)S(1)} %gate.29), channel_id=1, source_target_pairs={{0,2},{2,0},{4,6},{6,4},{8,10},{10,8},{12,14},{14,12},{1,3},{3,1},... | collective-permute-start | bytes 786440 | tf_op jit(solution)/shard_map/ppermute | solution.py:43
  136.3 2.5 %collective-permute-start.28 = (bf16[512,896]{1,0:T(8,128)(2,1)S(1)}, bf16[512,896]{1,0:T(8,128)(2,1)S(1)}, u32[]{:S(2)}, u32[]{:S(2)}) collective-permute-start(bf16[512,896]{1,0:T(8,128)(2,1)S(1)} %finish0.1), channel_id=1, source_target_pairs={{0,1},{1,0},{2,3},{3,2},{4,5},{5,4},{6,7},{7,6},{8,9},{9,8},{10,11... | collective-permute-start | bytes 2752520 | tf_op jit(solution)/shard_map/ppermute | solution.py:47
  (3 other events, 13.0 us)

commit v5 on v3

--- a/solution.py
+++ b/solution.py
@@ -13,7 +13,17 @@
 MASKED = -1e30
 LANES = 128
 STEP = 4
-PIECES = (1, 2, 2, 2, 1)
+PLAN = ((4, 0), (8, 0), (6, 0), (8, 0), (6, 1))
+FAR, SIDE, CROSS, NEAR, BOTH = "far", "side", "cross", "near", "both"
+ATTEND, STACK, PROJECT, OWN = "attend", "stack", "project", "own"
+ORDER = (
+    (ATTEND, 0), (ATTEND, 1), (STACK, 0), (FAR, 1), (ATTEND, 2), (BOTH, 0, (SIDE, 1), (SIDE, 2)),
+    (CROSS, 0), (FAR, 2), (STACK, 1, (FAR, 0)), (ATTEND, 3, (CROSS, 0)), (ATTEND, 4),
+    (CROSS, 1, (BOTH, 0)), (PROJECT, 0, (SIDE, 3)), (STACK, 2), (FAR, 3, (NEAR, 1)),
+    (CROSS, 2, (CROSS, 1)), (FAR, 4, (NEAR, 2)), (BOTH, 2, (CROSS, 2)), (STACK, 3),
+    (CROSS, 3, (BOTH, 1)), (PROJECT, 1), (STACK, 4), (CROSS, 4), (PROJECT, 2), (BOTH, 3), (BOTH, 4),
+    (PROJECT, 3, (NEAR, 4)),
+)
 LOCAL = pl.BlockSpec(memory_space=pltpu.VMEM)
 ANYWHERE = pl.BlockSpec(memory_space=pl.ANY)
 SCALARS = pl.BlockSpec(memory_space=pltpu.SMEM)
@@ -71,12 +81,36 @@
     return pairs
 
 
-def pack_kernel(own, latent_ref, rope_ref, out_ref):
+def gate_kernel(x_ref, *refs):
+    refs[-1][...] = x_ref[...]
+
+
+def gate(x, after):
+    return pl.pallas_call(
+        gate_kernel,
+        in_specs=[LOCAL] + [ANYWHERE] * len(after),
+        out_specs=LOCAL,
+        out_shape=pltpu.VMEM(x.shape, x.dtype),
+        compiler_params=params(2),
+        cost_estimate=cost(0, 1024),
+        name="gate",
+    )(held(x), *after)
+
+
+def pack_kernel(own, latent_hbm, rope_hbm, out_ref, latent_ref, rope_ref, sem):
+    copies = (
+        pltpu.make_async_copy(latent_hbm, latent_ref, sem.at[0]),
+        pltpu.make_async_copy(rope_hbm, rope_ref, sem.at[1]),
+    )
+    for copy in copies:
+        copy.start()
     rows, latent = latent_ref.shape
     rope = rope_ref.shape[0]
     side = lax.axis_index("head")
+    out_ref[:, latent:] = jnp.zeros((own, out_ref.shape[1] - latent), BF16)
+    for copy in copies:
+        copy.wait()
     turned = rope_ref[...].astype(F32).T.astype(BF16)
-    out_ref[:, latent:] = jnp.zeros((own, out_ref.shape[1] - latent), BF16)
     for at in range(2):
         span = slice(0, own) if at == 0 else slice(rows - own, rows)
 
@@ -87,15 +121,18 @@
 
 
 def pack(latent_cache, rope_keys, own, depth):
+    arrays = (latent_cache, rope_keys.T)
     return pl.pallas_call(
         functools.partial(pack_kernel, own),
-        in_specs=[LOCAL, LOCAL],
+        in_specs=[ANYWHERE] * 2,
         out_specs=LOCAL,
         out_shape=pltpu.VMEM((own, depth), BF16),
+        scratch_shapes=[pltpu.VMEM(x.shape, x.dtype) for x in arrays]
+        + [pltpu.SemaphoreType.DMA((2,))],
         compiler_params=params(2),
         cost_estimate=cost(0, 1024),
         name="pack",
-    )(latent_cache, rope_keys.T)
+    )(*(pltpu.with_memory_space_constraint(x, pltpu.HBM) for x in arrays))
 
 
 def mask_kernel(own, owners, span_ref, valid_ref, bias_ref):
@@ -263,53 +300,74 @@
             pltpu.VMEM((2, 2 * tokens, keys), BF16),
         ],
         compiler_params=params(12),
-        cost_estimate=cost(heads << 30, 1024),
+        cost_estimate=cost(0, 1024),
         name=f"attend{start}",
     )(held(queries), held(bias), held(w_value), held(kv), *after)
 
 
-def project_kernel(start, groups, fresh, w_ref, *refs):
-    pairs = refs[:groups]
+def gather_into(rows_of, parts, side):
+    tokens = parts[0][0].shape[-2]
+    for at, part in enumerate(parts):
+        rows = pl.ds(at * tokens, tokens)
+        if len(part) == 1:
+            rows_of[rows] = part[0][side]
+        elif isinstance(side, int):
+            rows_of[rows] = part[side][...]
+        else:
+            for which in range(2):
+
+                @pl.when(side == which)
+                def _(rows=rows, part=part, which=which):
+                    rows_of[rows] = part[which][...]
+
+
+def grouped(refs, sizes):
+    refs = iter(refs)
+    return [tuple(next(refs) for _ in range(size)) for size in sizes]
+
+
+def project_kernel(start, sizes, fresh, w_ref, *refs):
     out_ref, gathered = refs[-2:]
-    tokens, depth = pairs[0].shape[1:]
+    parts = grouped(refs, sizes)
+    tokens, depth = parts[0][0].shape[-2:]
     for side in range(2):
-        for at in range(groups):
-            gathered[side, at * tokens : (at + 1) * tokens] = pairs[at][side]
+        gather_into(gathered.at[side], parts, side)
     weights = w_ref[start : start + depth]
     each = 2 * tokens
     for side in range(2):
-        for row in range(0, groups * tokens, each):
+        for row in range(0, len(parts) * tokens, each):
             rows = slice(row, row + each)
             product = jnp.dot(gathered[side, rows], weights, preferred_element_type=F32)
-            out_ref[side, rows] = product if fresh else refs[groups][side, rows] + product
-
-
-def project(start, pairs, w_output, acc):
-    groups = len(pairs)
-    _, tokens, depth = pairs[0].shape
+            out_ref[side, rows] = product if fresh else refs[sum(sizes)][side, rows] + product
+
+
+def project(start, parts, w_output, acc, after=()):
+    sizes = tuple(map(len, parts))
+    blocks = [block for part in parts for block in part]
+    tokens, depth = blocks[0].shape[-2:]
     columns = w_output.shape[1]
-    return pl.pallas_call(
-        functools.partial(project_kernel, start, groups, acc is None),
-        in_specs=[LOCAL] * (1 + groups + (acc is not None)),
-        out_specs=LOCAL,
-        out_shape=pltpu.VMEM((2, groups * tokens, columns), F32),
-        scratch_shapes=[pltpu.VMEM((2, groups * tokens, depth), BF16)],
-        input_output_aliases={} if acc is None else {1 + groups: 0},
+    operands = [w_output, *blocks] + ([] if acc is None else [acc])
+    return pl.pallas_call(
+        functools.partial(project_kernel, start, sizes, acc is None),
+        in_specs=[LOCAL] * len(operands) + [ANYWHERE] * len(after),
+        out_specs=LOCAL,
+        out_shape=pltpu.VMEM((2, len(parts) * tokens, columns), F32),
+        scratch_shapes=[pltpu.VMEM((2, len(parts) * tokens, depth), BF16)],
+        input_output_aliases={} if acc is None else {len(operands) - 1: 0},
         compiler_params=params(12),
         cost_estimate=cost(0, 1024),
         name=f"project{start}",
-    )(held(w_output), *map(held, pairs), *([] if acc is None else [held(acc)]))
-
-
-def finish_kernel(start, keys, far, keep, w_ref, *refs):
+    )(*map(held, operands), *after)
+
+
+def finish_kernel(start, keys, far, keep, sizes, w_ref, *refs):
     groups = len(keys)
-    pairs = refs[:groups]
-    acc_ref, out_ref, gathered = refs[groups:]
-    tokens, depth = pairs[0].shape[1:]
+    acc_ref, out_ref, gathered = refs[-3:]
+    parts = grouped(refs, sizes)
+    tokens, depth = parts[0][0].shape[-2:]
     me, side = lax.axis_index("ctx"), lax.axis_index("head")
     other = ((me // groups) ^ side ^ (1 - keep)).astype(jnp.int32)
-    for at in range(groups):
-        gathered[at * tokens : (at + 1) * tokens] = pairs[at][other]
+    gather_into(gathered, parts, other)
     product = jnp.dot(
         gathered[...], w_ref[start : start + depth], preferred_element_type=F32
     )
@@ -320,21 +378,73 @@
         out_ref[to, :] = (acc_ref[other, rows] + product[rows]).astype(out_ref.dtype)
 
 
-def finish(start, keys, far, keep, pairs, w_output, acc, dtype):
-    groups = len(pairs)
-    _, tokens, depth = pairs[0].shape
+def finish(start, keys, far, keep, parts, w_output, acc, dtype):
+    sizes = tuple(map(len, parts))
+    blocks = [block for part in parts for block in part]
+    tokens, depth = blocks[0].shape[-2:]
     columns = w_output.shape[1]
-    rows = groups * tokens
-    return pl.pallas_call(
-        functools.partial(finish_kernel, start, keys, far, keep),
-        in_specs=[LOCAL] * (2 + groups),
+    rows = len(parts) * tokens
+    return pl.pallas_call(
+        functools.partial(finish_kernel, start, keys, far, keep, sizes),
+        in_specs=[LOCAL] * (2 + len(blocks)),
         out_specs=LOCAL,
         out_shape=pltpu.VMEM((rows, columns), dtype),
         scratch_shapes=[pltpu.VMEM((rows, depth), BF16)],
         compiler_params=params(12),
         cost_estimate=cost(0, 1024),
         name=f"finish{keep}",
-    )(held(w_output), *map(held, pairs), held(acc))
+    )(*map(held, [w_output, *blocks, acc]))
+
+
+def overlap(heads, starts, queries, bias, w_value, kv, w_output, scale):
+    value = w_value.shape[2]
+    got, ready = {}, {}
+    last, acc = [], None
+    held_back = {entry[:2] for entry in ORDER}
+
+    def send(name, chunk, after=None):
+        nonlocal last
+        x, mask = ready.pop((name, chunk))
+        if after is not None:
+            x = gate(x, after)
+            last = [x]
+        got[name, chunk] = exchange(x, mask, 8)
+        if name == FAR:
+            offer(CROSS, chunk, got[FAR, chunk], 1)
+        if name == NEAR and not PLAN[chunk][1]:
+            offer(BOTH, chunk, got[NEAR, chunk], 1)
+
+    def offer(name, chunk, x, mask):
+        ready[name, chunk] = x, mask
+        if (name, chunk) not in held_back:
+            send(name, chunk)
+
+    def parts_of(chunk):
+        apart = [(OWN, FAR), (SIDE, CROSS)], [(NEAR,), (BOTH,)]
+        return [tuple(got[name, chunk] for name in names) for half in apart for names in half]
+
+    for action, chunk, *waits in ORDER:
+        after = last + [got[wait] for wait in waits]
+        if action == ATTEND:
+            out = attend(starts[chunk], heads[chunk], queries, bias, w_value, kv, scale, after)
+            last = [out]
+            got[OWN, chunk] = out
+            offer(FAR, chunk, out, 6)
+            offer(SIDE, chunk, out, 1)
+        elif action == STACK:
+            base = stack(got[OWN, chunk], got[FAR, chunk], after)
+            last = [base]
+            offer(NEAR, chunk, base, 2)
+        elif action == PROJECT:
+            acc = project(starts[chunk] * value, parts_of(chunk), w_output, acc, after)
+            last = [acc]
+        elif action == BOTH and PLAN[chunk][1]:
+            pair = stack(got[SIDE, chunk], got[CROSS, chunk], after)
+            last = [pair]
+            got[BOTH, chunk] = exchange(pair, 2, 8)
+        else:
+            send(action, chunk, after)
+    return parts_of(len(heads) - 1), acc
 
 
 def local(
@@ -360,28 +470,23 @@
     bias = mask(span_offset, valid_lengths, owners, tokens, per_shard, own)
     kv = join([mine[key] for key in keys], [theirs[key] for key in keys], per_shard)
 
-    acc = None
-    start = 0
-    sent = []
-    for chunk, piece in enumerate(PIECES):
-        heads = piece * head_count // sum(PIECES)
-        after = [sent[-2][0]] if chunk > 1 else []
-        if chunk > 2:
-            after += [sent[-3][key] for key in basis_of(shards)[1:]]
-        if chunk > 3:
-            after += [sent[-4][key] for key in keys]
-        out = attend(start, heads, queries, bias, w_value, kv, scale, after)
-        gathered = spread(out, shards)
-        pairs = [gathered[key] for key in keys]
-        sent.append(gathered)
-        row = start * value
-        if chunk < len(PIECES) - 1:
-            acc = project(row, pairs, w_output, acc)
-        start += heads
-
-    given = finish(row, keys, far, 0, pairs, w_output, acc, BF16)
+    heads = [count * head_count // 32 for count, _ in PLAN]
+    starts = [sum(heads[:chunk]) for chunk in range(len(heads))]
+    if shards == 8:
+        parts, acc = overlap(heads, starts, queries, bias, w_value, kv, w_output, scale)
+    else:
+        acc = None
+        for chunk, start in enumerate(starts):
+            out = attend(start, heads[chunk], queries, bias, w_value, kv, scale)
+            gathered = spread(out, shards)
+            parts = [(gathered[key],) for key in keys]
+            if chunk < len(heads) - 1:
+                acc = project(start * value, parts, w_output, acc)
+    row = starts[-1] * value
+
+    given = finish(row, keys, far, 0, parts, w_output, acc, BF16)
     other = sibling(given)
-    kept = finish(row, keys, far, 1, pairs, w_output, acc, F32)
+    kept = finish(row, keys, far, 1, parts, w_output, acc, F32)
     return (kept + other.astype(F32)).astype(BF16)
 
 

time: 146 us -> 130 us (0.89)
  waiting for transfers between devices: 69.8 us -> 51.5 us
  starting transfers between devices: 37.1 us -> 39.2 us
  local copies, waits for them, and re-layouts: 1.69 us -> 0.02 us
  Pallas kernels: 35.3 us -> 36.8 us
    ppermute x24 -> x29, waiting for transfers between devices: 68 us -> 50 us  [exchange(): return lax.ppermute(x, 'ctx', [(i, i ^ mask) for i in range(shards)])]
    ppermute x24 -> x29, starting transfers between devices: 36.5 us -> 38.6 us  [exchange(): return lax.ppermute(x, 'ctx', [(i, i ^ mask) for i in range(shards)])]
    unnamed x12 -> x8, local copies, waits for them, and re-layouts: 1.69 us -> 0.02 us
    pallas_call x7 -> x19, Pallas kernels: 11.2 us -> 12.7 us  [the longest x4 9.35 us: project(): pl.pallas_call(functools.partial(project_kernel, start, sizes, acc is Non...]
  transfers between devices with their start and end apart: 29 -> 34, of which waited for: 13 -> 18; matrix products, arithmetic and copies ran while one was open for 0% -> 0% of each run, Pallas kernels for 22% -> 25%
where the time goes in v5:
time: 130 us
  waiting for transfers between devices  51.5 us (40%)
  starting transfers between devices  39.2 us (30%)
  Pallas kernels  36.8 us (28%)
    ppermute x29, waiting for transfers between devices, exchange(): return lax.ppermute(x, 'ctx', [(i, i ^ mask) for i in range(shards)])  50 us
    ppermute x29, starting transfers between devices, exchange(): return lax.ppermute(x, 'ctx', [(i, i ^ mask) for i in range(shards)])  38.6 us
    pallas_call x5, Pallas kernels, attend(): pl.pallas_call(functools.partial(attend_kernel, scale * math.log2(math.e)...  19 us
    pallas_call x4, Pallas kernels, project(): pl.pallas_call(functools.partial(project_kernel, start, sizes, acc is Non...  9.35 us
    pallas_call x1, Pallas kernels, prep(): pl.pallas_call(prep_kernel, in_specs=[ANYWHERE] * 3, out_specs=LOCAL, out...  3.98 us
  transfers between devices with their start and end apart: 34, of which 18 were waited for; matrix products, arithmetic and copies ran while one was open for 0% of the time, Pallas kernels for 25%

profile of v5, /device:TPU:0, one launch (start us, length us, event | category | flops | bytes accessed | tf_op | source)
XLA Modules:
  0.0 129.6 jit_solution(4287554622192185782)
XLA Ops:
  1.0 5.1 %collective-permute-start = (bf16[80,640]{1,0:T(8,128)(2,1)S(1)}, bf16[80,640]{1,0:T(8,128)(2,1)S(1)}, u32[]{:S(2)}, u32[]{:S(2)}) collective-permute-start(bf16[80,640]{1,0:T(8,128)(2,1)S(1)} %pack.1.first_ref), channel_id=1, source_target_pairs={{0,12},{2,14},{4,8},{6,10},{8,4},{10,6},{12,0},{14,2},{1,13},{3,15... | collective-permute-start | bytes 307208 | tf_op jit(solution)/shard_map/ppermute | solution.py:51
  6.2 4.0 %prep.1.refs_0_.q_ref = bf16[4096,640]{1,0:T(8,128)(2,1)S(1)} custom-call(bf16[128,4096]{1,0:T(8,128)(2,1)} %q_hbm.1, bf16[128,2048]{1,0:T(8,128)(2,1)} %r_hbm.1, bf16[32,128,512]{2,1,0:T(8,128)(2,1)} %w_hbm.1), custom_call_target="tpu_custom_call" | custom-call | bytes 1024 | tf_op jit(solution)/shard_map/prep/pallas_call | solution.py:204
  11.0 1.5 %collective-permute-start.1 = (bf16[2,80,640]{2,1,0:T(8,128)(2,1)S(1)}, bf16[2,80,640]{2,1,0:T(8,128)(2,1)S(1)}, u32[]{:S(2)}, u32[]{:S(2)}) collective-permute-start(bf16[2,80,640]{2,1,0:T(8,128)(2,1)S(1)} %stack.7.refs_0_), channel_id=1, source_target_pairs={{0,2},{2,0},{4,6},{6,4},{8,10},{10,8},{12,14},{14,12},{1,3},{3,1},... | collective-permute-start | bytes 614408 | tf_op jit(solution)/shard_map/ppermute | solution.py:51
  12.6 4.3 %collective-permute-done.2.refs_2_ = bf16[2,80,640]{2,1,0:T(8,128)(2,1)S(1)} collective-permute-done((bf16[2,80,640]{2,1,0:T(8,128)(2,1)S(1)}, bf16[2,80,640]{2,1,0:T(8,128)(2,1)S(1)}, u32[]{:S(2)}, u32[]{:S(2)}) %collective-permute-start.2) | collective-permute-done | bytes 204832 | tf_op jit(solution)/shard_map/ppermute | solution.py:51
  16.8 1.5 %collective-permute-start.3 = (bf16[2,80,640]{2,1,0:T(8,128)(2,1)S(1)}, bf16[2,80,640]{2,1,0:T(8,128)(2,1)S(1)}, u32[]{:S(2)}, u32[]{:S(2)}) collective-permute-start(bf16[2,80,640]{2,1,0:T(8,128)(2,1)S(1)} %collective-permute-done.2.refs_2_), channel_id=1, source_target_pairs={{0,2},{2,0},{4,6},{6,4},{8,10},{10,8},{12,14},{14,12},{1,3},{3,1},... | collective-permute-start | bytes 614408 | tf_op jit(solution)/shard_map/ppermute | solution.py:51
  18.9 3.7 %collective-permute-done.3.refs_3_ = bf16[2,80,640]{2,1,0:T(8,128)(2,1)S(1)} collective-permute-done((bf16[2,80,640]{2,1,0:T(8,128)(2,1)S(1)}, bf16[2,80,640]{2,1,0:T(8,128)(2,1)S(1)}, u32[]{:S(2)}, u32[]{:S(2)}) %collective-permute-start.3) | collective-permute-done | bytes 204832 | tf_op jit(solution)/shard_map/ppermute | solution.py:51
  24.3 2.4 %attend0.1.refs_0_.first_ref = bf16[128,512]{1,0:T(8,128)(2,1)S(1)} custom-call(bf16[4096,640]{1,0:T(8,128)(2,1)S(1)} %prep.1.refs_0_.q_ref, f32[128,1152]{1,0:T(8,128)S(1)} %mask.1.bias_ref, bf16[32,512,128]{2,1,0:T(8,128)(2,1)S(1)} %copy-done, bf16[1152,640]{1,0:T(8,128)(2,1)S(1)} %join.1.kv_ref), custom_call_target="tpu_custom_call" | custom-call | bytes 1024 | tf_op jit(solution)/shard_map/attend0/pallas_call | solution.py:293
  26.7 1.8 %collective-permute-start.8 = (bf16[128,512]{1,0:T(8,128)(2,1)S(1)}, bf16[128,512]{1,0:T(8,128)(2,1)S(1)}, u32[]{:S(2)}, u32[]{:S(2)}) collective-permute-start(bf16[128,512]{1,0:T(8,128)(2,1)S(1)} %attend0.1.refs_0_.first_ref), channel_id=1, source_target_pairs={{0,12},{2,14},{4,8},{6,10},{8,4},{10,6},{12,0},{14,2},{1,13},{3,15... | collective-permute-start | bytes 393224 | tf_op jit(solution)/shard_map/ppermute | solution.py:51
  28.5 4.7 %attend4.1.refs_0_.x_ref.first_ref = bf16[128,1024]{1,0:T(8,128)(2,1)S(1)} custom-call(bf16[4096,640]{1,0:T(8,128)(2,1)S(1)} %prep.1.refs_0_.q_ref, f32[128,1152]{1,0:T(8,128)S(1)} %mask.1.bias_ref, bf16[32,512,128]{2,1,0:T(8,128)(2,1)S(1)} %copy-done, bf16[1152,640]{1,0:T(8,128)(2,1)S(1)} %join.1.kv_ref, bf16[128,512]{1,0:T(8,128)(2,1)S(1)} %attend0.1.refs_0_.first_ref), custom_call_target="tpu_custom_call" | custom-call | bytes 1024 | tf_op jit(solution)/shard_map/attend4/pallas_call | solution.py:293
  33.2 1.6 %collective-permute-start.11 = (bf16[128,1024]{1,0:T(8,128)(2,1)S(1)}, bf16[128,1024]{1,0:T(8,128)(2,1)S(1)}, u32[]{:S(2)}, u32[]{:S(2)}) collective-permute-start(bf16[128,1024]{1,0:T(8,128)(2,1)S(1)} %attend4.1.refs_0_.x_ref.first_ref), channel_id=1, source_target_pairs={{0,2},{2,0},{4,6},{6,4},{8,10},{10,8},{12,14},{14,12},{1,3},{3,1},... | collective-permute-start | bytes 786440 | tf_op jit(solution)/shard_map/ppermute | solution.py:51
  35.9 2.2 %collective-permute-start.9 = (bf16[128,1024]{1,0:T(8,128)(2,1)S(1)}, bf16[128,1024]{1,0:T(8,128)(2,1)S(1)}, u32[]{:S(2)}, u32[]{:S(2)}) collective-permute-start(bf16[128,1024]{1,0:T(8,128)(2,1)S(1)} %gate.12.refs_0_), channel_id=1, source_target_pairs={{0,12},{2,14},{4,8},{6,10},{8,4},{10,6},{12,0},{14,2},{1,13},{3,15... | collective-permute-start | bytes 786440 | tf_op jit(solution)/shard_map/ppermute | solution.py:51
  38.1 3.5 %attend12.1.refs_0_.x_ref.first_ref = bf16[128,768]{1,0:T(8,128)(2,1)S(1)} custom-call(bf16[4096,640]{1,0:T(8,128)(2,1)S(1)} %prep.1.refs_0_.q_ref, f32[128,1152]{1,0:T(8,128)S(1)} %mask.1.bias_ref, bf16[32,512,128]{2,1,0:T(8,128)(2,1)S(1)} %copy-done, bf16[1152,640]{1,0:T(8,128)(2,1)S(1)} %join.1.kv_ref, bf16[128,1024]{1,0:T(8,128)(2,1)S(1)} %gate.12.refs_0_), custom_call_target="tpu_custom_call" | custom-call | bytes 1024 | tf_op jit(solution)/shard_map/attend12/pallas_call | solution.py:293
  41.6 1.6 %collective-permute-start.12 = (bf16[128,768]{1,0:T(8,128)(2,1)S(1)}, bf16[128,768]{1,0:T(8,128)(2,1)S(1)}, u32[]{:S(2)}, u32[]{:S(2)}) collective-permute-start(bf16[128,768]{1,0:T(8,128)(2,1)S(1)} %attend12.1.refs_0_.x_ref.first_ref), channel_id=1, source_target_pairs={{0,2},{2,0},{4,6},{6,4},{8,10},{10,8},{12,14},{14,12},{1,3},{3,1},... | collective-permute-start | bytes 589832 | tf_op jit(solution)/shard_map/ppermute | solution.py:51
  43.2 4.3 %collective-permute-done.12.refs_2_ = bf16[128,768]{1,0:T(8,128)(2,1)S(1)} collective-permute-done((bf16[128,768]{1,0:T(8,128)(2,1)S(1)}, bf16[128,768]{1,0:T(8,128)(2,1)S(1)}, u32[]{:S(2)}, u32[]{:S(2)}) %collective-permute-start.12) | collective-permute-done | bytes 196640 | tf_op jit(solution)/shard_map/ppermute | solution.py:51
  47.5 1.6 %collective-permute-start.13 = (bf16[128,512]{1,0:T(8,128)(2,1)S(1)}, bf16[128,512]{1,0:T(8,128)(2,1)S(1)}, u32[]{:S(2)}, u32[]{:S(2)}) collective-permute-start(bf16[128,512]{1,0:T(8,128)(2,1)S(1)} %gate.14.refs_0_), channel_id=1, source_target_pairs={{0,2},{2,0},{4,6},{6,4},{8,10},{10,8},{12,14},{14,12},{1,3},{3,1},... | collective-permute-start | bytes 393224 | tf_op jit(solution)/shard_map/ppermute | solution.py:51
  51.0 2.9 %collective-permute-done.13.refs_1_.refs_3_ = bf16[128,512]{1,0:T(8,128)(2,1)S(1)} collective-permute-done((bf16[128,512]{1,0:T(8,128)(2,1)S(1)}, bf16[128,512]{1,0:T(8,128)(2,1)S(1)}, u32[]{:S(2)}, u32[]{:S(2)}) %collective-permute-start.13) | collective-permute-done | bytes 131104 | tf_op jit(solution)/shard_map/ppermute | solution.py:51
  53.9 4.9 %attend18.1.refs_0_.x_ref.first_ref = bf16[128,1024]{1,0:T(8,128)(2,1)S(1)} custom-call(bf16[4096,640]{1,0:T(8,128)(2,1)S(1)} %prep.1.refs_0_.q_ref, f32[128,1152]{1,0:T(8,128)S(1)} %mask.1.bias_ref, bf16[32,512,128]{2,1,0:T(8,128)(2,1)S(1)} %copy-done, bf16[1152,640]{1,0:T(8,128)(2,1)S(1)} %join.1.kv_ref, bf16[2,128,1024]{2,1,0:T(8,128)(2,1)S(1)} %stack.9.refs_0_, ...), custom_call_target="tpu_custom_call" | custom-call | bytes 1024 | tf_op jit(solution)/shard_map/attend18/pallas_call | solution.py:293
  60.3 1.7 %collective-permute-start.14 = (bf16[128,768]{1,0:T(8,128)(2,1)S(1)}, bf16[128,768]{1,0:T(8,128)(2,1)S(1)}, u32[]{:S(2)}, u32[]{:S(2)}) collective-permute-start(bf16[128,768]{1,0:T(8,128)(2,1)S(1)} %gate.15.refs_0_), channel_id=1, source_target_pairs={{0,12},{2,14},{4,8},{6,10},{8,4},{10,6},{12,0},{14,2},{1,13},{3,15... | collective-permute-start | bytes 589832 | tf_op jit(solution)/shard_map/ppermute | solution.py:51
  62.6 3.5 %attend26.1.refs_0_.x_ref.first_ref = bf16[128,768]{1,0:T(8,128)(2,1)S(1)} custom-call(bf16[4096,640]{1,0:T(8,128)(2,1)S(1)} %prep.1.refs_0_.q_ref, f32[128,1152]{1,0:T(8,128)S(1)} %mask.1.bias_ref, bf16[32,512,128]{2,1,0:T(8,128)(2,1)S(1)} %copy-done, bf16[1152,640]{1,0:T(8,128)(2,1)S(1)} %join.1.kv_ref, bf16[128,1024]{1,0:T(8,128)(2,1)S(1)} %attend18.1.refs_0_.x_ref.first_ref), custom_call_target="tpu_custom_call" | custom-call | bytes 1024 | tf_op jit(solution)/shard_map/attend26/pallas_call | solution.py:293
  66.2 1.5 %collective-permute-start.19 = (bf16[128,1024]{1,0:T(8,128)(2,1)S(1)}, bf16[128,1024]{1,0:T(8,128)(2,1)S(1)}, u32[]{:S(2)}, u32[]{:S(2)}) collective-permute-start(bf16[128,1024]{1,0:T(8,128)(2,1)S(1)} %gate.16.refs_6_), channel_id=1, source_target_pairs={{0,2},{2,0},{4,6},{6,4},{8,10},{10,8},{12,14},{14,12},{1,3},{3,1},... | collective-permute-start | bytes 786440 | tf_op jit(solution)/shard_map/ppermute | solution.py:51
  67.7 1.8 %collective-permute-done.15.refs_2_ = bf16[128,512]{1,0:T(8,128)(2,1)S(1)} collective-permute-done((bf16[128,512]{1,0:T(8,128)(2,1)S(1)}, bf16[128,512]{1,0:T(8,128)(2,1)S(1)}, u32[]{:S(2)}, u32[]{:S(2)}) %collective-permute-start.15) | collective-permute-done | bytes 131104 | tf_op jit(solution)/shard_map/ppermute | solution.py:51
  75.3 5.2 %collective-permute-done.20.refs_1_.x_ref.refs_4_ = bf16[2,128,768]{2,1,0:T(8,128)(2,1)S(1)} collective-permute-done((bf16[2,128,768]{2,1,0:T(8,128)(2,1)S(1)}, bf16[2,128,768]{2,1,0:T(8,128)(2,1)S(1)}, u32[]{:S(2)}, u32[]{:S(2)}) %collective-permute-start.20) | collective-permute-done | bytes 393248 | tf_op jit(solution)/shard_map/ppermute | solution.py:51
  81.2 4.5 %collective-permute-done.24.second_ref.x_ref.refs_1_ = bf16[128,1024]{1,0:T(8,128)(2,1)S(1)} collective-permute-done((bf16[128,1024]{1,0:T(8,128)(2,1)S(1)}, bf16[128,1024]{1,0:T(8,128)(2,1)S(1)}, u32[]{:S(2)}, u32[]{:S(2)}) %collective-permute-start.24) | collective-permute-done | bytes 262176 | tf_op jit(solution)/shard_map/ppermute | solution.py:51
  86.5 3.1 %collective-permute-start.21 = (bf16[128,768]{1,0:T(8,128)(2,1)S(1)}, bf16[128,768]{1,0:T(8,128)(2,1)S(1)}, u32[]{:S(2)}, u32[]{:S(2)}) collective-permute-start(bf16[128,768]{1,0:T(8,128)(2,1)S(1)} %gate.19.refs_0_), channel_id=1, source_target_pairs={{0,12},{2,14},{4,8},{6,10},{8,4},{10,6},{12,0},{14,2},{1,13},{3,15... | collective-permute-start | bytes 589832 | tf_op jit(solution)/shard_map/ppermute | solution.py:51
  89.6 2.7 %collective-permute-done.23.refs_1_.refs_5_ = bf16[2,128,1024]{2,1,0:T(8,128)(2,1)S(1)} collective-permute-done((bf16[2,128,1024]{2,1,0:T(8,128)(2,1)S(1)}, bf16[2,128,1024]{2,1,0:T(8,128)(2,1)S(1)}, u32[]{:S(2)}, u32[]{:S(2)}) %collective-permute-start.23) | collective-permute-done | bytes 524320 | tf_op jit(solution)/shard_map/ppermute | solution.py:51
  92.4 2.8 %project512.1.refs_0_.refs_6_ = f32[2,512,896]{2,1,0:T(8,128)S(1)} custom-call(bf16[4096,896]{1,0:T(8,128)(2,1)S(1)} %bitcast.2, bf16[128,1024]{1,0:T(8,128)(2,1)S(1)} %attend4.1.refs_0_.x_ref.first_ref, bf16[128,1024]{1,0:T(8,128)(2,1)S(1)} %collective-permute-done.9.second_ref.x_ref.refs_1_, ...), custom_call_target="tpu_custom_call", output_to_operand_aliasing={{}: (7, {})} | custom-call | bytes 1024 | tf_op jit(solution)/shard_map/project512/pallas_call | solution.py:350
  95.2 2.2 %collective-permute-done.21.second_ref.x_ref.refs_1_ = bf16[128,768]{1,0:T(8,128)(2,1)S(1)} collective-permute-done((bf16[128,768]{1,0:T(8,128)(2,1)S(1)}, bf16[128,768]{1,0:T(8,128)(2,1)S(1)}, u32[]{:S(2)}, u32[]{:S(2)}) %collective-permute-start.21) | collective-permute-done | bytes 196640 | tf_op jit(solution)/shard_map/ppermute | solution.py:51
  98.9 1.9 %collective-permute-done.29.refs_5_ = bf16[2,128,768]{2,1,0:T(8,128)(2,1)S(1)} collective-permute-done((bf16[2,128,768]{2,1,0:T(8,128)(2,1)S(1)}, bf16[2,128,768]{2,1,0:T(8,128)(2,1)S(1)}, u32[]{:S(2)}, u32[]{:S(2)}) %collective-permute-start.29) | collective-permute-done | bytes 393248 | tf_op jit(solution)/shard_map/ppermute | solution.py:51
  100.8 2.2 %project1536.1.refs_0_.refs_6_ = f32[2,512,896]{2,1,0:T(8,128)S(1)} custom-call(bf16[4096,896]{1,0:T(8,128)(2,1)S(1)} %bitcast.2, bf16[128,768]{1,0:T(8,128)(2,1)S(1)} %attend12.1.refs_0_.x_ref.first_ref, bf16[128,768]{1,0:T(8,128)(2,1)S(1)} %collective-permute-done.14.second_ref.x_ref.refs_1_, ...), custom_call_target="tpu_custom_call", output_to_operand_aliasing={{}: (7, {})} | custom-call | bytes 1024 | tf_op jit(solution)/shard_map/project1536/pallas_call | solution.py:350
  105.0 4.2 %collective-permute-done.26.second_ref.refs_3_ = bf16[128,768]{1,0:T(8,128)(2,1)S(1)} collective-permute-done((bf16[128,768]{1,0:T(8,128)(2,1)S(1)}, bf16[128,768]{1,0:T(8,128)(2,1)S(1)}, u32[]{:S(2)}, u32[]{:S(2)}) %collective-permute-start.26) | collective-permute-done | bytes 196640 | tf_op jit(solution)/shard_map/ppermute | solution.py:51
  111.1 10.7 %collective-permute-done.31.refs_3_ = bf16[128,1024]{1,0:T(8,128)(2,1)S(1)} collective-permute-done((bf16[128,1024]{1,0:T(8,128)(2,1)S(1)}, bf16[128,1024]{1,0:T(8,128)(2,1)S(1)}, u32[]{:S(2)}, u32[]{:S(2)}) %collective-permute-start.31) | collective-permute-done | bytes 262176 | tf_op jit(solution)/shard_map/ppermute | solution.py:51
  121.8 3.1 %project2304.1.refs_6_ = f32[2,512,896]{2,1,0:T(8,128)S(1)} custom-call(bf16[4096,896]{1,0:T(8,128)(2,1)S(1)} %bitcast.2, bf16[128,1024]{1,0:T(8,128)(2,1)S(1)} %attend18.1.refs_0_.x_ref.first_ref, bf16[128,1024]{1,0:T(8,128)(2,1)S(1)} %collective-permute-done.24.second_ref.x_ref.refs_1_, ...), custom_call_target="tpu_custom_call", output_to_operand_aliasing={{}: (7, {})} | custom-call | bytes 1024 | tf_op jit(solution)/shard_map/project2304/pallas_call | solution.py:350
  (80 shorter events, 26.0 us)
Async XLA Ops:
  1.0 9.1 %collective-permute-start = (bf16[80,640]{1,0:T(8,128)(2,1)S(1)}, bf16[80,640]{1,0:T(8,128)(2,1)S(1)}, u32[]{:S(2)}, u32[]{:S(2)}) collective-permute-start(bf16[80,640]{1,0:T(8,128)(2,1)S(1)} %pack.1.first_ref), channel_id=1, source_target_pairs={{0,12},{2,14},{4,8},{6,10},{8,4},{10,6},{12,0},{14,2},{1,13},{3,15... | collective-permute-start | bytes 307208 | tf_op jit(solution)/shard_map/ppermute | solution.py:51
  10.2 6.6 %collective-permute-start.2 = (bf16[2,80,640]{2,1,0:T(8,128)(2,1)S(1)}, bf16[2,80,640]{2,1,0:T(8,128)(2,1)S(1)}, u32[]{:S(2)}, u32[]{:S(2)}) collective-permute-start(bf16[2,80,640]{2,1,0:T(8,128)(2,1)S(1)} %stack.7.refs_0_), channel_id=1, source_target_pairs={{0,4},{2,6},{4,0},{6,2},{8,12},{10,14},{12,8},{14,10},{1,5},{3,7},... | collective-permute-start | bytes 614408 | tf_op jit(solution)/shard_map/ppermute | solution.py:51
  11.0 7.8 %collective-permute-start.1 = (bf16[2,80,640]{2,1,0:T(8,128)(2,1)S(1)}, bf16[2,80,640]{2,1,0:T(8,128)(2,1)S(1)}, u32[]{:S(2)}, u32[]{:S(2)}) collective-permute-start(bf16[2,80,640]{2,1,0:T(8,128)(2,1)S(1)} %stack.7.refs_0_), channel_id=1, source_target_pairs={{0,2},{2,0},{4,6},{6,4},{8,10},{10,8},{12,14},{14,12},{1,3},{3,1},... | collective-permute-start | bytes 614408 | tf_op jit(solution)/shard_map/ppermute | solution.py:51
  16.8 5.8 %collective-permute-start.3 = (bf16[2,80,640]{2,1,0:T(8,128)(2,1)S(1)}, bf16[2,80,640]{2,1,0:T(8,128)(2,1)S(1)}, u32[]{:S(2)}, u32[]{:S(2)}) collective-permute-start(bf16[2,80,640]{2,1,0:T(8,128)(2,1)S(1)} %collective-permute-done.2.refs_2_), channel_id=1, source_target_pairs={{0,2},{2,0},{4,6},{6,4},{8,10},{10,8},{12,14},{14,12},{1,3},{3,1},... | collective-permute-start | bytes 614408 | tf_op jit(solution)/shard_map/ppermute | solution.py:51
  18.3 5.5 %collective-permute-start.4 = (bf16[2,80,640]{2,1,0:T(8,128)(2,1)S(1)}, bf16[2,80,640]{2,1,0:T(8,128)(2,1)S(1)}, u32[]{:S(2)}, u32[]{:S(2)}) collective-permute-start(bf16[2,80,640]{2,1,0:T(8,128)(2,1)S(1)} %stack.7.refs_0_), channel_id=1, source_target_pairs={{0,1},{1,0},{2,3},{3,2},{4,5},{5,4},{6,7},{7,6},{8,9},{9,8},{10,11... | collective-permute-start | bytes 614408 | tf_op jit(solution)/shard_map/ppermute | solution.py:55
  18.3 5.5 %collective-permute-start.6 = (bf16[2,80,640]{2,1,0:T(8,128)(2,1)S(1)}, bf16[2,80,640]{2,1,0:T(8,128)(2,1)S(1)}, u32[]{:S(2)}, u32[]{:S(2)}) collective-permute-start(bf16[2,80,640]{2,1,0:T(8,128)(2,1)S(1)} %collective-permute-done.2.refs_2_), channel_id=1, source_target_pairs={{0,1},{1,0},{2,3},{3,2},{4,5},{5,4},{6,7},{7,6},{8,9},{9,8},{10,11... | collective-permute-start | bytes 614408 | tf_op jit(solution)/shard_map/ppermute | solution.py:55
  18.9 5.0 %collective-permute-start.5 = (bf16[2,80,640]{2,1,0:T(8,128)(2,1)S(1)}, bf16[2,80,640]{2,1,0:T(8,128)(2,1)S(1)}, u32[]{:S(2)}, u32[]{:S(2)}) collective-permute-start(bf16[2,80,640]{2,1,0:T(8,128)(2,1)S(1)} %collective-permute-done.1.refs_1_), channel_id=1, source_target_pairs={{0,1},{1,0},{2,3},{3,2},{4,5},{5,4},{6,7},{7,6},{8,9},{9,8},{10,11... | collective-permute-start | bytes 614408 | tf_op jit(solution)/shard_map/ppermute | solution.py:55
  26.7 8.1 %collective-permute-start.8 = (bf16[128,512]{1,0:T(8,128)(2,1)S(1)}, bf16[128,512]{1,0:T(8,128)(2,1)S(1)}, u32[]{:S(2)}, u32[]{:S(2)}) collective-permute-start(bf16[128,512]{1,0:T(8,128)(2,1)S(1)} %attend0.1.refs_0_.first_ref), channel_id=1, source_target_pairs={{0,12},{2,14},{4,8},{6,10},{8,4},{10,6},{12,0},{14,2},{1,13},{3,15... | collective-permute-start | bytes 393224 | tf_op jit(solution)/shard_map/ppermute | solution.py:51
  33.2 9.9 %collective-permute-start.11 = (bf16[128,1024]{1,0:T(8,128)(2,1)S(1)}, bf16[128,1024]{1,0:T(8,128)(2,1)S(1)}, u32[]{:S(2)}, u32[]{:S(2)}) collective-permute-start(bf16[128,1024]{1,0:T(8,128)(2,1)S(1)} %attend4.1.refs_0_.x_ref.first_ref), channel_id=1, source_target_pairs={{0,2},{2,0},{4,6},{6,4},{8,10},{10,8},{12,14},{14,12},{1,3},{3,1},... | collective-permute-start | bytes 786440 | tf_op jit(solution)/shard_map/ppermute | solution.py:51
  34.8 12.6 %collective-permute-start.10 = (bf16[2,128,512]{2,1,0:T(8,128)(2,1)S(1)}, bf16[2,128,512]{2,1,0:T(8,128)(2,1)S(1)}, u32[]{:S(2)}, u32[]{:S(2)}) collective-permute-start(bf16[2,128,512]{2,1,0:T(8,128)(2,1)S(1)} %stack.8.refs_0_), channel_id=1, source_target_pairs={{0,4},{2,6},{4,0},{6,2},{8,12},{10,14},{12,8},{14,10},{1,5},{3,7},... | collective-permute-start | bytes 786440 | tf_op jit(solution)/shard_map/ppermute | solution.py:51
  35.9 13.6 %collective-permute-start.9 = (bf16[128,1024]{1,0:T(8,128)(2,1)S(1)}, bf16[128,1024]{1,0:T(8,128)(2,1)S(1)}, u32[]{:S(2)}, u32[]{:S(2)}) collective-permute-start(bf16[128,1024]{1,0:T(8,128)(2,1)S(1)} %gate.12.refs_0_), channel_id=1, source_target_pairs={{0,12},{2,14},{4,8},{6,10},{8,4},{10,6},{12,0},{14,2},{1,13},{3,15... | collective-permute-start | bytes 786440 | tf_op jit(solution)/shard_map/ppermute | solution.py:51
  41.6 5.9 %collective-permute-start.12 = (bf16[128,768]{1,0:T(8,128)(2,1)S(1)}, bf16[128,768]{1,0:T(8,128)(2,1)S(1)}, u32[]{:S(2)}, u32[]{:S(2)}) collective-permute-start(bf16[128,768]{1,0:T(8,128)(2,1)S(1)} %attend12.1.refs_0_.x_ref.first_ref), channel_id=1, source_target_pairs={{0,2},{2,0},{4,6},{6,4},{8,10},{10,8},{12,14},{14,12},{1,3},{3,1},... | collective-permute-start | bytes 589832 | tf_op jit(solution)/shard_map/ppermute | solution.py:51
  47.5 6.4 %collective-permute-start.13 = (bf16[128,512]{1,0:T(8,128)(2,1)S(1)}, bf16[128,512]{1,0:T(8,128)(2,1)S(1)}, u32[]{:S(2)}, u32[]{:S(2)}) collective-permute-start(bf16[128,512]{1,0:T(8,128)(2,1)S(1)} %gate.14.refs_0_), channel_id=1, source_target_pairs={{0,2},{2,0},{4,6},{6,4},{8,10},{10,8},{12,14},{14,12},{1,3},{3,1},... | collective-permute-start | bytes 393224 | tf_op jit(solution)/shard_map/ppermute | solution.py:51
  49.5 21.7 %collective-permute-start.18 = (bf16[2,128,1024]{2,1,0:T(8,128)(2,1)S(1)}, bf16[2,128,1024]{2,1,0:T(8,128)(2,1)S(1)}, u32[]{:S(2)}, u32[]{:S(2)}) collective-permute-start(bf16[2,128,1024]{2,1,0:T(8,128)(2,1)S(1)} %stack.9.refs_0_), channel_id=1, source_target_pairs={{0,4},{2,6},{4,0},{6,2},{8,12},{10,14},{12,8},{14,10},{1,5},{3,7},... | collective-permute-start | bytes 1572872 | tf_op jit(solution)/shard_map/ppermute | solution.py:51
  50.5 15.7 %collective-permute-start.16 = (bf16[2,128,512]{2,1,0:T(8,128)(2,1)S(1)}, bf16[2,128,512]{2,1,0:T(8,128)(2,1)S(1)}, u32[]{:S(2)}, u32[]{:S(2)}) collective-permute-start(bf16[2,128,512]{2,1,0:T(8,128)(2,1)S(1)} %gate.13.refs_0_), channel_id=1, source_target_pairs={{0,2},{2,0},{4,6},{6,4},{8,10},{10,8},{12,14},{14,12},{1,3},{3,1},... | collective-permute-start | bytes 786440 | tf_op jit(solution)/shard_map/ppermute | solution.py:51
  58.8 10.7 %collective-permute-start.17 = (bf16[128,1024]{1,0:T(8,128)(2,1)S(1)}, bf16[128,1024]{1,0:T(8,128)(2,1)S(1)}, u32[]{:S(2)}, u32[]{:S(2)}) collective-permute-start(bf16[128,1024]{1,0:T(8,128)(2,1)S(1)} %attend18.1.refs_0_.x_ref.first_ref), channel_id=1, source_target_pairs={{0,2},{2,0},{4,6},{6,4},{8,10},{10,8},{12,14},{14,12},{1,3},{3,1},... | collective-permute-start | bytes 786440 | tf_op jit(solution)/shard_map/ppermute | solution.py:51
  60.3 10.4 %collective-permute-start.14 = (bf16[128,768]{1,0:T(8,128)(2,1)S(1)}, bf16[128,768]{1,0:T(8,128)(2,1)S(1)}, u32[]{:S(2)}, u32[]{:S(2)}) collective-permute-start(bf16[128,768]{1,0:T(8,128)(2,1)S(1)} %gate.15.refs_0_), channel_id=1, source_target_pairs={{0,12},{2,14},{4,8},{6,10},{8,4},{10,6},{12,0},{14,2},{1,13},{3,15... | collective-permute-start | bytes 589832 | tf_op jit(solution)/shard_map/ppermute | solution.py:51
  62.0 7.4 %collective-permute-start.15 = (bf16[128,512]{1,0:T(8,128)(2,1)S(1)}, bf16[128,512]{1,0:T(8,128)(2,1)S(1)}, u32[]{:S(2)}, u32[]{:S(2)}) collective-permute-start(bf16[128,512]{1,0:T(8,128)(2,1)S(1)} %attend0.1.refs_0_.first_ref), channel_id=1, source_target_pairs={{0,2},{2,0},{4,6},{6,4},{8,10},{10,8},{12,14},{14,12},{1,3},{3,1},... | collective-permute-start | bytes 393224 | tf_op jit(solution)/shard_map/ppermute | solution.py:51
  66.2 7.0 %collective-permute-start.19 = (bf16[128,1024]{1,0:T(8,128)(2,1)S(1)}, bf16[128,1024]{1,0:T(8,128)(2,1)S(1)}, u32[]{:S(2)}, u32[]{:S(2)}) collective-permute-start(bf16[128,1024]{1,0:T(8,128)(2,1)S(1)} %gate.16.refs_6_), channel_id=1, source_target_pairs={{0,2},{2,0},{4,6},{6,4},{8,10},{10,8},{12,14},{14,12},{1,3},{3,1},... | collective-permute-start | bytes 786440 | tf_op jit(solution)/shard_map/ppermute | solution.py:51
  70.8 9.7 %collective-permute-start.20 = (bf16[2,128,768]{2,1,0:T(8,128)(2,1)S(1)}, bf16[2,128,768]{2,1,0:T(8,128)(2,1)S(1)}, u32[]{:S(2)}, u32[]{:S(2)}) collective-permute-start(bf16[2,128,768]{2,1,0:T(8,128)(2,1)S(1)} %stack.10.refs_0_), channel_id=1, source_target_pairs={{0,4},{2,6},{4,0},{6,2},{8,12},{10,14},{12,8},{14,10},{1,5},{3,7},... | collective-permute-start | bytes 1179656 | tf_op jit(solution)/shard_map/ppermute | solution.py:51
  71.2 14.4 %collective-permute-start.24 = (bf16[128,1024]{1,0:T(8,128)(2,1)S(1)}, bf16[128,1024]{1,0:T(8,128)(2,1)S(1)}, u32[]{:S(2)}, u32[]{:S(2)}) collective-permute-start(bf16[128,1024]{1,0:T(8,128)(2,1)S(1)} %gate.17.refs_0_), channel_id=1, source_target_pairs={{0,12},{2,14},{4,8},{6,10},{8,4},{10,6},{12,0},{14,2},{1,13},{3,15... | collective-permute-start | bytes 786440 | tf_op jit(solution)/shard_map/ppermute | solution.py:51
  73.2 7.9 %collective-permute-start.25 = (bf16[128,768]{1,0:T(8,128)(2,1)S(1)}, bf16[128,768]{1,0:T(8,128)(2,1)S(1)}, u32[]{:S(2)}, u32[]{:S(2)}) collective-permute-start(bf16[128,768]{1,0:T(8,128)(2,1)S(1)} %gate.18.refs_0_), channel_id=1, source_target_pairs={{0,2},{2,0},{4,6},{6,4},{8,10},{10,8},{12,14},{14,12},{1,3},{3,1},... | collective-permute-start | bytes 589832 | tf_op jit(solution)/shard_map/ppermute | solution.py:51
  74.6 17.7 %collective-permute-start.23 = (bf16[2,128,1024]{2,1,0:T(8,128)(2,1)S(1)}, bf16[2,128,1024]{2,1,0:T(8,128)(2,1)S(1)}, u32[]{:S(2)}, u32[]{:S(2)}) collective-permute-start(bf16[2,128,1024]{2,1,0:T(8,128)(2,1)S(1)} %collective-permute-done.18.refs_1_.refs_4_), channel_id=1, source_target_pairs={{0,2},{2,0},{4,6},{6,4},{8,10},{10,8},{12,14},{14,12},{1,3},{3,1},... | collective-permute-start | bytes 1572872 | tf_op jit(solution)/shard_map/ppermute | solution.py:51
  85.7 17.3 %collective-permute-start.28 = (bf16[2,128,1024]{2,1,0:T(8,128)(2,1)S(1)}, bf16[2,128,1024]{2,1,0:T(8,128)(2,1)S(1)}, u32[]{:S(2)}, u32[]{:S(2)}) collective-permute-start(bf16[2,128,1024]{2,1,0:T(8,128)(2,1)S(1)} %stack.11.refs_0_), channel_id=1, source_target_pairs={{0,4},{2,6},{4,0},{6,2},{8,12},{10,14},{12,8},{14,10},{1,5},{3,7},... | collective-permute-start | bytes 1572872 | tf_op jit(solution)/shard_map/ppermute | solution.py:51
  85.8 15.0 %collective-permute-start.29 = (bf16[2,128,768]{2,1,0:T(8,128)(2,1)S(1)}, bf16[2,128,768]{2,1,0:T(8,128)(2,1)S(1)}, u32[]{:S(2)}, u32[]{:S(2)}) collective-permute-start(bf16[2,128,768]{2,1,0:T(8,128)(2,1)S(1)} %gate.20.refs_0_), channel_id=1, source_target_pairs={{0,2},{2,0},{4,6},{6,4},{8,10},{10,8},{12,14},{14,12},{1,3},{3,1},... | collective-permute-start | bytes 1179656 | tf_op jit(solution)/shard_map/ppermute | solution.py:51
  86.5 10.9 %collective-permute-start.21 = (bf16[128,768]{1,0:T(8,128)(2,1)S(1)}, bf16[128,768]{1,0:T(8,128)(2,1)S(1)}, u32[]{:S(2)}, u32[]{:S(2)}) collective-permute-start(bf16[128,768]{1,0:T(8,128)(2,1)S(1)} %gate.19.refs_0_), channel_id=1, source_target_pairs={{0,12},{2,14},{4,8},{6,10},{8,4},{10,6},{12,0},{14,2},{1,13},{3,15... | collective-permute-start | bytes 589832 | tf_op jit(solution)/shard_map/ppermute | solution.py:51
  89.6 15.4 %collective-permute-start.22 = (bf16[128,768]{1,0:T(8,128)(2,1)S(1)}, bf16[128,768]{1,0:T(8,128)(2,1)S(1)}, u32[]{:S(2)}, u32[]{:S(2)}) collective-permute-start(bf16[128,768]{1,0:T(8,128)(2,1)S(1)} %attend26.1.refs_0_.x_ref.first_ref), channel_id=1, source_target_pairs={{0,2},{2,0},{4,6},{6,4},{8,10},{10,8},{12,14},{14,12},{1,3},{3,1},... | collective-permute-start | bytes 589832 | tf_op jit(solution)/shard_map/ppermute | solution.py:51
  97.4 11.8 %collective-permute-start.26 = (bf16[128,768]{1,0:T(8,128)(2,1)S(1)}, bf16[128,768]{1,0:T(8,128)(2,1)S(1)}, u32[]{:S(2)}, u32[]{:S(2)}) collective-permute-start(bf16[128,768]{1,0:T(8,128)(2,1)S(1)} %gate.22.refs_7_), channel_id=1, source_target_pairs={{0,2},{2,0},{4,6},{6,4},{8,10},{10,8},{12,14},{14,12},{1,3},{3,1},... | collective-permute-start | bytes 589832 | tf_op jit(solution)/shard_map/ppermute | solution.py:51
  103.1 18.7 %collective-permute-start.32 = (bf16[2,128,1024]{2,1,0:T(8,128)(2,1)S(1)}, bf16[2,128,1024]{2,1,0:T(8,128)(2,1)S(1)}, u32[]{:S(2)}, u32[]{:S(2)}) collective-permute-start(bf16[2,128,1024]{2,1,0:T(8,128)(2,1)S(1)} %gate.23.refs_0_), channel_id=1, source_target_pairs={{0,2},{2,0},{4,6},{6,4},{8,10},{10,8},{12,14},{14,12},{1,3},{3,1},... | collective-permute-start | bytes 1572872 | tf_op jit(solution)/shard_map/ppermute | solution.py:51
  104.5 17.3 %collective-permute-start.27 = (bf16[2,128,768]{2,1,0:T(8,128)(2,1)S(1)}, bf16[2,128,768]{2,1,0:T(8,128)(2,1)S(1)}, u32[]{:S(2)}, u32[]{:S(2)}) collective-permute-start(bf16[2,128,768]{2,1,0:T(8,128)(2,1)S(1)} %stack.12.refs_0_), channel_id=1, source_target_pairs={{0,4},{2,6},{4,0},{6,2},{8,12},{10,14},{12,8},{14,10},{1,5},{3,7},... | collective-permute-start | bytes 1179656 | tf_op jit(solution)/shard_map/ppermute | solution.py:51
  109.3 15.6 %collective-permute-start.30 = (bf16[2,128,768]{2,1,0:T(8,128)(2,1)S(1)}, bf16[2,128,768]{2,1,0:T(8,128)(2,1)S(1)}, u32[]{:S(2)}, u32[]{:S(2)}) collective-permute-start(bf16[2,128,768]{2,1,0:T(8,128)(2,1)S(1)} %stack.13.refs_7_), channel_id=1, source_target_pairs={{0,4},{2,6},{4,0},{6,2},{8,12},{10,14},{12,8},{14,10},{1,5},{3,7},... | collective-permute-start | bytes 1179656 | tf_op jit(solution)/shard_map/ppermute | solution.py:51
  109.8 12.0 %collective-permute-start.31 = (bf16[128,1024]{1,0:T(8,128)(2,1)S(1)}, bf16[128,1024]{1,0:T(8,128)(2,1)S(1)}, u32[]{:S(2)}, u32[]{:S(2)}) collective-permute-start(bf16[128,1024]{1,0:T(8,128)(2,1)S(1)} %gate.21.refs_7_), channel_id=1, source_target_pairs={{0,2},{2,0},{4,6},{6,4},{8,10},{10,8},{12,14},{14,12},{1,3},{3,1},... | collective-permute-start | bytes 786440 | tf_op jit(solution)/shard_map/ppermute | solution.py:51
  (6 other events, 57.5 us)

commit v6 on v5

--- a/solution.py
+++ b/solution.py
@@ -13,16 +13,18 @@
 MASKED = -1e30
 LANES = 128
 STEP = 4
-PLAN = ((4, 0), (8, 0), (6, 0), (8, 0), (6, 1))
+WIDE = 256
+ROWS = 32
+PLAN = ((4, 0, 0), (8, 0, 0), (6, 0, 0), (8, 0, 0), (6, 1, 0))
 FAR, SIDE, CROSS, NEAR, BOTH = "far", "side", "cross", "near", "both"
 ATTEND, STACK, PROJECT, OWN = "attend", "stack", "project", "own"
 ORDER = (
-    (ATTEND, 0), (ATTEND, 1), (STACK, 0), (FAR, 1), (ATTEND, 2), (BOTH, 0, (SIDE, 1), (SIDE, 2)),
-    (CROSS, 0), (FAR, 2), (STACK, 1, (FAR, 0)), (ATTEND, 3, (CROSS, 0)), (ATTEND, 4),
-    (CROSS, 1, (BOTH, 0)), (PROJECT, 0, (SIDE, 3)), (STACK, 2), (FAR, 3, (NEAR, 1)),
-    (CROSS, 2, (CROSS, 1)), (FAR, 4, (NEAR, 2)), (BOTH, 2, (CROSS, 2)), (STACK, 3),
-    (CROSS, 3, (BOTH, 1)), (PROJECT, 1), (STACK, 4), (CROSS, 4), (PROJECT, 2), (BOTH, 3), (BOTH, 4),
-    (PROJECT, 3, (NEAR, 4)),
+    (ATTEND, 0), (ATTEND, 1), (CROSS, 0), (STACK, 0), (ATTEND, 2), (STACK, 1, (FAR, 0)), (FAR, 2),
+    (BOTH, 0, (SIDE, 1), (SIDE, 2)), (ATTEND, 3, (CROSS, 0)), (ATTEND, 4),
+    (CROSS, 1, (BOTH, 0), (FAR, 1)), (PROJECT, 0, (SIDE, 3)), (STACK, 2), (FAR, 3, (NEAR, 1)),
+    (CROSS, 2, (CROSS, 1)), (BOTH, 1, (SIDE, 4)), (FAR, 4, (NEAR, 2)), (BOTH, 2, (CROSS, 2)),
+    (STACK, 3), (CROSS, 3, (BOTH, 1)), (PROJECT, 1, (NEAR, 1)), (CROSS, 4), (STACK, 4),
+    (PROJECT, 2), (BOTH, 4), (PROJECT, 3, (NEAR, 4)),
 )
 LOCAL = pl.BlockSpec(memory_space=pltpu.VMEM)
 ANYWHERE = pl.BlockSpec(memory_space=pl.ANY)
@@ -97,7 +99,7 @@
     )(held(x), *after)
 
 
-def pack_kernel(own, latent_hbm, rope_hbm, out_ref, latent_ref, rope_ref, sem):
+def pack_kernel(latent_hbm, rope_hbm, out_ref, latent_ref, rope_ref, sem):
     copies = (
         pltpu.make_async_copy(latent_hbm, latent_ref, sem.at[0]),
         pltpu.make_async_copy(rope_hbm, rope_ref, sem.at[1]),
@@ -106,27 +108,40 @@
         copy.start()
     rows, latent = latent_ref.shape
     rope = rope_ref.shape[0]
+    tiles = latent // LANES // 2
+    pairs, own = packed_rows(rows)
     side = lax.axis_index("head")
-    out_ref[:, latent:] = jnp.zeros((own, out_ref.shape[1] - latent), BF16)
     for copy in copies:
         copy.wait()
     turned = rope_ref[...].astype(F32).T.astype(BF16)
     for at in range(2):
-        span = slice(0, own) if at == 0 else slice(rows - own, rows)
 
         @pl.when(side == at)
-        def _(span=span):
-            out_ref[:, :latent] = latent_ref[span, :]
-            out_ref[:, latent : latent + rope] = turned[span, :]
-
-
-def pack(latent_cache, rope_keys, own, depth):
+        def _(at=at):
+            for tile in range(tiles):
+                lanes = slice((at * tiles + tile) * LANES, (at * tiles + tile + 1) * LANES)
+                out_ref[tile * rows : (tile + 1) * rows, :] = latent_ref[:, lanes]
+            first = at * (pairs - own)
+            to = slice(tiles * rows, tiles * rows + own)
+            out_ref[to, :rope] = turned[first : first + own, :]
+            second = first + rows - pairs
+            out_ref[to, rope:] = turned[second : second + own, :]
+
+
+def packed_rows(rows):
+    pairs = -(-rows // 32) * 16
+    return pairs, -(-pairs // 32) * 16
+
+
+def pack(latent_cache, rope_keys):
     arrays = (latent_cache, rope_keys.T)
-    return pl.pallas_call(
-        functools.partial(pack_kernel, own),
+    rows, latent = latent_cache.shape
+    _, own = packed_rows(rows)
+    return pl.pallas_call(
+        pack_kernel,
         in_specs=[ANYWHERE] * 2,
         out_specs=LOCAL,
-        out_shape=pltpu.VMEM((own, depth), BF16),
+        out_shape=pltpu.VMEM((latent // LANES // 2 * rows + own, LANES), BF16),
         scratch_shapes=[pltpu.VMEM(x.shape, x.dtype) for x in arrays]
         + [pltpu.SemaphoreType.DMA((2,))],
         compiler_params=params(2),
@@ -135,38 +150,10 @@
     )(*(pltpu.with_memory_space_constraint(x, pltpu.HBM) for x in arrays))
 
 
-def mask_kernel(own, owners, span_ref, valid_ref, bias_ref):
+def prep_kernel(
+    owners, q_hbm, r_hbm, w_hbm, span_ref, valid_ref, lat_ref, bias_ref, q_ref, r_ref, w_ref, sem
+):
     tokens, keys = bias_ref.shape
-    per_shard = keys // len(owners)
-    me, side = lax.axis_index("ctx"), lax.axis_index("head")
-    column = lax.broadcasted_iota(jnp.int32, (1, keys), 1)
-    place = jnp.full((1, keys), 2**30, jnp.int32)
-    for at, owner in enumerate(owners):
-        shard = me ^ owner
-        inner = column - at * per_shard
-        mine = jnp.where(side == 0, inner, inner + (per_shard - own))
-        others = jnp.where(side == 0, inner, inner - own)
-        row = jnp.where(inner < own, mine, others)
-        here = (inner >= 0) & (inner < per_shard) & (row < valid_ref[shard])
-        place = jnp.where(here, row + shard * per_shard, place)
-    position = span_ref[0] + me * tokens + lax.broadcasted_iota(jnp.int32, (tokens, keys), 0)
-    bias_ref[...] = jnp.where(place <= position, F32(0.0), F32(MASKED))
-
-
-def mask(span_offset, valid_lengths, owners, tokens, per_shard, own):
-    return pl.pallas_call(
-        functools.partial(mask_kernel, own, owners),
-        in_specs=[SCALARS, SCALARS],
-        out_specs=LOCAL,
-        out_shape=pltpu.VMEM((tokens, per_shard * len(owners)), F32),
-        compiler_params=params(4),
-        cost_estimate=cost(0, 1024),
-        name="mask",
-    )(span_offset, valid_lengths)
-
-
-def prep_kernel(q_hbm, r_hbm, w_hbm, lat_ref, q_ref, r_ref, w_ref, sem):
-    tokens = q_ref.shape[0]
     heads, nope, latent = w_ref.shape
     rope = r_ref.shape[1] // heads
     whole = (
@@ -181,9 +168,20 @@
     ]
     for copy in (*whole, *pieces):
         copy.start()
-    lat_ref[:, latent + rope :] = jnp.zeros(
-        (heads * tokens, lat_ref.shape[1] - latent - rope), BF16
-    )
+
+    per_shard = keys // len(owners)
+    me = lax.axis_index("ctx")
+    column = lax.broadcasted_iota(jnp.int32, (1, keys), 1)
+    place = jnp.full((1, keys), 2**30, jnp.int32)
+    for at, owner in enumerate(owners):
+        shard = me ^ owner
+        row = column - at * per_shard
+        here = (row >= 0) & (row < valid_ref[shard])
+        here = here & (row < per_shard)
+        place = jnp.where(here, row + shard * per_shard, place)
+    position = span_ref[0] + me * tokens + lax.broadcasted_iota(jnp.int32, (tokens, keys), 0)
+    bias_ref[...] = jnp.where(place <= position, F32(0.0), F32(MASKED))
+
     for copy in whole:
         copy.wait()
     for head in range(heads):
@@ -194,97 +192,132 @@
             q_ref[:, head * nope : (head + 1) * nope], w_ref[head], preferred_element_type=F32
         )
         lat_ref[rows, :latent] = lat.astype(BF16)
-        lat_ref[rows, latent : latent + rope] = r_ref[:, head * rope : (head + 1) * rope]
-
-
-def prep(q_nope, q_rope, w_absorb, depth):
-    heads = w_absorb.shape[0]
+        turned = r_ref[:, head * rope : (head + 1) * rope]
+        lat_ref[rows, latent : latent + rope] = turned
+        lat_ref[rows, latent + rope :] = turned
+
+
+def prep(q_nope, q_rope, w_absorb, span_offset, valid_lengths, owners, per_shard):
+    heads, _, latent = w_absorb.shape
     tokens = q_nope.shape[0]
     arrays = (q_nope, q_rope, w_absorb)
     return pl.pallas_call(
-        prep_kernel,
-        in_specs=[ANYWHERE] * 3,
-        out_specs=LOCAL,
-        out_shape=pltpu.VMEM((heads * tokens, depth), BF16),
+        functools.partial(prep_kernel, owners),
+        in_specs=[ANYWHERE] * 3 + [SCALARS] * 2,
+        out_specs=[LOCAL] * 2,
+        out_shape=[
+            pltpu.VMEM((heads * tokens, latent + LANES), BF16),
+            pltpu.VMEM((tokens, per_shard * len(owners)), F32),
+        ],
         scratch_shapes=[pltpu.VMEM(x.shape, x.dtype) for x in arrays]
         + [pltpu.SemaphoreType.DMA((2 + heads // STEP,))],
-        compiler_params=params(10),
+        compiler_params=params(12),
         cost_estimate=cost(0, 1024),
         name="prep",
-    )(*(pltpu.with_memory_space_constraint(x, pltpu.HBM) for x in arrays))
-
-
-def join_kernel(groups, own, *refs):
+    )(*(pltpu.with_memory_space_constraint(x, pltpu.HBM) for x in arrays), span_offset, valid_lengths)
+
+
+def join_kernel(groups, *refs):
     mine = refs[:groups]
     theirs = refs[groups : 2 * groups]
     out_ref = refs[-1]
-    per_shard = out_ref.shape[0] // (2 * groups)
-    rest = per_shard - own
+    rows = out_ref.shape[0] // (2 * groups)
+    latent = out_ref.shape[1] - LANES
+    tiles = latent // LANES // 2
+    pairs, own = packed_rows(rows)
     side = lax.axis_index("head")
-    for at in range(2 * groups):
-        group, inner = at // 2, at % 2
-        start = at * per_shard
-        out_ref[start : start + own] = mine[group][inner]
-    for half in range(2):
-
-        @pl.when(side == half)
-        def _(skip=(1 - half) * (own - rest)):
+    half = lax.broadcasted_iota(jnp.int32, (pairs, LANES), 1) < LANES // 2
+    nothing = jnp.zeros((pairs, LANES), BF16)
+    for which in range(2):
+
+        @pl.when(side == which)
+        def _(which=which):
             for at in range(2 * groups):
-                start = at * per_shard + own
-                out_ref[start : start + rest] = theirs[at // 2][at % 2, skip : skip + rest]
-
-
-def join(mine, theirs, per_shard):
+                start = at * rows
+                sides = [mine[at // 2], theirs[at // 2]][:: 1 - 2 * which]
+                for tile in range(2 * tiles):
+                    block = sides[tile // tiles][at % 2, tile % tiles * rows : (tile % tiles + 1) * rows]
+                    out_ref[start : start + rows, tile * LANES : (tile + 1) * LANES] = block
+                low = sides[0][at % 2, tiles * rows : tiles * rows + own]
+                high = sides[1][at % 2, tiles * rows + 2 * own - pairs : tiles * rows + own]
+                both = jnp.concatenate([low, high], axis=0)
+                out_ref[start : start + pairs, latent:] = jnp.where(half, both, nothing)
+                rest = jnp.where(half, nothing, both)[2 * pairs - rows :]
+                out_ref[start + pairs : start + rows, latent:] = rest
+
+
+def join(mine, theirs, per_shard, depth):
     groups = len(mine)
-    _, own, depth = mine[0].shape
-    return pl.pallas_call(
-        functools.partial(join_kernel, groups, own),
+    return pl.pallas_call(
+        functools.partial(join_kernel, groups),
         in_specs=[LOCAL] * (2 * groups),
         out_specs=LOCAL,
         out_shape=pltpu.VMEM((2 * groups * per_shard, depth), BF16),
-        compiler_params=params(2),
+        compiler_params=params(4),
         cost_estimate=cost(0, 1024),
         name="join",
     )(*map(held, mine), *map(held, theirs))
 
 
+def interleave(first, second):
+    steps = [((at + 0.5) / len(x), which, step) for which, x in enumerate((first, second)) for at, step in enumerate(x)]
+    for *_, step in sorted(steps, key=lambda entry: entry[:2]):
+        step()
+
+
 def attend_kernel(scale, start, heads, q_ref, bias_ref, w_ref, kv_ref, *refs):
-    out_ref, scores, probs = refs[-3:]
-    tokens = bias_ref.shape[0]
+    out_ref, scores, probs, totals, mixed = refs[-5:]
+    tokens, keys = bias_ref.shape
     _, latent, value = w_ref.shape
-    pair = scores.shape[1] // tokens
+    block = scores.shape[1]
+    pair = block // tokens
 
     def score(at):
-        row = (start + at * pair) * tokens
-        scores[at % 2] = lax.dot_general(
-            q_ref[row : row + pair * tokens, :],
-            kv_ref[...],
-            (((1,), (1,)), ((), ())),
-            preferred_element_type=F32,
-        )
-
-    def weigh(at):
-        totals = []
-        for head in range(pair):
-            rows = slice(head * tokens, (head + 1) * tokens)
-            masked = scores[at % 2, rows, :] + bias_ref[...]
+        row = start * tokens + at * block
+
+        def part(low):
+            span = slice(low, min(low + WIDE, keys))
+            scores[at % 2, :, span] = lax.dot_general(
+                q_ref[row : row + block, :],
+                kv_ref[span, :],
+                (((1,), (1,)), ((), ())),
+                preferred_element_type=F32,
+            )
+
+        return [functools.partial(part, low) for low in range(0, keys, WIDE)]
+
+    def soften(at):
+        def part(low):
+            rows = slice(low, low + ROWS)
+            masked = scores[at % 2, rows, :] + bias_ref[low % tokens : low % tokens + ROWS, :]
             top = jnp.max(masked, axis=-1, keepdims=True)
             expo = jnp.exp2((masked - top) * F32(scale))
-            totals.append(jnp.sum(expo, axis=-1, keepdims=True))
+            totals[at % 2, rows, :] = jnp.sum(expo, axis=-1, keepdims=True)
             probs[at % 2, rows, :] = expo.astype(BF16)
-        weighted = jnp.dot(probs[at % 2], kv_ref[:, :latent], preferred_element_type=F32)
-        for head in range(pair):
+
+        return [functools.partial(part, low) for low in range(0, block, ROWS)]
+
+    def weigh(at):
+        def part(low):
+            span = slice(low, low + WIDE)
+            weighted = jnp.dot(probs[at % 2], kv_ref[:, span], preferred_element_type=F32)
+            mixed[:, span] = (weighted / totals[at % 2]).astype(BF16)
+
+        def last(head):
+            which = at * pair + head
             rows = slice(head * tokens, (head + 1) * tokens)
-            mixed = (weighted[rows, :] / totals[head]).astype(BF16)
-            which = at * pair + head
-            out = jnp.dot(mixed, w_ref[start + which], preferred_element_type=F32)
+            out = jnp.dot(mixed[rows, :], w_ref[start + which], preferred_element_type=F32)
             out_ref[:, which * value : (which + 1) * value] = out.astype(BF16)
 
-    score(0)
-    for at in range(heads // pair):
-        if at + 1 < heads // pair:
-            score(at + 1)
-        weigh(at)
+        parts = [functools.partial(part, low) for low in range(0, latent, WIDE)]
+        return parts + [functools.partial(last, head) for head in range(pair)]
+
+    blocks = heads // pair
+    for step in range(blocks + 2):
+        products = weigh(step - 2) if step > 1 else []
+        if step < blocks:
+            products = products + score(step)
+        interleave(products, soften(step - 1) if 0 < step <= blocks else [])
 
 
 def attend(start, heads, queries, bias, w_value, kv, scale, after=()):
@@ -298,6 +331,8 @@
         scratch_shapes=[
             pltpu.VMEM((2, 2 * tokens, keys), F32),
             pltpu.VMEM((2, 2 * tokens, keys), BF16),
+            pltpu.VMEM((2, 2 * tokens, 1), F32),
+            pltpu.VMEM((2 * tokens, w_value.shape[1]), BF16),
         ],
         compiler_params=params(12),
         cost_estimate=cost(0, 1024),
@@ -409,10 +444,13 @@
             x = gate(x, after)
             last = [x]
         got[name, chunk] = exchange(x, mask, 8)
-        if name == FAR:
+        along_z, paired = PLAN[chunk][1:]
+        if name == FAR and not paired:
             offer(CROSS, chunk, got[FAR, chunk], 1)
-        if name == NEAR and not PLAN[chunk][1]:
+        if name == NEAR and not along_z:
             offer(BOTH, chunk, got[NEAR, chunk], 1)
+        if name == SIDE and along_z and paired:
+            offer(BOTH, chunk, got[SIDE, chunk], 2)
 
     def offer(name, chunk, x, mask):
         ready[name, chunk] = x, mask
@@ -420,8 +458,9 @@
             send(name, chunk)
 
     def parts_of(chunk):
-        apart = [(OWN, FAR), (SIDE, CROSS)], [(NEAR,), (BOTH,)]
-        return [tuple(got[name, chunk] for name in names) for half in apart for names in half]
+        sides = (SIDE,) if PLAN[chunk][2] else (SIDE, CROSS)
+        names = (OWN, FAR), sides, (NEAR,), (BOTH,)
+        return [tuple(got[name, chunk] for name in part) for part in names]
 
     for action, chunk, *waits in ORDER:
         after = last + [got[wait] for wait in waits]
@@ -430,15 +469,18 @@
             last = [out]
             got[OWN, chunk] = out
             offer(FAR, chunk, out, 6)
-            offer(SIDE, chunk, out, 1)
+            if not PLAN[chunk][2]:
+                offer(SIDE, chunk, out, 1)
         elif action == STACK:
             base = stack(got[OWN, chunk], got[FAR, chunk], after)
             last = [base]
             offer(NEAR, chunk, base, 2)
+            if PLAN[chunk][2]:
+                offer(SIDE, chunk, base, 1)
         elif action == PROJECT:
             acc = project(starts[chunk] * value, parts_of(chunk), w_output, acc, after)
             last = [acc]
-        elif action == BOTH and PLAN[chunk][1]:
+        elif action == BOTH and PLAN[chunk][1:] == (1, 0):
             pair = stack(got[SIDE, chunk], got[CROSS, chunk], after)
             last = [pair]
             got[BOTH, chunk] = exchange(pair, 2, 8)
@@ -456,21 +498,23 @@
     per_shard = latent_cache.shape[0]
     shards = valid_lengths.shape[0]
     value = w_value.shape[2]
-    depth = -(-(latent + rope_dim) // LANES) * LANES
-    own = -(-per_shard // 32) * 16
     scale = 1.0 / math.sqrt(nope_dim + rope_dim)
 
-    far = basis_of(shards)[0]
-    packed = pack(latent_cache, rope_keys, own, depth)
-    queries = prep(q_nope, q_rope, w_absorb, depth)
+    far, *rest = basis_of(shards)
+    keys = [0]
+    for mask in rest:
+        keys += [key ^ mask for key in keys]
+    keys = sorted(keys)
+    owners = [key ^ (far * inner) for key in keys for inner in range(2)]
+    packed = pack(latent_cache, rope_keys)
+    queries, bias = prep(
+        q_nope, q_rope, w_absorb, span_offset, valid_lengths, owners, per_shard
+    )
     mine = spread(packed, shards, [queries])
-    keys = sorted(mine)
     theirs = {key: sibling(pair) for key, pair in mine.items()}
-    owners = [key ^ (far * inner) for key in keys for inner in range(2)]
-    bias = mask(span_offset, valid_lengths, owners, tokens, per_shard, own)
-    kv = join([mine[key] for key in keys], [theirs[key] for key in keys], per_shard)
-
-    heads = [count * head_count // 32 for count, _ in PLAN]
+    kv = join([mine[key] for key in keys], [theirs[key] for key in keys], per_shard, latent + LANES)
+
+    heads = [count * head_count // 32 for count, *_ in PLAN]
     starts = [sum(heads[:chunk]) for chunk in range(len(heads))]
     if shards == 8:
         parts, acc = overlap(heads, starts, queries, bias, w_value, kv, w_output, scale)

time: 130 us -> 129 us (level)
  waiting for transfers between devices: 51.5 us -> 49.8 us
    ppermute x29, waiting for transfers between devices: 50 us -> 47 us  [exchange(): return lax.ppermute(x, 'ctx', [(i, i ^ mask) for i in range(shards)])]
    pallas_call x4 -> x3, Pallas kernels: 5.92 us -> 5.96 us  [the longest x1 4.44 us: prep(): pl.pallas_call(functools.partial(prep_kernel, owners), in_specs=[ANYWHERE...]
  transfers between devices with their start and end apart: 34 -> 34, of which waited for: 18 -> 15; matrix products, arithmetic and copies ran while one was open for 0% -> 0% of each run, Pallas kernels for 25% -> 25%
where the time goes in v6:
time: 129 us
  waiting for transfers between devices  49.8 us (39%)
  starting transfers between devices  39.1 us (30%)
  Pallas kernels  37 us (29%)
    ppermute x29, waiting for transfers between devices, exchange(): return lax.ppermute(x, 'ctx', [(i, i ^ mask) for i in range(shards)])  47 us
    ppermute x29, starting transfers between devices, exchange(): return lax.ppermute(x, 'ctx', [(i, i ^ mask) for i in range(shards)])  38.5 us
    pallas_call x5, Pallas kernels, attend(): pl.pallas_call(functools.partial(attend_kernel, scale * math.log2(math.e)...  19.2 us
    pallas_call x4, Pallas kernels, project(): pl.pallas_call(functools.partial(project_kernel, start, sizes, acc is Non...  9.33 us
    pallas_call x1, Pallas kernels, prep(): pl.pallas_call(functools.partial(prep_kernel, owners), in_specs=[ANYWHERE...  4.44 us
    ppermute x5, waiting for transfers between devices, sibling(): return lax.ppermute(x, 'head', [(0, 1), (1, 0)])  2.77 us
  transfers between devices with their start and end apart: 34, of which 15 were waited for; matrix products, arithmetic and copies ran while one was open for 0% of the time, Pallas kernels for 25%

profile of v6, /device:TPU:0, one launch (start us, length us, event | category | flops | bytes accessed | tf_op | source)
XLA Modules:
  0.0 128.7 jit_solution(3524174512219601584)
XLA Ops:
  1.1 5.1 %collective-permute-start = (bf16[336,128]{1,0:T(8,128)(2,1)S(1)}, bf16[336,128]{1,0:T(8,128)(2,1)S(1)}, u32[]{:S(2)}, u32[]{:S(2)}) collective-permute-start(bf16[336,128]{1,0:T(8,128)(2,1)S(1)} %pack.1.first_ref), channel_id=1, source_target_pairs={{0,12},{2,14},{4,8},{6,10},{8,4},{10,6},{12,0},{14,2},{1,13},{3,15... | collective-permute-start | bytes 258056 | tf_op jit(solution)/shard_map/ppermute | solution.py:53
  7.5 4.4 %prep.1 = (bf16[4096,640]{1,0:T(8,128)(2,1)S(1)}, f32[128,1152]{1,0:T(8,128)S(1)}) custom-call(bf16[128,4096]{1,0:T(8,128)(2,1)} %q_hbm.1, bf16[128,2048]{1,0:T(8,128)(2,1)} %r_hbm.1, bf16[32,128,512]{2,1,0:T(8,128)(2,1)} %w_hbm.1, s32[1]{0:T(128)S(6)} %copy.16.span_ref, s32[8]{0:T(128)S(1)} %copy-done.1), custom_call_target="tpu_custom_call" | custom-call | bytes 1024 | tf_op jit(solution)/shard_map/prep/pallas_call | solution.py:204
  12.1 1.6 %collective-permute-start.1 = (bf16[2,336,128]{2,1,0:T(8,128)(2,1)S(1)}, bf16[2,336,128]{2,1,0:T(8,128)(2,1)S(1)}, u32[]{:S(2)}, u32[]{:S(2)}) collective-permute-start(bf16[2,336,128]{2,1,0:T(8,128)(2,1)S(1)} %stack.7.refs_0_), channel_id=1, source_target_pairs={{0,2},{2,0},{4,6},{6,4},{8,10},{10,8},{12,14},{14,12},{1,3},{3,1},... | collective-permute-start | bytes 516104 | tf_op jit(solution)/shard_map/ppermute | solution.py:53
  13.7 4.2 %collective-permute-done.2.refs_2_ = bf16[2,336,128]{2,1,0:T(8,128)(2,1)S(1)} collective-permute-done((bf16[2,336,128]{2,1,0:T(8,128)(2,1)S(1)}, bf16[2,336,128]{2,1,0:T(8,128)(2,1)S(1)}, u32[]{:S(2)}, u32[]{:S(2)}) %collective-permute-start.2) | collective-permute-done | bytes 172064 | tf_op jit(solution)/shard_map/ppermute | solution.py:53
  17.9 1.5 %collective-permute-start.3 = (bf16[2,336,128]{2,1,0:T(8,128)(2,1)S(1)}, bf16[2,336,128]{2,1,0:T(8,128)(2,1)S(1)}, u32[]{:S(2)}, u32[]{:S(2)}) collective-permute-start(bf16[2,336,128]{2,1,0:T(8,128)(2,1)S(1)} %collective-permute-done.2.refs_2_), channel_id=1, source_target_pairs={{0,2},{2,0},{4,6},{6,4},{8,10},{10,8},{12,14},{14,12},{1,3},{3,1},... | collective-permute-start | bytes 516104 | tf_op jit(solution)/shard_map/ppermute | solution.py:53
  20.0 3.4 %collective-permute-done.3.refs_3_ = bf16[2,336,128]{2,1,0:T(8,128)(2,1)S(1)} collective-permute-done((bf16[2,336,128]{2,1,0:T(8,128)(2,1)S(1)}, bf16[2,336,128]{2,1,0:T(8,128)(2,1)S(1)}, u32[]{:S(2)}, u32[]{:S(2)}) %collective-permute-start.3) | collective-permute-done | bytes 172064 | tf_op jit(solution)/shard_map/ppermute | solution.py:53
  23.3 1.4 %collective-permute-done.7.refs_7_ = bf16[2,336,128]{2,1,0:T(8,128)(2,1)S(1)} collective-permute-done((bf16[2,336,128]{2,1,0:T(8,128)(2,1)S(1)}, bf16[2,336,128]{2,1,0:T(8,128)(2,1)S(1)}, u32[]{:S(2)}, u32[]{:S(2)}) %collective-permute-start.7) | collective-permute-done | bytes 172064 | tf_op jit(solution)/shard_map/ppermute | solution.py:57
  25.2 2.4 %attend0.1.refs_0_.first_ref = bf16[128,512]{1,0:T(8,128)(2,1)S(1)} custom-call(bf16[4096,640]{1,0:T(8,128)(2,1)S(1)} %get-tuple-element.7.refs_0_.q_ref, f32[128,1152]{1,0:T(8,128)S(1)} %get-tuple-element.8.bias_ref, bf16[32,512,128]{2,1,0:T(8,128)(2,1)S(1)} %copy-done, bf16[1152,640]{1,0:T(8,128)(2,1)S(1)} %join.1.kv_ref), custom_call_target="tpu_custom_call" | custom-call | bytes 1024 | tf_op jit(solution)/shard_map/attend0/pallas_call | solution.py:326
  28.0 4.7 %attend4.1.refs_0_.first_ref = bf16[128,1024]{1,0:T(8,128)(2,1)S(1)} custom-call(bf16[4096,640]{1,0:T(8,128)(2,1)S(1)} %get-tuple-element.7.refs_0_.q_ref, f32[128,1152]{1,0:T(8,128)S(1)} %get-tuple-element.8.bias_ref, bf16[32,512,128]{2,1,0:T(8,128)(2,1)S(1)} %copy-done, bf16[1152,640]{1,0:T(8,128)(2,1)S(1)} %join.1.kv_ref, ...), custom_call_target="tpu_custom_call" | custom-call | bytes 1024 | tf_op jit(solution)/shard_map/attend4/pallas_call | solution.py:326
  32.7 3.6 %collective-permute-start.10 = (bf16[128,1024]{1,0:T(8,128)(2,1)S(1)}, bf16[128,1024]{1,0:T(8,128)(2,1)S(1)}, u32[]{:S(2)}, u32[]{:S(2)}) collective-permute-start(bf16[128,1024]{1,0:T(8,128)(2,1)S(1)} %attend4.1.refs_0_.first_ref), channel_id=1, source_target_pairs={{0,12},{2,14},{4,8},{6,10},{8,4},{10,6},{12,0},{14,2},{1,13},{3,15... | collective-permute-start | bytes 786440 | tf_op jit(solution)/shard_map/ppermute | solution.py:53
  36.3 1.5 %collective-permute-start.11 = (bf16[128,1024]{1,0:T(8,128)(2,1)S(1)}, bf16[128,1024]{1,0:T(8,128)(2,1)S(1)}, u32[]{:S(2)}, u32[]{:S(2)}) collective-permute-start(bf16[128,1024]{1,0:T(8,128)(2,1)S(1)} %attend4.1.refs_0_.first_ref), channel_id=1, source_target_pairs={{0,2},{2,0},{4,6},{6,4},{8,10},{10,8},{12,14},{14,12},{1,3},{3,1},... | collective-permute-start | bytes 786440 | tf_op jit(solution)/shard_map/ppermute | solution.py:53
  37.9 3.6 %attend12.1.refs_0_.x_ref.first_ref = bf16[128,768]{1,0:T(8,128)(2,1)S(1)} custom-call(bf16[4096,640]{1,0:T(8,128)(2,1)S(1)} %get-tuple-element.7.refs_0_.q_ref, f32[128,1152]{1,0:T(8,128)S(1)} %get-tuple-element.8.bias_ref, bf16[32,512,128]{2,1,0:T(8,128)(2,1)S(1)} %copy-done, bf16[1152,640]{1,0:T(8,128)(2,1)S(1)} %join.1.kv_ref, ...), custom_call_target="tpu_custom_call" | custom-call | bytes 1024 | tf_op jit(solution)/shard_map/attend12/pallas_call | solution.py:326
  42.1 1.5 %collective-permute-start.13 = (bf16[128,512]{1,0:T(8,128)(2,1)S(1)}, bf16[128,512]{1,0:T(8,128)(2,1)S(1)}, u32[]{:S(2)}, u32[]{:S(2)}) collective-permute-start(bf16[128,512]{1,0:T(8,128)(2,1)S(1)} %gate.11.refs_0_), channel_id=1, source_target_pairs={{0,2},{2,0},{4,6},{6,4},{8,10},{10,8},{12,14},{14,12},{1,3},{3,1},... | collective-permute-start | bytes 393224 | tf_op jit(solution)/shard_map/ppermute | solution.py:53
  43.8 3.8 %collective-permute-start.14 = (bf16[2,128,1024]{2,1,0:T(8,128)(2,1)S(1)}, bf16[2,128,1024]{2,1,0:T(8,128)(2,1)S(1)}, u32[]{:S(2)}, u32[]{:S(2)}) collective-permute-start(bf16[2,128,1024]{2,1,0:T(8,128)(2,1)S(1)} %stack.9.refs_0_), channel_id=1, source_target_pairs={{0,4},{2,6},{4,0},{6,2},{8,12},{10,14},{12,8},{14,10},{1,5},{3,7},... | collective-permute-start | bytes 1572872 | tf_op jit(solution)/shard_map/ppermute | solution.py:53
  47.7 1.8 %collective-permute-done.12.refs_2_ = bf16[128,768]{1,0:T(8,128)(2,1)S(1)} collective-permute-done((bf16[128,768]{1,0:T(8,128)(2,1)S(1)}, bf16[128,768]{1,0:T(8,128)(2,1)S(1)}, u32[]{:S(2)}, u32[]{:S(2)}) %collective-permute-start.12) | collective-permute-done | bytes 196640 | tf_op jit(solution)/shard_map/ppermute | solution.py:53
  49.5 1.8 %collective-permute-start.17 = (bf16[2,128,512]{2,1,0:T(8,128)(2,1)S(1)}, bf16[2,128,512]{2,1,0:T(8,128)(2,1)S(1)}, u32[]{:S(2)}, u32[]{:S(2)}) collective-permute-start(bf16[2,128,512]{2,1,0:T(8,128)(2,1)S(1)} %gate.13.refs_0_), channel_id=1, source_target_pairs={{0,2},{2,0},{4,6},{6,4},{8,10},{10,8},{12,14},{14,12},{1,3},{3,1},... | collective-permute-start | bytes 786440 | tf_op jit(solution)/shard_map/ppermute | solution.py:53
  51.3 4.9 %attend18.1.refs_0_.x_ref.first_ref = bf16[128,1024]{1,0:T(8,128)(2,1)S(1)} custom-call(bf16[4096,640]{1,0:T(8,128)(2,1)S(1)} %get-tuple-element.7.refs_0_.q_ref, f32[128,1152]{1,0:T(8,128)S(1)} %get-tuple-element.8.bias_ref, bf16[32,512,128]{2,1,0:T(8,128)(2,1)S(1)} %copy-done, bf16[1152,640]{1,0:T(8,128)(2,1)S(1)} %join.1.kv_ref, ...), custom_call_target="tpu_custom_call" | custom-call | bytes 1024 | tf_op jit(solution)/shard_map/attend18/pallas_call | solution.py:326
  57.6 1.5 %collective-permute-start.15 = (bf16[128,768]{1,0:T(8,128)(2,1)S(1)}, bf16[128,768]{1,0:T(8,128)(2,1)S(1)}, u32[]{:S(2)}, u32[]{:S(2)}) collective-permute-start(bf16[128,768]{1,0:T(8,128)(2,1)S(1)} %gate.12.refs_0_), channel_id=1, source_target_pairs={{0,12},{2,14},{4,8},{6,10},{8,4},{10,6},{12,0},{14,2},{1,13},{3,15... | collective-permute-start | bytes 589832 | tf_op jit(solution)/shard_map/ppermute | solution.py:53
  60.1 3.6 %attend26.1.refs_0_.x_ref.first_ref = bf16[128,768]{1,0:T(8,128)(2,1)S(1)} custom-call(bf16[4096,640]{1,0:T(8,128)(2,1)S(1)} %get-tuple-element.7.refs_0_.q_ref, f32[128,1152]{1,0:T(8,128)S(1)} %get-tuple-element.8.bias_ref, bf16[32,512,128]{2,1,0:T(8,128)(2,1)S(1)} %copy-done, bf16[1152,640]{1,0:T(8,128)(2,1)S(1)} %join.1.kv_ref, ...), custom_call_target="tpu_custom_call" | custom-call | bytes 1024 | tf_op jit(solution)/shard_map/attend26/pallas_call | solution.py:326
  64.8 3.5 %collective-permute-done.16.refs_2_ = bf16[128,512]{1,0:T(8,128)(2,1)S(1)} collective-permute-done((bf16[128,512]{1,0:T(8,128)(2,1)S(1)}, bf16[128,512]{1,0:T(8,128)(2,1)S(1)}, u32[]{:S(2)}, u32[]{:S(2)}) %collective-permute-start.16) | collective-permute-done | bytes 131104 | tf_op jit(solution)/shard_map/ppermute | solution.py:53
  71.8 2.2 %collective-permute-done.19.refs_1_.refs_3_ = bf16[128,1024]{1,0:T(8,128)(2,1)S(1)} collective-permute-done((bf16[128,1024]{1,0:T(8,128)(2,1)S(1)}, bf16[128,1024]{1,0:T(8,128)(2,1)S(1)}, u32[]{:S(2)}, u32[]{:S(2)}) %collective-permute-start.19) | collective-permute-done | bytes 262176 | tf_op jit(solution)/shard_map/ppermute | solution.py:53
  75.0 3.4 %collective-permute-done.20.refs_1_.first_ref.refs_2_ = bf16[128,768]{1,0:T(8,128)(2,1)S(1)} collective-permute-done((bf16[128,768]{1,0:T(8,128)(2,1)S(1)}, bf16[128,768]{1,0:T(8,128)(2,1)S(1)}, u32[]{:S(2)}, u32[]{:S(2)}) %collective-permute-start.20) | collective-permute-done | bytes 196640 | tf_op jit(solution)/shard_map/ppermute | solution.py:53
  79.4 3.5 %collective-permute-done.21.refs_1_.x_ref.refs_4_ = bf16[2,128,768]{2,1,0:T(8,128)(2,1)S(1)} collective-permute-done((bf16[2,128,768]{2,1,0:T(8,128)(2,1)S(1)}, bf16[2,128,768]{2,1,0:T(8,128)(2,1)S(1)}, u32[]{:S(2)}, u32[]{:S(2)}) %collective-permute-start.21) | collective-permute-done | bytes 393248 | tf_op jit(solution)/shard_map/ppermute | solution.py:53
  84.0 1.7 %collective-permute-start.22 = (bf16[128,768]{1,0:T(8,128)(2,1)S(1)}, bf16[128,768]{1,0:T(8,128)(2,1)S(1)}, u32[]{:S(2)}, u32[]{:S(2)}) collective-permute-start(bf16[128,768]{1,0:T(8,128)(2,1)S(1)} %gate.18.refs_0_), channel_id=1, source_target_pairs={{0,12},{2,14},{4,8},{6,10},{8,4},{10,6},{12,0},{14,2},{1,13},{3,15... | collective-permute-start | bytes 589832 | tf_op jit(solution)/shard_map/ppermute | solution.py:53
  86.3 7.6 %collective-permute-done.23.refs_1_.refs_5_ = bf16[2,128,1024]{2,1,0:T(8,128)(2,1)S(1)} collective-permute-done((bf16[2,128,1024]{2,1,0:T(8,128)(2,1)S(1)}, bf16[2,128,1024]{2,1,0:T(8,128)(2,1)S(1)}, u32[]{:S(2)}, u32[]{:S(2)}) %collective-permute-start.23) | collective-permute-done | bytes 524320 | tf_op jit(solution)/shard_map/ppermute | solution.py:53
  93.9 2.8 %project512.1.refs_0_.refs_6_ = f32[2,512,896]{2,1,0:T(8,128)S(1)} custom-call(bf16[4096,896]{1,0:T(8,128)(2,1)S(1)} %bitcast.2, bf16[128,1024]{1,0:T(8,128)(2,1)S(1)} %attend4.1.refs_0_.first_ref, bf16[128,1024]{1,0:T(8,128)(2,1)S(1)} %collective-permute-done.10.second_ref.x_ref.refs_2_.refs_1_, ...), custom_call_target="tpu_custom_call", output_to_operand_aliasing={{}: (7, {})} | custom-call | bytes 1024 | tf_op jit(solution)/shard_map/project512/pallas_call | solution.py:385
  100.2 2.2 %collective-permute-done.28.refs_5_ = bf16[2,128,768]{2,1,0:T(8,128)(2,1)S(1)} collective-permute-done((bf16[2,128,768]{2,1,0:T(8,128)(2,1)S(1)}, bf16[2,128,768]{2,1,0:T(8,128)(2,1)S(1)}, u32[]{:S(2)}, u32[]{:S(2)}) %collective-permute-start.28) | collective-permute-done | bytes 393248 | tf_op jit(solution)/shard_map/ppermute | solution.py:53
  102.3 2.2 %project1536.1.refs_0_.refs_6_ = f32[2,512,896]{2,1,0:T(8,128)S(1)} custom-call(bf16[4096,896]{1,0:T(8,128)(2,1)S(1)} %bitcast.2, bf16[128,768]{1,0:T(8,128)(2,1)S(1)} %attend12.1.refs_0_.x_ref.first_ref, bf16[128,768]{1,0:T(8,128)(2,1)S(1)} %collective-permute-done.15.second_ref.x_ref.refs_1_, ...), custom_call_target="tpu_custom_call", output_to_operand_aliasing={{}: (7, {})} | custom-call | bytes 1024 | tf_op jit(solution)/shard_map/project1536/pallas_call | solution.py:385
  104.6 2.0 %collective-permute-done.26.second_ref.refs_3_ = bf16[128,768]{1,0:T(8,128)(2,1)S(1)} collective-permute-done((bf16[128,768]{1,0:T(8,128)(2,1)S(1)}, bf16[128,768]{1,0:T(8,128)(2,1)S(1)}, u32[]{:S(2)}, u32[]{:S(2)}) %collective-permute-start.26) | collective-permute-done | bytes 196640 | tf_op jit(solution)/shard_map/ppermute | solution.py:53
  108.8 12.1 %collective-permute-done.30.refs_3_ = bf16[128,1024]{1,0:T(8,128)(2,1)S(1)} collective-permute-done((bf16[128,1024]{1,0:T(8,128)(2,1)S(1)}, bf16[128,1024]{1,0:T(8,128)(2,1)S(1)}, u32[]{:S(2)}, u32[]{:S(2)}) %collective-permute-start.30) | collective-permute-done | bytes 262176 | tf_op jit(solution)/shard_map/ppermute | solution.py:53
  120.9 3.1 %project2304.1.refs_6_ = f32[2,512,896]{2,1,0:T(8,128)S(1)} custom-call(bf16[4096,896]{1,0:T(8,128)(2,1)S(1)} %bitcast.2, bf16[128,1024]{1,0:T(8,128)(2,1)S(1)} %attend18.1.refs_0_.x_ref.first_ref, bf16[128,1024]{1,0:T(8,128)(2,1)S(1)} %collective-permute-done.24.second_ref.x_ref.refs_1_, ...), custom_call_target="tpu_custom_call", output_to_operand_aliasing={{}: (7, {})} | custom-call | bytes 1024 | tf_op jit(solution)/shard_map/project2304/pallas_call | solution.py:385
  126.2 1.4 %collective-permute-done.33 = bf16[512,896]{1,0:T(8,128)(2,1)S(1)} collective-permute-done((bf16[512,896]{1,0:T(8,128)(2,1)S(1)}, bf16[512,896]{1,0:T(8,128)(2,1)S(1)}, u32[]{:S(2)}, u32[]{:S(2)}) %collective-permute-start.33) | collective-permute-done | bytes 917536 | tf_op jit(solution)/shard_map/ppermute | solution.py:57
  (78 shorter events, 23.5 us)
Async XLA Ops:
  1.1 10.9 %collective-permute-start = (bf16[336,128]{1,0:T(8,128)(2,1)S(1)}, bf16[336,128]{1,0:T(8,128)(2,1)S(1)}, u32[]{:S(2)}, u32[]{:S(2)}) collective-permute-start(bf16[336,128]{1,0:T(8,128)(2,1)S(1)} %pack.1.first_ref), channel_id=1, source_target_pairs={{0,12},{2,14},{4,8},{6,10},{8,4},{10,6},{12,0},{14,2},{1,13},{3,15... | collective-permute-start | bytes 258056 | tf_op jit(solution)/shard_map/ppermute | solution.py:53
  12.0 5.9 %collective-permute-start.2 = (bf16[2,336,128]{2,1,0:T(8,128)(2,1)S(1)}, bf16[2,336,128]{2,1,0:T(8,128)(2,1)S(1)}, u32[]{:S(2)}, u32[]{:S(2)}) collective-permute-start(bf16[2,336,128]{2,1,0:T(8,128)(2,1)S(1)} %stack.7.refs_0_), channel_id=1, source_target_pairs={{0,4},{2,6},{4,0},{6,2},{8,12},{10,14},{12,8},{14,10},{1,5},{3,7},... | collective-permute-start | bytes 516104 | tf_op jit(solution)/shard_map/ppermute | solution.py:53
  12.1 7.9 %collective-permute-start.1 = (bf16[2,336,128]{2,1,0:T(8,128)(2,1)S(1)}, bf16[2,336,128]{2,1,0:T(8,128)(2,1)S(1)}, u32[]{:S(2)}, u32[]{:S(2)}) collective-permute-start(bf16[2,336,128]{2,1,0:T(8,128)(2,1)S(1)} %stack.7.refs_0_), channel_id=1, source_target_pairs={{0,2},{2,0},{4,6},{6,4},{8,10},{10,8},{12,14},{14,12},{1,3},{3,1},... | collective-permute-start | bytes 516104 | tf_op jit(solution)/shard_map/ppermute | solution.py:53
  17.9 5.4 %collective-permute-start.3 = (bf16[2,336,128]{2,1,0:T(8,128)(2,1)S(1)}, bf16[2,336,128]{2,1,0:T(8,128)(2,1)S(1)}, u32[]{:S(2)}, u32[]{:S(2)}) collective-permute-start(bf16[2,336,128]{2,1,0:T(8,128)(2,1)S(1)} %collective-permute-done.2.refs_2_), channel_id=1, source_target_pairs={{0,2},{2,0},{4,6},{6,4},{8,10},{10,8},{12,14},{14,12},{1,3},{3,1},... | collective-permute-start | bytes 516104 | tf_op jit(solution)/shard_map/ppermute | solution.py:53
  19.4 3.9 %collective-permute-start.4 = (bf16[2,336,128]{2,1,0:T(8,128)(2,1)S(1)}, bf16[2,336,128]{2,1,0:T(8,128)(2,1)S(1)}, u32[]{:S(2)}, u32[]{:S(2)}) collective-permute-start(bf16[2,336,128]{2,1,0:T(8,128)(2,1)S(1)} %stack.7.refs_0_), channel_id=1, source_target_pairs={{0,1},{1,0},{2,3},{3,2},{4,5},{5,4},{6,7},{7,6},{8,9},{9,8},{10,11... | collective-permute-start | bytes 516104 | tf_op jit(solution)/shard_map/ppermute | solution.py:57
  19.4 3.9 %collective-permute-start.6 = (bf16[2,336,128]{2,1,0:T(8,128)(2,1)S(1)}, bf16[2,336,128]{2,1,0:T(8,128)(2,1)S(1)}, u32[]{:S(2)}, u32[]{:S(2)}) collective-permute-start(bf16[2,336,128]{2,1,0:T(8,128)(2,1)S(1)} %collective-permute-done.2.refs_2_), channel_id=1, source_target_pairs={{0,1},{1,0},{2,3},{3,2},{4,5},{5,4},{6,7},{7,6},{8,9},{9,8},{10,11... | collective-permute-start | bytes 516104 | tf_op jit(solution)/shard_map/ppermute | solution.py:57
  20.0 3.4 %collective-permute-start.5 = (bf16[2,336,128]{2,1,0:T(8,128)(2,1)S(1)}, bf16[2,336,128]{2,1,0:T(8,128)(2,1)S(1)}, u32[]{:S(2)}, u32[]{:S(2)}) collective-permute-start(bf16[2,336,128]{2,1,0:T(8,128)(2,1)S(1)} %collective-permute-done.1.refs_1_), channel_id=1, source_target_pairs={{0,1},{1,0},{2,3},{3,2},{4,5},{5,4},{6,7},{7,6},{8,9},{9,8},{10,11... | collective-permute-start | bytes 516104 | tf_op jit(solution)/shard_map/ppermute | solution.py:57
  27.6 10.2 %collective-permute-start.8 = (bf16[128,512]{1,0:T(8,128)(2,1)S(1)}, bf16[128,512]{1,0:T(8,128)(2,1)S(1)}, u32[]{:S(2)}, u32[]{:S(2)}) collective-permute-start(bf16[128,512]{1,0:T(8,128)(2,1)S(1)} %attend0.1.refs_0_.first_ref), channel_id=1, source_target_pairs={{0,12},{2,14},{4,8},{6,10},{8,4},{10,6},{12,0},{14,2},{1,13},{3,15... | collective-permute-start | bytes 393224 | tf_op jit(solution)/shard_map/ppermute | solution.py:53
  32.7 11.1 %collective-permute-start.10 = (bf16[128,1024]{1,0:T(8,128)(2,1)S(1)}, bf16[128,1024]{1,0:T(8,128)(2,1)S(1)}, u32[]{:S(2)}, u32[]{:S(2)}) collective-permute-start(bf16[128,1024]{1,0:T(8,128)(2,1)S(1)} %attend4.1.refs_0_.first_ref), channel_id=1, source_target_pairs={{0,12},{2,14},{4,8},{6,10},{8,4},{10,6},{12,0},{14,2},{1,13},{3,15... | collective-permute-start | bytes 786440 | tf_op jit(solution)/shard_map/ppermute | solution.py:53
  36.3 11.4 %collective-permute-start.11 = (bf16[128,1024]{1,0:T(8,128)(2,1)S(1)}, bf16[128,1024]{1,0:T(8,128)(2,1)S(1)}, u32[]{:S(2)}, u32[]{:S(2)}) collective-permute-start(bf16[128,1024]{1,0:T(8,128)(2,1)S(1)} %attend4.1.refs_0_.first_ref), channel_id=1, source_target_pairs={{0,2},{2,0},{4,6},{6,4},{8,10},{10,8},{12,14},{14,12},{1,3},{3,1},... | collective-permute-start | bytes 786440 | tf_op jit(solution)/shard_map/ppermute | solution.py:53
  37.9 11.6 %collective-permute-start.9 = (bf16[2,128,512]{2,1,0:T(8,128)(2,1)S(1)}, bf16[2,128,512]{2,1,0:T(8,128)(2,1)S(1)}, u32[]{:S(2)}, u32[]{:S(2)}) collective-permute-start(bf16[2,128,512]{2,1,0:T(8,128)(2,1)S(1)} %stack.8.refs_0_), channel_id=1, source_target_pairs={{0,4},{2,6},{4,0},{6,2},{8,12},{10,14},{12,8},{14,10},{1,5},{3,7},... | collective-permute-start | bytes 786440 | tf_op jit(solution)/shard_map/ppermute | solution.py:53
  41.5 7.9 %collective-permute-start.12 = (bf16[128,768]{1,0:T(8,128)(2,1)S(1)}, bf16[128,768]{1,0:T(8,128)(2,1)S(1)}, u32[]{:S(2)}, u32[]{:S(2)}) collective-permute-start(bf16[128,768]{1,0:T(8,128)(2,1)S(1)} %attend12.1.refs_0_.x_ref.first_ref), channel_id=1, source_target_pairs={{0,2},{2,0},{4,6},{6,4},{8,10},{10,8},{12,14},{14,12},{1,3},{3,1},... | collective-permute-start | bytes 589832 | tf_op jit(solution)/shard_map/ppermute | solution.py:53
  42.1 9.2 %collective-permute-start.13 = (bf16[128,512]{1,0:T(8,128)(2,1)S(1)}, bf16[128,512]{1,0:T(8,128)(2,1)S(1)}, u32[]{:S(2)}, u32[]{:S(2)}) collective-permute-start(bf16[128,512]{1,0:T(8,128)(2,1)S(1)} %gate.11.refs_0_), channel_id=1, source_target_pairs={{0,2},{2,0},{4,6},{6,4},{8,10},{10,8},{12,14},{14,12},{1,3},{3,1},... | collective-permute-start | bytes 393224 | tf_op jit(solution)/shard_map/ppermute | solution.py:53
  43.8 27.6 %collective-permute-start.14 = (bf16[2,128,1024]{2,1,0:T(8,128)(2,1)S(1)}, bf16[2,128,1024]{2,1,0:T(8,128)(2,1)S(1)}, u32[]{:S(2)}, u32[]{:S(2)}) collective-permute-start(bf16[2,128,1024]{2,1,0:T(8,128)(2,1)S(1)} %stack.9.refs_0_), channel_id=1, source_target_pairs={{0,4},{2,6},{4,0},{6,2},{8,12},{10,14},{12,8},{14,10},{1,5},{3,7},... | collective-permute-start | bytes 1572872 | tf_op jit(solution)/shard_map/ppermute | solution.py:53
  49.5 14.2 %collective-permute-start.17 = (bf16[2,128,512]{2,1,0:T(8,128)(2,1)S(1)}, bf16[2,128,512]{2,1,0:T(8,128)(2,1)S(1)}, u32[]{:S(2)}, u32[]{:S(2)}) collective-permute-start(bf16[2,128,512]{2,1,0:T(8,128)(2,1)S(1)} %gate.13.refs_0_), channel_id=1, source_target_pairs={{0,2},{2,0},{4,6},{6,4},{8,10},{10,8},{12,14},{14,12},{1,3},{3,1},... | collective-permute-start | bytes 786440 | tf_op jit(solution)/shard_map/ppermute | solution.py:53
  56.3 12.1 %collective-permute-start.18 = (bf16[128,1024]{1,0:T(8,128)(2,1)S(1)}, bf16[128,1024]{1,0:T(8,128)(2,1)S(1)}, u32[]{:S(2)}, u32[]{:S(2)}) collective-permute-start(bf16[128,1024]{1,0:T(8,128)(2,1)S(1)} %attend18.1.refs_0_.x_ref.first_ref), channel_id=1, source_target_pairs={{0,2},{2,0},{4,6},{6,4},{8,10},{10,8},{12,14},{14,12},{1,3},{3,1},... | collective-permute-start | bytes 786440 | tf_op jit(solution)/shard_map/ppermute | solution.py:53
  57.6 12.0 %collective-permute-start.15 = (bf16[128,768]{1,0:T(8,128)(2,1)S(1)}, bf16[128,768]{1,0:T(8,128)(2,1)S(1)}, u32[]{:S(2)}, u32[]{:S(2)}) collective-permute-start(bf16[128,768]{1,0:T(8,128)(2,1)S(1)} %gate.12.refs_0_), channel_id=1, source_target_pairs={{0,12},{2,14},{4,8},{6,10},{8,4},{10,6},{12,0},{14,2},{1,13},{3,15... | collective-permute-start | bytes 589832 | tf_op jit(solution)/shard_map/ppermute | solution.py:53
  59.1 9.3 %collective-permute-start.16 = (bf16[128,512]{1,0:T(8,128)(2,1)S(1)}, bf16[128,512]{1,0:T(8,128)(2,1)S(1)}, u32[]{:S(2)}, u32[]{:S(2)}) collective-permute-start(bf16[128,512]{1,0:T(8,128)(2,1)S(1)} %attend0.1.refs_0_.first_ref), channel_id=1, source_target_pairs={{0,2},{2,0},{4,6},{6,4},{8,10},{10,8},{12,14},{14,12},{1,3},{3,1},... | collective-permute-start | bytes 393224 | tf_op jit(solution)/shard_map/ppermute | solution.py:53
  63.7 10.3 %collective-permute-start.19 = (bf16[128,1024]{1,0:T(8,128)(2,1)S(1)}, bf16[128,1024]{1,0:T(8,128)(2,1)S(1)}, u32[]{:S(2)}, u32[]{:S(2)}) collective-permute-start(bf16[128,1024]{1,0:T(8,128)(2,1)S(1)} %gate.14.refs_6_), channel_id=1, source_target_pairs={{0,2},{2,0},{4,6},{6,4},{8,10},{10,8},{12,14},{14,12},{1,3},{3,1},... | collective-permute-start | bytes 786440 | tf_op jit(solution)/shard_map/ppermute | solution.py:53
  69.7 13.2 %collective-permute-start.21 = (bf16[2,128,768]{2,1,0:T(8,128)(2,1)S(1)}, bf16[2,128,768]{2,1,0:T(8,128)(2,1)S(1)}, u32[]{:S(2)}, u32[]{:S(2)}) collective-permute-start(bf16[2,128,768]{2,1,0:T(8,128)(2,1)S(1)} %stack.10.refs_0_), channel_id=1, source_target_pairs={{0,4},{2,6},{4,0},{6,2},{8,12},{10,14},{12,8},{14,10},{1,5},{3,7},... | collective-permute-start | bytes 1179656 | tf_op jit(solution)/shard_map/ppermute | solution.py:53
  70.6 7.8 %collective-permute-start.20 = (bf16[128,768]{1,0:T(8,128)(2,1)S(1)}, bf16[128,768]{1,0:T(8,128)(2,1)S(1)}, u32[]{:S(2)}, u32[]{:S(2)}) collective-permute-start(bf16[128,768]{1,0:T(8,128)(2,1)S(1)} %attend26.1.refs_0_.x_ref.first_ref), channel_id=1, source_target_pairs={{0,2},{2,0},{4,6},{6,4},{8,10},{10,8},{12,14},{14,12},{1,3},{3,1},... | collective-permute-start | bytes 589832 | tf_op jit(solution)/shard_map/ppermute | solution.py:53
  71.4 11.5 %collective-permute-start.24 = (bf16[128,1024]{1,0:T(8,128)(2,1)S(1)}, bf16[128,1024]{1,0:T(8,128)(2,1)S(1)}, u32[]{:S(2)}, u32[]{:S(2)}) collective-permute-start(bf16[128,1024]{1,0:T(8,128)(2,1)S(1)} %gate.15.refs_0_), channel_id=1, source_target_pairs={{0,12},{2,14},{4,8},{6,10},{8,4},{10,6},{12,0},{14,2},{1,13},{3,15... | collective-permute-start | bytes 786440 | tf_op jit(solution)/shard_map/ppermute | solution.py:53
  74.0 8.9 %collective-permute-start.25 = (bf16[128,768]{1,0:T(8,128)(2,1)S(1)}, bf16[128,768]{1,0:T(8,128)(2,1)S(1)}, u32[]{:S(2)}, u32[]{:S(2)}) collective-permute-start(bf16[128,768]{1,0:T(8,128)(2,1)S(1)} %gate.16.refs_0_), channel_id=1, source_target_pairs={{0,2},{2,0},{4,6},{6,4},{8,10},{10,8},{12,14},{14,12},{1,3},{3,1},... | collective-permute-start | bytes 589832 | tf_op jit(solution)/shard_map/ppermute | solution.py:53
  78.5 15.4 %collective-permute-start.23 = (bf16[2,128,1024]{2,1,0:T(8,128)(2,1)S(1)}, bf16[2,128,1024]{2,1,0:T(8,128)(2,1)S(1)}, u32[]{:S(2)}, u32[]{:S(2)}) collective-permute-start(bf16[2,128,1024]{2,1,0:T(8,128)(2,1)S(1)} %gate.17.refs_0_), channel_id=1, source_target_pairs={{0,2},{2,0},{4,6},{6,4},{8,10},{10,8},{12,14},{14,12},{1,3},{3,1},... | collective-permute-start | bytes 1572872 | tf_op jit(solution)/shard_map/ppermute | solution.py:53
  83.0 15.9 %collective-permute-start.31 = (bf16[2,128,1024]{2,1,0:T(8,128)(2,1)S(1)}, bf16[2,128,1024]{2,1,0:T(8,128)(2,1)S(1)}, u32[]{:S(2)}, u32[]{:S(2)}) collective-permute-start(bf16[2,128,1024]{2,1,0:T(8,128)(2,1)S(1)} %stack.11.refs_0_), channel_id=1, source_target_pairs={{0,4},{2,6},{4,0},{6,2},{8,12},{10,14},{12,8},{14,10},{1,5},{3,7},... | collective-permute-start | bytes 1572872 | tf_op jit(solution)/shard_map/ppermute | solution.py:53
  84.0 13.6 %collective-permute-start.22 = (bf16[128,768]{1,0:T(8,128)(2,1)S(1)}, bf16[128,768]{1,0:T(8,128)(2,1)S(1)}, u32[]{:S(2)}, u32[]{:S(2)}) collective-permute-start(bf16[128,768]{1,0:T(8,128)(2,1)S(1)} %gate.18.refs_0_), channel_id=1, source_target_pairs={{0,12},{2,14},{4,8},{6,10},{8,4},{10,6},{12,0},{14,2},{1,13},{3,15... | collective-permute-start | bytes 589832 | tf_op jit(solution)/shard_map/ppermute | solution.py:53
  85.7 16.6 %collective-permute-start.28 = (bf16[2,128,768]{2,1,0:T(8,128)(2,1)S(1)}, bf16[2,128,768]{2,1,0:T(8,128)(2,1)S(1)}, u32[]{:S(2)}, u32[]{:S(2)}) collective-permute-start(bf16[2,128,768]{2,1,0:T(8,128)(2,1)S(1)} %gate.19.refs_0_), channel_id=1, source_target_pairs={{0,2},{2,0},{4,6},{6,4},{8,10},{10,8},{12,14},{14,12},{1,3},{3,1},... | collective-permute-start | bytes 1179656 | tf_op jit(solution)/shard_map/ppermute | solution.py:53
  97.6 8.9 %collective-permute-start.26 = (bf16[128,768]{1,0:T(8,128)(2,1)S(1)}, bf16[128,768]{1,0:T(8,128)(2,1)S(1)}, u32[]{:S(2)}, u32[]{:S(2)}) collective-permute-start(bf16[128,768]{1,0:T(8,128)(2,1)S(1)} %gate.21.refs_0_), channel_id=1, source_target_pairs={{0,2},{2,0},{4,6},{6,4},{8,10},{10,8},{12,14},{14,12},{1,3},{3,1},... | collective-permute-start | bytes 589832 | tf_op jit(solution)/shard_map/ppermute | solution.py:53
  98.9 21.9 %collective-permute-start.32 = (bf16[2,128,1024]{2,1,0:T(8,128)(2,1)S(1)}, bf16[2,128,1024]{2,1,0:T(8,128)(2,1)S(1)}, u32[]{:S(2)}, u32[]{:S(2)}) collective-permute-start(bf16[2,128,1024]{2,1,0:T(8,128)(2,1)S(1)} %collective-permute-done.31.refs_4_), channel_id=1, source_target_pairs={{0,2},{2,0},{4,6},{6,4},{8,10},{10,8},{12,14},{14,12},{1,3},{3,1},... | collective-permute-start | bytes 1572872 | tf_op jit(solution)/shard_map/ppermute | solution.py:53
  99.8 21.1 %collective-permute-start.27 = (bf16[2,128,768]{2,1,0:T(8,128)(2,1)S(1)}, bf16[2,128,768]{2,1,0:T(8,128)(2,1)S(1)}, u32[]{:S(2)}, u32[]{:S(2)}) collective-permute-start(bf16[2,128,768]{2,1,0:T(8,128)(2,1)S(1)} %stack.12.refs_7_), channel_id=1, source_target_pairs={{0,4},{2,6},{4,0},{6,2},{8,12},{10,14},{12,8},{14,10},{1,5},{3,7},... | collective-permute-start | bytes 1179656 | tf_op jit(solution)/shard_map/ppermute | solution.py:53
  106.6 17.4 %collective-permute-start.29 = (bf16[2,128,768]{2,1,0:T(8,128)(2,1)S(1)}, bf16[2,128,768]{2,1,0:T(8,128)(2,1)S(1)}, u32[]{:S(2)}, u32[]{:S(2)}) collective-permute-start(bf16[2,128,768]{2,1,0:T(8,128)(2,1)S(1)} %stack.13.refs_7_), channel_id=1, source_target_pairs={{0,4},{2,6},{4,0},{6,2},{8,12},{10,14},{12,8},{14,10},{1,5},{3,7},... | collective-permute-start | bytes 1179656 | tf_op jit(solution)/shard_map/ppermute | solution.py:53
  107.8 13.0 %collective-permute-start.30 = (bf16[128,1024]{1,0:T(8,128)(2,1)S(1)}, bf16[128,1024]{1,0:T(8,128)(2,1)S(1)}, u32[]{:S(2)}, u32[]{:S(2)}) collective-permute-start(bf16[128,1024]{1,0:T(8,128)(2,1)S(1)} %gate.20.refs_7_), channel_id=1, source_target_pairs={{0,2},{2,0},{4,6},{6,4},{8,10},{10,8},{12,14},{14,12},{1,3},{3,1},... | collective-permute-start | bytes 786440 | tf_op jit(solution)/shard_map/ppermute | solution.py:53
  (6 other events, 47.0 us)

commit v7 on v6

--- a/solution.py
+++ b/solution.py
@@ -17,14 +17,14 @@
 ROWS = 32
 PLAN = ((4, 0, 0), (8, 0, 0), (6, 0, 0), (8, 0, 0), (6, 1, 0))
 FAR, SIDE, CROSS, NEAR, BOTH = "far", "side", "cross", "near", "both"
-ATTEND, STACK, PROJECT, OWN = "attend", "stack", "project", "own"
+ATTEND, STACK, PROJECT, FINISH, OWN = "attend", "stack", "project", "finish", "own"
 ORDER = (
-    (ATTEND, 0), (ATTEND, 1), (CROSS, 0), (STACK, 0), (ATTEND, 2), (STACK, 1, (FAR, 0)), (FAR, 2),
-    (BOTH, 0, (SIDE, 1), (SIDE, 2)), (ATTEND, 3, (CROSS, 0)), (ATTEND, 4),
-    (CROSS, 1, (BOTH, 0), (FAR, 1)), (PROJECT, 0, (SIDE, 3)), (STACK, 2), (FAR, 3, (NEAR, 1)),
-    (CROSS, 2, (CROSS, 1)), (BOTH, 1, (SIDE, 4)), (FAR, 4, (NEAR, 2)), (BOTH, 2, (CROSS, 2)),
-    (STACK, 3), (CROSS, 3, (BOTH, 1)), (PROJECT, 1, (NEAR, 1)), (CROSS, 4), (STACK, 4),
-    (PROJECT, 2), (BOTH, 4), (PROJECT, 3, (NEAR, 4)),
+    (ATTEND, 0), (ATTEND, 1), (STACK, 0), (ATTEND, 2), (FAR, 2), (STACK, 1, (FAR, 0)),
+    (BOTH, 0, (SIDE, 1), (SIDE, 2)), (CROSS, 0), (ATTEND, 3, (CROSS, 0)), (ATTEND, 4),
+    (CROSS, 1, (FAR, 1)), (PROJECT, 0, (SIDE, 3)), (FAR, 3, (NEAR, 1)), (STACK, 2),
+    (BOTH, 1, (SIDE, 4)), (NEAR, 2), (FAR, 4, (NEAR, 2)), (STACK, 3), (BOTH, 2, (CROSS, 2)),
+    (CROSS, 3), (PROJECT, 1, (FAR, 2)), (STACK, 4), (PROJECT, 2), (BOTH, 4, (NEAR, 0)),
+    (PROJECT, 3), (FINISH, 4),
 )
 LOCAL = pl.BlockSpec(memory_space=pltpu.VMEM)
 ANYWHERE = pl.BlockSpec(memory_space=pl.ANY)
@@ -150,10 +150,35 @@
     )(*(pltpu.with_memory_space_constraint(x, pltpu.HBM) for x in arrays))
 
 
-def prep_kernel(
-    owners, q_hbm, r_hbm, w_hbm, span_ref, valid_ref, lat_ref, bias_ref, q_ref, r_ref, w_ref, sem
-):
+def mask_kernel(owners, span_ref, valid_ref, bias_ref):
     tokens, keys = bias_ref.shape
+    per_shard = keys // len(owners)
+    me = lax.axis_index("ctx")
+    column = lax.broadcasted_iota(jnp.int32, (1, keys), 1)
+    place = jnp.full((1, keys), 2**30, jnp.int32)
+    for at, owner in enumerate(owners):
+        shard = me ^ owner
+        row = column - at * per_shard
+        here = (row >= 0) & (row < per_shard) & (row < valid_ref[shard])
+        place = jnp.where(here, row + shard * per_shard, place)
+    position = span_ref[0] + me * tokens + lax.broadcasted_iota(jnp.int32, (tokens, keys), 0)
+    bias_ref[...] = jnp.where(place <= position, F32(0.0), F32(MASKED))
+
+
+def mask(span_offset, valid_lengths, owners, tokens, per_shard):
+    return pl.pallas_call(
+        functools.partial(mask_kernel, owners),
+        in_specs=[SCALARS, SCALARS],
+        out_specs=LOCAL,
+        out_shape=pltpu.VMEM((tokens, per_shard * len(owners)), F32),
+        compiler_params=params(4),
+        cost_estimate=cost(0, 1024),
+        name="mask",
+    )(span_offset, valid_lengths)
+
+
+def prep_kernel(q_hbm, r_hbm, w_hbm, lat_ref, q_ref, r_ref, w_ref, sem):
+    tokens = q_ref.shape[0]
     heads, nope, latent = w_ref.shape
     rope = r_ref.shape[1] // heads
     whole = (
@@ -168,20 +193,6 @@
     ]
     for copy in (*whole, *pieces):
         copy.start()
-
-    per_shard = keys // len(owners)
-    me = lax.axis_index("ctx")
-    column = lax.broadcasted_iota(jnp.int32, (1, keys), 1)
-    place = jnp.full((1, keys), 2**30, jnp.int32)
-    for at, owner in enumerate(owners):
-        shard = me ^ owner
-        row = column - at * per_shard
-        here = (row >= 0) & (row < valid_ref[shard])
-        here = here & (row < per_shard)
-        place = jnp.where(here, row + shard * per_shard, place)
-    position = span_ref[0] + me * tokens + lax.broadcasted_iota(jnp.int32, (tokens, keys), 0)
-    bias_ref[...] = jnp.where(place <= position, F32(0.0), F32(MASKED))
-
     for copy in whole:
         copy.wait()
     for head in range(heads):
@@ -197,24 +208,21 @@
         lat_ref[rows, latent + rope :] = turned
 
 
-def prep(q_nope, q_rope, w_absorb, span_offset, valid_lengths, owners, per_shard):
+def prep(q_nope, q_rope, w_absorb):
     heads, _, latent = w_absorb.shape
     tokens = q_nope.shape[0]
     arrays = (q_nope, q_rope, w_absorb)
     return pl.pallas_call(
-        functools.partial(prep_kernel, owners),
-        in_specs=[ANYWHERE] * 3 + [SCALARS] * 2,
-        out_specs=[LOCAL] * 2,
-        out_shape=[
-            pltpu.VMEM((heads * tokens, latent + LANES), BF16),
-            pltpu.VMEM((tokens, per_shard * len(owners)), F32),
-        ],
+        prep_kernel,
+        in_specs=[ANYWHERE] * 3,
+        out_specs=LOCAL,
+        out_shape=pltpu.VMEM((heads * tokens, latent + LANES), BF16),
         scratch_shapes=[pltpu.VMEM(x.shape, x.dtype) for x in arrays]
         + [pltpu.SemaphoreType.DMA((2 + heads // STEP,))],
-        compiler_params=params(12),
+        compiler_params=params(10),
         cost_estimate=cost(0, 1024),
         name="prep",
-    )(*(pltpu.with_memory_space_constraint(x, pltpu.HBM) for x in arrays), span_offset, valid_lengths)
+    )(*(pltpu.with_memory_space_constraint(x, pltpu.HBM) for x in arrays))
 
 
 def join_kernel(groups, *refs):
@@ -323,18 +331,19 @@
 def attend(start, heads, queries, bias, w_value, kv, scale, after=()):
     tokens, keys = bias.shape
     value = w_value.shape[2]
+    block = next(count for count in (4, 3, 2, 1) if heads % count == 0) * tokens
     return pl.pallas_call(
         functools.partial(attend_kernel, scale * math.log2(math.e), start, heads),
         in_specs=[LOCAL] * 4 + [ANYWHERE] * len(after),
         out_specs=LOCAL,
         out_shape=pltpu.VMEM((tokens, heads * value), BF16),
         scratch_shapes=[
-            pltpu.VMEM((2, 2 * tokens, keys), F32),
-            pltpu.VMEM((2, 2 * tokens, keys), BF16),
-            pltpu.VMEM((2, 2 * tokens, 1), F32),
-            pltpu.VMEM((2 * tokens, w_value.shape[1]), BF16),
+            pltpu.VMEM((2, block, keys), F32),
+            pltpu.VMEM((2, block, keys), BF16),
+            pltpu.VMEM((2, block, 1), F32),
+            pltpu.VMEM((block, w_value.shape[1]), BF16),
         ],
-        compiler_params=params(12),
+        compiler_params=params(20),
         cost_estimate=cost(0, 1024),
         name=f"attend{start}",
     )(held(queries), held(bias), held(w_value), held(kv), *after)
@@ -361,32 +370,34 @@
     return [tuple(next(refs) for _ in range(size)) for size in sizes]
 
 
-def project_kernel(start, sizes, fresh, w_ref, *refs):
+def project_kernel(start, sizes, first, fresh, w_ref, *refs):
     out_ref, gathered = refs[-2:]
     parts = grouped(refs, sizes)
     tokens, depth = parts[0][0].shape[-2:]
     for side in range(2):
         gather_into(gathered.at[side], parts, side)
     weights = w_ref[start : start + depth]
-    each = 2 * tokens
+    each = min(2, len(parts)) * tokens
     for side in range(2):
         for row in range(0, len(parts) * tokens, each):
-            rows = slice(row, row + each)
+            rows = slice(row, min(row + each, len(parts) * tokens))
+            to = slice(first * tokens + rows.start, first * tokens + rows.stop)
             product = jnp.dot(gathered[side, rows], weights, preferred_element_type=F32)
-            out_ref[side, rows] = product if fresh else refs[sum(sizes)][side, rows] + product
-
-
-def project(start, parts, w_output, acc, after=()):
+            out_ref[side, to] = product if fresh else refs[sum(sizes)][side, to] + product
+
+
+def project(start, parts, w_output, acc, after=(), first=0):
     sizes = tuple(map(len, parts))
     blocks = [block for part in parts for block in part]
     tokens, depth = blocks[0].shape[-2:]
     columns = w_output.shape[1]
     operands = [w_output, *blocks] + ([] if acc is None else [acc])
-    return pl.pallas_call(
-        functools.partial(project_kernel, start, sizes, acc is None),
+    shape = (2, len(parts) * tokens, columns) if acc is None else acc.shape
+    return pl.pallas_call(
+        functools.partial(project_kernel, start, sizes, first, acc is None),
         in_specs=[LOCAL] * len(operands) + [ANYWHERE] * len(after),
         out_specs=LOCAL,
-        out_shape=pltpu.VMEM((2, len(parts) * tokens, columns), F32),
+        out_shape=pltpu.VMEM(shape, F32),
         scratch_shapes=[pltpu.VMEM((2, len(parts) * tokens, depth), BF16)],
         input_output_aliases={} if acc is None else {len(operands) - 1: 0},
         compiler_params=params(12),
@@ -395,40 +406,76 @@
     )(*map(held, operands), *after)
 
 
-def finish_kernel(start, keys, far, keep, sizes, w_ref, *refs):
-    groups = len(keys)
-    acc_ref, out_ref, gathered = refs[-3:]
+def other_half(groups, keep):
+    me, side = lax.axis_index("ctx"), lax.axis_index("head")
+    return ((me // groups) ^ side ^ (1 - keep)).astype(jnp.int32)
+
+
+def finish_kernel(start, sizes, first, w_ref, *refs):
+    given_ref, kept_ref, gathered = refs[-3:]
+    acc_ref = refs[sum(sizes)]
     parts = grouped(refs, sizes)
     tokens, depth = parts[0][0].shape[-2:]
-    me, side = lax.axis_index("ctx"), lax.axis_index("head")
-    other = ((me // groups) ^ side ^ (1 - keep)).astype(jnp.int32)
-    gather_into(gathered, parts, other)
-    product = jnp.dot(
-        gathered[...], w_ref[start : start + depth], preferred_element_type=F32
-    )
-    for at, key in enumerate(keys):
-        rows = slice(at * tokens, (at + 1) * tokens)
-        place = (me ^ key ^ (far * other)) % groups
-        to = pl.ds(pl.multiple_of(place * tokens, tokens), tokens)
-        out_ref[to, :] = (acc_ref[other, rows] + product[rows]).astype(out_ref.dtype)
-
-
-def finish(start, keys, far, keep, parts, w_output, acc, dtype):
+    rows = slice(first * tokens, (first + len(parts)) * tokens)
+    for keep, out_ref in enumerate((given_ref, kept_ref)):
+        other = other_half(acc_ref.shape[1] // tokens, keep)
+        gather_into(gathered.at[keep], parts, other)
+        product = jnp.dot(
+            gathered[keep], w_ref[start : start + depth], preferred_element_type=F32
+        )
+        out_ref[...] = (acc_ref[other, rows] + product).astype(out_ref.dtype)
+
+
+def finish(start, parts, w_output, acc, after=(), first=0):
     sizes = tuple(map(len, parts))
     blocks = [block for part in parts for block in part]
     tokens, depth = blocks[0].shape[-2:]
     columns = w_output.shape[1]
     rows = len(parts) * tokens
     return pl.pallas_call(
-        functools.partial(finish_kernel, start, keys, far, keep, sizes),
-        in_specs=[LOCAL] * (2 + len(blocks)),
-        out_specs=LOCAL,
-        out_shape=pltpu.VMEM((rows, columns), dtype),
-        scratch_shapes=[pltpu.VMEM((rows, depth), BF16)],
+        functools.partial(finish_kernel, start, sizes, first),
+        in_specs=[LOCAL] * (2 + len(blocks)) + [ANYWHERE] * len(after),
+        out_specs=[LOCAL] * 2,
+        out_shape=[pltpu.VMEM((rows, columns), BF16), pltpu.VMEM((rows, columns), F32)],
+        scratch_shapes=[pltpu.VMEM((2, rows, depth), BF16)],
         compiler_params=params(12),
         cost_estimate=cost(0, 1024),
-        name=f"finish{keep}",
-    )(*map(held, [w_output, *blocks, acc]))
+        name="finish",
+    )(*map(held, [w_output, *blocks, acc]), *after)
+
+
+def total_kernel(keys, far, groups, mine_ref, other_ref, *refs):
+    out_ref, rounded, sem = refs[-3:]
+    tokens = mine_ref.shape[0] // len(keys)
+    me = lax.axis_index("ctx")
+    other = other_half(groups, 1)
+    copies = []
+    for at, key in enumerate(keys):
+        rows = pl.ds(at * tokens, tokens)
+        place = (me ^ key ^ (far * other)) % groups
+        to = pl.ds(pl.multiple_of(place * tokens, tokens), tokens)
+        rounded[rows] = (mine_ref[rows] + other_ref[rows].astype(F32)).astype(BF16)
+        copies.append(pltpu.make_async_copy(rounded.at[rows], out_ref.at[to], sem.at[at]))
+        copies[-1].start()
+    for copy in copies:
+        copy.wait()
+
+
+def total(keys, far, groups, mine, other, out, after):
+    rows, columns = mine.shape
+    tokens = rows // len(keys)
+    given = [] if out is None else [out]
+    return pl.pallas_call(
+        functools.partial(total_kernel, keys, far, groups),
+        in_specs=[LOCAL] * 2 + [ANYWHERE] * (len(given) + len(after)),
+        out_specs=ANYWHERE,
+        out_shape=jax.ShapeDtypeStruct((groups * tokens, columns), BF16),
+        scratch_shapes=[pltpu.VMEM((rows, columns), BF16), pltpu.SemaphoreType.DMA((len(keys),))],
+        input_output_aliases={2: 0} if given else {},
+        compiler_params=params(4),
+        cost_estimate=cost(0, 1024),
+        name="total",
+    )(held(mine), held(other), *given, *after)
 
 
 def overlap(heads, starts, queries, bias, w_value, kv, w_output, scale):
@@ -478,15 +525,22 @@
             if PLAN[chunk][2]:
                 offer(SIDE, chunk, base, 1)
         elif action == PROJECT:
-            acc = project(starts[chunk] * value, parts_of(chunk), w_output, acc, after)
+            some = parts_of(chunk)[: 3 if chunk == len(heads) - 2 else 4]
+            acc = project(starts[chunk] * value, some, w_output, acc, after)
             last = [acc]
+        elif action == FINISH:
+            sums = [finish(starts[chunk] * value, parts_of(chunk)[:3], w_output, acc, after)]
+            last = [sums[0][1]]
         elif action == BOTH and PLAN[chunk][1:] == (1, 0):
             pair = stack(got[SIDE, chunk], got[CROSS, chunk], after)
             last = [pair]
             got[BOTH, chunk] = exchange(pair, 2, 8)
         else:
             send(action, chunk, after)
-    return parts_of(len(heads) - 1), acc
+    before, row = (start * value for start in starts[-2:])
+    rests = [parts_of(chunk)[3:] for chunk in range(len(heads))][-2:]
+    acc = project(before, rests[0], w_output, acc, last, 3)
+    return [*sums, finish(row, rests[1], w_output, acc, [acc], 3)]
 
 
 def local(
@@ -502,14 +556,13 @@
 
     far, *rest = basis_of(shards)
     keys = [0]
-    for mask in rest:
-        keys += [key ^ mask for key in keys]
+    for bit in rest:
+        keys += [key ^ bit for key in keys]
     keys = sorted(keys)
     owners = [key ^ (far * inner) for key in keys for inner in range(2)]
     packed = pack(latent_cache, rope_keys)
-    queries, bias = prep(
-        q_nope, q_rope, w_absorb, span_offset, valid_lengths, owners, per_shard
-    )
+    queries = prep(q_nope, q_rope, w_absorb)
+    bias = mask(span_offset, valid_lengths, owners, tokens, per_shard)
     mine = spread(packed, shards, [queries])
     theirs = {key: sibling(pair) for key, pair in mine.items()}
     kv = join([mine[key] for key in keys], [theirs[key] for key in keys], per_shard, latent + LANES)
@@ -517,7 +570,8 @@
     heads = [count * head_count // 32 for count, *_ in PLAN]
     starts = [sum(heads[:chunk]) for chunk in range(len(heads))]
     if shards == 8:
-        parts, acc = overlap(heads, starts, queries, bias, w_value, kv, w_output, scale)
+        sums = overlap(heads, starts, queries, bias, w_value, kv, w_output, scale)
+        split = (keys[:3], keys[3:])
     else:
         acc = None
         for chunk, start in enumerate(starts):
@@ -526,12 +580,15 @@
             parts = [(gathered[key],) for key in keys]
             if chunk < len(heads) - 1:
                 acc = project(start * value, parts, w_output, acc)
-    row = starts[-1] * value
-
-    given = finish(row, keys, far, 0, parts, w_output, acc, BF16)
-    other = sibling(given)
-    kept = finish(row, keys, far, 1, parts, w_output, acc, F32)
-    return (kept + other.astype(F32)).astype(BF16)
+        sums = [finish(starts[-1] * value, parts, w_output, acc)]
+        split = (keys,)
+
+    out, after = None, [sums[-1][1]]
+    others = [sibling(given) for given, _ in sums]
+    for some, (_, kept), other in zip(split, sums, others):
+        out = total(some, far, len(keys), kept, other, out, after)
+        after = []
+    return out
 
 
 def solution(mesh):

time: 129 us -> 135 us (1.047)
  starting transfers between devices: 39.1 us -> 46.2 us
  Pallas kernels: 37 us -> 38.4 us
    ppermute x29, starting transfers between devices: 38.5 us -> 45.6 us  [exchange(): return lax.ppermute(x, 'ctx', [(i, i ^ mask) for i in range(shards)])]
    ppermute x5 -> x6, waiting for transfers between devices: 2.77 us -> 0.66 us  [sibling(): return lax.ppermute(x, 'head', [(0, 1), (1, 0)])]
    pallas_call x7 -> x11, Pallas kernels: 15.9 us -> 17.9 us  [the longest x5 9.24 us: project(): pl.pallas_call(functools.partial(project_kernel, start, sizes, first, acc...]
    ppermute x29, waiting for transfers between devices: 47 us -> 48.7 us  [exchange(): return lax.ppermute(x, 'ctx', [(i, i ^ mask) for i in range(shards)])]
  transfers between devices with their start and end apart: 34 -> 35, of which waited for: 15 -> 17; matrix products, arithmetic and copies ran while one was open for 0% -> 0% of each run, Pallas kernels for 25% -> 25%
where the time goes in v7:
time: 135 us
  waiting for transfers between devices  49.4 us (37%)
  starting transfers between devices  46.2 us (34%)
  Pallas kernels  38.4 us (28%)
    ppermute x29, waiting for transfers between devices, exchange(): return lax.ppermute(x, 'ctx', [(i, i ^ mask) for i in range(shards)])  48.7 us
    ppermute x29, starting transfers between devices, exchange(): return lax.ppermute(x, 'ctx', [(i, i ^ mask) for i in range(shards)])  45.6 us
    pallas_call x5, Pallas kernels, attend(): pl.pallas_call(functools.partial(attend_kernel, scale * math.log2(math.e)...  18.6 us
    pallas_call x5, Pallas kernels, project(): pl.pallas_call(functools.partial(project_kernel, start, sizes, first, acc...  9.24 us
    pallas_call x1, Pallas kernels, prep(): pl.pallas_call(prep_kernel, in_specs=[ANYWHERE] * 3, out_specs=LOCAL, out...  3.89 us
  transfers between devices with their start and end apart: 35, of which 17 were waited for; matrix products, arithmetic and copies ran while one was open for 0% of the time, Pallas kernels for 25%

profile of v7, /device:TPU:0, one launch (start us, length us, event | category | flops | bytes accessed | tf_op | source)
XLA Modules:
  0.0 135.3 jit_solution(17105054181024022406)
XLA Ops:
  1.1 5.1 %collective-permute-start = (bf16[336,128]{1,0:T(8,128)(2,1)S(1)}, bf16[336,128]{1,0:T(8,128)(2,1)S(1)}, u32[]{:S(2)}, u32[]{:S(2)}) collective-permute-start(bf16[336,128]{1,0:T(8,128)(2,1)S(1)} %pack.1.first_ref), channel_id=1, source_target_pairs={{0,12},{2,14},{4,8},{6,10},{8,4},{10,6},{12,0},{14,2},{1,13},{3,15... | collective-permute-start | bytes 258056 | tf_op jit(solution)/shard_map/ppermute | solution.py:53
  6.2 3.9 %prep.1.refs_0_.q_ref = bf16[4096,640]{1,0:T(8,128)(2,1)S(1)} custom-call(bf16[128,4096]{1,0:T(8,128)(2,1)} %q_hbm.1, bf16[128,2048]{1,0:T(8,128)(2,1)} %r_hbm.1, bf16[32,128,512]{2,1,0:T(8,128)(2,1)} %w_hbm.1), custom_call_target="tpu_custom_call" | custom-call | bytes 1024 | tf_op jit(solution)/shard_map/prep/pallas_call | solution.py:215
  11.9 4.2 %collective-permute-done.2.refs_2_ = bf16[2,336,128]{2,1,0:T(8,128)(2,1)S(1)} collective-permute-done((bf16[2,336,128]{2,1,0:T(8,128)(2,1)S(1)}, bf16[2,336,128]{2,1,0:T(8,128)(2,1)S(1)}, u32[]{:S(2)}, u32[]{:S(2)}) %collective-permute-start.2) | collective-permute-done | bytes 172064 | tf_op jit(solution)/shard_map/ppermute | solution.py:53
  18.1 3.4 %collective-permute-done.3.refs_3_ = bf16[2,336,128]{2,1,0:T(8,128)(2,1)S(1)} collective-permute-done((bf16[2,336,128]{2,1,0:T(8,128)(2,1)S(1)}, bf16[2,336,128]{2,1,0:T(8,128)(2,1)S(1)}, u32[]{:S(2)}, u32[]{:S(2)}) %collective-permute-start.3) | collective-permute-done | bytes 172064 | tf_op jit(solution)/shard_map/ppermute | solution.py:53
  23.4 2.6 %attend0.1.refs_0_.first_ref = bf16[128,512]{1,0:T(8,128)(2,1)S(1)} custom-call(bf16[4096,640]{1,0:T(8,128)(2,1)S(1)} %prep.1.refs_0_.q_ref, f32[128,1152]{1,0:T(8,128)S(1)} %mask.1.bias_ref, bf16[32,512,128]{2,1,0:T(8,128)(2,1)S(1)} %copy-done, bf16[1152,640]{1,0:T(8,128)(2,1)S(1)} %join.1.kv_ref), custom_call_target="tpu_custom_call" | custom-call | bytes 1024 | tf_op jit(solution)/shard_map/attend0/pallas_call | solution.py:335
  26.0 1.9 %collective-permute-start.8 = (bf16[128,512]{1,0:T(8,128)(2,1)S(1)}, bf16[128,512]{1,0:T(8,128)(2,1)S(1)}, u32[]{:S(2)}, u32[]{:S(2)}) collective-permute-start(bf16[128,512]{1,0:T(8,128)(2,1)S(1)} %attend0.1.refs_0_.first_ref), channel_id=1, source_target_pairs={{0,12},{2,14},{4,8},{6,10},{8,4},{10,6},{12,0},{14,2},{1,13},{3,15... | collective-permute-start | bytes 393224 | tf_op jit(solution)/shard_map/ppermute | solution.py:53
  27.9 4.4 %attend4.1.refs_0_.first_ref = bf16[128,1024]{1,0:T(8,128)(2,1)S(1)} custom-call(bf16[4096,640]{1,0:T(8,128)(2,1)S(1)} %prep.1.refs_0_.q_ref, f32[128,1152]{1,0:T(8,128)S(1)} %mask.1.bias_ref, bf16[32,512,128]{2,1,0:T(8,128)(2,1)S(1)} %copy-done, bf16[1152,640]{1,0:T(8,128)(2,1)S(1)} %join.1.kv_ref, bf16[128,512]{1,0:T(8,128)(2,1)S(1)} %attend0.1.refs_0_.first_ref), custom_call_target="tpu_custom_call" | custom-call | bytes 1024 | tf_op jit(solution)/shard_map/attend4/pallas_call | solution.py:335
  32.4 2.0 %collective-permute-start.10 = (bf16[128,1024]{1,0:T(8,128)(2,1)S(1)}, bf16[128,1024]{1,0:T(8,128)(2,1)S(1)}, u32[]{:S(2)}, u32[]{:S(2)}) collective-permute-start(bf16[128,1024]{1,0:T(8,128)(2,1)S(1)} %attend4.1.refs_0_.first_ref), channel_id=1, source_target_pairs={{0,12},{2,14},{4,8},{6,10},{8,4},{10,6},{12,0},{14,2},{1,13},{3,15... | collective-permute-start | bytes 786440 | tf_op jit(solution)/shard_map/ppermute | solution.py:53
  36.0 3.5 %attend12.1.x_ref.refs_0_.first_ref = bf16[128,768]{1,0:T(8,128)(2,1)S(1)} custom-call(bf16[4096,640]{1,0:T(8,128)(2,1)S(1)} %prep.1.refs_0_.q_ref, f32[128,1152]{1,0:T(8,128)S(1)} %mask.1.bias_ref, bf16[32,512,128]{2,1,0:T(8,128)(2,1)S(1)} %copy-done, bf16[1152,640]{1,0:T(8,128)(2,1)S(1)} %join.1.kv_ref, bf16[2,128,512]{2,1,0:T(8,128)(2,1)S(1)} %stack.8.refs_0_), custom_call_target="tpu_custom_call" | custom-call | bytes 1024 | tf_op jit(solution)/shard_map/attend12/pallas_call | solution.py:335
  40.4 3.0 %collective-permute-done.10.second_ref.x_ref.refs_1_ = bf16[128,1024]{1,0:T(8,128)(2,1)S(1)} collective-permute-done((bf16[128,1024]{1,0:T(8,128)(2,1)S(1)}, bf16[128,1024]{1,0:T(8,128)(2,1)S(1)}, u32[]{:S(2)}, u32[]{:S(2)}) %collective-permute-start.10) | collective-permute-done | bytes 262176 | tf_op jit(solution)/shard_map/ppermute | solution.py:53
  43.5 2.8 %collective-permute-start.19 = (bf16[2,128,1024]{2,1,0:T(8,128)(2,1)S(1)}, bf16[2,128,1024]{2,1,0:T(8,128)(2,1)S(1)}, u32[]{:S(2)}, u32[]{:S(2)}) collective-permute-start(bf16[2,128,1024]{2,1,0:T(8,128)(2,1)S(1)} %stack.9.refs_0_), channel_id=1, source_target_pairs={{0,4},{2,6},{4,0},{6,2},{8,12},{10,14},{12,8},{14,10},{1,5},{3,7},... | collective-permute-start | bytes 1572872 | tf_op jit(solution)/shard_map/ppermute | solution.py:53
  52.1 2.8 %collective-permute-done.13.refs_1_.refs_3_ = bf16[128,512]{1,0:T(8,128)(2,1)S(1)} collective-permute-done((bf16[128,512]{1,0:T(8,128)(2,1)S(1)}, bf16[128,512]{1,0:T(8,128)(2,1)S(1)}, u32[]{:S(2)}, u32[]{:S(2)}) %collective-permute-start.13) | collective-permute-done | bytes 131104 | tf_op jit(solution)/shard_map/ppermute | solution.py:53
  54.9 4.7 %attend18.1.refs_0_.x_ref.first_ref = bf16[128,1024]{1,0:T(8,128)(2,1)S(1)} custom-call(bf16[4096,640]{1,0:T(8,128)(2,1)S(1)} %prep.1.refs_0_.q_ref, f32[128,1152]{1,0:T(8,128)S(1)} %mask.1.bias_ref, bf16[32,512,128]{2,1,0:T(8,128)(2,1)S(1)} %copy-done, bf16[1152,640]{1,0:T(8,128)(2,1)S(1)} %join.1.kv_ref, bf16[128,512]{1,0:T(8,128)(2,1)S(1)} %gate.12.refs_0_, ...), custom_call_target="tpu_custom_call" | custom-call | bytes 1024 | tf_op jit(solution)/shard_map/attend18/pallas_call | solution.py:335
  61.2 1.9 %collective-permute-start.15 = (bf16[128,768]{1,0:T(8,128)(2,1)S(1)}, bf16[128,768]{1,0:T(8,128)(2,1)S(1)}, u32[]{:S(2)}, u32[]{:S(2)}) collective-permute-start(bf16[128,768]{1,0:T(8,128)(2,1)S(1)} %gate.10.refs_0_), channel_id=1, source_target_pairs={{0,12},{2,14},{4,8},{6,10},{8,4},{10,6},{12,0},{14,2},{1,13},{3,15... | collective-permute-start | bytes 589832 | tf_op jit(solution)/shard_map/ppermute | solution.py:53
  63.1 3.4 %attend26.1.refs_0_.x_ref.first_ref = bf16[128,768]{1,0:T(8,128)(2,1)S(1)} custom-call(bf16[4096,640]{1,0:T(8,128)(2,1)S(1)} %prep.1.refs_0_.q_ref, f32[128,1152]{1,0:T(8,128)S(1)} %mask.1.bias_ref, bf16[32,512,128]{2,1,0:T(8,128)(2,1)S(1)} %copy-done, bf16[1152,640]{1,0:T(8,128)(2,1)S(1)} %join.1.kv_ref, bf16[128,1024]{1,0:T(8,128)(2,1)S(1)} %attend18.1.refs_0_.x_ref.first_ref), custom_call_target="tpu_custom_call" | custom-call | bytes 1024 | tf_op jit(solution)/shard_map/attend26/pallas_call | solution.py:335
  67.2 1.8 %collective-permute-done.18.refs_7_.refs_2_ = bf16[128,1024]{1,0:T(8,128)(2,1)S(1)} collective-permute-done((bf16[128,1024]{1,0:T(8,128)(2,1)S(1)}, bf16[128,1024]{1,0:T(8,128)(2,1)S(1)}, u32[]{:S(2)}, u32[]{:S(2)}) %collective-permute-start.18) | collective-permute-done | bytes 262176 | tf_op jit(solution)/shard_map/ppermute | solution.py:53
  70.3 2.0 %collective-permute-done.14.refs_1_.first_ref.refs_2_ = bf16[128,768]{1,0:T(8,128)(2,1)S(1)} collective-permute-done((bf16[128,768]{1,0:T(8,128)(2,1)S(1)}, bf16[128,768]{1,0:T(8,128)(2,1)S(1)}, u32[]{:S(2)}, u32[]{:S(2)}) %collective-permute-start.14) | collective-permute-done | bytes 196640 | tf_op jit(solution)/shard_map/ppermute | solution.py:53
  73.9 1.9 %collective-permute-start.24 = (bf16[128,1024]{1,0:T(8,128)(2,1)S(1)}, bf16[128,1024]{1,0:T(8,128)(2,1)S(1)}, u32[]{:S(2)}, u32[]{:S(2)}) collective-permute-start(bf16[128,1024]{1,0:T(8,128)(2,1)S(1)} %gate.14.refs_0_), channel_id=1, source_target_pairs={{0,12},{2,14},{4,8},{6,10},{8,4},{10,6},{12,0},{14,2},{1,13},{3,15... | collective-permute-start | bytes 786440 | tf_op jit(solution)/shard_map/ppermute | solution.py:53
  77.8 6.1 %collective-permute-done.20.refs_1_.x_ref.refs_4_ = bf16[2,128,768]{2,1,0:T(8,128)(2,1)S(1)} collective-permute-done((bf16[2,128,768]{2,1,0:T(8,128)(2,1)S(1)}, bf16[2,128,768]{2,1,0:T(8,128)(2,1)S(1)}, u32[]{:S(2)}, u32[]{:S(2)}) %collective-permute-start.20) | collective-permute-done | bytes 393248 | tf_op jit(solution)/shard_map/ppermute | solution.py:53
  83.9 2.2 %collective-permute-start.21 = (bf16[128,768]{1,0:T(8,128)(2,1)S(1)}, bf16[128,768]{1,0:T(8,128)(2,1)S(1)}, u32[]{:S(2)}, u32[]{:S(2)}) collective-permute-start(bf16[128,768]{1,0:T(8,128)(2,1)S(1)} %gate.17.refs_0_), channel_id=1, source_target_pairs={{0,12},{2,14},{4,8},{6,10},{8,4},{10,6},{12,0},{14,2},{1,13},{3,15... | collective-permute-start | bytes 589832 | tf_op jit(solution)/shard_map/ppermute | solution.py:53
  86.1 3.9 %collective-permute-done.24.second_ref.x_ref.refs_1_ = bf16[128,1024]{1,0:T(8,128)(2,1)S(1)} collective-permute-done((bf16[128,1024]{1,0:T(8,128)(2,1)S(1)}, bf16[128,1024]{1,0:T(8,128)(2,1)S(1)}, u32[]{:S(2)}, u32[]{:S(2)}) %collective-permute-start.24) | collective-permute-done | bytes 262176 | tf_op jit(solution)/shard_map/ppermute | solution.py:53
  90.1 3.6 %collective-permute-start.29 = (bf16[2,128,1024]{2,1,0:T(8,128)(2,1)S(1)}, bf16[2,128,1024]{2,1,0:T(8,128)(2,1)S(1)}, u32[]{:S(2)}, u32[]{:S(2)}) collective-permute-start(bf16[2,128,1024]{2,1,0:T(8,128)(2,1)S(1)} %stack.11.refs_0_), channel_id=1, source_target_pairs={{0,4},{2,6},{4,0},{6,2},{8,12},{10,14},{12,8},{14,10},{1,5},{3,7},... | collective-permute-start | bytes 1572872 | tf_op jit(solution)/shard_map/ppermute | solution.py:53
  94.6 1.8 %collective-permute-start.25 = (bf16[2,128,768]{2,1,0:T(8,128)(2,1)S(1)}, bf16[2,128,768]{2,1,0:T(8,128)(2,1)S(1)}, u32[]{:S(2)}, u32[]{:S(2)}) collective-permute-start(bf16[2,128,768]{2,1,0:T(8,128)(2,1)S(1)} %gate.18.refs_0_), channel_id=1, source_target_pairs={{0,2},{2,0},{4,6},{6,4},{8,10},{10,8},{12,14},{14,12},{1,3},{3,1},... | collective-permute-start | bytes 1179656 | tf_op jit(solution)/shard_map/ppermute | solution.py:53
  96.4 2.8 %project512.1.refs_0_.refs_6_ = f32[2,512,896]{2,1,0:T(8,128)S(1)} custom-call(bf16[4096,896]{1,0:T(8,128)(2,1)S(1)} %bitcast.2, bf16[128,1024]{1,0:T(8,128)(2,1)S(1)} %attend4.1.refs_0_.first_ref, bf16[128,1024]{1,0:T(8,128)(2,1)S(1)} %collective-permute-done.10.second_ref.x_ref.refs_1_, ...), custom_call_target="tpu_custom_call", output_to_operand_aliasing={{}: (7, {})} | custom-call | bytes 1024 | tf_op jit(solution)/shard_map/project512/pallas_call | solution.py:396
  103.0 2.3 %collective-permute-done.29.refs_4_ = bf16[2,128,1024]{2,1,0:T(8,128)(2,1)S(1)} collective-permute-done((bf16[2,128,1024]{2,1,0:T(8,128)(2,1)S(1)}, bf16[2,128,1024]{2,1,0:T(8,128)(2,1)S(1)}, u32[]{:S(2)}, u32[]{:S(2)}) %collective-permute-start.29) | collective-permute-done | bytes 524320 | tf_op jit(solution)/shard_map/ppermute | solution.py:53
  106.7 2.2 %project1536.1.refs_0_.refs_5_ = f32[2,512,896]{2,1,0:T(8,128)S(1)} custom-call(bf16[4096,896]{1,0:T(8,128)(2,1)S(1)} %bitcast.2, bf16[128,768]{1,0:T(8,128)(2,1)S(1)} %attend12.1.x_ref.refs_0_.first_ref, bf16[128,768]{1,0:T(8,128)(2,1)S(1)} %collective-permute-done.15.second_ref.refs_8_.refs_1_, ...), custom_call_target="tpu_custom_call", output_to_operand_aliasing={{}: (7, {})} | custom-call | bytes 1024 | tf_op jit(solution)/shard_map/project1536/pallas_call | solution.py:396
  108.9 7.3 %collective-permute-done.22.second_ref.refs_3_ = bf16[128,768]{1,0:T(8,128)(2,1)S(1)} collective-permute-done((bf16[128,768]{1,0:T(8,128)(2,1)S(1)}, bf16[128,768]{1,0:T(8,128)(2,1)S(1)}, u32[]{:S(2)}, u32[]{:S(2)}) %collective-permute-start.22) | collective-permute-done | bytes 196640 | tf_op jit(solution)/shard_map/ppermute | solution.py:53
  116.2 2.2 %project2304.2.refs_5_.refs_6_.refs_1_ = f32[2,512,896]{2,1,0:T(8,128)S(1)} custom-call(bf16[4096,896]{1,0:T(8,128)(2,1)S(1)} %bitcast.2, bf16[128,1024]{1,0:T(8,128)(2,1)S(1)} %attend18.1.refs_0_.x_ref.first_ref, bf16[128,1024]{1,0:T(8,128)(2,1)S(1)} %collective-permute-done.24.second_ref.x_ref.refs_1_, ...), custom_call_target="tpu_custom_call", output_to_operand_aliasing={{}: (6, {})} | custom-call | bytes 1024 | tf_op jit(solution)/shard_map/project2304/pallas_call | solution.py:396
  118.4 1.9 %finish.2 = (bf16[384,896]{1,0:T(8,128)(2,1)S(1)}, f32[384,896]{1,0:T(8,128)S(1)}) custom-call(bf16[4096,896]{1,0:T(8,128)(2,1)S(1)} %bitcast.2, bf16[128,768]{1,0:T(8,128)(2,1)S(1)} %attend26.1.refs_0_.x_ref.first_ref, bf16[128,768]{1,0:T(8,128)(2,1)S(1)} %collective-permute-done.21.second_ref.refs_1_, ...), custom_call_target="tpu_custom_call" | custom-call | bytes 1024 | tf_op jit(solution)/shard_map/finish/pallas_call | solution.py:435
  120.4 2.1 %collective-permute-start.28 = (bf16[2,128,768]{2,1,0:T(8,128)(2,1)S(1)}, bf16[2,128,768]{2,1,0:T(8,128)(2,1)S(1)}, u32[]{:S(2)}, u32[]{:S(2)}) collective-permute-start(bf16[2,128,768]{2,1,0:T(8,128)(2,1)S(1)} %stack.13.refs_6_), channel_id=1, source_target_pairs={{0,4},{2,6},{4,0},{6,2},{8,12},{10,14},{12,8},{14,10},{1,5},{3,7},... | collective-permute-start | bytes 1179656 | tf_op jit(solution)/shard_map/ppermute | solution.py:53
  122.5 2.1 %collective-permute-done.30.refs_0_ = bf16[2,128,1024]{2,1,0:T(8,128)(2,1)S(1)} collective-permute-done((bf16[2,128,1024]{2,1,0:T(8,128)(2,1)S(1)}, bf16[2,128,1024]{2,1,0:T(8,128)(2,1)S(1)}, u32[]{:S(2)}, u32[]{:S(2)}) %collective-permute-start.30) | collective-permute-done | bytes 524320 | tf_op jit(solution)/shard_map/ppermute | solution.py:53
  125.4 6.8 %collective-permute-done.28.refs_0_ = bf16[2,128,768]{2,1,0:T(8,128)(2,1)S(1)} collective-permute-done((bf16[2,128,768]{2,1,0:T(8,128)(2,1)S(1)}, bf16[2,128,768]{2,1,0:T(8,128)(2,1)S(1)}, u32[]{:S(2)}, u32[]{:S(2)}) %collective-permute-start.28) | collective-permute-done | bytes 393248 | tf_op jit(solution)/shard_map/ppermute | solution.py:53
  (82 shorter events, 31.4 us)
Async XLA Ops:
  1.1 9.0 %collective-permute-start = (bf16[336,128]{1,0:T(8,128)(2,1)S(1)}, bf16[336,128]{1,0:T(8,128)(2,1)S(1)}, u32[]{:S(2)}, u32[]{:S(2)}) collective-permute-start(bf16[336,128]{1,0:T(8,128)(2,1)S(1)} %pack.1.first_ref), channel_id=1, source_target_pairs={{0,12},{2,14},{4,8},{6,10},{8,4},{10,6},{12,0},{14,2},{1,13},{3,15... | collective-permute-start | bytes 258056 | tf_op jit(solution)/shard_map/ppermute | solution.py:53
  10.2 5.9 %collective-permute-start.2 = (bf16[2,336,128]{2,1,0:T(8,128)(2,1)S(1)}, bf16[2,336,128]{2,1,0:T(8,128)(2,1)S(1)}, u32[]{:S(2)}, u32[]{:S(2)}) collective-permute-start(bf16[2,336,128]{2,1,0:T(8,128)(2,1)S(1)} %stack.7.refs_0_), channel_id=1, source_target_pairs={{0,4},{2,6},{4,0},{6,2},{8,12},{10,14},{12,8},{14,10},{1,5},{3,7},... | collective-permute-start | bytes 516104 | tf_op jit(solution)/shard_map/ppermute | solution.py:53
  10.4 7.7 %collective-permute-start.1 = (bf16[2,336,128]{2,1,0:T(8,128)(2,1)S(1)}, bf16[2,336,128]{2,1,0:T(8,128)(2,1)S(1)}, u32[]{:S(2)}, u32[]{:S(2)}) collective-permute-start(bf16[2,336,128]{2,1,0:T(8,128)(2,1)S(1)} %stack.7.refs_0_), channel_id=1, source_target_pairs={{0,2},{2,0},{4,6},{6,4},{8,10},{10,8},{12,14},{14,12},{1,3},{3,1},... | collective-permute-start | bytes 516104 | tf_op jit(solution)/shard_map/ppermute | solution.py:53
  16.1 5.4 %collective-permute-start.3 = (bf16[2,336,128]{2,1,0:T(8,128)(2,1)S(1)}, bf16[2,336,128]{2,1,0:T(8,128)(2,1)S(1)}, u32[]{:S(2)}, u32[]{:S(2)}) collective-permute-start(bf16[2,336,128]{2,1,0:T(8,128)(2,1)S(1)} %collective-permute-done.2.refs_2_), channel_id=1, source_target_pairs={{0,2},{2,0},{4,6},{6,4},{8,10},{10,8},{12,14},{14,12},{1,3},{3,1},... | collective-permute-start | bytes 516104 | tf_op jit(solution)/shard_map/ppermute | solution.py:53
  17.6 5.2 %collective-permute-start.4 = (bf16[2,336,128]{2,1,0:T(8,128)(2,1)S(1)}, bf16[2,336,128]{2,1,0:T(8,128)(2,1)S(1)}, u32[]{:S(2)}, u32[]{:S(2)}) collective-permute-start(bf16[2,336,128]{2,1,0:T(8,128)(2,1)S(1)} %stack.7.refs_0_), channel_id=1, source_target_pairs={{0,1},{1,0},{2,3},{3,2},{4,5},{5,4},{6,7},{7,6},{8,9},{9,8},{10,11... | collective-permute-start | bytes 516104 | tf_op jit(solution)/shard_map/ppermute | solution.py:57
  17.6 5.2 %collective-permute-start.6 = (bf16[2,336,128]{2,1,0:T(8,128)(2,1)S(1)}, bf16[2,336,128]{2,1,0:T(8,128)(2,1)S(1)}, u32[]{:S(2)}, u32[]{:S(2)}) collective-permute-start(bf16[2,336,128]{2,1,0:T(8,128)(2,1)S(1)} %collective-permute-done.2.refs_2_), channel_id=1, source_target_pairs={{0,1},{1,0},{2,3},{3,2},{4,5},{5,4},{6,7},{7,6},{8,9},{9,8},{10,11... | collective-permute-start | bytes 516104 | tf_op jit(solution)/shard_map/ppermute | solution.py:57
  26.0 9.9 %collective-permute-start.8 = (bf16[128,512]{1,0:T(8,128)(2,1)S(1)}, bf16[128,512]{1,0:T(8,128)(2,1)S(1)}, u32[]{:S(2)}, u32[]{:S(2)}) collective-permute-start(bf16[128,512]{1,0:T(8,128)(2,1)S(1)} %attend0.1.refs_0_.first_ref), channel_id=1, source_target_pairs={{0,12},{2,14},{4,8},{6,10},{8,4},{10,6},{12,0},{14,2},{1,13},{3,15... | collective-permute-start | bytes 393224 | tf_op jit(solution)/shard_map/ppermute | solution.py:53
  32.4 11.1 %collective-permute-start.10 = (bf16[128,1024]{1,0:T(8,128)(2,1)S(1)}, bf16[128,1024]{1,0:T(8,128)(2,1)S(1)}, u32[]{:S(2)}, u32[]{:S(2)}) collective-permute-start(bf16[128,1024]{1,0:T(8,128)(2,1)S(1)} %attend4.1.refs_0_.first_ref), channel_id=1, source_target_pairs={{0,12},{2,14},{4,8},{6,10},{8,4},{10,6},{12,0},{14,2},{1,13},{3,15... | collective-permute-start | bytes 786440 | tf_op jit(solution)/shard_map/ppermute | solution.py:53
  34.4 12.0 %collective-permute-start.11 = (bf16[128,1024]{1,0:T(8,128)(2,1)S(1)}, bf16[128,1024]{1,0:T(8,128)(2,1)S(1)}, u32[]{:S(2)}, u32[]{:S(2)}) collective-permute-start(bf16[128,1024]{1,0:T(8,128)(2,1)S(1)} %attend4.1.refs_0_.first_ref), channel_id=1, source_target_pairs={{0,2},{2,0},{4,6},{6,4},{8,10},{10,8},{12,14},{14,12},{1,3},{3,1},... | collective-permute-start | bytes 786440 | tf_op jit(solution)/shard_map/ppermute | solution.py:53
  35.9 12.5 %collective-permute-start.9 = (bf16[2,128,512]{2,1,0:T(8,128)(2,1)S(1)}, bf16[2,128,512]{2,1,0:T(8,128)(2,1)S(1)}, u32[]{:S(2)}, u32[]{:S(2)}) collective-permute-start(bf16[2,128,512]{2,1,0:T(8,128)(2,1)S(1)} %stack.8.refs_0_), channel_id=1, source_target_pairs={{0,4},{2,6},{4,0},{6,2},{8,12},{10,14},{12,8},{14,10},{1,5},{3,7},... | collective-permute-start | bytes 786440 | tf_op jit(solution)/shard_map/ppermute | solution.py:53
  39.4 7.2 %collective-permute-start.12 = (bf16[128,768]{1,0:T(8,128)(2,1)S(1)}, bf16[128,768]{1,0:T(8,128)(2,1)S(1)}, u32[]{:S(2)}, u32[]{:S(2)}) collective-permute-start(bf16[128,768]{1,0:T(8,128)(2,1)S(1)} %attend12.1.x_ref.refs_0_.first_ref), channel_id=1, source_target_pairs={{0,2},{2,0},{4,6},{6,4},{8,10},{10,8},{12,14},{14,12},{1,3},{3,1},... | collective-permute-start | bytes 589832 | tf_op jit(solution)/shard_map/ppermute | solution.py:53
  43.5 26.7 %collective-permute-start.19 = (bf16[2,128,1024]{2,1,0:T(8,128)(2,1)S(1)}, bf16[2,128,1024]{2,1,0:T(8,128)(2,1)S(1)}, u32[]{:S(2)}, u32[]{:S(2)}) collective-permute-start(bf16[2,128,1024]{2,1,0:T(8,128)(2,1)S(1)} %stack.9.refs_0_), channel_id=1, source_target_pairs={{0,4},{2,6},{4,0},{6,2},{8,12},{10,14},{12,8},{14,10},{1,5},{3,7},... | collective-permute-start | bytes 1572872 | tf_op jit(solution)/shard_map/ppermute | solution.py:53
  48.4 6.4 %collective-permute-start.13 = (bf16[128,512]{1,0:T(8,128)(2,1)S(1)}, bf16[128,512]{1,0:T(8,128)(2,1)S(1)}, u32[]{:S(2)}, u32[]{:S(2)}) collective-permute-start(bf16[128,512]{1,0:T(8,128)(2,1)S(1)} %gate.12.refs_0_), channel_id=1, source_target_pairs={{0,2},{2,0},{4,6},{6,4},{8,10},{10,8},{12,14},{14,12},{1,3},{3,1},... | collective-permute-start | bytes 393224 | tf_op jit(solution)/shard_map/ppermute | solution.py:53
  50.1 16.5 %collective-permute-start.16 = (bf16[128,512]{1,0:T(8,128)(2,1)S(1)}, bf16[128,512]{1,0:T(8,128)(2,1)S(1)}, u32[]{:S(2)}, u32[]{:S(2)}) collective-permute-start(bf16[128,512]{1,0:T(8,128)(2,1)S(1)} %attend0.1.refs_0_.first_ref), channel_id=1, source_target_pairs={{0,2},{2,0},{4,6},{6,4},{8,10},{10,8},{12,14},{14,12},{1,3},{3,1},... | collective-permute-start | bytes 393224 | tf_op jit(solution)/shard_map/ppermute | solution.py:53
  50.5 16.6 %collective-permute-start.17 = (bf16[2,128,512]{2,1,0:T(8,128)(2,1)S(1)}, bf16[2,128,512]{2,1,0:T(8,128)(2,1)S(1)}, u32[]{:S(2)}, u32[]{:S(2)}) collective-permute-start(bf16[2,128,512]{2,1,0:T(8,128)(2,1)S(1)} %gate.11.refs_0_), channel_id=1, source_target_pairs={{0,2},{2,0},{4,6},{6,4},{8,10},{10,8},{12,14},{14,12},{1,3},{3,1},... | collective-permute-start | bytes 786440 | tf_op jit(solution)/shard_map/ppermute | solution.py:53
  59.6 9.4 %collective-permute-start.18 = (bf16[128,1024]{1,0:T(8,128)(2,1)S(1)}, bf16[128,1024]{1,0:T(8,128)(2,1)S(1)}, u32[]{:S(2)}, u32[]{:S(2)}) collective-permute-start(bf16[128,1024]{1,0:T(8,128)(2,1)S(1)} %attend18.1.refs_0_.x_ref.first_ref), channel_id=1, source_target_pairs={{0,2},{2,0},{4,6},{6,4},{8,10},{10,8},{12,14},{14,12},{1,3},{3,1},... | collective-permute-start | bytes 786440 | tf_op jit(solution)/shard_map/ppermute | solution.py:53
  61.2 9.1 %collective-permute-start.15 = (bf16[128,768]{1,0:T(8,128)(2,1)S(1)}, bf16[128,768]{1,0:T(8,128)(2,1)S(1)}, u32[]{:S(2)}, u32[]{:S(2)}) collective-permute-start(bf16[128,768]{1,0:T(8,128)(2,1)S(1)} %gate.10.refs_0_), channel_id=1, source_target_pairs={{0,12},{2,14},{4,8},{6,10},{8,4},{10,6},{12,0},{14,2},{1,13},{3,15... | collective-permute-start | bytes 589832 | tf_op jit(solution)/shard_map/ppermute | solution.py:53
  66.6 5.7 %collective-permute-start.14 = (bf16[128,768]{1,0:T(8,128)(2,1)S(1)}, bf16[128,768]{1,0:T(8,128)(2,1)S(1)}, u32[]{:S(2)}, u32[]{:S(2)}) collective-permute-start(bf16[128,768]{1,0:T(8,128)(2,1)S(1)} %attend26.1.refs_0_.x_ref.first_ref), channel_id=1, source_target_pairs={{0,2},{2,0},{4,6},{6,4},{8,10},{10,8},{12,14},{14,12},{1,3},{3,1},... | collective-permute-start | bytes 589832 | tf_op jit(solution)/shard_map/ppermute | solution.py:53
  72.4 11.6 %collective-permute-start.20 = (bf16[2,128,768]{2,1,0:T(8,128)(2,1)S(1)}, bf16[2,128,768]{2,1,0:T(8,128)(2,1)S(1)}, u32[]{:S(2)}, u32[]{:S(2)}) collective-permute-start(bf16[2,128,768]{2,1,0:T(8,128)(2,1)S(1)} %gate.16.refs_0_), channel_id=1, source_target_pairs={{0,4},{2,6},{4,0},{6,2},{8,12},{10,14},{12,8},{14,10},{1,5},{3,7},... | collective-permute-start | bytes 1179656 | tf_op jit(solution)/shard_map/ppermute | solution.py:53
  72.4 24.0 %collective-permute-start.27 = (bf16[2,128,1024]{2,1,0:T(8,128)(2,1)S(1)}, bf16[2,128,1024]{2,1,0:T(8,128)(2,1)S(1)}, u32[]{:S(2)}, u32[]{:S(2)}) collective-permute-start(bf16[2,128,1024]{2,1,0:T(8,128)(2,1)S(1)} %gate.15.refs_0_), channel_id=1, source_target_pairs={{0,2},{2,0},{4,6},{6,4},{8,10},{10,8},{12,14},{14,12},{1,3},{3,1},... | collective-permute-start | bytes 1572872 | tf_op jit(solution)/shard_map/ppermute | solution.py:53
  73.9 16.2 %collective-permute-start.24 = (bf16[128,1024]{1,0:T(8,128)(2,1)S(1)}, bf16[128,1024]{1,0:T(8,128)(2,1)S(1)}, u32[]{:S(2)}, u32[]{:S(2)}) collective-permute-start(bf16[128,1024]{1,0:T(8,128)(2,1)S(1)} %gate.14.refs_0_), channel_id=1, source_target_pairs={{0,12},{2,14},{4,8},{6,10},{8,4},{10,6},{12,0},{14,2},{1,13},{3,15... | collective-permute-start | bytes 786440 | tf_op jit(solution)/shard_map/ppermute | solution.py:53
  75.8 20.6 %collective-permute-start.26 = (bf16[128,1024]{1,0:T(8,128)(2,1)S(1)}, bf16[128,1024]{1,0:T(8,128)(2,1)S(1)}, u32[]{:S(2)}, u32[]{:S(2)}) collective-permute-start(bf16[128,1024]{1,0:T(8,128)(2,1)S(1)} %gate.13.refs_6_), channel_id=1, source_target_pairs={{0,2},{2,0},{4,6},{6,4},{8,10},{10,8},{12,14},{14,12},{1,3},{3,1},... | collective-permute-start | bytes 786440 | tf_op jit(solution)/shard_map/ppermute | solution.py:53
  76.4 18.1 %collective-permute-start.23 = (bf16[128,768]{1,0:T(8,128)(2,1)S(1)}, bf16[128,768]{1,0:T(8,128)(2,1)S(1)}, u32[]{:S(2)}, u32[]{:S(2)}) collective-permute-start(bf16[128,768]{1,0:T(8,128)(2,1)S(1)} %collective-permute-done.15.second_ref.refs_8_.refs_1_), channel_id=1, source_target_pairs={{0,2},{2,0},{4,6},{6,4},{8,10},{10,8},{12,14},{14,12},{1,3},{3,1},... | collective-permute-start | bytes 589832 | tf_op jit(solution)/shard_map/ppermute | solution.py:53
  83.9 15.3 %collective-permute-start.21 = (bf16[128,768]{1,0:T(8,128)(2,1)S(1)}, bf16[128,768]{1,0:T(8,128)(2,1)S(1)}, u32[]{:S(2)}, u32[]{:S(2)}) collective-permute-start(bf16[128,768]{1,0:T(8,128)(2,1)S(1)} %gate.17.refs_0_), channel_id=1, source_target_pairs={{0,12},{2,14},{4,8},{6,10},{8,4},{10,6},{12,0},{14,2},{1,13},{3,15... | collective-permute-start | bytes 589832 | tf_op jit(solution)/shard_map/ppermute | solution.py:53
  90.1 15.3 %collective-permute-start.29 = (bf16[2,128,1024]{2,1,0:T(8,128)(2,1)S(1)}, bf16[2,128,1024]{2,1,0:T(8,128)(2,1)S(1)}, u32[]{:S(2)}, u32[]{:S(2)}) collective-permute-start(bf16[2,128,1024]{2,1,0:T(8,128)(2,1)S(1)} %stack.11.refs_0_), channel_id=1, source_target_pairs={{0,4},{2,6},{4,0},{6,2},{8,12},{10,14},{12,8},{14,10},{1,5},{3,7},... | collective-permute-start | bytes 1572872 | tf_op jit(solution)/shard_map/ppermute | solution.py:53
  94.6 12.1 %collective-permute-start.25 = (bf16[2,128,768]{2,1,0:T(8,128)(2,1)S(1)}, bf16[2,128,768]{2,1,0:T(8,128)(2,1)S(1)}, u32[]{:S(2)}, u32[]{:S(2)}) collective-permute-start(bf16[2,128,768]{2,1,0:T(8,128)(2,1)S(1)} %gate.18.refs_0_), channel_id=1, source_target_pairs={{0,2},{2,0},{4,6},{6,4},{8,10},{10,8},{12,14},{14,12},{1,3},{3,1},... | collective-permute-start | bytes 1179656 | tf_op jit(solution)/shard_map/ppermute | solution.py:53
  99.3 19.1 %collective-permute-start.32 = (bf16[2,128,768]{2,1,0:T(8,128)(2,1)S(1)}, bf16[2,128,768]{2,1,0:T(8,128)(2,1)S(1)}, u32[]{:S(2)}, u32[]{:S(2)}) collective-permute-start(bf16[2,128,768]{2,1,0:T(8,128)(2,1)S(1)} %stack.12.refs_7_), channel_id=1, source_target_pairs={{0,4},{2,6},{4,0},{6,2},{8,12},{10,14},{12,8},{14,10},{1,5},{3,7},... | collective-permute-start | bytes 1179656 | tf_op jit(solution)/shard_map/ppermute | solution.py:53
  101.0 15.2 %collective-permute-start.31 = (bf16[128,1024]{1,0:T(8,128)(2,1)S(1)}, bf16[128,1024]{1,0:T(8,128)(2,1)S(1)}, u32[]{:S(2)}, u32[]{:S(2)}) collective-permute-start(bf16[128,1024]{1,0:T(8,128)(2,1)S(1)} %gate.19.refs_7_), channel_id=1, source_target_pairs={{0,2},{2,0},{4,6},{6,4},{8,10},{10,8},{12,14},{14,12},{1,3},{3,1},... | collective-permute-start | bytes 786440 | tf_op jit(solution)/shard_map/ppermute | solution.py:53
  101.3 14.9 %collective-permute-start.22 = (bf16[128,768]{1,0:T(8,128)(2,1)S(1)}, bf16[128,768]{1,0:T(8,128)(2,1)S(1)}, u32[]{:S(2)}, u32[]{:S(2)}) collective-permute-start(bf16[128,768]{1,0:T(8,128)(2,1)S(1)} %collective-permute-done.21.second_ref.refs_1_), channel_id=1, source_target_pairs={{0,2},{2,0},{4,6},{6,4},{8,10},{10,8},{12,14},{14,12},{1,3},{3,1},... | collective-permute-start | bytes 589832 | tf_op jit(solution)/shard_map/ppermute | solution.py:53
  105.4 19.2 %collective-permute-start.30 = (bf16[2,128,1024]{2,1,0:T(8,128)(2,1)S(1)}, bf16[2,128,1024]{2,1,0:T(8,128)(2,1)S(1)}, u32[]{:S(2)}, u32[]{:S(2)}) collective-permute-start(bf16[2,128,1024]{2,1,0:T(8,128)(2,1)S(1)} %collective-permute-done.29.refs_4_), channel_id=1, source_target_pairs={{0,2},{2,0},{4,6},{6,4},{8,10},{10,8},{12,14},{14,12},{1,3},{3,1},... | collective-permute-start | bytes 1572872 | tf_op jit(solution)/shard_map/ppermute | solution.py:53
  120.3 12.5 %collective-permute-start.34 = (bf16[384,896]{1,0:T(8,128)(2,1)S(1)}, bf16[384,896]{1,0:T(8,128)(2,1)S(1)}, u32[]{:S(2)}, u32[]{:S(2)}) collective-permute-start(bf16[384,896]{1,0:T(8,128)(2,1)S(1)} %get-tuple-element.12), channel_id=1, source_target_pairs={{0,1},{1,0},{2,3},{3,2},{4,5},{5,4},{6,7},{7,6},{8,9},{9,8},{10,11... | collective-permute-start | bytes 2064392 | tf_op jit(solution)/shard_map/ppermute | solution.py:57
  120.4 11.8 %collective-permute-start.28 = (bf16[2,128,768]{2,1,0:T(8,128)(2,1)S(1)}, bf16[2,128,768]{2,1,0:T(8,128)(2,1)S(1)}, u32[]{:S(2)}, u32[]{:S(2)}) collective-permute-start(bf16[2,128,768]{2,1,0:T(8,128)(2,1)S(1)} %stack.13.refs_6_), channel_id=1, source_target_pairs={{0,4},{2,6},{4,0},{6,2},{8,12},{10,14},{12,8},{14,10},{1,5},{3,7},... | collective-permute-start | bytes 1179656 | tf_op jit(solution)/shard_map/ppermute | solution.py:53
  (7 other events, 56.3 us)

commit v8 on v7

--- a/solution.py
+++ b/solution.py
@@ -19,12 +19,12 @@
 FAR, SIDE, CROSS, NEAR, BOTH = "far", "side", "cross", "near", "both"
 ATTEND, STACK, PROJECT, FINISH, OWN = "attend", "stack", "project", "finish", "own"
 ORDER = (
-    (ATTEND, 0), (ATTEND, 1), (STACK, 0), (ATTEND, 2), (FAR, 2), (STACK, 1, (FAR, 0)),
-    (BOTH, 0, (SIDE, 1), (SIDE, 2)), (CROSS, 0), (ATTEND, 3, (CROSS, 0)), (ATTEND, 4),
-    (CROSS, 1, (FAR, 1)), (PROJECT, 0, (SIDE, 3)), (FAR, 3, (NEAR, 1)), (STACK, 2),
-    (BOTH, 1, (SIDE, 4)), (NEAR, 2), (FAR, 4, (NEAR, 2)), (STACK, 3), (BOTH, 2, (CROSS, 2)),
-    (CROSS, 3), (PROJECT, 1, (FAR, 2)), (STACK, 4), (PROJECT, 2), (BOTH, 4, (NEAR, 0)),
-    (PROJECT, 3), (FINISH, 4),
+    (ATTEND, 0), (ATTEND, 1), (CROSS, 0), (STACK, 0), (ATTEND, 2), (STACK, 1, (FAR, 0)), (FAR, 2),
+    (BOTH, 0, (SIDE, 1), (SIDE, 2)), (ATTEND, 3, (CROSS, 0)), (ATTEND, 4),
+    (CROSS, 1, (BOTH, 0), (FAR, 1)), (PROJECT, 0, (SIDE, 3)), (STACK, 2), (FAR, 3, (NEAR, 1)),
+    (CROSS, 2, (CROSS, 1)), (BOTH, 1, (SIDE, 4)), (FAR, 4, (NEAR, 2)), (BOTH, 2, (CROSS, 2)),
+    (STACK, 3), (CROSS, 3, (BOTH, 1)), (PROJECT, 1, (NEAR, 1)), (CROSS, 4), (STACK, 4),
+    (PROJECT, 2, (CROSS, 3)), (BOTH, 4), (PROJECT, 3, (NEAR, 4)),
 )
 LOCAL = pl.BlockSpec(memory_space=pltpu.VMEM)
 ANYWHERE = pl.BlockSpec(memory_space=pl.ANY)
@@ -481,7 +481,7 @@
 def overlap(heads, starts, queries, bias, w_value, kv, w_output, scale):
     value = w_value.shape[2]
     got, ready = {}, {}
-    last, acc = [], None
+    last, acc, sums = [], None, []
     held_back = {entry[:2] for entry in ORDER}
 
     def send(name, chunk, after=None):
@@ -537,10 +537,14 @@
             got[BOTH, chunk] = exchange(pair, 2, 8)
         else:
             send(action, chunk, after)
-    before, row = (start * value for start in starts[-2:])
-    rests = [parts_of(chunk)[3:] for chunk in range(len(heads))][-2:]
-    acc = project(before, rests[0], w_output, acc, last, 3)
-    return [*sums, finish(row, rests[1], w_output, acc, [acc], 3)]
+    chunk = len(heads) - 2
+    first = 3 if (PROJECT, chunk) in held_back else 0
+    some = parts_of(chunk)[first:]
+    acc = project(starts[chunk] * value, some, w_output, acc, last, first)
+    chunk += 1
+    first = 3 if sums else 0
+    some = parts_of(chunk)[first:]
+    return [*sums, finish(starts[chunk] * value, some, w_output, acc, [acc], first)]
 
 
 def local(
@@ -571,7 +575,7 @@
     starts = [sum(heads[:chunk]) for chunk in range(len(heads))]
     if shards == 8:
         sums = overlap(heads, starts, queries, bias, w_value, kv, w_output, scale)
-        split = (keys[:3], keys[3:])
+        split = (keys[:3], keys[3:]) if len(sums) > 1 else (keys,)
     else:
         acc = None
         for chunk, start in enumerate(starts):

time: 135 us -> 127 us (0.941)
  starting transfers between devices: 46.2 us -> 38.7 us
    ppermute x29, starting transfers between devices: 45.6 us -> 38.1 us  [exchange(): return lax.ppermute(x, 'ctx', [(i, i ^ mask) for i in range(shards)])]
    ppermute x29, waiting for transfers between devices: 48.7 us -> 46.6 us  [exchange(): return lax.ppermute(x, 'ctx', [(i, i ^ mask) for i in range(shards)])]
    ppermute x6 -> x5, waiting for transfers between devices: 0.66 us -> 2.56 us  [sibling(): return lax.ppermute(x, 'head', [(0, 1), (1, 0)])]
  transfers between devices with their start and end apart: 35 -> 34, of which waited for: 17 -> 19; matrix products, arithmetic and copies ran while one was open for 0% -> 0% of each run, Pallas kernels for 25% -> 24%
where the time goes in v8:
time: 127 us
  waiting for transfers between devices  49.1 us (39%)
  starting transfers between devices  38.7 us (30%)
  Pallas kernels  37.6 us (30%)
    ppermute x29, waiting for transfers between devices, exchange(): return lax.ppermute(x, 'ctx', [(i, i ^ mask) for i in range(shards)])  46.6 us
    ppermute x29, starting transfers between devices, exchange(): return lax.ppermute(x, 'ctx', [(i, i ^ mask) for i in range(shards)])  38.1 us
    pallas_call x5, Pallas kernels, attend(): pl.pallas_call(functools.partial(attend_kernel, scale * math.log2(math.e)...  18.6 us
    pallas_call x5, Pallas kernels, project(): pl.pallas_call(functools.partial(project_kernel, start, sizes, first, acc...  9.49 us
    pallas_call x1, Pallas kernels, prep(): pl.pallas_call(prep_kernel, in_specs=[ANYWHERE] * 3, out_specs=LOCAL, out...  3.89 us
    ppermute x5, waiting for transfers between devices, sibling(): return lax.ppermute(x, 'head', [(0, 1), (1, 0)])  2.56 us
  transfers between devices with their start and end apart: 34, of which 19 were waited for; matrix products, arithmetic and copies ran while one was open for 0% of the time, Pallas kernels for 24%

profile of v8, /device:TPU:0, one launch (start us, length us, event | category | flops | bytes accessed | tf_op | source)
XLA Modules:
  0.0 126.8 jit_solution(5934736955384731438)
XLA Ops:
  1.1 5.1 %collective-permute-start = (bf16[336,128]{1,0:T(8,128)(2,1)S(1)}, bf16[336,128]{1,0:T(8,128)(2,1)S(1)}, u32[]{:S(2)}, u32[]{:S(2)}) collective-permute-start(bf16[336,128]{1,0:T(8,128)(2,1)S(1)} %pack.1.first_ref), channel_id=1, source_target_pairs={{0,12},{2,14},{4,8},{6,10},{8,4},{10,6},{12,0},{14,2},{1,13},{3,15... | collective-permute-start | bytes 258056 | tf_op jit(solution)/shard_map/ppermute | solution.py:53
  6.2 3.9 %prep.1.refs_0_.q_ref = bf16[4096,640]{1,0:T(8,128)(2,1)S(1)} custom-call(bf16[128,4096]{1,0:T(8,128)(2,1)} %q_hbm.1, bf16[128,2048]{1,0:T(8,128)(2,1)} %r_hbm.1, bf16[32,128,512]{2,1,0:T(8,128)(2,1)} %w_hbm.1), custom_call_target="tpu_custom_call" | custom-call | bytes 1024 | tf_op jit(solution)/shard_map/prep/pallas_call | solution.py:215
  10.4 1.5 %collective-permute-start.1 = (bf16[2,336,128]{2,1,0:T(8,128)(2,1)S(1)}, bf16[2,336,128]{2,1,0:T(8,128)(2,1)S(1)}, u32[]{:S(2)}, u32[]{:S(2)}) collective-permute-start(bf16[2,336,128]{2,1,0:T(8,128)(2,1)S(1)} %stack.7.refs_0_), channel_id=1, source_target_pairs={{0,2},{2,0},{4,6},{6,4},{8,10},{10,8},{12,14},{14,12},{1,3},{3,1},... | collective-permute-start | bytes 516104 | tf_op jit(solution)/shard_map/ppermute | solution.py:53
  11.9 4.2 %collective-permute-done.2.refs_2_ = bf16[2,336,128]{2,1,0:T(8,128)(2,1)S(1)} collective-permute-done((bf16[2,336,128]{2,1,0:T(8,128)(2,1)S(1)}, bf16[2,336,128]{2,1,0:T(8,128)(2,1)S(1)}, u32[]{:S(2)}, u32[]{:S(2)}) %collective-permute-start.2) | collective-permute-done | bytes 172064 | tf_op jit(solution)/shard_map/ppermute | solution.py:53
  18.1 3.4 %collective-permute-done.3.refs_3_ = bf16[2,336,128]{2,1,0:T(8,128)(2,1)S(1)} collective-permute-done((bf16[2,336,128]{2,1,0:T(8,128)(2,1)S(1)}, bf16[2,336,128]{2,1,0:T(8,128)(2,1)S(1)}, u32[]{:S(2)}, u32[]{:S(2)}) %collective-permute-start.3) | collective-permute-done | bytes 172064 | tf_op jit(solution)/shard_map/ppermute | solution.py:53
  23.4 2.6 %attend0.1.refs_0_.first_ref = bf16[128,512]{1,0:T(8,128)(2,1)S(1)} custom-call(bf16[4096,640]{1,0:T(8,128)(2,1)S(1)} %prep.1.refs_0_.q_ref, f32[128,1152]{1,0:T(8,128)S(1)} %mask.1.bias_ref, bf16[32,512,128]{2,1,0:T(8,128)(2,1)S(1)} %copy-done, bf16[1152,640]{1,0:T(8,128)(2,1)S(1)} %join.1.kv_ref), custom_call_target="tpu_custom_call" | custom-call | bytes 1024 | tf_op jit(solution)/shard_map/attend0/pallas_call | solution.py:335
  26.0 1.9 %collective-permute-start.8 = (bf16[128,512]{1,0:T(8,128)(2,1)S(1)}, bf16[128,512]{1,0:T(8,128)(2,1)S(1)}, u32[]{:S(2)}, u32[]{:S(2)}) collective-permute-start(bf16[128,512]{1,0:T(8,128)(2,1)S(1)} %attend0.1.refs_0_.first_ref), channel_id=1, source_target_pairs={{0,12},{2,14},{4,8},{6,10},{8,4},{10,6},{12,0},{14,2},{1,13},{3,15... | collective-permute-start | bytes 393224 | tf_op jit(solution)/shard_map/ppermute | solution.py:53
  27.9 4.4 %attend4.1.refs_0_.first_ref = bf16[128,1024]{1,0:T(8,128)(2,1)S(1)} custom-call(bf16[4096,640]{1,0:T(8,128)(2,1)S(1)} %prep.1.refs_0_.q_ref, f32[128,1152]{1,0:T(8,128)S(1)} %mask.1.bias_ref, bf16[32,512,128]{2,1,0:T(8,128)(2,1)S(1)} %copy-done, bf16[1152,640]{1,0:T(8,128)(2,1)S(1)} %join.1.kv_ref, bf16[128,512]{1,0:T(8,128)(2,1)S(1)} %attend0.1.refs_0_.first_ref), custom_call_target="tpu_custom_call" | custom-call | bytes 1024 | tf_op jit(solution)/shard_map/attend4/pallas_call | solution.py:335
  32.4 2.0 %collective-permute-start.10 = (bf16[128,1024]{1,0:T(8,128)(2,1)S(1)}, bf16[128,1024]{1,0:T(8,128)(2,1)S(1)}, u32[]{:S(2)}, u32[]{:S(2)}) collective-permute-start(bf16[128,1024]{1,0:T(8,128)(2,1)S(1)} %attend4.1.refs_0_.first_ref), channel_id=1, source_target_pairs={{0,12},{2,14},{4,8},{6,10},{8,4},{10,6},{12,0},{14,2},{1,13},{3,15... | collective-permute-start | bytes 786440 | tf_op jit(solution)/shard_map/ppermute | solution.py:53
  36.0 3.5 %attend12.1.refs_0_.x_ref.first_ref = bf16[128,768]{1,0:T(8,128)(2,1)S(1)} custom-call(bf16[4096,640]{1,0:T(8,128)(2,1)S(1)} %prep.1.refs_0_.q_ref, f32[128,1152]{1,0:T(8,128)S(1)} %mask.1.bias_ref, bf16[32,512,128]{2,1,0:T(8,128)(2,1)S(1)} %copy-done, bf16[1152,640]{1,0:T(8,128)(2,1)S(1)} %join.1.kv_ref, bf16[2,128,512]{2,1,0:T(8,128)(2,1)S(1)} %stack.8.refs_0_), custom_call_target="tpu_custom_call" | custom-call | bytes 1024 | tf_op jit(solution)/shard_map/attend12/pallas_call | solution.py:335
  41.6 1.9 %collective-permute-done.10.second_ref.x_ref.refs_2_.refs_1_ = bf16[128,1024]{1,0:T(8,128)(2,1)S(1)} collective-permute-done((bf16[128,1024]{1,0:T(8,128)(2,1)S(1)}, bf16[128,1024]{1,0:T(8,128)(2,1)S(1)}, u32[]{:S(2)}, u32[]{:S(2)}) %collective-permute-start.10) | collective-permute-done | bytes 262176 | tf_op jit(solution)/shard_map/ppermute | solution.py:53
  43.5 2.8 %collective-permute-start.14 = (bf16[2,128,1024]{2,1,0:T(8,128)(2,1)S(1)}, bf16[2,128,1024]{2,1,0:T(8,128)(2,1)S(1)}, u32[]{:S(2)}, u32[]{:S(2)}) collective-permute-start(bf16[2,128,1024]{2,1,0:T(8,128)(2,1)S(1)} %stack.9.refs_0_), channel_id=1, source_target_pairs={{0,4},{2,6},{4,0},{6,2},{8,12},{10,14},{12,8},{14,10},{1,5},{3,7},... | collective-permute-start | bytes 1572872 | tf_op jit(solution)/shard_map/ppermute | solution.py:53
  48.4 1.6 %collective-permute-start.17 = (bf16[2,128,512]{2,1,0:T(8,128)(2,1)S(1)}, bf16[2,128,512]{2,1,0:T(8,128)(2,1)S(1)}, u32[]{:S(2)}, u32[]{:S(2)}) collective-permute-start(bf16[2,128,512]{2,1,0:T(8,128)(2,1)S(1)} %gate.13.refs_0_), channel_id=1, source_target_pairs={{0,2},{2,0},{4,6},{6,4},{8,10},{10,8},{12,14},{14,12},{1,3},{3,1},... | collective-permute-start | bytes 786440 | tf_op jit(solution)/shard_map/ppermute | solution.py:53
  50.0 4.7 %attend18.1.refs_0_.x_ref.first_ref = bf16[128,1024]{1,0:T(8,128)(2,1)S(1)} custom-call(bf16[4096,640]{1,0:T(8,128)(2,1)S(1)} %prep.1.refs_0_.q_ref, f32[128,1152]{1,0:T(8,128)S(1)} %mask.1.bias_ref, bf16[32,512,128]{2,1,0:T(8,128)(2,1)S(1)} %copy-done, bf16[1152,640]{1,0:T(8,128)(2,1)S(1)} %join.1.kv_ref, bf16[2,128,512]{2,1,0:T(8,128)(2,1)S(1)} %gate.13.refs_0_, ...), custom_call_target="tpu_custom_call" | custom-call | bytes 1024 | tf_op jit(solution)/shard_map/attend18/pallas_call | solution.py:335
  55.8 1.9 %collective-permute-start.15 = (bf16[128,768]{1,0:T(8,128)(2,1)S(1)}, bf16[128,768]{1,0:T(8,128)(2,1)S(1)}, u32[]{:S(2)}, u32[]{:S(2)}) collective-permute-start(bf16[128,768]{1,0:T(8,128)(2,1)S(1)} %gate.12.refs_0_), channel_id=1, source_target_pairs={{0,12},{2,14},{4,8},{6,10},{8,4},{10,6},{12,0},{14,2},{1,13},{3,15... | collective-permute-start | bytes 589832 | tf_op jit(solution)/shard_map/ppermute | solution.py:53
  58.8 3.4 %attend26.1.refs_0_.x_ref.first_ref = bf16[128,768]{1,0:T(8,128)(2,1)S(1)} custom-call(bf16[4096,640]{1,0:T(8,128)(2,1)S(1)} %prep.1.refs_0_.q_ref, f32[128,1152]{1,0:T(8,128)S(1)} %mask.1.bias_ref, bf16[32,512,128]{2,1,0:T(8,128)(2,1)S(1)} %copy-done, bf16[1152,640]{1,0:T(8,128)(2,1)S(1)} %join.1.kv_ref, bf16[128,1024]{1,0:T(8,128)(2,1)S(1)} %attend18.1.refs_0_.x_ref.first_ref), custom_call_target="tpu_custom_call" | custom-call | bytes 1024 | tf_op jit(solution)/shard_map/attend26/pallas_call | solution.py:335
  63.3 3.6 %collective-permute-done.16.refs_2_ = bf16[128,512]{1,0:T(8,128)(2,1)S(1)} collective-permute-done((bf16[128,512]{1,0:T(8,128)(2,1)S(1)}, bf16[128,512]{1,0:T(8,128)(2,1)S(1)}, u32[]{:S(2)}, u32[]{:S(2)}) %collective-permute-start.16) | collective-permute-done | bytes 131104 | tf_op jit(solution)/shard_map/ppermute | solution.py:53
  69.4 2.0 %collective-permute-start.24 = (bf16[128,1024]{1,0:T(8,128)(2,1)S(1)}, bf16[128,1024]{1,0:T(8,128)(2,1)S(1)}, u32[]{:S(2)}, u32[]{:S(2)}) collective-permute-start(bf16[128,1024]{1,0:T(8,128)(2,1)S(1)} %gate.15.refs_0_), channel_id=1, source_target_pairs={{0,12},{2,14},{4,8},{6,10},{8,4},{10,6},{12,0},{14,2},{1,13},{3,15... | collective-permute-start | bytes 786440 | tf_op jit(solution)/shard_map/ppermute | solution.py:53
  73.5 3.1 %collective-permute-done.20.refs_1_.first_ref.refs_2_ = bf16[128,768]{1,0:T(8,128)(2,1)S(1)} collective-permute-done((bf16[128,768]{1,0:T(8,128)(2,1)S(1)}, bf16[128,768]{1,0:T(8,128)(2,1)S(1)}, u32[]{:S(2)}, u32[]{:S(2)}) %collective-permute-start.20) | collective-permute-done | bytes 196640 | tf_op jit(solution)/shard_map/ppermute | solution.py:53
  77.8 1.7 %collective-permute-done.21.refs_1_.x_ref.refs_4_ = bf16[2,128,768]{2,1,0:T(8,128)(2,1)S(1)} collective-permute-done((bf16[2,128,768]{2,1,0:T(8,128)(2,1)S(1)}, bf16[2,128,768]{2,1,0:T(8,128)(2,1)S(1)}, u32[]{:S(2)}, u32[]{:S(2)}) %collective-permute-start.21) | collective-permute-done | bytes 393248 | tf_op jit(solution)/shard_map/ppermute | solution.py:53
  80.9 2.6 %collective-permute-done.24.second_ref.x_ref.refs_1_ = bf16[128,1024]{1,0:T(8,128)(2,1)S(1)} collective-permute-done((bf16[128,1024]{1,0:T(8,128)(2,1)S(1)}, bf16[128,1024]{1,0:T(8,128)(2,1)S(1)}, u32[]{:S(2)}, u32[]{:S(2)}) %collective-permute-start.24) | collective-permute-done | bytes 262176 | tf_op jit(solution)/shard_map/ppermute | solution.py:53
  84.5 1.7 %collective-permute-start.22 = (bf16[128,768]{1,0:T(8,128)(2,1)S(1)}, bf16[128,768]{1,0:T(8,128)(2,1)S(1)}, u32[]{:S(2)}, u32[]{:S(2)}) collective-permute-start(bf16[128,768]{1,0:T(8,128)(2,1)S(1)} %gate.18.refs_0_), channel_id=1, source_target_pairs={{0,12},{2,14},{4,8},{6,10},{8,4},{10,6},{12,0},{14,2},{1,13},{3,15... | collective-permute-start | bytes 589832 | tf_op jit(solution)/shard_map/ppermute | solution.py:53
  86.2 5.9 %collective-permute-done.23.refs_1_.refs_5_ = bf16[2,128,1024]{2,1,0:T(8,128)(2,1)S(1)} collective-permute-done((bf16[2,128,1024]{2,1,0:T(8,128)(2,1)S(1)}, bf16[2,128,1024]{2,1,0:T(8,128)(2,1)S(1)}, u32[]{:S(2)}, u32[]{:S(2)}) %collective-permute-start.23) | collective-permute-done | bytes 524320 | tf_op jit(solution)/shard_map/ppermute | solution.py:53
  93.2 2.8 %project512.1.refs_0_.refs_6_ = f32[2,512,896]{2,1,0:T(8,128)S(1)} custom-call(bf16[4096,896]{1,0:T(8,128)(2,1)S(1)} %bitcast.2, bf16[128,1024]{1,0:T(8,128)(2,1)S(1)} %attend4.1.refs_0_.first_ref, bf16[128,1024]{1,0:T(8,128)(2,1)S(1)} %collective-permute-done.10.second_ref.x_ref.refs_2_.refs_1_, ...), custom_call_target="tpu_custom_call", output_to_operand_aliasing={{}: (7, {})} | custom-call | bytes 1024 | tf_op jit(solution)/shard_map/project512/pallas_call | solution.py:396
  96.0 1.9 %collective-permute-done.22.x_ref.second_ref.refs_1_ = bf16[128,768]{1,0:T(8,128)(2,1)S(1)} collective-permute-done((bf16[128,768]{1,0:T(8,128)(2,1)S(1)}, bf16[128,768]{1,0:T(8,128)(2,1)S(1)}, u32[]{:S(2)}, u32[]{:S(2)}) %collective-permute-start.22) | collective-permute-done | bytes 196640 | tf_op jit(solution)/shard_map/ppermute | solution.py:53
  100.5 5.6 %collective-permute-done.29.refs_8_.refs_3_ = bf16[128,1024]{1,0:T(8,128)(2,1)S(1)} collective-permute-done((bf16[128,1024]{1,0:T(8,128)(2,1)S(1)}, bf16[128,1024]{1,0:T(8,128)(2,1)S(1)}, u32[]{:S(2)}, u32[]{:S(2)}) %collective-permute-start.29) | collective-permute-done | bytes 262176 | tf_op jit(solution)/shard_map/ppermute | solution.py:53
  106.2 2.2 %project1536.1.refs_0_.refs_5_ = f32[2,512,896]{2,1,0:T(8,128)S(1)} custom-call(bf16[4096,896]{1,0:T(8,128)(2,1)S(1)} %bitcast.2, bf16[128,768]{1,0:T(8,128)(2,1)S(1)} %attend12.1.refs_0_.x_ref.first_ref, bf16[128,768]{1,0:T(8,128)(2,1)S(1)} %collective-permute-done.15.second_ref.x_ref.refs_1_, ...), custom_call_target="tpu_custom_call", output_to_operand_aliasing={{}: (7, {})} | custom-call | bytes 1024 | tf_op jit(solution)/shard_map/project1536/pallas_call | solution.py:396
  108.4 2.0 %collective-permute-done.26.second_ref.refs_3_ = bf16[128,768]{1,0:T(8,128)(2,1)S(1)} collective-permute-done((bf16[128,768]{1,0:T(8,128)(2,1)S(1)}, bf16[128,768]{1,0:T(8,128)(2,1)S(1)}, u32[]{:S(2)}, u32[]{:S(2)}) %collective-permute-start.26) | collective-permute-done | bytes 196640 | tf_op jit(solution)/shard_map/ppermute | solution.py:53
  111.9 2.4 %project2304.2.refs_2_ = f32[2,512,896]{2,1,0:T(8,128)S(1)} custom-call(bf16[4096,896]{1,0:T(8,128)(2,1)S(1)} %bitcast.2, bf16[128,1024]{1,0:T(8,128)(2,1)S(1)} %attend18.1.refs_0_.x_ref.first_ref, bf16[128,1024]{1,0:T(8,128)(2,1)S(1)} %collective-permute-done.24.second_ref.x_ref.refs_1_, ...), custom_call_target="tpu_custom_call", output_to_operand_aliasing={{}: (6, {})} | custom-call | bytes 1024 | tf_op jit(solution)/shard_map/project2304/pallas_call | solution.py:396
  114.6 5.7 %collective-permute-done.32.refs_0_ = bf16[2,128,1024]{2,1,0:T(8,128)(2,1)S(1)} collective-permute-done((bf16[2,128,1024]{2,1,0:T(8,128)(2,1)S(1)}, bf16[2,128,1024]{2,1,0:T(8,128)(2,1)S(1)}, u32[]{:S(2)}, u32[]{:S(2)}) %collective-permute-start.32) | collective-permute-done | bytes 524320 | tf_op jit(solution)/shard_map/ppermute | solution.py:53
  121.1 2.0 %finish.1 = (bf16[512,896]{1,0:T(8,128)(2,1)S(1)}, f32[512,896]{1,0:T(8,128)S(1)}) custom-call(bf16[4096,896]{1,0:T(8,128)(2,1)S(1)} %bitcast.2, bf16[128,768]{1,0:T(8,128)(2,1)S(1)} %attend26.1.refs_0_.x_ref.first_ref, bf16[128,768]{1,0:T(8,128)(2,1)S(1)} %collective-permute-done.22.x_ref.second_ref.refs_1_, ...), custom_call_target="tpu_custom_call" | custom-call | bytes 1024 | tf_op jit(solution)/shard_map/finish/pallas_call | solution.py:435
  123.2 2.5 %collective-permute-done.33.other_ref = bf16[512,896]{1,0:T(8,128)(2,1)S(1)} collective-permute-done((bf16[512,896]{1,0:T(8,128)(2,1)S(1)}, bf16[512,896]{1,0:T(8,128)(2,1)S(1)}, u32[]{:S(2)}, u32[]{:S(2)}) %collective-permute-start.33) | collective-permute-done | bytes 917536 | tf_op jit(solution)/shard_map/ppermute | solution.py:57
  (80 shorter events, 29.0 us)
Async XLA Ops:
  1.1 9.0 %collective-permute-start = (bf16[336,128]{1,0:T(8,128)(2,1)S(1)}, bf16[336,128]{1,0:T(8,128)(2,1)S(1)}, u32[]{:S(2)}, u32[]{:S(2)}) collective-permute-start(bf16[336,128]{1,0:T(8,128)(2,1)S(1)} %pack.1.first_ref), channel_id=1, source_target_pairs={{0,12},{2,14},{4,8},{6,10},{8,4},{10,6},{12,0},{14,2},{1,13},{3,15... | collective-permute-start | bytes 258056 | tf_op jit(solution)/shard_map/ppermute | solution.py:53
  10.2 5.9 %collective-permute-start.2 = (bf16[2,336,128]{2,1,0:T(8,128)(2,1)S(1)}, bf16[2,336,128]{2,1,0:T(8,128)(2,1)S(1)}, u32[]{:S(2)}, u32[]{:S(2)}) collective-permute-start(bf16[2,336,128]{2,1,0:T(8,128)(2,1)S(1)} %stack.7.refs_0_), channel_id=1, source_target_pairs={{0,4},{2,6},{4,0},{6,2},{8,12},{10,14},{12,8},{14,10},{1,5},{3,7},... | collective-permute-start | bytes 516104 | tf_op jit(solution)/shard_map/ppermute | solution.py:53
  10.4 7.7 %collective-permute-start.1 = (bf16[2,336,128]{2,1,0:T(8,128)(2,1)S(1)}, bf16[2,336,128]{2,1,0:T(8,128)(2,1)S(1)}, u32[]{:S(2)}, u32[]{:S(2)}) collective-permute-start(bf16[2,336,128]{2,1,0:T(8,128)(2,1)S(1)} %stack.7.refs_0_), channel_id=1, source_target_pairs={{0,2},{2,0},{4,6},{6,4},{8,10},{10,8},{12,14},{14,12},{1,3},{3,1},... | collective-permute-start | bytes 516104 | tf_op jit(solution)/shard_map/ppermute | solution.py:53
  16.1 5.4 %collective-permute-start.3 = (bf16[2,336,128]{2,1,0:T(8,128)(2,1)S(1)}, bf16[2,336,128]{2,1,0:T(8,128)(2,1)S(1)}, u32[]{:S(2)}, u32[]{:S(2)}) collective-permute-start(bf16[2,336,128]{2,1,0:T(8,128)(2,1)S(1)} %collective-permute-done.2.refs_2_), channel_id=1, source_target_pairs={{0,2},{2,0},{4,6},{6,4},{8,10},{10,8},{12,14},{14,12},{1,3},{3,1},... | collective-permute-start | bytes 516104 | tf_op jit(solution)/shard_map/ppermute | solution.py:53
  17.6 5.2 %collective-permute-start.4 = (bf16[2,336,128]{2,1,0:T(8,128)(2,1)S(1)}, bf16[2,336,128]{2,1,0:T(8,128)(2,1)S(1)}, u32[]{:S(2)}, u32[]{:S(2)}) collective-permute-start(bf16[2,336,128]{2,1,0:T(8,128)(2,1)S(1)} %stack.7.refs_0_), channel_id=1, source_target_pairs={{0,1},{1,0},{2,3},{3,2},{4,5},{5,4},{6,7},{7,6},{8,9},{9,8},{10,11... | collective-permute-start | bytes 516104 | tf_op jit(solution)/shard_map/ppermute | solution.py:57
  17.6 5.2 %collective-permute-start.6 = (bf16[2,336,128]{2,1,0:T(8,128)(2,1)S(1)}, bf16[2,336,128]{2,1,0:T(8,128)(2,1)S(1)}, u32[]{:S(2)}, u32[]{:S(2)}) collective-permute-start(bf16[2,336,128]{2,1,0:T(8,128)(2,1)S(1)} %collective-permute-done.2.refs_2_), channel_id=1, source_target_pairs={{0,1},{1,0},{2,3},{3,2},{4,5},{5,4},{6,7},{7,6},{8,9},{9,8},{10,11... | collective-permute-start | bytes 516104 | tf_op jit(solution)/shard_map/ppermute | solution.py:57
  18.1 4.7 %collective-permute-start.5 = (bf16[2,336,128]{2,1,0:T(8,128)(2,1)S(1)}, bf16[2,336,128]{2,1,0:T(8,128)(2,1)S(1)}, u32[]{:S(2)}, u32[]{:S(2)}) collective-permute-start(bf16[2,336,128]{2,1,0:T(8,128)(2,1)S(1)} %collective-permute-done.1.refs_1_), channel_id=1, source_target_pairs={{0,1},{1,0},{2,3},{3,2},{4,5},{5,4},{6,7},{7,6},{8,9},{9,8},{10,11... | collective-permute-start | bytes 516104 | tf_op jit(solution)/shard_map/ppermute | solution.py:57
  26.0 9.9 %collective-permute-start.8 = (bf16[128,512]{1,0:T(8,128)(2,1)S(1)}, bf16[128,512]{1,0:T(8,128)(2,1)S(1)}, u32[]{:S(2)}, u32[]{:S(2)}) collective-permute-start(bf16[128,512]{1,0:T(8,128)(2,1)S(1)} %attend0.1.refs_0_.first_ref), channel_id=1, source_target_pairs={{0,12},{2,14},{4,8},{6,10},{8,4},{10,6},{12,0},{14,2},{1,13},{3,15... | collective-permute-start | bytes 393224 | tf_op jit(solution)/shard_map/ppermute | solution.py:53
  32.4 11.1 %collective-permute-start.10 = (bf16[128,1024]{1,0:T(8,128)(2,1)S(1)}, bf16[128,1024]{1,0:T(8,128)(2,1)S(1)}, u32[]{:S(2)}, u32[]{:S(2)}) collective-permute-start(bf16[128,1024]{1,0:T(8,128)(2,1)S(1)} %attend4.1.refs_0_.first_ref), channel_id=1, source_target_pairs={{0,12},{2,14},{4,8},{6,10},{8,4},{10,6},{12,0},{14,2},{1,13},{3,15... | collective-permute-start | bytes 786440 | tf_op jit(solution)/shard_map/ppermute | solution.py:53
  34.4 12.0 %collective-permute-start.11 = (bf16[128,1024]{1,0:T(8,128)(2,1)S(1)}, bf16[128,1024]{1,0:T(8,128)(2,1)S(1)}, u32[]{:S(2)}, u32[]{:S(2)}) collective-permute-start(bf16[128,1024]{1,0:T(8,128)(2,1)S(1)} %attend4.1.refs_0_.first_ref), channel_id=1, source_target_pairs={{0,2},{2,0},{4,6},{6,4},{8,10},{10,8},{12,14},{14,12},{1,3},{3,1},... | collective-permute-start | bytes 786440 | tf_op jit(solution)/shard_map/ppermute | solution.py:53
  35.9 12.5 %collective-permute-start.9 = (bf16[2,128,512]{2,1,0:T(8,128)(2,1)S(1)}, bf16[2,128,512]{2,1,0:T(8,128)(2,1)S(1)}, u32[]{:S(2)}, u32[]{:S(2)}) collective-permute-start(bf16[2,128,512]{2,1,0:T(8,128)(2,1)S(1)} %stack.8.refs_0_), channel_id=1, source_target_pairs={{0,4},{2,6},{4,0},{6,2},{8,12},{10,14},{12,8},{14,10},{1,5},{3,7},... | collective-permute-start | bytes 786440 | tf_op jit(solution)/shard_map/ppermute | solution.py:53
  39.5 7.9 %collective-permute-start.12 = (bf16[128,768]{1,0:T(8,128)(2,1)S(1)}, bf16[128,768]{1,0:T(8,128)(2,1)S(1)}, u32[]{:S(2)}, u32[]{:S(2)}) collective-permute-start(bf16[128,768]{1,0:T(8,128)(2,1)S(1)} %attend12.1.refs_0_.x_ref.first_ref), channel_id=1, source_target_pairs={{0,2},{2,0},{4,6},{6,4},{8,10},{10,8},{12,14},{14,12},{1,3},{3,1},... | collective-permute-start | bytes 589832 | tf_op jit(solution)/shard_map/ppermute | solution.py:53
  40.4 9.6 %collective-permute-start.13 = (bf16[128,512]{1,0:T(8,128)(2,1)S(1)}, bf16[128,512]{1,0:T(8,128)(2,1)S(1)}, u32[]{:S(2)}, u32[]{:S(2)}) collective-permute-start(bf16[128,512]{1,0:T(8,128)(2,1)S(1)} %gate.11.refs_0_), channel_id=1, source_target_pairs={{0,2},{2,0},{4,6},{6,4},{8,10},{10,8},{12,14},{14,12},{1,3},{3,1},... | collective-permute-start | bytes 393224 | tf_op jit(solution)/shard_map/ppermute | solution.py:53
  43.5 25.9 %collective-permute-start.14 = (bf16[2,128,1024]{2,1,0:T(8,128)(2,1)S(1)}, bf16[2,128,1024]{2,1,0:T(8,128)(2,1)S(1)}, u32[]{:S(2)}, u32[]{:S(2)}) collective-permute-start(bf16[2,128,1024]{2,1,0:T(8,128)(2,1)S(1)} %stack.9.refs_0_), channel_id=1, source_target_pairs={{0,4},{2,6},{4,0},{6,2},{8,12},{10,14},{12,8},{14,10},{1,5},{3,7},... | collective-permute-start | bytes 1572872 | tf_op jit(solution)/shard_map/ppermute | solution.py:53
  48.4 13.8 %collective-permute-start.17 = (bf16[2,128,512]{2,1,0:T(8,128)(2,1)S(1)}, bf16[2,128,512]{2,1,0:T(8,128)(2,1)S(1)}, u32[]{:S(2)}, u32[]{:S(2)}) collective-permute-start(bf16[2,128,512]{2,1,0:T(8,128)(2,1)S(1)} %gate.13.refs_0_), channel_id=1, source_target_pairs={{0,2},{2,0},{4,6},{6,4},{8,10},{10,8},{12,14},{14,12},{1,3},{3,1},... | collective-permute-start | bytes 786440 | tf_op jit(solution)/shard_map/ppermute | solution.py:53
  54.7 12.1 %collective-permute-start.18 = (bf16[128,1024]{1,0:T(8,128)(2,1)S(1)}, bf16[128,1024]{1,0:T(8,128)(2,1)S(1)}, u32[]{:S(2)}, u32[]{:S(2)}) collective-permute-start(bf16[128,1024]{1,0:T(8,128)(2,1)S(1)} %attend18.1.refs_0_.x_ref.first_ref), channel_id=1, source_target_pairs={{0,2},{2,0},{4,6},{6,4},{8,10},{10,8},{12,14},{14,12},{1,3},{3,1},... | collective-permute-start | bytes 786440 | tf_op jit(solution)/shard_map/ppermute | solution.py:53
  55.8 12.3 %collective-permute-start.15 = (bf16[128,768]{1,0:T(8,128)(2,1)S(1)}, bf16[128,768]{1,0:T(8,128)(2,1)S(1)}, u32[]{:S(2)}, u32[]{:S(2)}) collective-permute-start(bf16[128,768]{1,0:T(8,128)(2,1)S(1)} %gate.12.refs_0_), channel_id=1, source_target_pairs={{0,12},{2,14},{4,8},{6,10},{8,4},{10,6},{12,0},{14,2},{1,13},{3,15... | collective-permute-start | bytes 589832 | tf_op jit(solution)/shard_map/ppermute | solution.py:53
  57.7 9.2 %collective-permute-start.16 = (bf16[128,512]{1,0:T(8,128)(2,1)S(1)}, bf16[128,512]{1,0:T(8,128)(2,1)S(1)}, u32[]{:S(2)}, u32[]{:S(2)}) collective-permute-start(bf16[128,512]{1,0:T(8,128)(2,1)S(1)} %attend0.1.refs_0_.first_ref), channel_id=1, source_target_pairs={{0,2},{2,0},{4,6},{6,4},{8,10},{10,8},{12,14},{14,12},{1,3},{3,1},... | collective-permute-start | bytes 393224 | tf_op jit(solution)/shard_map/ppermute | solution.py:53
  62.2 10.2 %collective-permute-start.19 = (bf16[128,1024]{1,0:T(8,128)(2,1)S(1)}, bf16[128,1024]{1,0:T(8,128)(2,1)S(1)}, u32[]{:S(2)}, u32[]{:S(2)}) collective-permute-start(bf16[128,1024]{1,0:T(8,128)(2,1)S(1)} %gate.14.refs_6_), channel_id=1, source_target_pairs={{0,2},{2,0},{4,6},{6,4},{8,10},{10,8},{12,14},{14,12},{1,3},{3,1},... | collective-permute-start | bytes 786440 | tf_op jit(solution)/shard_map/ppermute | solution.py:53
  68.2 11.3 %collective-permute-start.21 = (bf16[2,128,768]{2,1,0:T(8,128)(2,1)S(1)}, bf16[2,128,768]{2,1,0:T(8,128)(2,1)S(1)}, u32[]{:S(2)}, u32[]{:S(2)}) collective-permute-start(bf16[2,128,768]{2,1,0:T(8,128)(2,1)S(1)} %stack.10.refs_0_), channel_id=1, source_target_pairs={{0,4},{2,6},{4,0},{6,2},{8,12},{10,14},{12,8},{14,10},{1,5},{3,7},... | collective-permute-start | bytes 1179656 | tf_op jit(solution)/shard_map/ppermute | solution.py:53
  68.7 8.0 %collective-permute-start.20 = (bf16[128,768]{1,0:T(8,128)(2,1)S(1)}, bf16[128,768]{1,0:T(8,128)(2,1)S(1)}, u32[]{:S(2)}, u32[]{:S(2)}) collective-permute-start(bf16[128,768]{1,0:T(8,128)(2,1)S(1)} %attend26.1.refs_0_.x_ref.first_ref), channel_id=1, source_target_pairs={{0,2},{2,0},{4,6},{6,4},{8,10},{10,8},{12,14},{14,12},{1,3},{3,1},... | collective-permute-start | bytes 589832 | tf_op jit(solution)/shard_map/ppermute | solution.py:53
  69.4 14.1 %collective-permute-start.24 = (bf16[128,1024]{1,0:T(8,128)(2,1)S(1)}, bf16[128,1024]{1,0:T(8,128)(2,1)S(1)}, u32[]{:S(2)}, u32[]{:S(2)}) collective-permute-start(bf16[128,1024]{1,0:T(8,128)(2,1)S(1)} %gate.15.refs_0_), channel_id=1, source_target_pairs={{0,12},{2,14},{4,8},{6,10},{8,4},{10,6},{12,0},{14,2},{1,13},{3,15... | collective-permute-start | bytes 786440 | tf_op jit(solution)/shard_map/ppermute | solution.py:53
  72.5 8.4 %collective-permute-start.25 = (bf16[128,768]{1,0:T(8,128)(2,1)S(1)}, bf16[128,768]{1,0:T(8,128)(2,1)S(1)}, u32[]{:S(2)}, u32[]{:S(2)}) collective-permute-start(bf16[128,768]{1,0:T(8,128)(2,1)S(1)} %gate.16.refs_0_), channel_id=1, source_target_pairs={{0,2},{2,0},{4,6},{6,4},{8,10},{10,8},{12,14},{14,12},{1,3},{3,1},... | collective-permute-start | bytes 589832 | tf_op jit(solution)/shard_map/ppermute | solution.py:53
  76.7 15.4 %collective-permute-start.23 = (bf16[2,128,1024]{2,1,0:T(8,128)(2,1)S(1)}, bf16[2,128,1024]{2,1,0:T(8,128)(2,1)S(1)}, u32[]{:S(2)}, u32[]{:S(2)}) collective-permute-start(bf16[2,128,1024]{2,1,0:T(8,128)(2,1)S(1)} %gate.17.refs_0_), channel_id=1, source_target_pairs={{0,2},{2,0},{4,6},{6,4},{8,10},{10,8},{12,14},{14,12},{1,3},{3,1},... | collective-permute-start | bytes 1572872 | tf_op jit(solution)/shard_map/ppermute | solution.py:53
  83.5 15.7 %collective-permute-start.31 = (bf16[2,128,1024]{2,1,0:T(8,128)(2,1)S(1)}, bf16[2,128,1024]{2,1,0:T(8,128)(2,1)S(1)}, u32[]{:S(2)}, u32[]{:S(2)}) collective-permute-start(bf16[2,128,1024]{2,1,0:T(8,128)(2,1)S(1)} %stack.11.refs_0_), channel_id=1, source_target_pairs={{0,4},{2,6},{4,0},{6,2},{8,12},{10,14},{12,8},{14,10},{1,5},{3,7},... | collective-permute-start | bytes 1572872 | tf_op jit(solution)/shard_map/ppermute | solution.py:53
  83.6 16.9 %collective-permute-start.28 = (bf16[2,128,768]{2,1,0:T(8,128)(2,1)S(1)}, bf16[2,128,768]{2,1,0:T(8,128)(2,1)S(1)}, u32[]{:S(2)}, u32[]{:S(2)}) collective-permute-start(bf16[2,128,768]{2,1,0:T(8,128)(2,1)S(1)} %gate.19.refs_0_), channel_id=1, source_target_pairs={{0,2},{2,0},{4,6},{6,4},{8,10},{10,8},{12,14},{14,12},{1,3},{3,1},... | collective-permute-start | bytes 1179656 | tf_op jit(solution)/shard_map/ppermute | solution.py:53
  84.5 13.4 %collective-permute-start.22 = (bf16[128,768]{1,0:T(8,128)(2,1)S(1)}, bf16[128,768]{1,0:T(8,128)(2,1)S(1)}, u32[]{:S(2)}, u32[]{:S(2)}) collective-permute-start(bf16[128,768]{1,0:T(8,128)(2,1)S(1)} %gate.18.refs_0_), channel_id=1, source_target_pairs={{0,12},{2,14},{4,8},{6,10},{8,4},{10,6},{12,0},{14,2},{1,13},{3,15... | collective-permute-start | bytes 589832 | tf_op jit(solution)/shard_map/ppermute | solution.py:53
  92.1 14.0 %collective-permute-start.29 = (bf16[128,1024]{1,0:T(8,128)(2,1)S(1)}, bf16[128,1024]{1,0:T(8,128)(2,1)S(1)}, u32[]{:S(2)}, u32[]{:S(2)}) collective-permute-start(bf16[128,1024]{1,0:T(8,128)(2,1)S(1)} %gate.20.refs_7_), channel_id=1, source_target_pairs={{0,2},{2,0},{4,6},{6,4},{8,10},{10,8},{12,14},{14,12},{1,3},{3,1},... | collective-permute-start | bytes 786440 | tf_op jit(solution)/shard_map/ppermute | solution.py:53
  97.9 12.5 %collective-permute-start.26 = (bf16[128,768]{1,0:T(8,128)(2,1)S(1)}, bf16[128,768]{1,0:T(8,128)(2,1)S(1)}, u32[]{:S(2)}, u32[]{:S(2)}) collective-permute-start(bf16[128,768]{1,0:T(8,128)(2,1)S(1)} %gate.21.refs_0_), channel_id=1, source_target_pairs={{0,2},{2,0},{4,6},{6,4},{8,10},{10,8},{12,14},{14,12},{1,3},{3,1},... | collective-permute-start | bytes 589832 | tf_op jit(solution)/shard_map/ppermute | solution.py:53
  99.3 21.0 %collective-permute-start.32 = (bf16[2,128,1024]{2,1,0:T(8,128)(2,1)S(1)}, bf16[2,128,1024]{2,1,0:T(8,128)(2,1)S(1)}, u32[]{:S(2)}, u32[]{:S(2)}) collective-permute-start(bf16[2,128,1024]{2,1,0:T(8,128)(2,1)S(1)} %collective-permute-done.31.refs_4_), channel_id=1, source_target_pairs={{0,2},{2,0},{4,6},{6,4},{8,10},{10,8},{12,14},{14,12},{1,3},{3,1},... | collective-permute-start | bytes 1572872 | tf_op jit(solution)/shard_map/ppermute | solution.py:53
  100.0 11.9 %collective-permute-start.27 = (bf16[2,128,768]{2,1,0:T(8,128)(2,1)S(1)}, bf16[2,128,768]{2,1,0:T(8,128)(2,1)S(1)}, u32[]{:S(2)}, u32[]{:S(2)}) collective-permute-start(bf16[2,128,768]{2,1,0:T(8,128)(2,1)S(1)} %stack.12.refs_7_), channel_id=1, source_target_pairs={{0,4},{2,6},{4,0},{6,2},{8,12},{10,14},{12,8},{14,10},{1,5},{3,7},... | collective-permute-start | bytes 1179656 | tf_op jit(solution)/shard_map/ppermute | solution.py:53
  110.4 10.7 %collective-permute-start.30 = (bf16[2,128,768]{2,1,0:T(8,128)(2,1)S(1)}, bf16[2,128,768]{2,1,0:T(8,128)(2,1)S(1)}, u32[]{:S(2)}, u32[]{:S(2)}) collective-permute-start(bf16[2,128,768]{2,1,0:T(8,128)(2,1)S(1)} %stack.13.refs_6_), channel_id=1, source_target_pairs={{0,4},{2,6},{4,0},{6,2},{8,12},{10,14},{12,8},{14,10},{1,5},{3,7},... | collective-permute-start | bytes 1179656 | tf_op jit(solution)/shard_map/ppermute | solution.py:53
  (6 other events, 58.1 us)

commit v9 on v8

--- a/solution.py
+++ b/solution.py
@@ -19,11 +19,11 @@
 FAR, SIDE, CROSS, NEAR, BOTH = "far", "side", "cross", "near", "both"
 ATTEND, STACK, PROJECT, FINISH, OWN = "attend", "stack", "project", "finish", "own"
 ORDER = (
-    (ATTEND, 0), (ATTEND, 1), (CROSS, 0), (STACK, 0), (ATTEND, 2), (STACK, 1, (FAR, 0)), (FAR, 2),
-    (BOTH, 0, (SIDE, 1), (SIDE, 2)), (ATTEND, 3, (CROSS, 0)), (ATTEND, 4),
-    (CROSS, 1, (BOTH, 0), (FAR, 1)), (PROJECT, 0, (SIDE, 3)), (STACK, 2), (FAR, 3, (NEAR, 1)),
-    (CROSS, 2, (CROSS, 1)), (BOTH, 1, (SIDE, 4)), (FAR, 4, (NEAR, 2)), (BOTH, 2, (CROSS, 2)),
-    (STACK, 3), (CROSS, 3, (BOTH, 1)), (PROJECT, 1, (NEAR, 1)), (CROSS, 4), (STACK, 4),
+    (ATTEND, 0), (ATTEND, 1), (STACK, 0), (ATTEND, 2), (CROSS, 0), (STACK, 1), (FAR, 2),
+    (BOTH, 0, (SIDE, 1), (SIDE, 2)), (ATTEND, 3, (CROSS, 0)), (ATTEND, 4), (CROSS, 1, (BOTH, 0)),
+    (PROJECT, 0, (SIDE, 3), (NEAR, 0)), (STACK, 2), (FAR, 3, (NEAR, 1)), (CROSS, 2, (CROSS, 1)),
+    (BOTH, 1, (SIDE, 4)), (BOTH, 2, (CROSS, 2)), (FAR, 4, (NEAR, 2)), (STACK, 3),
+    (CROSS, 3, (BOTH, 1), (SIDE, 3)), (PROJECT, 1, (NEAR, 1)), (CROSS, 4), (STACK, 4),
     (PROJECT, 2, (CROSS, 3)), (BOTH, 4), (PROJECT, 3, (NEAR, 4)),
 )
 LOCAL = pl.BlockSpec(memory_space=pltpu.VMEM)
@@ -331,7 +331,7 @@
 def attend(start, heads, queries, bias, w_value, kv, scale, after=()):
     tokens, keys = bias.shape
     value = w_value.shape[2]
-    block = next(count for count in (4, 3, 2, 1) if heads % count == 0) * tokens
+    block = next(count for count in (4, 3, 2, 1) if heads % count == 0 and heads > count) * tokens
     return pl.pallas_call(
         functools.partial(attend_kernel, scale * math.log2(math.e), start, heads),
         in_specs=[LOCAL] * 4 + [ANYWHERE] * len(after),
@@ -411,19 +411,18 @@
     return ((me // groups) ^ side ^ (1 - keep)).astype(jnp.int32)
 
 
-def finish_kernel(start, sizes, first, w_ref, *refs):
-    given_ref, kept_ref, gathered = refs[-3:]
+def finish_kernel(start, sizes, first, keep, w_ref, *refs):
+    out_ref, gathered = refs[-2:]
     acc_ref = refs[sum(sizes)]
     parts = grouped(refs, sizes)
     tokens, depth = parts[0][0].shape[-2:]
     rows = slice(first * tokens, (first + len(parts)) * tokens)
-    for keep, out_ref in enumerate((given_ref, kept_ref)):
-        other = other_half(acc_ref.shape[1] // tokens, keep)
-        gather_into(gathered.at[keep], parts, other)
-        product = jnp.dot(
-            gathered[keep], w_ref[start : start + depth], preferred_element_type=F32
-        )
-        out_ref[...] = (acc_ref[other, rows] + product).astype(out_ref.dtype)
+    other = other_half(acc_ref.shape[1] // tokens, keep)
+    gather_into(gathered, parts, other)
+    product = jnp.dot(
+        gathered[...], w_ref[start : start + depth], preferred_element_type=F32
+    )
+    out_ref[...] = (acc_ref[other, rows] + product).astype(out_ref.dtype)
 
 
 def finish(start, parts, w_output, acc, after=(), first=0):
@@ -432,16 +431,22 @@
     tokens, depth = blocks[0].shape[-2:]
     columns = w_output.shape[1]
     rows = len(parts) * tokens
-    return pl.pallas_call(
-        functools.partial(finish_kernel, start, sizes, first),
-        in_specs=[LOCAL] * (2 + len(blocks)) + [ANYWHERE] * len(after),
-        out_specs=[LOCAL] * 2,
-        out_shape=[pltpu.VMEM((rows, columns), BF16), pltpu.VMEM((rows, columns), F32)],
-        scratch_shapes=[pltpu.VMEM((2, rows, depth), BF16)],
-        compiler_params=params(12),
-        cost_estimate=cost(0, 1024),
-        name="finish",
-    )(*map(held, [w_output, *blocks, acc]), *after)
+    outs = []
+    for keep, dtype in enumerate((BF16, F32)):
+        after = [*after, *outs]
+        outs.append(
+            pl.pallas_call(
+                functools.partial(finish_kernel, start, sizes, first, keep),
+                in_specs=[LOCAL] * (2 + len(blocks)) + [ANYWHERE] * len(after),
+                out_specs=LOCAL,
+                out_shape=pltpu.VMEM((rows, columns), dtype),
+                scratch_shapes=[pltpu.VMEM((rows, depth), BF16)],
+                compiler_params=params(12),
+                cost_estimate=cost(0, 1024),
+                name=f"finish{keep}",
+            )(*map(held, [w_output, *blocks, acc]), *after)
+        )
+    return outs
 
 
 def total_kernel(keys, far, groups, mine_ref, other_ref, *refs):

time: 127 us -> 126 us (level)
  transfers between devices with their start and end apart: 34 -> 34, of which waited for: 19 -> 19; matrix products, arithmetic and copies ran while one was open for 0% -> 0% of each run, Pallas kernels for 24% -> 25%
where the time goes in v9:
time: 126 us
  waiting for transfers between devices  48 us (38%)
  starting transfers between devices  38.8 us (31%)
  Pallas kernels  37.4 us (30%)
    ppermute x29, waiting for transfers between devices, exchange(): return lax.ppermute(x, 'ctx', [(i, i ^ mask) for i in range(shards)])  46.4 us
    ppermute x29, starting transfers between devices, exchange(): return lax.ppermute(x, 'ctx', [(i, i ^ mask) for i in range(shards)])  38.2 us
    pallas_call x5, Pallas kernels, attend(): pl.pallas_call(functools.partial(attend_kernel, scale * math.log2(math.e)...  18.4 us
    pallas_call x5, Pallas kernels, project(): pl.pallas_call(functools.partial(project_kernel, start, sizes, first, acc...  9.49 us
    pallas_call x1, Pallas kernels, prep(): pl.pallas_call(prep_kernel, in_specs=[ANYWHERE] * 3, out_specs=LOCAL, out...  3.89 us
  transfers between devices with their start and end apart: 34, of which 19 were waited for; matrix products, arithmetic and copies ran while one was open for 0% of the time, Pallas kernels for 25%

profile of v9, /device:TPU:0, one launch (start us, length us, event | category | flops | bytes accessed | tf_op | source)
XLA Modules:
  0.0 125.6 jit_solution(5194660365743978258)
XLA Ops:
  1.1 5.1 %collective-permute-start = (bf16[336,128]{1,0:T(8,128)(2,1)S(1)}, bf16[336,128]{1,0:T(8,128)(2,1)S(1)}, u32[]{:S(2)}, u32[]{:S(2)}) collective-permute-start(bf16[336,128]{1,0:T(8,128)(2,1)S(1)} %pack.1.first_ref), channel_id=1, source_target_pairs={{0,12},{2,14},{4,8},{6,10},{8,4},{10,6},{12,0},{14,2},{1,13},{3,15... | collective-permute-start | bytes 258056 | tf_op jit(solution)/shard_map/ppermute | solution.py:53
  6.2 3.9 %prep.1.refs_0_.q_ref = bf16[4096,640]{1,0:T(8,128)(2,1)S(1)} custom-call(bf16[128,4096]{1,0:T(8,128)(2,1)} %q_hbm.1, bf16[128,2048]{1,0:T(8,128)(2,1)} %r_hbm.1, bf16[32,128,512]{2,1,0:T(8,128)(2,1)} %w_hbm.1), custom_call_target="tpu_custom_call" | custom-call | bytes 1024 | tf_op jit(solution)/shard_map/prep/pallas_call | solution.py:215
  10.4 1.5 %collective-permute-start.1 = (bf16[2,336,128]{2,1,0:T(8,128)(2,1)S(1)}, bf16[2,336,128]{2,1,0:T(8,128)(2,1)S(1)}, u32[]{:S(2)}, u32[]{:S(2)}) collective-permute-start(bf16[2,336,128]{2,1,0:T(8,128)(2,1)S(1)} %stack.7.refs_0_), channel_id=1, source_target_pairs={{0,2},{2,0},{4,6},{6,4},{8,10},{10,8},{12,14},{14,12},{1,3},{3,1},... | collective-permute-start | bytes 516104 | tf_op jit(solution)/shard_map/ppermute | solution.py:53
  11.9 4.2 %collective-permute-done.2.refs_2_ = bf16[2,336,128]{2,1,0:T(8,128)(2,1)S(1)} collective-permute-done((bf16[2,336,128]{2,1,0:T(8,128)(2,1)S(1)}, bf16[2,336,128]{2,1,0:T(8,128)(2,1)S(1)}, u32[]{:S(2)}, u32[]{:S(2)}) %collective-permute-start.2) | collective-permute-done | bytes 172064 | tf_op jit(solution)/shard_map/ppermute | solution.py:53
  16.1 1.5 %collective-permute-start.3 = (bf16[2,336,128]{2,1,0:T(8,128)(2,1)S(1)}, bf16[2,336,128]{2,1,0:T(8,128)(2,1)S(1)}, u32[]{:S(2)}, u32[]{:S(2)}) collective-permute-start(bf16[2,336,128]{2,1,0:T(8,128)(2,1)S(1)} %collective-permute-done.2.refs_2_), channel_id=1, source_target_pairs={{0,2},{2,0},{4,6},{6,4},{8,10},{10,8},{12,14},{14,12},{1,3},{3,1},... | collective-permute-start | bytes 516104 | tf_op jit(solution)/shard_map/ppermute | solution.py:53
  18.1 3.4 %collective-permute-done.3.refs_3_ = bf16[2,336,128]{2,1,0:T(8,128)(2,1)S(1)} collective-permute-done((bf16[2,336,128]{2,1,0:T(8,128)(2,1)S(1)}, bf16[2,336,128]{2,1,0:T(8,128)(2,1)S(1)}, u32[]{:S(2)}, u32[]{:S(2)}) %collective-permute-start.3) | collective-permute-done | bytes 172064 | tf_op jit(solution)/shard_map/ppermute | solution.py:53
  23.4 2.4 %attend0.1.refs_0_.first_ref = bf16[128,512]{1,0:T(8,128)(2,1)S(1)} custom-call(bf16[4096,640]{1,0:T(8,128)(2,1)S(1)} %prep.1.refs_0_.q_ref, f32[128,1152]{1,0:T(8,128)S(1)} %mask.1.bias_ref, bf16[32,512,128]{2,1,0:T(8,128)(2,1)S(1)} %copy-done, bf16[1152,640]{1,0:T(8,128)(2,1)S(1)} %join.1.kv_ref), custom_call_target="tpu_custom_call" | custom-call | bytes 1024 | tf_op jit(solution)/shard_map/attend0/pallas_call | solution.py:335
  25.8 2.0 %collective-permute-start.8 = (bf16[128,512]{1,0:T(8,128)(2,1)S(1)}, bf16[128,512]{1,0:T(8,128)(2,1)S(1)}, u32[]{:S(2)}, u32[]{:S(2)}) collective-permute-start(bf16[128,512]{1,0:T(8,128)(2,1)S(1)} %attend0.1.refs_0_.first_ref), channel_id=1, source_target_pairs={{0,12},{2,14},{4,8},{6,10},{8,4},{10,6},{12,0},{14,2},{1,13},{3,15... | collective-permute-start | bytes 393224 | tf_op jit(solution)/shard_map/ppermute | solution.py:53
  27.7 4.4 %attend4.1.refs_0_.first_ref = bf16[128,1024]{1,0:T(8,128)(2,1)S(1)} custom-call(bf16[4096,640]{1,0:T(8,128)(2,1)S(1)} %prep.1.refs_0_.q_ref, f32[128,1152]{1,0:T(8,128)S(1)} %mask.1.bias_ref, bf16[32,512,128]{2,1,0:T(8,128)(2,1)S(1)} %copy-done, bf16[1152,640]{1,0:T(8,128)(2,1)S(1)} %join.1.kv_ref, bf16[128,512]{1,0:T(8,128)(2,1)S(1)} %attend0.1.refs_0_.first_ref), custom_call_target="tpu_custom_call" | custom-call | bytes 1024 | tf_op jit(solution)/shard_map/attend4/pallas_call | solution.py:335
  32.2 2.0 %collective-permute-start.10 = (bf16[128,1024]{1,0:T(8,128)(2,1)S(1)}, bf16[128,1024]{1,0:T(8,128)(2,1)S(1)}, u32[]{:S(2)}, u32[]{:S(2)}) collective-permute-start(bf16[128,1024]{1,0:T(8,128)(2,1)S(1)} %attend4.1.refs_0_.first_ref), channel_id=1, source_target_pairs={{0,12},{2,14},{4,8},{6,10},{8,4},{10,6},{12,0},{14,2},{1,13},{3,15... | collective-permute-start | bytes 786440 | tf_op jit(solution)/shard_map/ppermute | solution.py:53
  34.2 1.5 %collective-permute-start.11 = (bf16[128,1024]{1,0:T(8,128)(2,1)S(1)}, bf16[128,1024]{1,0:T(8,128)(2,1)S(1)}, u32[]{:S(2)}, u32[]{:S(2)}) collective-permute-start(bf16[128,1024]{1,0:T(8,128)(2,1)S(1)} %attend4.1.refs_0_.first_ref), channel_id=1, source_target_pairs={{0,2},{2,0},{4,6},{6,4},{8,10},{10,8},{12,14},{14,12},{1,3},{3,1},... | collective-permute-start | bytes 786440 | tf_op jit(solution)/shard_map/ppermute | solution.py:53
  35.8 3.5 %attend12.1.refs_0_.x_ref.first_ref = bf16[128,768]{1,0:T(8,128)(2,1)S(1)} custom-call(bf16[4096,640]{1,0:T(8,128)(2,1)S(1)} %prep.1.refs_0_.q_ref, f32[128,1152]{1,0:T(8,128)S(1)} %mask.1.bias_ref, bf16[32,512,128]{2,1,0:T(8,128)(2,1)S(1)} %copy-done, bf16[1152,640]{1,0:T(8,128)(2,1)S(1)} %join.1.kv_ref, bf16[2,128,512]{2,1,0:T(8,128)(2,1)S(1)} %stack.8.refs_0_), custom_call_target="tpu_custom_call" | custom-call | bytes 1024 | tf_op jit(solution)/shard_map/attend12/pallas_call | solution.py:335
  41.4 1.8 %collective-permute-done.10.second_ref.x_ref.refs_1_ = bf16[128,1024]{1,0:T(8,128)(2,1)S(1)} collective-permute-done((bf16[128,1024]{1,0:T(8,128)(2,1)S(1)}, bf16[128,1024]{1,0:T(8,128)(2,1)S(1)}, u32[]{:S(2)}, u32[]{:S(2)}) %collective-permute-start.10) | collective-permute-done | bytes 262176 | tf_op jit(solution)/shard_map/ppermute | solution.py:53
  43.3 2.8 %collective-permute-start.19 = (bf16[2,128,1024]{2,1,0:T(8,128)(2,1)S(1)}, bf16[2,128,1024]{2,1,0:T(8,128)(2,1)S(1)}, u32[]{:S(2)}, u32[]{:S(2)}) collective-permute-start(bf16[2,128,1024]{2,1,0:T(8,128)(2,1)S(1)} %stack.9.refs_0_), channel_id=1, source_target_pairs={{0,4},{2,6},{4,0},{6,2},{8,12},{10,14},{12,8},{14,10},{1,5},{3,7},... | collective-permute-start | bytes 1572872 | tf_op jit(solution)/shard_map/ppermute | solution.py:53
  48.2 1.6 %collective-permute-start.16 = (bf16[2,128,512]{2,1,0:T(8,128)(2,1)S(1)}, bf16[2,128,512]{2,1,0:T(8,128)(2,1)S(1)}, u32[]{:S(2)}, u32[]{:S(2)}) collective-permute-start(bf16[2,128,512]{2,1,0:T(8,128)(2,1)S(1)} %gate.13.refs_0_), channel_id=1, source_target_pairs={{0,2},{2,0},{4,6},{6,4},{8,10},{10,8},{12,14},{14,12},{1,3},{3,1},... | collective-permute-start | bytes 786440 | tf_op jit(solution)/shard_map/ppermute | solution.py:53
  49.8 4.7 %attend18.1.refs_0_.x_ref.first_ref = bf16[128,1024]{1,0:T(8,128)(2,1)S(1)} custom-call(bf16[4096,640]{1,0:T(8,128)(2,1)S(1)} %prep.1.refs_0_.q_ref, f32[128,1152]{1,0:T(8,128)S(1)} %mask.1.bias_ref, bf16[32,512,128]{2,1,0:T(8,128)(2,1)S(1)} %copy-done, bf16[1152,640]{1,0:T(8,128)(2,1)S(1)} %join.1.kv_ref, bf16[2,128,512]{2,1,0:T(8,128)(2,1)S(1)} %gate.13.refs_0_, ...), custom_call_target="tpu_custom_call" | custom-call | bytes 1024 | tf_op jit(solution)/shard_map/attend18/pallas_call | solution.py:335
  55.6 1.9 %collective-permute-start.14 = (bf16[128,768]{1,0:T(8,128)(2,1)S(1)}, bf16[128,768]{1,0:T(8,128)(2,1)S(1)}, u32[]{:S(2)}, u32[]{:S(2)}) collective-permute-start(bf16[128,768]{1,0:T(8,128)(2,1)S(1)} %gate.12.refs_0_), channel_id=1, source_target_pairs={{0,12},{2,14},{4,8},{6,10},{8,4},{10,6},{12,0},{14,2},{1,13},{3,15... | collective-permute-start | bytes 589832 | tf_op jit(solution)/shard_map/ppermute | solution.py:53
  58.6 3.5 %attend26.1.refs_0_.x_ref.first_ref = bf16[128,768]{1,0:T(8,128)(2,1)S(1)} custom-call(bf16[4096,640]{1,0:T(8,128)(2,1)S(1)} %prep.1.refs_0_.q_ref, f32[128,1152]{1,0:T(8,128)S(1)} %mask.1.bias_ref, bf16[32,512,128]{2,1,0:T(8,128)(2,1)S(1)} %copy-done, bf16[1152,640]{1,0:T(8,128)(2,1)S(1)} %join.1.kv_ref, bf16[128,1024]{1,0:T(8,128)(2,1)S(1)} %attend18.1.refs_0_.x_ref.first_ref), custom_call_target="tpu_custom_call" | custom-call | bytes 1024 | tf_op jit(solution)/shard_map/attend26/pallas_call | solution.py:335
  63.0 3.6 %collective-permute-done.15.refs_2_ = bf16[128,512]{1,0:T(8,128)(2,1)S(1)} collective-permute-done((bf16[128,512]{1,0:T(8,128)(2,1)S(1)}, bf16[128,512]{1,0:T(8,128)(2,1)S(1)}, u32[]{:S(2)}, u32[]{:S(2)}) %collective-permute-start.15) | collective-permute-done | bytes 131104 | tf_op jit(solution)/shard_map/ppermute | solution.py:53
  69.2 2.0 %collective-permute-start.25 = (bf16[128,1024]{1,0:T(8,128)(2,1)S(1)}, bf16[128,1024]{1,0:T(8,128)(2,1)S(1)}, u32[]{:S(2)}, u32[]{:S(2)}) collective-permute-start(bf16[128,1024]{1,0:T(8,128)(2,1)S(1)} %gate.15.refs_0_), channel_id=1, source_target_pairs={{0,12},{2,14},{4,8},{6,10},{8,4},{10,6},{12,0},{14,2},{1,13},{3,15... | collective-permute-start | bytes 786440 | tf_op jit(solution)/shard_map/ppermute | solution.py:53
  73.3 3.1 %collective-permute-done.21.refs_1_.first_ref.refs_2_ = bf16[128,768]{1,0:T(8,128)(2,1)S(1)} collective-permute-done((bf16[128,768]{1,0:T(8,128)(2,1)S(1)}, bf16[128,768]{1,0:T(8,128)(2,1)S(1)}, u32[]{:S(2)}, u32[]{:S(2)}) %collective-permute-start.21) | collective-permute-done | bytes 196640 | tf_op jit(solution)/shard_map/ppermute | solution.py:53
  77.5 1.7 %collective-permute-done.18.x_ref.refs_1_.refs_4_ = bf16[2,128,768]{2,1,0:T(8,128)(2,1)S(1)} collective-permute-done((bf16[2,128,768]{2,1,0:T(8,128)(2,1)S(1)}, bf16[2,128,768]{2,1,0:T(8,128)(2,1)S(1)}, u32[]{:S(2)}, u32[]{:S(2)}) %collective-permute-start.18) | collective-permute-done | bytes 393248 | tf_op jit(solution)/shard_map/ppermute | solution.py:53
  80.7 2.5 %collective-permute-done.25.second_ref.x_ref.refs_1_ = bf16[128,1024]{1,0:T(8,128)(2,1)S(1)} collective-permute-done((bf16[128,1024]{1,0:T(8,128)(2,1)S(1)}, bf16[128,1024]{1,0:T(8,128)(2,1)S(1)}, u32[]{:S(2)}, u32[]{:S(2)}) %collective-permute-start.25) | collective-permute-done | bytes 262176 | tf_op jit(solution)/shard_map/ppermute | solution.py:53
  84.3 1.7 %collective-permute-start.23 = (bf16[128,768]{1,0:T(8,128)(2,1)S(1)}, bf16[128,768]{1,0:T(8,128)(2,1)S(1)}, u32[]{:S(2)}, u32[]{:S(2)}) collective-permute-start(bf16[128,768]{1,0:T(8,128)(2,1)S(1)} %gate.19.refs_0_), channel_id=1, source_target_pairs={{0,12},{2,14},{4,8},{6,10},{8,4},{10,6},{12,0},{14,2},{1,13},{3,15... | collective-permute-start | bytes 589832 | tf_op jit(solution)/shard_map/ppermute | solution.py:53
  86.0 5.9 %collective-permute-done.24.refs_1_.refs_5_ = bf16[2,128,1024]{2,1,0:T(8,128)(2,1)S(1)} collective-permute-done((bf16[2,128,1024]{2,1,0:T(8,128)(2,1)S(1)}, bf16[2,128,1024]{2,1,0:T(8,128)(2,1)S(1)}, u32[]{:S(2)}, u32[]{:S(2)}) %collective-permute-start.24) | collective-permute-done | bytes 524320 | tf_op jit(solution)/shard_map/ppermute | solution.py:53
  93.0 2.8 %project512.1.refs_0_.refs_6_ = f32[2,512,896]{2,1,0:T(8,128)S(1)} custom-call(bf16[4096,896]{1,0:T(8,128)(2,1)S(1)} %bitcast.2, bf16[128,1024]{1,0:T(8,128)(2,1)S(1)} %attend4.1.refs_0_.first_ref, bf16[128,1024]{1,0:T(8,128)(2,1)S(1)} %collective-permute-done.10.second_ref.x_ref.refs_1_, ...), custom_call_target="tpu_custom_call", output_to_operand_aliasing={{}: (7, {})} | custom-call | bytes 1024 | tf_op jit(solution)/shard_map/project512/pallas_call | solution.py:396
  95.8 1.9 %collective-permute-done.23.x_ref.second_ref.refs_1_ = bf16[128,768]{1,0:T(8,128)(2,1)S(1)} collective-permute-done((bf16[128,768]{1,0:T(8,128)(2,1)S(1)}, bf16[128,768]{1,0:T(8,128)(2,1)S(1)}, u32[]{:S(2)}, u32[]{:S(2)}) %collective-permute-start.23) | collective-permute-done | bytes 196640 | tf_op jit(solution)/shard_map/ppermute | solution.py:53
  100.3 5.6 %collective-permute-done.29.refs_8_.refs_3_ = bf16[128,1024]{1,0:T(8,128)(2,1)S(1)} collective-permute-done((bf16[128,1024]{1,0:T(8,128)(2,1)S(1)}, bf16[128,1024]{1,0:T(8,128)(2,1)S(1)}, u32[]{:S(2)}, u32[]{:S(2)}) %collective-permute-start.29) | collective-permute-done | bytes 262176 | tf_op jit(solution)/shard_map/ppermute | solution.py:53
  106.0 2.2 %project1536.1.refs_0_.refs_5_ = f32[2,512,896]{2,1,0:T(8,128)S(1)} custom-call(bf16[4096,896]{1,0:T(8,128)(2,1)S(1)} %bitcast.2, bf16[128,768]{1,0:T(8,128)(2,1)S(1)} %attend12.1.refs_0_.x_ref.first_ref, bf16[128,768]{1,0:T(8,128)(2,1)S(1)} %collective-permute-done.14.second_ref.x_ref.refs_1_, ...), custom_call_target="tpu_custom_call", output_to_operand_aliasing={{}: (7, {})} | custom-call | bytes 1024 | tf_op jit(solution)/shard_map/project1536/pallas_call | solution.py:396
  108.2 2.0 %collective-permute-done.26.second_ref.refs_3_ = bf16[128,768]{1,0:T(8,128)(2,1)S(1)} collective-permute-done((bf16[128,768]{1,0:T(8,128)(2,1)S(1)}, bf16[128,768]{1,0:T(8,128)(2,1)S(1)}, u32[]{:S(2)}, u32[]{:S(2)}) %collective-permute-start.26) | collective-permute-done | bytes 196640 | tf_op jit(solution)/shard_map/ppermute | solution.py:53
  111.7 2.4 %project2304.2.refs_2_ = f32[2,512,896]{2,1,0:T(8,128)S(1)} custom-call(bf16[4096,896]{1,0:T(8,128)(2,1)S(1)} %bitcast.2, bf16[128,1024]{1,0:T(8,128)(2,1)S(1)} %attend18.1.refs_0_.x_ref.first_ref, bf16[128,1024]{1,0:T(8,128)(2,1)S(1)} %collective-permute-done.25.second_ref.x_ref.refs_1_, ...), custom_call_target="tpu_custom_call", output_to_operand_aliasing={{}: (6, {})} | custom-call | bytes 1024 | tf_op jit(solution)/shard_map/project2304/pallas_call | solution.py:396
  114.4 5.7 %collective-permute-done.32.refs_0_ = bf16[2,128,1024]{2,1,0:T(8,128)(2,1)S(1)} collective-permute-done((bf16[2,128,1024]{2,1,0:T(8,128)(2,1)S(1)}, bf16[2,128,1024]{2,1,0:T(8,128)(2,1)S(1)}, u32[]{:S(2)}, u32[]{:S(2)}) %collective-permute-start.32) | collective-permute-done | bytes 524320 | tf_op jit(solution)/shard_map/ppermute | solution.py:53
  (81 shorter events, 29.6 us)
Async XLA Ops:
  1.1 9.0 %collective-permute-start = (bf16[336,128]{1,0:T(8,128)(2,1)S(1)}, bf16[336,128]{1,0:T(8,128)(2,1)S(1)}, u32[]{:S(2)}, u32[]{:S(2)}) collective-permute-start(bf16[336,128]{1,0:T(8,128)(2,1)S(1)} %pack.1.first_ref), channel_id=1, source_target_pairs={{0,12},{2,14},{4,8},{6,10},{8,4},{10,6},{12,0},{14,2},{1,13},{3,15... | collective-permute-start | bytes 258056 | tf_op jit(solution)/shard_map/ppermute | solution.py:53
  10.2 5.9 %collective-permute-start.2 = (bf16[2,336,128]{2,1,0:T(8,128)(2,1)S(1)}, bf16[2,336,128]{2,1,0:T(8,128)(2,1)S(1)}, u32[]{:S(2)}, u32[]{:S(2)}) collective-permute-start(bf16[2,336,128]{2,1,0:T(8,128)(2,1)S(1)} %stack.7.refs_0_), channel_id=1, source_target_pairs={{0,4},{2,6},{4,0},{6,2},{8,12},{10,14},{12,8},{14,10},{1,5},{3,7},... | collective-permute-start | bytes 516104 | tf_op jit(solution)/shard_map/ppermute | solution.py:53
  10.4 7.7 %collective-permute-start.1 = (bf16[2,336,128]{2,1,0:T(8,128)(2,1)S(1)}, bf16[2,336,128]{2,1,0:T(8,128)(2,1)S(1)}, u32[]{:S(2)}, u32[]{:S(2)}) collective-permute-start(bf16[2,336,128]{2,1,0:T(8,128)(2,1)S(1)} %stack.7.refs_0_), channel_id=1, source_target_pairs={{0,2},{2,0},{4,6},{6,4},{8,10},{10,8},{12,14},{14,12},{1,3},{3,1},... | collective-permute-start | bytes 516104 | tf_op jit(solution)/shard_map/ppermute | solution.py:53
  16.1 5.4 %collective-permute-start.3 = (bf16[2,336,128]{2,1,0:T(8,128)(2,1)S(1)}, bf16[2,336,128]{2,1,0:T(8,128)(2,1)S(1)}, u32[]{:S(2)}, u32[]{:S(2)}) collective-permute-start(bf16[2,336,128]{2,1,0:T(8,128)(2,1)S(1)} %collective-permute-done.2.refs_2_), channel_id=1, source_target_pairs={{0,2},{2,0},{4,6},{6,4},{8,10},{10,8},{12,14},{14,12},{1,3},{3,1},... | collective-permute-start | bytes 516104 | tf_op jit(solution)/shard_map/ppermute | solution.py:53
  17.6 5.2 %collective-permute-start.4 = (bf16[2,336,128]{2,1,0:T(8,128)(2,1)S(1)}, bf16[2,336,128]{2,1,0:T(8,128)(2,1)S(1)}, u32[]{:S(2)}, u32[]{:S(2)}) collective-permute-start(bf16[2,336,128]{2,1,0:T(8,128)(2,1)S(1)} %stack.7.refs_0_), channel_id=1, source_target_pairs={{0,1},{1,0},{2,3},{3,2},{4,5},{5,4},{6,7},{7,6},{8,9},{9,8},{10,11... | collective-permute-start | bytes 516104 | tf_op jit(solution)/shard_map/ppermute | solution.py:57
  17.6 5.2 %collective-permute-start.6 = (bf16[2,336,128]{2,1,0:T(8,128)(2,1)S(1)}, bf16[2,336,128]{2,1,0:T(8,128)(2,1)S(1)}, u32[]{:S(2)}, u32[]{:S(2)}) collective-permute-start(bf16[2,336,128]{2,1,0:T(8,128)(2,1)S(1)} %collective-permute-done.2.refs_2_), channel_id=1, source_target_pairs={{0,1},{1,0},{2,3},{3,2},{4,5},{5,4},{6,7},{7,6},{8,9},{9,8},{10,11... | collective-permute-start | bytes 516104 | tf_op jit(solution)/shard_map/ppermute | solution.py:57
  18.1 4.7 %collective-permute-start.5 = (bf16[2,336,128]{2,1,0:T(8,128)(2,1)S(1)}, bf16[2,336,128]{2,1,0:T(8,128)(2,1)S(1)}, u32[]{:S(2)}, u32[]{:S(2)}) collective-permute-start(bf16[2,336,128]{2,1,0:T(8,128)(2,1)S(1)} %collective-permute-done.1.refs_1_), channel_id=1, source_target_pairs={{0,1},{1,0},{2,3},{3,2},{4,5},{5,4},{6,7},{7,6},{8,9},{9,8},{10,11... | collective-permute-start | bytes 516104 | tf_op jit(solution)/shard_map/ppermute | solution.py:57
  25.8 9.9 %collective-permute-start.8 = (bf16[128,512]{1,0:T(8,128)(2,1)S(1)}, bf16[128,512]{1,0:T(8,128)(2,1)S(1)}, u32[]{:S(2)}, u32[]{:S(2)}) collective-permute-start(bf16[128,512]{1,0:T(8,128)(2,1)S(1)} %attend0.1.refs_0_.first_ref), channel_id=1, source_target_pairs={{0,12},{2,14},{4,8},{6,10},{8,4},{10,6},{12,0},{14,2},{1,13},{3,15... | collective-permute-start | bytes 393224 | tf_op jit(solution)/shard_map/ppermute | solution.py:53
  32.2 11.1 %collective-permute-start.10 = (bf16[128,1024]{1,0:T(8,128)(2,1)S(1)}, bf16[128,1024]{1,0:T(8,128)(2,1)S(1)}, u32[]{:S(2)}, u32[]{:S(2)}) collective-permute-start(bf16[128,1024]{1,0:T(8,128)(2,1)S(1)} %attend4.1.refs_0_.first_ref), channel_id=1, source_target_pairs={{0,12},{2,14},{4,8},{6,10},{8,4},{10,6},{12,0},{14,2},{1,13},{3,15... | collective-permute-start | bytes 786440 | tf_op jit(solution)/shard_map/ppermute | solution.py:53
  34.2 12.0 %collective-permute-start.11 = (bf16[128,1024]{1,0:T(8,128)(2,1)S(1)}, bf16[128,1024]{1,0:T(8,128)(2,1)S(1)}, u32[]{:S(2)}, u32[]{:S(2)}) collective-permute-start(bf16[128,1024]{1,0:T(8,128)(2,1)S(1)} %attend4.1.refs_0_.first_ref), channel_id=1, source_target_pairs={{0,2},{2,0},{4,6},{6,4},{8,10},{10,8},{12,14},{14,12},{1,3},{3,1},... | collective-permute-start | bytes 786440 | tf_op jit(solution)/shard_map/ppermute | solution.py:53
  35.7 12.5 %collective-permute-start.9 = (bf16[2,128,512]{2,1,0:T(8,128)(2,1)S(1)}, bf16[2,128,512]{2,1,0:T(8,128)(2,1)S(1)}, u32[]{:S(2)}, u32[]{:S(2)}) collective-permute-start(bf16[2,128,512]{2,1,0:T(8,128)(2,1)S(1)} %stack.8.refs_0_), channel_id=1, source_target_pairs={{0,4},{2,6},{4,0},{6,2},{8,12},{10,14},{12,8},{14,10},{1,5},{3,7},... | collective-permute-start | bytes 786440 | tf_op jit(solution)/shard_map/ppermute | solution.py:53
  39.3 7.9 %collective-permute-start.12 = (bf16[128,768]{1,0:T(8,128)(2,1)S(1)}, bf16[128,768]{1,0:T(8,128)(2,1)S(1)}, u32[]{:S(2)}, u32[]{:S(2)}) collective-permute-start(bf16[128,768]{1,0:T(8,128)(2,1)S(1)} %attend12.1.refs_0_.x_ref.first_ref), channel_id=1, source_target_pairs={{0,2},{2,0},{4,6},{6,4},{8,10},{10,8},{12,14},{14,12},{1,3},{3,1},... | collective-permute-start | bytes 589832 | tf_op jit(solution)/shard_map/ppermute | solution.py:53
  40.2 9.6 %collective-permute-start.13 = (bf16[128,512]{1,0:T(8,128)(2,1)S(1)}, bf16[128,512]{1,0:T(8,128)(2,1)S(1)}, u32[]{:S(2)}, u32[]{:S(2)}) collective-permute-start(bf16[128,512]{1,0:T(8,128)(2,1)S(1)} %gate.11.refs_0_), channel_id=1, source_target_pairs={{0,2},{2,0},{4,6},{6,4},{8,10},{10,8},{12,14},{14,12},{1,3},{3,1},... | collective-permute-start | bytes 393224 | tf_op jit(solution)/shard_map/ppermute | solution.py:53
  43.3 25.9 %collective-permute-start.19 = (bf16[2,128,1024]{2,1,0:T(8,128)(2,1)S(1)}, bf16[2,128,1024]{2,1,0:T(8,128)(2,1)S(1)}, u32[]{:S(2)}, u32[]{:S(2)}) collective-permute-start(bf16[2,128,1024]{2,1,0:T(8,128)(2,1)S(1)} %stack.9.refs_0_), channel_id=1, source_target_pairs={{0,4},{2,6},{4,0},{6,2},{8,12},{10,14},{12,8},{14,10},{1,5},{3,7},... | collective-permute-start | bytes 1572872 | tf_op jit(solution)/shard_map/ppermute | solution.py:53
  48.2 13.8 %collective-permute-start.16 = (bf16[2,128,512]{2,1,0:T(8,128)(2,1)S(1)}, bf16[2,128,512]{2,1,0:T(8,128)(2,1)S(1)}, u32[]{:S(2)}, u32[]{:S(2)}) collective-permute-start(bf16[2,128,512]{2,1,0:T(8,128)(2,1)S(1)} %gate.13.refs_0_), channel_id=1, source_target_pairs={{0,2},{2,0},{4,6},{6,4},{8,10},{10,8},{12,14},{14,12},{1,3},{3,1},... | collective-permute-start | bytes 786440 | tf_op jit(solution)/shard_map/ppermute | solution.py:53
  54.5 12.1 %collective-permute-start.17 = (bf16[128,1024]{1,0:T(8,128)(2,1)S(1)}, bf16[128,1024]{1,0:T(8,128)(2,1)S(1)}, u32[]{:S(2)}, u32[]{:S(2)}) collective-permute-start(bf16[128,1024]{1,0:T(8,128)(2,1)S(1)} %attend18.1.refs_0_.x_ref.first_ref), channel_id=1, source_target_pairs={{0,2},{2,0},{4,6},{6,4},{8,10},{10,8},{12,14},{14,12},{1,3},{3,1},... | collective-permute-start | bytes 786440 | tf_op jit(solution)/shard_map/ppermute | solution.py:53
  55.6 12.4 %collective-permute-start.14 = (bf16[128,768]{1,0:T(8,128)(2,1)S(1)}, bf16[128,768]{1,0:T(8,128)(2,1)S(1)}, u32[]{:S(2)}, u32[]{:S(2)}) collective-permute-start(bf16[128,768]{1,0:T(8,128)(2,1)S(1)} %gate.12.refs_0_), channel_id=1, source_target_pairs={{0,12},{2,14},{4,8},{6,10},{8,4},{10,6},{12,0},{14,2},{1,13},{3,15... | collective-permute-start | bytes 589832 | tf_op jit(solution)/shard_map/ppermute | solution.py:53
  57.5 9.2 %collective-permute-start.15 = (bf16[128,512]{1,0:T(8,128)(2,1)S(1)}, bf16[128,512]{1,0:T(8,128)(2,1)S(1)}, u32[]{:S(2)}, u32[]{:S(2)}) collective-permute-start(bf16[128,512]{1,0:T(8,128)(2,1)S(1)} %attend0.1.refs_0_.first_ref), channel_id=1, source_target_pairs={{0,2},{2,0},{4,6},{6,4},{8,10},{10,8},{12,14},{14,12},{1,3},{3,1},... | collective-permute-start | bytes 393224 | tf_op jit(solution)/shard_map/ppermute | solution.py:53
  62.1 10.2 %collective-permute-start.20 = (bf16[128,1024]{1,0:T(8,128)(2,1)S(1)}, bf16[128,1024]{1,0:T(8,128)(2,1)S(1)}, u32[]{:S(2)}, u32[]{:S(2)}) collective-permute-start(bf16[128,1024]{1,0:T(8,128)(2,1)S(1)} %gate.14.refs_6_), channel_id=1, source_target_pairs={{0,2},{2,0},{4,6},{6,4},{8,10},{10,8},{12,14},{14,12},{1,3},{3,1},... | collective-permute-start | bytes 786440 | tf_op jit(solution)/shard_map/ppermute | solution.py:53
  68.0 11.3 %collective-permute-start.18 = (bf16[2,128,768]{2,1,0:T(8,128)(2,1)S(1)}, bf16[2,128,768]{2,1,0:T(8,128)(2,1)S(1)}, u32[]{:S(2)}, u32[]{:S(2)}) collective-permute-start(bf16[2,128,768]{2,1,0:T(8,128)(2,1)S(1)} %stack.10.refs_0_), channel_id=1, source_target_pairs={{0,4},{2,6},{4,0},{6,2},{8,12},{10,14},{12,8},{14,10},{1,5},{3,7},... | collective-permute-start | bytes 1179656 | tf_op jit(solution)/shard_map/ppermute | solution.py:53
  68.5 8.0 %collective-permute-start.21 = (bf16[128,768]{1,0:T(8,128)(2,1)S(1)}, bf16[128,768]{1,0:T(8,128)(2,1)S(1)}, u32[]{:S(2)}, u32[]{:S(2)}) collective-permute-start(bf16[128,768]{1,0:T(8,128)(2,1)S(1)} %attend26.1.refs_0_.x_ref.first_ref), channel_id=1, source_target_pairs={{0,2},{2,0},{4,6},{6,4},{8,10},{10,8},{12,14},{14,12},{1,3},{3,1},... | collective-permute-start | bytes 589832 | tf_op jit(solution)/shard_map/ppermute | solution.py:53
  69.2 14.1 %collective-permute-start.25 = (bf16[128,1024]{1,0:T(8,128)(2,1)S(1)}, bf16[128,1024]{1,0:T(8,128)(2,1)S(1)}, u32[]{:S(2)}, u32[]{:S(2)}) collective-permute-start(bf16[128,1024]{1,0:T(8,128)(2,1)S(1)} %gate.15.refs_0_), channel_id=1, source_target_pairs={{0,12},{2,14},{4,8},{6,10},{8,4},{10,6},{12,0},{14,2},{1,13},{3,15... | collective-permute-start | bytes 786440 | tf_op jit(solution)/shard_map/ppermute | solution.py:53
  72.3 8.4 %collective-permute-start.22 = (bf16[128,768]{1,0:T(8,128)(2,1)S(1)}, bf16[128,768]{1,0:T(8,128)(2,1)S(1)}, u32[]{:S(2)}, u32[]{:S(2)}) collective-permute-start(bf16[128,768]{1,0:T(8,128)(2,1)S(1)} %gate.16.refs_0_), channel_id=1, source_target_pairs={{0,2},{2,0},{4,6},{6,4},{8,10},{10,8},{12,14},{14,12},{1,3},{3,1},... | collective-permute-start | bytes 589832 | tf_op jit(solution)/shard_map/ppermute | solution.py:53
  76.5 15.4 %collective-permute-start.24 = (bf16[2,128,1024]{2,1,0:T(8,128)(2,1)S(1)}, bf16[2,128,1024]{2,1,0:T(8,128)(2,1)S(1)}, u32[]{:S(2)}, u32[]{:S(2)}) collective-permute-start(bf16[2,128,1024]{2,1,0:T(8,128)(2,1)S(1)} %gate.17.refs_0_), channel_id=1, source_target_pairs={{0,2},{2,0},{4,6},{6,4},{8,10},{10,8},{12,14},{14,12},{1,3},{3,1},... | collective-permute-start | bytes 1572872 | tf_op jit(solution)/shard_map/ppermute | solution.py:53
  83.3 15.8 %collective-permute-start.31 = (bf16[2,128,1024]{2,1,0:T(8,128)(2,1)S(1)}, bf16[2,128,1024]{2,1,0:T(8,128)(2,1)S(1)}, u32[]{:S(2)}, u32[]{:S(2)}) collective-permute-start(bf16[2,128,1024]{2,1,0:T(8,128)(2,1)S(1)} %stack.11.refs_0_), channel_id=1, source_target_pairs={{0,4},{2,6},{4,0},{6,2},{8,12},{10,14},{12,8},{14,10},{1,5},{3,7},... | collective-permute-start | bytes 1572872 | tf_op jit(solution)/shard_map/ppermute | solution.py:53
  83.4 16.9 %collective-permute-start.28 = (bf16[2,128,768]{2,1,0:T(8,128)(2,1)S(1)}, bf16[2,128,768]{2,1,0:T(8,128)(2,1)S(1)}, u32[]{:S(2)}, u32[]{:S(2)}) collective-permute-start(bf16[2,128,768]{2,1,0:T(8,128)(2,1)S(1)} %gate.18.refs_0_), channel_id=1, source_target_pairs={{0,2},{2,0},{4,6},{6,4},{8,10},{10,8},{12,14},{14,12},{1,3},{3,1},... | collective-permute-start | bytes 1179656 | tf_op jit(solution)/shard_map/ppermute | solution.py:53
  84.3 13.4 %collective-permute-start.23 = (bf16[128,768]{1,0:T(8,128)(2,1)S(1)}, bf16[128,768]{1,0:T(8,128)(2,1)S(1)}, u32[]{:S(2)}, u32[]{:S(2)}) collective-permute-start(bf16[128,768]{1,0:T(8,128)(2,1)S(1)} %gate.19.refs_0_), channel_id=1, source_target_pairs={{0,12},{2,14},{4,8},{6,10},{8,4},{10,6},{12,0},{14,2},{1,13},{3,15... | collective-permute-start | bytes 589832 | tf_op jit(solution)/shard_map/ppermute | solution.py:53
  91.9 14.0 %collective-permute-start.29 = (bf16[128,1024]{1,0:T(8,128)(2,1)S(1)}, bf16[128,1024]{1,0:T(8,128)(2,1)S(1)}, u32[]{:S(2)}, u32[]{:S(2)}) collective-permute-start(bf16[128,1024]{1,0:T(8,128)(2,1)S(1)} %gate.20.refs_7_), channel_id=1, source_target_pairs={{0,2},{2,0},{4,6},{6,4},{8,10},{10,8},{12,14},{14,12},{1,3},{3,1},... | collective-permute-start | bytes 786440 | tf_op jit(solution)/shard_map/ppermute | solution.py:53
  97.7 12.5 %collective-permute-start.26 = (bf16[128,768]{1,0:T(8,128)(2,1)S(1)}, bf16[128,768]{1,0:T(8,128)(2,1)S(1)}, u32[]{:S(2)}, u32[]{:S(2)}) collective-permute-start(bf16[128,768]{1,0:T(8,128)(2,1)S(1)} %gate.21.refs_0_), channel_id=1, source_target_pairs={{0,2},{2,0},{4,6},{6,4},{8,10},{10,8},{12,14},{14,12},{1,3},{3,1},... | collective-permute-start | bytes 589832 | tf_op jit(solution)/shard_map/ppermute | solution.py:53
  99.1 21.0 %collective-permute-start.32 = (bf16[2,128,1024]{2,1,0:T(8,128)(2,1)S(1)}, bf16[2,128,1024]{2,1,0:T(8,128)(2,1)S(1)}, u32[]{:S(2)}, u32[]{:S(2)}) collective-permute-start(bf16[2,128,1024]{2,1,0:T(8,128)(2,1)S(1)} %collective-permute-done.31.refs_4_), channel_id=1, source_target_pairs={{0,2},{2,0},{4,6},{6,4},{8,10},{10,8},{12,14},{14,12},{1,3},{3,1},... | collective-permute-start | bytes 1572872 | tf_op jit(solution)/shard_map/ppermute | solution.py:53
  99.8 11.9 %collective-permute-start.27 = (bf16[2,128,768]{2,1,0:T(8,128)(2,1)S(1)}, bf16[2,128,768]{2,1,0:T(8,128)(2,1)S(1)}, u32[]{:S(2)}, u32[]{:S(2)}) collective-permute-start(bf16[2,128,768]{2,1,0:T(8,128)(2,1)S(1)} %stack.12.refs_7_), channel_id=1, source_target_pairs={{0,4},{2,6},{4,0},{6,2},{8,12},{10,14},{12,8},{14,10},{1,5},{3,7},... | collective-permute-start | bytes 1179656 | tf_op jit(solution)/shard_map/ppermute | solution.py:53
  110.2 10.7 %collective-permute-start.30 = (bf16[2,128,768]{2,1,0:T(8,128)(2,1)S(1)}, bf16[2,128,768]{2,1,0:T(8,128)(2,1)S(1)}, u32[]{:S(2)}, u32[]{:S(2)}) collective-permute-start(bf16[2,128,768]{2,1,0:T(8,128)(2,1)S(1)} %stack.13.refs_6_), channel_id=1, source_target_pairs={{0,4},{2,6},{4,0},{6,2},{8,12},{10,14},{12,8},{14,10},{1,5},{3,7},... | collective-permute-start | bytes 1179656 | tf_op jit(solution)/shard_map/ppermute | solution.py:53
  (6 other events, 58.1 us)

commit v10 on v9

--- a/solution.py
+++ b/solution.py
@@ -549,7 +549,12 @@
     chunk += 1
     first = 3 if sums else 0
     some = parts_of(chunk)[first:]
-    return [*sums, finish(starts[chunk] * value, some, w_output, acc, [acc], first)]
+    row, after = starts[chunk] * value, [acc, some[-1][0]]
+    cuts = [some] if sums else [some[:2], some[2:]]
+    for cut in cuts:
+        sums.append(finish(row, cut, w_output, acc, after, first))
+        first, after = first + len(cut), [sums[-1][1]]
+    return sums
 
 
 def local(
@@ -580,7 +585,8 @@
     starts = [sum(heads[:chunk]) for chunk in range(len(heads))]
     if shards == 8:
         sums = overlap(heads, starts, queries, bias, w_value, kv, w_output, scale)
-        split = (keys[:3], keys[3:]) if len(sums) > 1 else (keys,)
+        cut = sums[0][1].shape[0] // tokens
+        split = (keys[:cut], keys[cut:])
     else:
         acc = None
         for chunk, start in enumerate(starts):

time: 126 us -> 126 us (level)
  waiting for transfers between devices: 48 us -> 46.6 us
    ppermute x5 -> x6, waiting for transfers between devices: 1.52 us -> 0.13 us  [sibling(): return lax.ppermute(x, 'head', [(0, 1), (1, 0)])]
  transfers between devices with their start and end apart: 34 -> 35, of which waited for: 19 -> 18; matrix products, arithmetic and copies ran while one was open for 0% -> 0% of each run, Pallas kernels for 25% -> 26%
where the time goes in v10:
time: 126 us
  waiting for transfers between devices  46.6 us (37%)
  starting transfers between devices  39.3 us (31%)
  Pallas kernels  38.4 us (30%)
    ppermute x29, waiting for transfers between devices, exchange(): return lax.ppermute(x, 'ctx', [(i, i ^ mask) for i in range(shards)])  46.5 us
    ppermute x29, starting transfers between devices, exchange(): return lax.ppermute(x, 'ctx', [(i, i ^ mask) for i in range(shards)])  38.2 us
    pallas_call x5, Pallas kernels, attend(): pl.pallas_call(functools.partial(attend_kernel, scale * math.log2(math.e)...  18.4 us
    pallas_call x5, Pallas kernels, project(): pl.pallas_call(functools.partial(project_kernel, start, sizes, first, acc...  9.49 us
    pallas_call x1, Pallas kernels, prep(): pl.pallas_call(prep_kernel, in_specs=[ANYWHERE] * 3, out_specs=LOCAL, out...  3.89 us
  transfers between devices with their start and end apart: 35, of which 18 were waited for; matrix products, arithmetic and copies ran while one was open for 0% of the time, Pallas kernels for 26%

profile of v10, /device:TPU:0, one launch (start us, length us, event | category | flops | bytes accessed | tf_op | source)
XLA Modules:
  0.0 125.8 jit_solution(15835912510873164470)
XLA Ops:
  1.1 5.1 %collective-permute-start = (bf16[336,128]{1,0:T(8,128)(2,1)S(1)}, bf16[336,128]{1,0:T(8,128)(2,1)S(1)}, u32[]{:S(2)}, u32[]{:S(2)}) collective-permute-start(bf16[336,128]{1,0:T(8,128)(2,1)S(1)} %pack.1.first_ref), channel_id=1, source_target_pairs={{0,12},{2,14},{4,8},{6,10},{8,4},{10,6},{12,0},{14,2},{1,13},{3,15... | collective-permute-start | bytes 258056 | tf_op jit(solution)/shard_map/ppermute | solution.py:53
  6.2 3.9 %prep.1.refs_0_.q_ref = bf16[4096,640]{1,0:T(8,128)(2,1)S(1)} custom-call(bf16[128,4096]{1,0:T(8,128)(2,1)} %q_hbm.1, bf16[128,2048]{1,0:T(8,128)(2,1)} %r_hbm.1, bf16[32,128,512]{2,1,0:T(8,128)(2,1)} %w_hbm.1), custom_call_target="tpu_custom_call" | custom-call | bytes 1024 | tf_op jit(solution)/shard_map/prep/pallas_call | solution.py:215
  10.4 1.5 %collective-permute-start.1 = (bf16[2,336,128]{2,1,0:T(8,128)(2,1)S(1)}, bf16[2,336,128]{2,1,0:T(8,128)(2,1)S(1)}, u32[]{:S(2)}, u32[]{:S(2)}) collective-permute-start(bf16[2,336,128]{2,1,0:T(8,128)(2,1)S(1)} %stack.7.refs_0_), channel_id=1, source_target_pairs={{0,2},{2,0},{4,6},{6,4},{8,10},{10,8},{12,14},{14,12},{1,3},{3,1},... | collective-permute-start | bytes 516104 | tf_op jit(solution)/shard_map/ppermute | solution.py:53
  11.9 4.2 %collective-permute-done.2.refs_2_ = bf16[2,336,128]{2,1,0:T(8,128)(2,1)S(1)} collective-permute-done((bf16[2,336,128]{2,1,0:T(8,128)(2,1)S(1)}, bf16[2,336,128]{2,1,0:T(8,128)(2,1)S(1)}, u32[]{:S(2)}, u32[]{:S(2)}) %collective-permute-start.2) | collective-permute-done | bytes 172064 | tf_op jit(solution)/shard_map/ppermute | solution.py:53
  16.1 1.5 %collective-permute-start.3 = (bf16[2,336,128]{2,1,0:T(8,128)(2,1)S(1)}, bf16[2,336,128]{2,1,0:T(8,128)(2,1)S(1)}, u32[]{:S(2)}, u32[]{:S(2)}) collective-permute-start(bf16[2,336,128]{2,1,0:T(8,128)(2,1)S(1)} %collective-permute-done.2.refs_2_), channel_id=1, source_target_pairs={{0,2},{2,0},{4,6},{6,4},{8,10},{10,8},{12,14},{14,12},{1,3},{3,1},... | collective-permute-start | bytes 516104 | tf_op jit(solution)/shard_map/ppermute | solution.py:53
  18.1 3.4 %collective-permute-done.3.refs_3_ = bf16[2,336,128]{2,1,0:T(8,128)(2,1)S(1)} collective-permute-done((bf16[2,336,128]{2,1,0:T(8,128)(2,1)S(1)}, bf16[2,336,128]{2,1,0:T(8,128)(2,1)S(1)}, u32[]{:S(2)}, u32[]{:S(2)}) %collective-permute-start.3) | collective-permute-done | bytes 172064 | tf_op jit(solution)/shard_map/ppermute | solution.py:53
  23.4 2.4 %attend0.1.refs_0_.first_ref = bf16[128,512]{1,0:T(8,128)(2,1)S(1)} custom-call(bf16[4096,640]{1,0:T(8,128)(2,1)S(1)} %prep.1.refs_0_.q_ref, f32[128,1152]{1,0:T(8,128)S(1)} %mask.1.bias_ref, bf16[32,512,128]{2,1,0:T(8,128)(2,1)S(1)} %copy-done, bf16[1152,640]{1,0:T(8,128)(2,1)S(1)} %join.1.kv_ref), custom_call_target="tpu_custom_call" | custom-call | bytes 1024 | tf_op jit(solution)/shard_map/attend0/pallas_call | solution.py:335
  25.8 2.0 %collective-permute-start.8 = (bf16[128,512]{1,0:T(8,128)(2,1)S(1)}, bf16[128,512]{1,0:T(8,128)(2,1)S(1)}, u32[]{:S(2)}, u32[]{:S(2)}) collective-permute-start(bf16[128,512]{1,0:T(8,128)(2,1)S(1)} %attend0.1.refs_0_.first_ref), channel_id=1, source_target_pairs={{0,12},{2,14},{4,8},{6,10},{8,4},{10,6},{12,0},{14,2},{1,13},{3,15... | collective-permute-start | bytes 393224 | tf_op jit(solution)/shard_map/ppermute | solution.py:53
  27.7 4.4 %attend4.1.refs_0_.first_ref = bf16[128,1024]{1,0:T(8,128)(2,1)S(1)} custom-call(bf16[4096,640]{1,0:T(8,128)(2,1)S(1)} %prep.1.refs_0_.q_ref, f32[128,1152]{1,0:T(8,128)S(1)} %mask.1.bias_ref, bf16[32,512,128]{2,1,0:T(8,128)(2,1)S(1)} %copy-done, bf16[1152,640]{1,0:T(8,128)(2,1)S(1)} %join.1.kv_ref, bf16[128,512]{1,0:T(8,128)(2,1)S(1)} %attend0.1.refs_0_.first_ref), custom_call_target="tpu_custom_call" | custom-call | bytes 1024 | tf_op jit(solution)/shard_map/attend4/pallas_call | solution.py:335
  32.2 2.0 %collective-permute-start.10 = (bf16[128,1024]{1,0:T(8,128)(2,1)S(1)}, bf16[128,1024]{1,0:T(8,128)(2,1)S(1)}, u32[]{:S(2)}, u32[]{:S(2)}) collective-permute-start(bf16[128,1024]{1,0:T(8,128)(2,1)S(1)} %attend4.1.refs_0_.first_ref), channel_id=1, source_target_pairs={{0,12},{2,14},{4,8},{6,10},{8,4},{10,6},{12,0},{14,2},{1,13},{3,15... | collective-permute-start | bytes 786440 | tf_op jit(solution)/shard_map/ppermute | solution.py:53
  34.2 1.5 %collective-permute-start.11 = (bf16[128,1024]{1,0:T(8,128)(2,1)S(1)}, bf16[128,1024]{1,0:T(8,128)(2,1)S(1)}, u32[]{:S(2)}, u32[]{:S(2)}) collective-permute-start(bf16[128,1024]{1,0:T(8,128)(2,1)S(1)} %attend4.1.refs_0_.first_ref), channel_id=1, source_target_pairs={{0,2},{2,0},{4,6},{6,4},{8,10},{10,8},{12,14},{14,12},{1,3},{3,1},... | collective-permute-start | bytes 786440 | tf_op jit(solution)/shard_map/ppermute | solution.py:53
  35.8 3.5 %attend12.1.refs_0_.x_ref.first_ref = bf16[128,768]{1,0:T(8,128)(2,1)S(1)} custom-call(bf16[4096,640]{1,0:T(8,128)(2,1)S(1)} %prep.1.refs_0_.q_ref, f32[128,1152]{1,0:T(8,128)S(1)} %mask.1.bias_ref, bf16[32,512,128]{2,1,0:T(8,128)(2,1)S(1)} %copy-done, bf16[1152,640]{1,0:T(8,128)(2,1)S(1)} %join.1.kv_ref, bf16[2,128,512]{2,1,0:T(8,128)(2,1)S(1)} %stack.8.refs_0_), custom_call_target="tpu_custom_call" | custom-call | bytes 1024 | tf_op jit(solution)/shard_map/attend12/pallas_call | solution.py:335
  41.4 1.8 %collective-permute-done.10.second_ref.x_ref.refs_1_ = bf16[128,1024]{1,0:T(8,128)(2,1)S(1)} collective-permute-done((bf16[128,1024]{1,0:T(8,128)(2,1)S(1)}, bf16[128,1024]{1,0:T(8,128)(2,1)S(1)}, u32[]{:S(2)}, u32[]{:S(2)}) %collective-permute-start.10) | collective-permute-done | bytes 262176 | tf_op jit(solution)/shard_map/ppermute | solution.py:53
  43.3 2.8 %collective-permute-start.19 = (bf16[2,128,1024]{2,1,0:T(8,128)(2,1)S(1)}, bf16[2,128,1024]{2,1,0:T(8,128)(2,1)S(1)}, u32[]{:S(2)}, u32[]{:S(2)}) collective-permute-start(bf16[2,128,1024]{2,1,0:T(8,128)(2,1)S(1)} %stack.9.refs_0_), channel_id=1, source_target_pairs={{0,4},{2,6},{4,0},{6,2},{8,12},{10,14},{12,8},{14,10},{1,5},{3,7},... | collective-permute-start | bytes 1572872 | tf_op jit(solution)/shard_map/ppermute | solution.py:53
  48.2 1.6 %collective-permute-start.16 = (bf16[2,128,512]{2,1,0:T(8,128)(2,1)S(1)}, bf16[2,128,512]{2,1,0:T(8,128)(2,1)S(1)}, u32[]{:S(2)}, u32[]{:S(2)}) collective-permute-start(bf16[2,128,512]{2,1,0:T(8,128)(2,1)S(1)} %gate.13.refs_0_), channel_id=1, source_target_pairs={{0,2},{2,0},{4,6},{6,4},{8,10},{10,8},{12,14},{14,12},{1,3},{3,1},... | collective-permute-start | bytes 786440 | tf_op jit(solution)/shard_map/ppermute | solution.py:53
  49.8 4.7 %attend18.1.refs_0_.x_ref.first_ref = bf16[128,1024]{1,0:T(8,128)(2,1)S(1)} custom-call(bf16[4096,640]{1,0:T(8,128)(2,1)S(1)} %prep.1.refs_0_.q_ref, f32[128,1152]{1,0:T(8,128)S(1)} %mask.1.bias_ref, bf16[32,512,128]{2,1,0:T(8,128)(2,1)S(1)} %copy-done, bf16[1152,640]{1,0:T(8,128)(2,1)S(1)} %join.1.kv_ref, bf16[2,128,512]{2,1,0:T(8,128)(2,1)S(1)} %gate.13.refs_0_, ...), custom_call_target="tpu_custom_call" | custom-call | bytes 1024 | tf_op jit(solution)/shard_map/attend18/pallas_call | solution.py:335
  55.6 1.9 %collective-permute-start.14 = (bf16[128,768]{1,0:T(8,128)(2,1)S(1)}, bf16[128,768]{1,0:T(8,128)(2,1)S(1)}, u32[]{:S(2)}, u32[]{:S(2)}) collective-permute-start(bf16[128,768]{1,0:T(8,128)(2,1)S(1)} %gate.12.refs_0_), channel_id=1, source_target_pairs={{0,12},{2,14},{4,8},{6,10},{8,4},{10,6},{12,0},{14,2},{1,13},{3,15... | collective-permute-start | bytes 589832 | tf_op jit(solution)/shard_map/ppermute | solution.py:53
  58.6 3.5 %attend26.1.refs_0_.x_ref.first_ref = bf16[128,768]{1,0:T(8,128)(2,1)S(1)} custom-call(bf16[4096,640]{1,0:T(8,128)(2,1)S(1)} %prep.1.refs_0_.q_ref, f32[128,1152]{1,0:T(8,128)S(1)} %mask.1.bias_ref, bf16[32,512,128]{2,1,0:T(8,128)(2,1)S(1)} %copy-done, bf16[1152,640]{1,0:T(8,128)(2,1)S(1)} %join.1.kv_ref, bf16[128,1024]{1,0:T(8,128)(2,1)S(1)} %attend18.1.refs_0_.x_ref.first_ref), custom_call_target="tpu_custom_call" | custom-call | bytes 1024 | tf_op jit(solution)/shard_map/attend26/pallas_call | solution.py:335
  63.0 3.6 %collective-permute-done.15.refs_2_ = bf16[128,512]{1,0:T(8,128)(2,1)S(1)} collective-permute-done((bf16[128,512]{1,0:T(8,128)(2,1)S(1)}, bf16[128,512]{1,0:T(8,128)(2,1)S(1)}, u32[]{:S(2)}, u32[]{:S(2)}) %collective-permute-start.15) | collective-permute-done | bytes 131104 | tf_op jit(solution)/shard_map/ppermute | solution.py:53
  69.2 2.0 %collective-permute-start.25 = (bf16[128,1024]{1,0:T(8,128)(2,1)S(1)}, bf16[128,1024]{1,0:T(8,128)(2,1)S(1)}, u32[]{:S(2)}, u32[]{:S(2)}) collective-permute-start(bf16[128,1024]{1,0:T(8,128)(2,1)S(1)} %gate.15.refs_0_), channel_id=1, source_target_pairs={{0,12},{2,14},{4,8},{6,10},{8,4},{10,6},{12,0},{14,2},{1,13},{3,15... | collective-permute-start | bytes 786440 | tf_op jit(solution)/shard_map/ppermute | solution.py:53
  73.3 3.1 %collective-permute-done.21.refs_1_.first_ref.refs_2_ = bf16[128,768]{1,0:T(8,128)(2,1)S(1)} collective-permute-done((bf16[128,768]{1,0:T(8,128)(2,1)S(1)}, bf16[128,768]{1,0:T(8,128)(2,1)S(1)}, u32[]{:S(2)}, u32[]{:S(2)}) %collective-permute-start.21) | collective-permute-done | bytes 196640 | tf_op jit(solution)/shard_map/ppermute | solution.py:53
  77.5 1.7 %collective-permute-done.18.x_ref.refs_1_.refs_4_ = bf16[2,128,768]{2,1,0:T(8,128)(2,1)S(1)} collective-permute-done((bf16[2,128,768]{2,1,0:T(8,128)(2,1)S(1)}, bf16[2,128,768]{2,1,0:T(8,128)(2,1)S(1)}, u32[]{:S(2)}, u32[]{:S(2)}) %collective-permute-start.18) | collective-permute-done | bytes 393248 | tf_op jit(solution)/shard_map/ppermute | solution.py:53
  80.7 2.5 %collective-permute-done.25.second_ref.x_ref.refs_1_ = bf16[128,1024]{1,0:T(8,128)(2,1)S(1)} collective-permute-done((bf16[128,1024]{1,0:T(8,128)(2,1)S(1)}, bf16[128,1024]{1,0:T(8,128)(2,1)S(1)}, u32[]{:S(2)}, u32[]{:S(2)}) %collective-permute-start.25) | collective-permute-done | bytes 262176 | tf_op jit(solution)/shard_map/ppermute | solution.py:53
  84.3 1.7 %collective-permute-start.23 = (bf16[128,768]{1,0:T(8,128)(2,1)S(1)}, bf16[128,768]{1,0:T(8,128)(2,1)S(1)}, u32[]{:S(2)}, u32[]{:S(2)}) collective-permute-start(bf16[128,768]{1,0:T(8,128)(2,1)S(1)} %gate.19.refs_0_), channel_id=1, source_target_pairs={{0,12},{2,14},{4,8},{6,10},{8,4},{10,6},{12,0},{14,2},{1,13},{3,15... | collective-permute-start | bytes 589832 | tf_op jit(solution)/shard_map/ppermute | solution.py:53
  86.0 5.9 %collective-permute-done.24.refs_1_.refs_5_ = bf16[2,128,1024]{2,1,0:T(8,128)(2,1)S(1)} collective-permute-done((bf16[2,128,1024]{2,1,0:T(8,128)(2,1)S(1)}, bf16[2,128,1024]{2,1,0:T(8,128)(2,1)S(1)}, u32[]{:S(2)}, u32[]{:S(2)}) %collective-permute-start.24) | collective-permute-done | bytes 524320 | tf_op jit(solution)/shard_map/ppermute | solution.py:53
  93.0 2.8 %project512.1.refs_0_.refs_6_ = f32[2,512,896]{2,1,0:T(8,128)S(1)} custom-call(bf16[4096,896]{1,0:T(8,128)(2,1)S(1)} %bitcast.2, bf16[128,1024]{1,0:T(8,128)(2,1)S(1)} %attend4.1.refs_0_.first_ref, bf16[128,1024]{1,0:T(8,128)(2,1)S(1)} %collective-permute-done.10.second_ref.x_ref.refs_1_, ...), custom_call_target="tpu_custom_call", output_to_operand_aliasing={{}: (7, {})} | custom-call | bytes 1024 | tf_op jit(solution)/shard_map/project512/pallas_call | solution.py:396
  95.8 1.9 %collective-permute-done.23.x_ref.second_ref.refs_1_ = bf16[128,768]{1,0:T(8,128)(2,1)S(1)} collective-permute-done((bf16[128,768]{1,0:T(8,128)(2,1)S(1)}, bf16[128,768]{1,0:T(8,128)(2,1)S(1)}, u32[]{:S(2)}, u32[]{:S(2)}) %collective-permute-start.23) | collective-permute-done | bytes 196640 | tf_op jit(solution)/shard_map/ppermute | solution.py:53
  100.3 5.6 %collective-permute-done.29.refs_8_.refs_3_ = bf16[128,1024]{1,0:T(8,128)(2,1)S(1)} collective-permute-done((bf16[128,1024]{1,0:T(8,128)(2,1)S(1)}, bf16[128,1024]{1,0:T(8,128)(2,1)S(1)}, u32[]{:S(2)}, u32[]{:S(2)}) %collective-permute-start.29) | collective-permute-done | bytes 262176 | tf_op jit(solution)/shard_map/ppermute | solution.py:53
  106.0 2.2 %project1536.1.refs_0_.refs_5_ = f32[2,512,896]{2,1,0:T(8,128)S(1)} custom-call(bf16[4096,896]{1,0:T(8,128)(2,1)S(1)} %bitcast.2, bf16[128,768]{1,0:T(8,128)(2,1)S(1)} %attend12.1.refs_0_.x_ref.first_ref, bf16[128,768]{1,0:T(8,128)(2,1)S(1)} %collective-permute-done.14.second_ref.x_ref.refs_1_, ...), custom_call_target="tpu_custom_call", output_to_operand_aliasing={{}: (7, {})} | custom-call | bytes 1024 | tf_op jit(solution)/shard_map/project1536/pallas_call | solution.py:396
  108.2 2.0 %collective-permute-done.27.second_ref.refs_3_ = bf16[128,768]{1,0:T(8,128)(2,1)S(1)} collective-permute-done((bf16[128,768]{1,0:T(8,128)(2,1)S(1)}, bf16[128,768]{1,0:T(8,128)(2,1)S(1)}, u32[]{:S(2)}, u32[]{:S(2)}) %collective-permute-start.27) | collective-permute-done | bytes 196640 | tf_op jit(solution)/shard_map/ppermute | solution.py:53
  111.7 2.4 %project2304.2.refs_2_ = f32[2,512,896]{2,1,0:T(8,128)S(1)} custom-call(bf16[4096,896]{1,0:T(8,128)(2,1)S(1)} %bitcast.2, bf16[128,1024]{1,0:T(8,128)(2,1)S(1)} %attend18.1.refs_0_.x_ref.first_ref, bf16[128,1024]{1,0:T(8,128)(2,1)S(1)} %collective-permute-done.25.second_ref.x_ref.refs_1_, ...), custom_call_target="tpu_custom_call", output_to_operand_aliasing={{}: (6, {})} | custom-call | bytes 1024 | tf_op jit(solution)/shard_map/project2304/pallas_call | solution.py:396
  114.4 5.7 %collective-permute-done.32.refs_0_ = bf16[2,128,1024]{2,1,0:T(8,128)(2,1)S(1)} collective-permute-done((bf16[2,128,1024]{2,1,0:T(8,128)(2,1)S(1)}, bf16[2,128,1024]{2,1,0:T(8,128)(2,1)S(1)}, u32[]{:S(2)}, u32[]{:S(2)}) %collective-permute-start.32) | collective-permute-done | bytes 524320 | tf_op jit(solution)/shard_map/ppermute | solution.py:53
  (86 shorter events, 29.7 us)
Async XLA Ops:
  1.1 9.0 %collective-permute-start = (bf16[336,128]{1,0:T(8,128)(2,1)S(1)}, bf16[336,128]{1,0:T(8,128)(2,1)S(1)}, u32[]{:S(2)}, u32[]{:S(2)}) collective-permute-start(bf16[336,128]{1,0:T(8,128)(2,1)S(1)} %pack.1.first_ref), channel_id=1, source_target_pairs={{0,12},{2,14},{4,8},{6,10},{8,4},{10,6},{12,0},{14,2},{1,13},{3,15... | collective-permute-start | bytes 258056 | tf_op jit(solution)/shard_map/ppermute | solution.py:53
  10.2 5.9 %collective-permute-start.2 = (bf16[2,336,128]{2,1,0:T(8,128)(2,1)S(1)}, bf16[2,336,128]{2,1,0:T(8,128)(2,1)S(1)}, u32[]{:S(2)}, u32[]{:S(2)}) collective-permute-start(bf16[2,336,128]{2,1,0:T(8,128)(2,1)S(1)} %stack.7.refs_0_), channel_id=1, source_target_pairs={{0,4},{2,6},{4,0},{6,2},{8,12},{10,14},{12,8},{14,10},{1,5},{3,7},... | collective-permute-start | bytes 516104 | tf_op jit(solution)/shard_map/ppermute | solution.py:53
  10.4 7.7 %collective-permute-start.1 = (bf16[2,336,128]{2,1,0:T(8,128)(2,1)S(1)}, bf16[2,336,128]{2,1,0:T(8,128)(2,1)S(1)}, u32[]{:S(2)}, u32[]{:S(2)}) collective-permute-start(bf16[2,336,128]{2,1,0:T(8,128)(2,1)S(1)} %stack.7.refs_0_), channel_id=1, source_target_pairs={{0,2},{2,0},{4,6},{6,4},{8,10},{10,8},{12,14},{14,12},{1,3},{3,1},... | collective-permute-start | bytes 516104 | tf_op jit(solution)/shard_map/ppermute | solution.py:53
  16.1 5.4 %collective-permute-start.3 = (bf16[2,336,128]{2,1,0:T(8,128)(2,1)S(1)}, bf16[2,336,128]{2,1,0:T(8,128)(2,1)S(1)}, u32[]{:S(2)}, u32[]{:S(2)}) collective-permute-start(bf16[2,336,128]{2,1,0:T(8,128)(2,1)S(1)} %collective-permute-done.2.refs_2_), channel_id=1, source_target_pairs={{0,2},{2,0},{4,6},{6,4},{8,10},{10,8},{12,14},{14,12},{1,3},{3,1},... | collective-permute-start | bytes 516104 | tf_op jit(solution)/shard_map/ppermute | solution.py:53
  17.6 5.2 %collective-permute-start.4 = (bf16[2,336,128]{2,1,0:T(8,128)(2,1)S(1)}, bf16[2,336,128]{2,1,0:T(8,128)(2,1)S(1)}, u32[]{:S(2)}, u32[]{:S(2)}) collective-permute-start(bf16[2,336,128]{2,1,0:T(8,128)(2,1)S(1)} %stack.7.refs_0_), channel_id=1, source_target_pairs={{0,1},{1,0},{2,3},{3,2},{4,5},{5,4},{6,7},{7,6},{8,9},{9,8},{10,11... | collective-permute-start | bytes 516104 | tf_op jit(solution)/shard_map/ppermute | solution.py:57
  17.6 5.2 %collective-permute-start.6 = (bf16[2,336,128]{2,1,0:T(8,128)(2,1)S(1)}, bf16[2,336,128]{2,1,0:T(8,128)(2,1)S(1)}, u32[]{:S(2)}, u32[]{:S(2)}) collective-permute-start(bf16[2,336,128]{2,1,0:T(8,128)(2,1)S(1)} %collective-permute-done.2.refs_2_), channel_id=1, source_target_pairs={{0,1},{1,0},{2,3},{3,2},{4,5},{5,4},{6,7},{7,6},{8,9},{9,8},{10,11... | collective-permute-start | bytes 516104 | tf_op jit(solution)/shard_map/ppermute | solution.py:57
  18.1 4.7 %collective-permute-start.5 = (bf16[2,336,128]{2,1,0:T(8,128)(2,1)S(1)}, bf16[2,336,128]{2,1,0:T(8,128)(2,1)S(1)}, u32[]{:S(2)}, u32[]{:S(2)}) collective-permute-start(bf16[2,336,128]{2,1,0:T(8,128)(2,1)S(1)} %collective-permute-done.1.refs_1_), channel_id=1, source_target_pairs={{0,1},{1,0},{2,3},{3,2},{4,5},{5,4},{6,7},{7,6},{8,9},{9,8},{10,11... | collective-permute-start | bytes 516104 | tf_op jit(solution)/shard_map/ppermute | solution.py:57
  25.8 9.9 %collective-permute-start.8 = (bf16[128,512]{1,0:T(8,128)(2,1)S(1)}, bf16[128,512]{1,0:T(8,128)(2,1)S(1)}, u32[]{:S(2)}, u32[]{:S(2)}) collective-permute-start(bf16[128,512]{1,0:T(8,128)(2,1)S(1)} %attend0.1.refs_0_.first_ref), channel_id=1, source_target_pairs={{0,12},{2,14},{4,8},{6,10},{8,4},{10,6},{12,0},{14,2},{1,13},{3,15... | collective-permute-start | bytes 393224 | tf_op jit(solution)/shard_map/ppermute | solution.py:53
  32.2 11.1 %collective-permute-start.10 = (bf16[128,1024]{1,0:T(8,128)(2,1)S(1)}, bf16[128,1024]{1,0:T(8,128)(2,1)S(1)}, u32[]{:S(2)}, u32[]{:S(2)}) collective-permute-start(bf16[128,1024]{1,0:T(8,128)(2,1)S(1)} %attend4.1.refs_0_.first_ref), channel_id=1, source_target_pairs={{0,12},{2,14},{4,8},{6,10},{8,4},{10,6},{12,0},{14,2},{1,13},{3,15... | collective-permute-start | bytes 786440 | tf_op jit(solution)/shard_map/ppermute | solution.py:53
  34.2 12.0 %collective-permute-start.11 = (bf16[128,1024]{1,0:T(8,128)(2,1)S(1)}, bf16[128,1024]{1,0:T(8,128)(2,1)S(1)}, u32[]{:S(2)}, u32[]{:S(2)}) collective-permute-start(bf16[128,1024]{1,0:T(8,128)(2,1)S(1)} %attend4.1.refs_0_.first_ref), channel_id=1, source_target_pairs={{0,2},{2,0},{4,6},{6,4},{8,10},{10,8},{12,14},{14,12},{1,3},{3,1},... | collective-permute-start | bytes 786440 | tf_op jit(solution)/shard_map/ppermute | solution.py:53
  35.7 12.5 %collective-permute-start.9 = (bf16[2,128,512]{2,1,0:T(8,128)(2,1)S(1)}, bf16[2,128,512]{2,1,0:T(8,128)(2,1)S(1)}, u32[]{:S(2)}, u32[]{:S(2)}) collective-permute-start(bf16[2,128,512]{2,1,0:T(8,128)(2,1)S(1)} %stack.8.refs_0_), channel_id=1, source_target_pairs={{0,4},{2,6},{4,0},{6,2},{8,12},{10,14},{12,8},{14,10},{1,5},{3,7},... | collective-permute-start | bytes 786440 | tf_op jit(solution)/shard_map/ppermute | solution.py:53
  39.3 7.9 %collective-permute-start.12 = (bf16[128,768]{1,0:T(8,128)(2,1)S(1)}, bf16[128,768]{1,0:T(8,128)(2,1)S(1)}, u32[]{:S(2)}, u32[]{:S(2)}) collective-permute-start(bf16[128,768]{1,0:T(8,128)(2,1)S(1)} %attend12.1.refs_0_.x_ref.first_ref), channel_id=1, source_target_pairs={{0,2},{2,0},{4,6},{6,4},{8,10},{10,8},{12,14},{14,12},{1,3},{3,1},... | collective-permute-start | bytes 589832 | tf_op jit(solution)/shard_map/ppermute | solution.py:53
  40.2 9.6 %collective-permute-start.13 = (bf16[128,512]{1,0:T(8,128)(2,1)S(1)}, bf16[128,512]{1,0:T(8,128)(2,1)S(1)}, u32[]{:S(2)}, u32[]{:S(2)}) collective-permute-start(bf16[128,512]{1,0:T(8,128)(2,1)S(1)} %gate.11.refs_0_), channel_id=1, source_target_pairs={{0,2},{2,0},{4,6},{6,4},{8,10},{10,8},{12,14},{14,12},{1,3},{3,1},... | collective-permute-start | bytes 393224 | tf_op jit(solution)/shard_map/ppermute | solution.py:53
  43.3 25.9 %collective-permute-start.19 = (bf16[2,128,1024]{2,1,0:T(8,128)(2,1)S(1)}, bf16[2,128,1024]{2,1,0:T(8,128)(2,1)S(1)}, u32[]{:S(2)}, u32[]{:S(2)}) collective-permute-start(bf16[2,128,1024]{2,1,0:T(8,128)(2,1)S(1)} %stack.9.refs_0_), channel_id=1, source_target_pairs={{0,4},{2,6},{4,0},{6,2},{8,12},{10,14},{12,8},{14,10},{1,5},{3,7},... | collective-permute-start | bytes 1572872 | tf_op jit(solution)/shard_map/ppermute | solution.py:53
  48.2 13.8 %collective-permute-start.16 = (bf16[2,128,512]{2,1,0:T(8,128)(2,1)S(1)}, bf16[2,128,512]{2,1,0:T(8,128)(2,1)S(1)}, u32[]{:S(2)}, u32[]{:S(2)}) collective-permute-start(bf16[2,128,512]{2,1,0:T(8,128)(2,1)S(1)} %gate.13.refs_0_), channel_id=1, source_target_pairs={{0,2},{2,0},{4,6},{6,4},{8,10},{10,8},{12,14},{14,12},{1,3},{3,1},... | collective-permute-start | bytes 786440 | tf_op jit(solution)/shard_map/ppermute | solution.py:53
  54.5 12.1 %collective-permute-start.17 = (bf16[128,1024]{1,0:T(8,128)(2,1)S(1)}, bf16[128,1024]{1,0:T(8,128)(2,1)S(1)}, u32[]{:S(2)}, u32[]{:S(2)}) collective-permute-start(bf16[128,1024]{1,0:T(8,128)(2,1)S(1)} %attend18.1.refs_0_.x_ref.first_ref), channel_id=1, source_target_pairs={{0,2},{2,0},{4,6},{6,4},{8,10},{10,8},{12,14},{14,12},{1,3},{3,1},... | collective-permute-start | bytes 786440 | tf_op jit(solution)/shard_map/ppermute | solution.py:53
  55.6 12.4 %collective-permute-start.14 = (bf16[128,768]{1,0:T(8,128)(2,1)S(1)}, bf16[128,768]{1,0:T(8,128)(2,1)S(1)}, u32[]{:S(2)}, u32[]{:S(2)}) collective-permute-start(bf16[128,768]{1,0:T(8,128)(2,1)S(1)} %gate.12.refs_0_), channel_id=1, source_target_pairs={{0,12},{2,14},{4,8},{6,10},{8,4},{10,6},{12,0},{14,2},{1,13},{3,15... | collective-permute-start | bytes 589832 | tf_op jit(solution)/shard_map/ppermute | solution.py:53
  57.5 9.2 %collective-permute-start.15 = (bf16[128,512]{1,0:T(8,128)(2,1)S(1)}, bf16[128,512]{1,0:T(8,128)(2,1)S(1)}, u32[]{:S(2)}, u32[]{:S(2)}) collective-permute-start(bf16[128,512]{1,0:T(8,128)(2,1)S(1)} %attend0.1.refs_0_.first_ref), channel_id=1, source_target_pairs={{0,2},{2,0},{4,6},{6,4},{8,10},{10,8},{12,14},{14,12},{1,3},{3,1},... | collective-permute-start | bytes 393224 | tf_op jit(solution)/shard_map/ppermute | solution.py:53
  62.1 10.2 %collective-permute-start.20 = (bf16[128,1024]{1,0:T(8,128)(2,1)S(1)}, bf16[128,1024]{1,0:T(8,128)(2,1)S(1)}, u32[]{:S(2)}, u32[]{:S(2)}) collective-permute-start(bf16[128,1024]{1,0:T(8,128)(2,1)S(1)} %gate.14.refs_6_), channel_id=1, source_target_pairs={{0,2},{2,0},{4,6},{6,4},{8,10},{10,8},{12,14},{14,12},{1,3},{3,1},... | collective-permute-start | bytes 786440 | tf_op jit(solution)/shard_map/ppermute | solution.py:53
  68.0 11.3 %collective-permute-start.18 = (bf16[2,128,768]{2,1,0:T(8,128)(2,1)S(1)}, bf16[2,128,768]{2,1,0:T(8,128)(2,1)S(1)}, u32[]{:S(2)}, u32[]{:S(2)}) collective-permute-start(bf16[2,128,768]{2,1,0:T(8,128)(2,1)S(1)} %stack.10.refs_0_), channel_id=1, source_target_pairs={{0,4},{2,6},{4,0},{6,2},{8,12},{10,14},{12,8},{14,10},{1,5},{3,7},... | collective-permute-start | bytes 1179656 | tf_op jit(solution)/shard_map/ppermute | solution.py:53
  68.5 8.0 %collective-permute-start.21 = (bf16[128,768]{1,0:T(8,128)(2,1)S(1)}, bf16[128,768]{1,0:T(8,128)(2,1)S(1)}, u32[]{:S(2)}, u32[]{:S(2)}) collective-permute-start(bf16[128,768]{1,0:T(8,128)(2,1)S(1)} %attend26.1.refs_0_.x_ref.first_ref), channel_id=1, source_target_pairs={{0,2},{2,0},{4,6},{6,4},{8,10},{10,8},{12,14},{14,12},{1,3},{3,1},... | collective-permute-start | bytes 589832 | tf_op jit(solution)/shard_map/ppermute | solution.py:53
  69.2 14.1 %collective-permute-start.25 = (bf16[128,1024]{1,0:T(8,128)(2,1)S(1)}, bf16[128,1024]{1,0:T(8,128)(2,1)S(1)}, u32[]{:S(2)}, u32[]{:S(2)}) collective-permute-start(bf16[128,1024]{1,0:T(8,128)(2,1)S(1)} %gate.15.refs_0_), channel_id=1, source_target_pairs={{0,12},{2,14},{4,8},{6,10},{8,4},{10,6},{12,0},{14,2},{1,13},{3,15... | collective-permute-start | bytes 786440 | tf_op jit(solution)/shard_map/ppermute | solution.py:53
  72.3 8.4 %collective-permute-start.22 = (bf16[128,768]{1,0:T(8,128)(2,1)S(1)}, bf16[128,768]{1,0:T(8,128)(2,1)S(1)}, u32[]{:S(2)}, u32[]{:S(2)}) collective-permute-start(bf16[128,768]{1,0:T(8,128)(2,1)S(1)} %gate.16.refs_0_), channel_id=1, source_target_pairs={{0,2},{2,0},{4,6},{6,4},{8,10},{10,8},{12,14},{14,12},{1,3},{3,1},... | collective-permute-start | bytes 589832 | tf_op jit(solution)/shard_map/ppermute | solution.py:53
  76.5 15.4 %collective-permute-start.24 = (bf16[2,128,1024]{2,1,0:T(8,128)(2,1)S(1)}, bf16[2,128,1024]{2,1,0:T(8,128)(2,1)S(1)}, u32[]{:S(2)}, u32[]{:S(2)}) collective-permute-start(bf16[2,128,1024]{2,1,0:T(8,128)(2,1)S(1)} %gate.17.refs_0_), channel_id=1, source_target_pairs={{0,2},{2,0},{4,6},{6,4},{8,10},{10,8},{12,14},{14,12},{1,3},{3,1},... | collective-permute-start | bytes 1572872 | tf_op jit(solution)/shard_map/ppermute | solution.py:53
  83.3 15.8 %collective-permute-start.31 = (bf16[2,128,1024]{2,1,0:T(8,128)(2,1)S(1)}, bf16[2,128,1024]{2,1,0:T(8,128)(2,1)S(1)}, u32[]{:S(2)}, u32[]{:S(2)}) collective-permute-start(bf16[2,128,1024]{2,1,0:T(8,128)(2,1)S(1)} %stack.11.refs_0_), channel_id=1, source_target_pairs={{0,4},{2,6},{4,0},{6,2},{8,12},{10,14},{12,8},{14,10},{1,5},{3,7},... | collective-permute-start | bytes 1572872 | tf_op jit(solution)/shard_map/ppermute | solution.py:53
  83.4 16.9 %collective-permute-start.28 = (bf16[2,128,768]{2,1,0:T(8,128)(2,1)S(1)}, bf16[2,128,768]{2,1,0:T(8,128)(2,1)S(1)}, u32[]{:S(2)}, u32[]{:S(2)}) collective-permute-start(bf16[2,128,768]{2,1,0:T(8,128)(2,1)S(1)} %gate.18.refs_0_), channel_id=1, source_target_pairs={{0,2},{2,0},{4,6},{6,4},{8,10},{10,8},{12,14},{14,12},{1,3},{3,1},... | collective-permute-start | bytes 1179656 | tf_op jit(solution)/shard_map/ppermute | solution.py:53
  84.3 13.4 %collective-permute-start.23 = (bf16[128,768]{1,0:T(8,128)(2,1)S(1)}, bf16[128,768]{1,0:T(8,128)(2,1)S(1)}, u32[]{:S(2)}, u32[]{:S(2)}) collective-permute-start(bf16[128,768]{1,0:T(8,128)(2,1)S(1)} %gate.19.refs_0_), channel_id=1, source_target_pairs={{0,12},{2,14},{4,8},{6,10},{8,4},{10,6},{12,0},{14,2},{1,13},{3,15... | collective-permute-start | bytes 589832 | tf_op jit(solution)/shard_map/ppermute | solution.py:53
  91.9 14.0 %collective-permute-start.29 = (bf16[128,1024]{1,0:T(8,128)(2,1)S(1)}, bf16[128,1024]{1,0:T(8,128)(2,1)S(1)}, u32[]{:S(2)}, u32[]{:S(2)}) collective-permute-start(bf16[128,1024]{1,0:T(8,128)(2,1)S(1)} %gate.20.refs_7_), channel_id=1, source_target_pairs={{0,2},{2,0},{4,6},{6,4},{8,10},{10,8},{12,14},{14,12},{1,3},{3,1},... | collective-permute-start | bytes 786440 | tf_op jit(solution)/shard_map/ppermute | solution.py:53
  97.7 12.5 %collective-permute-start.27 = (bf16[128,768]{1,0:T(8,128)(2,1)S(1)}, bf16[128,768]{1,0:T(8,128)(2,1)S(1)}, u32[]{:S(2)}, u32[]{:S(2)}) collective-permute-start(bf16[128,768]{1,0:T(8,128)(2,1)S(1)} %gate.21.refs_0_), channel_id=1, source_target_pairs={{0,2},{2,0},{4,6},{6,4},{8,10},{10,8},{12,14},{14,12},{1,3},{3,1},... | collective-permute-start | bytes 589832 | tf_op jit(solution)/shard_map/ppermute | solution.py:53
  99.1 21.0 %collective-permute-start.32 = (bf16[2,128,1024]{2,1,0:T(8,128)(2,1)S(1)}, bf16[2,128,1024]{2,1,0:T(8,128)(2,1)S(1)}, u32[]{:S(2)}, u32[]{:S(2)}) collective-permute-start(bf16[2,128,1024]{2,1,0:T(8,128)(2,1)S(1)} %collective-permute-done.31.refs_4_), channel_id=1, source_target_pairs={{0,2},{2,0},{4,6},{6,4},{8,10},{10,8},{12,14},{14,12},{1,3},{3,1},... | collective-permute-start | bytes 1572872 | tf_op jit(solution)/shard_map/ppermute | solution.py:53
  99.8 11.9 %collective-permute-start.26 = (bf16[2,128,768]{2,1,0:T(8,128)(2,1)S(1)}, bf16[2,128,768]{2,1,0:T(8,128)(2,1)S(1)}, u32[]{:S(2)}, u32[]{:S(2)}) collective-permute-start(bf16[2,128,768]{2,1,0:T(8,128)(2,1)S(1)} %stack.12.refs_7_), channel_id=1, source_target_pairs={{0,4},{2,6},{4,0},{6,2},{8,12},{10,14},{12,8},{14,10},{1,5},{3,7},... | collective-permute-start | bytes 1179656 | tf_op jit(solution)/shard_map/ppermute | solution.py:53
  110.2 10.7 %collective-permute-start.30 = (bf16[2,128,768]{2,1,0:T(8,128)(2,1)S(1)}, bf16[2,128,768]{2,1,0:T(8,128)(2,1)S(1)}, u32[]{:S(2)}, u32[]{:S(2)}) collective-permute-start(bf16[2,128,768]{2,1,0:T(8,128)(2,1)S(1)} %stack.13.refs_6_), channel_id=1, source_target_pairs={{0,4},{2,6},{4,0},{6,2},{8,12},{10,14},{12,8},{14,10},{1,5},{3,7},... | collective-permute-start | bytes 1179656 | tf_op jit(solution)/shard_map/ppermute | solution.py:53
  (7 other events, 60.0 us)
